TPU v7x, 128 devices: a whole 4x4x4 slice. The times are simulated.
128 devices in a mesh: strike: 4 (over x), dip: 8 (over y, core), layer: 4 (over z).
Axes of the slice: x: 4, y: 4, z: 4, core: 2. Of those that a mesh axis runs over, the one named last changes fastest.
Arguments:
- perm_class: int32 [64, 128, 512], P('strike', 'dip', 'layer'), may hold values from 0 to 15
- perm_table: float32 [16], replicated, may hold values from 0.3 to 3
- boreholes: int32 [32], replicated, may hold values from 0 to 4194303
- start_guess: float32 [32, 64, 128, 512], P(None, 'strike', 'dip', 'layer'), may hold values from -0.005859375 to 0.005859375
Outputs:
- solution: float32 [32, 64, 128, 512], P(None, 'strike', 'dip', 'layer')
- residual: float32 [32, 64, 128, 512], P(None, 'strike', 'dip', 'layer')
Inputs may be any that keep to these rules, and one draw needn't show every extreme that they name: boreholes[j] is the flat index (x * 128 + y) * 512 + z of the cell that right-hand side j drains.
All inputs are finite; a program needn't handle non-finite values.
Results may differ from a plain program's by a relative error of at most 0.0003.
Values sent between devices are 32-bit elements; how exact they have to be, the bound alone decides.
No kernel may reach another device: no remote copies, remote signals or barrier semaphores. Data moves between devices by JAX's collectives and lax.ppermute only.
A program may use at most 128 MiB of HBM per device.

v0:
```python
import jax
import jax.numpy as jnp
from jax import lax
from jax.sharding import PartitionSpec as P

ITERS = 2


leakage = 0.01
highest = lax.Precision.HIGHEST


def padded_2(cells, sides, width):
    for axis, dim in sides:
        count = lax.axis_size(axis)
        ends = count - 1
        head = lax.slice_in_dim(cells, 0, width, axis=dim)
        tail = lax.slice_in_dim(cells, cells.shape[dim] - width, cells.shape[dim], axis=dim)
        cells = jnp.concatenate(
            [
                lax.ppermute(tail, axis, [(i, (i + 1) % count) for i in range(ends)]),
                cells,
                lax.ppermute(head, axis, [((i + 1) % count, i) for i in range(ends)]),
            ],
            axis=dim,
        )
    return cells


def face_weight(center_k, beside_k):
    summed = center_k + beside_k
    divisor = jnp.where(summed > 0.0, summed, 1.0)
    return jnp.where(summed > 0.0, 2.0 * center_k * beside_k / divisor, 0.0)


def face_weights(padded_perm):
    center = padded_perm[1:-1, 1:-1, 1:-1]
    return (
        face_weight(center, padded_perm[:-2, 1:-1, 1:-1]),
        face_weight(center, padded_perm[2:, 1:-1, 1:-1]),
        face_weight(center, padded_perm[1:-1, :-2, 1:-1]),
        face_weight(center, padded_perm[1:-1, 2:, 1:-1]),
        face_weight(center, padded_perm[1:-1, 1:-1, :-2]),
        face_weight(center, padded_perm[1:-1, 1:-1, 2:]),
    )


def operate(padded, weights):
    center = padded[:, 1:-1, 1:-1, 1:-1]
    result = leakage * center
    result = result + weights[0][None] * (center - padded[:, :-2, 1:-1, 1:-1])
    result = result + weights[1][None] * (center - padded[:, 2:, 1:-1, 1:-1])
    result = result + weights[2][None] * (center - padded[:, 1:-1, :-2, 1:-1])
    result = result + weights[3][None] * (center - padded[:, 1:-1, 2:, 1:-1])
    result = result + weights[4][None] * (center - padded[:, 1:-1, 1:-1, :-2])
    result = result + weights[5][None] * (center - padded[:, 1:-1, 1:-1, 2:])
    return result


def products(former, latter):
    left_rows = former.reshape(former.shape[0], -1)
    right_rows = latter.reshape(latter.shape[0], -1)
    return lax.dot_general(
        left_rows,
        right_rows,
        (((1,), (1,)), ((), ())),
        precision=highest,
        preferred_element_type=jnp.float32,
    )


def combine(mixing, field):
    rows = field.reshape(field.shape[0], -1)
    mixed = lax.dot_general(
        mixing,
        rows,
        (((0,), (0,)), ((), ())),
        precision=highest,
        preferred_element_type=jnp.float32,
    )
    return mixed.reshape(field.shape)


def spd_solve(matrix, targets):
    factor = jnp.linalg.cholesky(matrix)
    partial_sol = lax.linalg.triangular_solve(factor, targets, left_side=True, lower=True)
    return lax.linalg.triangular_solve(
        factor, partial_sol, left_side=True, lower=True, transpose_a=True
    )


def sources(boreholes, extent, anchors, totals, margin):
    size_x, size_y, size_z = (extent[1], extent[2], extent[3])
    along_x = anchors[0] - margin + lax.broadcasted_iota(jnp.int32, (size_x + 2 * margin, 1, 1), 0)
    along_y = anchors[1] - margin + lax.broadcasted_iota(jnp.int32, (1, size_y + 2 * margin, 1), 1)
    along_z = anchors[2] - margin + lax.broadcasted_iota(jnp.int32, (1, 1, size_z + 2 * margin), 2)
    inside = (along_x >= 0) & (along_x < totals[0]) & (along_y >= 0) & (along_y < totals[1])
    inside = inside & (along_z >= 0) & (along_z < totals[2])
    flat_index = (along_x * totals[1] + along_y) * totals[2] + along_z
    matched = inside[None] & (flat_index[None] == boreholes[:, None, None, None])
    return jnp.where(matched, 1.0, 0.0).astype(jnp.float32)


def shards(perm_class, perm_table, boreholes, start_guess):
    columns, size_x, size_y, size_z = start_guess.shape
    anchors = (
        lax.axis_index("strike") * size_x,
        lax.axis_index("dip") * size_y,
        lax.axis_index("layer") * size_z,
    )
    totals = (
        size_x * lax.axis_size("strike"),
        size_y * lax.axis_size("dip"),
        size_z * lax.axis_size("layer"),
    )
    levels = lax.broadcasted_iota(jnp.int32, (perm_table.shape[0], 1, 1, 1), 0)
    permeability = jnp.sum(
        jnp.where(perm_class[None] == levels, perm_table[:, None, None, None], 0.0), axis=0
    )
    stacked = jnp.concatenate([start_guess, permeability[None]], axis=0)
    padded = padded_2(stacked, (("strike", 1), ("dip", 2), ("layer", 3)), 1)
    weights = face_weights(padded[columns])
    residual = sources(boreholes, start_guess.shape, anchors, totals, 0) - operate(
        padded[:columns], weights
    )
    applied = operate(padded_2(residual, (("strike", 1), ("dip", 2), ("layer", 3)), 1), weights)
    solution = start_guess
    direction = residual
    norm_now = None
    advance = None
    for iteration in range(ITERS):
        norm_fresh = lax.psum(products(residual, residual), ("strike", "dip", "layer"))
        if iteration == 0:
            norm_now = norm_fresh
        else:
            conjugate = spd_solve(norm_now, norm_fresh)
            direction = residual + combine(conjugate, direction)
            applied = operate(
                padded_2(direction, (("strike", 1), ("dip", 2), ("layer", 3)), 1), weights
            )
            norm_now = norm_fresh
        curvature = lax.psum(products(direction, applied), ("strike", "dip", "layer"))
        advance = spd_solve(curvature, norm_now)
        solution = solution + combine(advance, direction)
        residual = residual - combine(advance, applied)
    return (solution, residual)


def solution(mesh):
    placed = (P("strike", "dip", "layer"), P(), P(), P(None, "strike", "dip", "layer"))
    return jax.shard_map(
        shards,
        mesh=mesh,
        in_specs=placed,
        out_specs=(P(None, "strike", "dip", "layer"), P(None, "strike", "dip", "layer")),
        check_vma=False,
    )
```

profile of v0, /device:TPU:1, one launch (start us, length us, event | category | flops | bytes accessed | tf_op | source)
XLA Modules:
  0.0 554.0 jit_solution(374241403212673483)
XLA Ops:
  0.6 4.7 copy.126
  8.7 4.6 collective-permute-start
  13.5 4.8 collective-permute-done.1
  36.0 11.3 %fusion.100 = (f32[33,18,18,1]{3,0,2,1:T(8,128)}, f32[33,18,18,1]{3,0,2,1:T(8,128)}) fusion(f32[33,18,18,128]{3,0,2,1:T(8,128)} %pad_maximum_fusion), kind=kLoop, calls=%fused_computation.227 | loop fusion | bytes 171072 | tf_op jit(solution)/shard_map/slice | solution.py:18
  47.3 4.9 copy.105
  53.5 5.0 copy.104
  62.8 4.6 copy.107
  67.4 4.7 copy.106
  78.6 15.0 %fusion.39 = f32[32,16,16,128]{3,0,2,1:T(8,128)S(1)} fusion(f32[32,16,16,128]{3,0,2,1:T(8,128)S(1)} %copy-done.9, f32[33,18,18,1]{3,0,2,1:T(8,128)S(1)} %bitcast.141, f32[33,18,1,128]{3,0,2,1:T(8,128)S(1)} %copy-done.15, f32[33,18,1,128]{3,0,2,1:T(8,128)S(1)} %copy-done.17, f32[33,1,16,128]{3,0,2,1:T(8,128)S(1)} %collective-permute-done.1, ...), kind=kLoop, calls=%fused_computation.85 | loop fusion | flops 49283072 | bytes 10704544 | tf_op jit(solution)/shard_map/sub | solution.py:123
  94.9 4.9 collective-permute-start.6
  104.9 6.3 %collective-permute-start.8 = (f32[32,18,1,128]{3,0,2,1:T(8,128)S(1)}, f32[32,18,1,128]{3,0,2,1:T(8,128)S(1)}, u32[]{:S(2)}, u32[]{:S(2)}) collective-permute-start(f32[32,18,1,128]{3,0,2,1:T(8,128)S(1)} %get-tuple-element.25), channel_id=1, source_target_pairs={{0,4},{4,8},{8,12},{12,16},{16,20},{20,24},{24,28},{1,5},{5,9},{9,... | collective-permute-start | bytes 884744 | tf_op jit(solution)/shard_map/ppermute | solution.py:21
  115.7 6.2 %fusion.102 = (f32[32,18,18,1]{3,0,2,1:T(8,128)}, f32[32,18,18,1]{3,0,2,1:T(8,128)}) fusion(f32[32,18,18,128]{3,0,2,1:T(8,128)S(1)} %pad_maximum_fusion.1), kind=kLoop, calls=%fused_computation.229 | loop fusion | bytes 165888 | tf_op jit(solution)/shard_map/slice | solution.py:18
  131.9 4.4 collective-permute-start.10
  136.4 6.9 %convolution_bitcast_fusion.5 = f32[32,32]{0,1:T(8,128)S(1)} fusion(f32[32,16,16,128]{3,0,2,1:T(8,128)} %copy-done), kind=kOutput, calls=%fused_computation.145 | convolution fusion | flops 402653184 | bytes 4198400 | tf_op jit(solution)/shard_map/dot_general | solution.py:63
  159.0 15.9 %fusion.20 = f32[32,16,16,128]{3,0,2,1:T(8,128)S(1)} fusion(f32[32,16,16,128]{3,0,2,1:T(8,128)} %copy-done, f32[32,18,18,1]{3,0,2,1:T(8,128)} %copy.119, f32[32,18,1,128]{3,0,2,1:T(8,128)S(1)} %collective-permute-done.9, f32[32,18,1,128]{3,0,2,1:T(8,128)S(1)} %collective-permute-done.8, f32[32,1,16,128]{3,0,2,1:T(8,128)S(1)} %collective-permute-done.7, ...), kind=kLoop, calls=%fused_computation.48 | loop fusion | flops 38797312 | bytes 10372096 | tf_op jit(solution)/shard_map/add | solution.py:56
  178.5 4.4 copy.127
  182.9 68.4 %all-reduce = (f32[32,32]{0,1:T(8,128)S(1)}, f32[32,32]{0,1:T(8,128)S(1)}) all-reduce(f32[32,32]{0,1:T(8,128)S(1)} %convolution_bitcast_fusion.5, f32[32,32]{0,1:T(8,128)S(1)} %convolution_bitcast_fusion.6), channel_id=1, replica_groups=mesh['strike'=4,'dip'=8,'layer'=4] {'strike','dip','layer'}, use_global_device_ids=true, to_apply=%region_4.6 | all-reduce | flops 2048 | bytes 16384 | tf_op jit(solution)/shard_map/psum | solution.py:132
  258.6 4.6 copy.197
  265.4 5.9 %fusion.68 = f32[32,16,16,128]{3,0,2,1:T(8,128)S(1)} fusion(f32[32,16,16,128]{3,0,2,1:T(8,128)S(1)} %copy-done.3, f32[32,32,1,1]{0,1,3,2:T(8,128)S(1)} %convolution_bitcast_fusion.4, f32[16,16,128,32]{2,1,0,3:T(8,128)S(1)} %bitcast.148), kind=kOutput, calls=%fused_computation.136 | convolution fusion | flops 403701760 | bytes 12587008 | tf_op jit(solution)/shard_map/dot_general | solution.py:74
  277.0 62.6 %psum.30 = f32[32,32]{1,0:T(8,128)S(1)} all-reduce(f32[32,32]{1,0:T(8,128)S(1)} %convolution_bitcast_fusion.3), channel_id=1, replica_groups=mesh['strike'=4,'dip'=8,'layer'=4] {'strike','dip','layer'}, use_global_device_ids=true, to_apply=%region_5.9 | all-reduce | flops 1024 | bytes 8192 | tf_op jit(solution)/shard_map/psum | solution.py:132
  346.7 9.3 %fusion.65 = f32[32,16,16,128]{3,0,2,1:T(8,128)S(1)} fusion(f32[32,16,16,128]{3,0,2,1:T(8,128)} %copy-done.10, f32[32,32,1,1]{0,1,3,2:T(8,128)S(1)} %convolution_bitcast_fusion.2, f32[16,16,128,32]{2,1,0,3:T(8,128)} %bitcast.142), kind=kOutput, calls=%fused_computation.135 | convolution fusion | flops 403701760 | bytes 12587008 | tf_op jit(solution)/shard_map/dot_general | solution.py:74
  377.0 6.2 %fusion.101 = (f32[32,18,18,1]{3,0,2,1:T(8,128)}, f32[32,18,18,1]{3,0,2,1:T(8,128)}) fusion(f32[32,18,18,128]{3,0,2,1:T(8,128)S(1)} %pad_maximum_fusion.2), kind=kLoop, calls=%fused_computation.228 | loop fusion | bytes 165888 | tf_op jit(solution)/shard_map/slice | solution.py:18
  388.9 4.3 copy.133
  393.3 4.5 collective-permute-start.16
  397.8 10.0 %fusion.63 = f32[32,16,16,128]{3,0,2,1:T(8,128)} fusion(f32[32,32,1,1]{0,1,3,2:T(8,128)S(1)} %convolution_bitcast_fusion.4, f32[16,16,128,32]{2,1,0,3:T(8,128)} %bitcast.143), kind=kOutput, calls=%fused_computation.133 | convolution fusion | flops 402653184 | bytes 8392704 | tf_op jit(solution)/shard_map/dot_general | solution.py:74
  423.6 16.4 %fusion.2 = f32[32,16,16,128]{3,0,2,1:T(8,128)S(1)} fusion(f32[32,16,16,128]{3,0,2,1:T(8,128)} %copy-done.4, f32[32,18,18,1]{3,0,2,1:T(8,128)} %copy.136, f32[32,18,1,128]{3,0,2,1:T(8,128)S(1)} %collective-permute-done.15, f32[32,18,1,128]{3,0,2,1:T(8,128)S(1)} %collective-permute-done.14, f32[32,1,16,128]{3,0,2,1:T(8,128)S(1)} %collective-permute-done.13, ...), kind=kLoop, calls=%fused_computation.12 | loop fusion | flops 38797312 | bytes 10372096 | tf_op jit(solution)/shard_map/add | solution.py:56
  443.6 4.4 copy.142
  448.0 65.9 %psum.31 = f32[32,32]{0,1:T(8,128)S(1)} all-reduce(f32[32,32]{0,1:T(8,128)S(1)} %convolution_bitcast_fusion.1), channel_id=1, replica_groups=mesh['strike'=4,'dip'=8,'layer'=4] {'strike','dip','layer'}, use_global_device_ids=true, to_apply=%region_6.10 | all-reduce | flops 1024 | bytes 8192 | tf_op jit(solution)/shard_map/psum | solution.py:142
  521.1 13.1 %add_add_fusion = f32[32,16,16,128]{3,0,2,1:T(8,128)S(1)} fusion(f32[32,16,16,128]{3,0,2,1:T(8,128)} %fusion.63, f32[32,32,1,1]{0,1,3,2:T(8,128)S(1)} %convolution_bitcast_fusion, f32[16,16,128,32]{2,1,0,3:T(8,128)} %bitcast.144, f32[32,16,16,128]{3,2,1,0:T(8,128)} %param.12), kind=kOutput, calls=%fused_computation.130 | convolution fusion | flops 404750336 | bytes 16781312 | tf_op jit(solution)/shard_map/dot_general | solution.py:74
  534.2 4.4 copy.145
  543.5 5.9 %fusion.73 = f32[32,16,16,128]{3,0,2,1:T(8,128)S(1)} fusion(f32[32,16,16,128]{3,0,2,1:T(8,128)S(1)} %copy-done.11, f32[32,32,1,1]{0,1,3,2:T(8,128)S(1)} %convolution_bitcast_fusion, f32[16,16,128,32]{2,1,0,3:T(8,128)S(1)} %bitcast.147), kind=kOutput, calls=%fused_computation.137 | convolution fusion | flops 403701760 | bytes 12587008 | tf_op jit(solution)/shard_map/dot_general | solution.py:74
  549.4 4.4 copy.146
  (163 shorter events, 153.3 us)
Async XLA Ops:
  7.4 10.9 %collective-permute-start.1 = (f32[33,1,16,128]{3,0,2,1:T(8,128)S(1)}, f32[33,1,16,128]{3,0,2,1:T(8,128)S(1)}, u32[]{:S(2)}, u32[]{:S(2)}) collective-permute-start(f32[33,1,16,128]{3,0,2,1:T(8,128)S(1)} %get-tuple-element.28), channel_id=1, source_target_pairs={{32,0},{64,32},{96,64},{33,1},{65,33},{97,65},{34,2},{66,34},{98,6... | collective-permute-start | bytes 811016 | tf_op jit(solution)/shard_map/ppermute | solution.py:23
  8.7 10.4 %collective-permute-start = (f32[33,1,16,128]{3,0,2,1:T(8,128)S(1)}, f32[33,1,16,128]{3,0,2,1:T(8,128)S(1)}, u32[]{:S(2)}, u32[]{:S(2)}) collective-permute-start(f32[33,1,16,128]{3,0,2,1:T(8,128)S(1)} %get-tuple-element.27), channel_id=1, source_target_pairs={{0,32},{32,64},{64,96},{1,33},{33,65},{65,97},{2,34},{34,66},{66,9... | collective-permute-start | bytes 811016 | tf_op jit(solution)/shard_map/ppermute | solution.py:21
  13.3 19.4 %copy-start.8 = (f32[32,16,16,128]{3,0,2,1:T(8,128)S(1)}, f32[32,16,16,128]{3,0,2,1:T(8,128)}, u32[]{:S(2)}) copy-start(f32[32,16,16,128]{3,0,2,1:T(8,128)} %copy-done.7) | copy-start | bytes 12582916
  20.2 10.6 %collective-permute-start.3 = (f32[33,18,1,128]{3,0,2,1:T(8,128)S(1)}, f32[33,18,1,128]{3,0,2,1:T(8,128)S(1)}, u32[]{:S(2)}, u32[]{:S(2)}) collective-permute-start(f32[33,18,1,128]{3,0,2,1:T(8,128)S(1)} %get-tuple-element.22), channel_id=1, source_target_pairs={{4,0},{8,4},{12,8},{16,12},{20,16},{24,20},{28,24},{5,1},{9,5},{13... | collective-permute-start | bytes 912392 | tf_op jit(solution)/shard_map/ppermute | solution.py:23
  24.2 7.8 %collective-permute-start.2 = (f32[33,18,1,128]{3,0,2,1:T(8,128)S(1)}, f32[33,18,1,128]{3,0,2,1:T(8,128)S(1)}, u32[]{:S(2)}, u32[]{:S(2)}) collective-permute-start(f32[33,18,1,128]{3,0,2,1:T(8,128)S(1)} %get-tuple-element.21), channel_id=1, source_target_pairs={{0,4},{4,8},{8,12},{12,16},{16,20},{20,24},{24,28},{1,5},{5,9},{9,... | collective-permute-start | bytes 912392 | tf_op jit(solution)/shard_map/ppermute | solution.py:21
  52.2 10.6 %collective-permute-start.5 = (f32[33,18,18,1]{0,3,2,1:T(1,128)S(1)}, f32[33,18,18,1]{0,3,2,1:T(1,128)S(1)}, u32[]{:S(2)}, u32[]{:S(2)}) collective-permute-start(f32[33,18,18,1]{0,3,2,1:T(1,128)S(1)} %copy.105), channel_id=1, source_target_pairs={{1,0},{2,1},{3,2},{5,4},{6,5},{7,6},{9,8},{10,9},{11,10},{13,12},{... | collective-permute-start | bytes 128312 | tf_op jit(solution)/shard_map/ppermute | solution.py:23
  58.5 8.9 %collective-permute-start.4 = (f32[33,18,18,1]{0,3,2,1:T(1,128)S(1)}, f32[33,18,18,1]{0,3,2,1:T(1,128)S(1)}, u32[]{:S(2)}, u32[]{:S(2)}) collective-permute-start(f32[33,18,18,1]{0,3,2,1:T(1,128)S(1)} %copy.104), channel_id=1, source_target_pairs={{0,1},{1,2},{2,3},{4,5},{5,6},{6,7},{8,9},{9,10},{10,11},{12,13},{... | collective-permute-start | bytes 128312 | tf_op jit(solution)/shard_map/ppermute | solution.py:21
  67.3 9.3 %slice-start = ((s8[6635520]{0:T(1024)(128)(4,1)}), s8[2441216]{0:T(1024)(128)(4,1)S(1)}, s32[]{:S(2)}) async-start(s8[6635520]{0:T(1024)(128)(4,1)} %bitcast.140), calls=%async_computation | async-start | bytes 4882432
  76.6 16.9 %copy-start.18 = (f32[16,16,128]{2,1,0:T(8,128)}, f32[16,16,128]{2,1,0:T(8,128)S(1)}, u32[]{:S(2)}) copy-start(f32[16,16,128]{2,1,0:T(8,128)S(1)} %get-tuple-element.35) | copy-start | bytes 393220
  76.6 16.9 %copy-start.20 = (f32[16,16,128]{2,1,0:T(8,128)}, f32[16,16,128]{2,1,0:T(8,128)S(1)}, u32[]{:S(2)}) copy-start(f32[16,16,128]{2,1,0:T(8,128)S(1)} %get-tuple-element.36) | copy-start | bytes 393220
  76.6 16.9 %copy-start.22 = (f32[16,16,128]{2,1,0:T(8,128)}, f32[16,16,128]{2,1,0:T(8,128)S(1)}, u32[]{:S(2)}) copy-start(f32[16,16,128]{2,1,0:T(8,128)S(1)} %get-tuple-element.37) | copy-start | bytes 393220
  76.6 16.9 %copy-start.24 = (f32[16,16,128]{2,1,0:T(8,128)}, f32[16,16,128]{2,1,0:T(8,128)S(1)}, u32[]{:S(2)}) copy-start(f32[16,16,128]{2,1,0:T(8,128)S(1)} %get-tuple-element.38) | copy-start | bytes 393220
  93.6 21.3 %copy-start = (f32[32,16,16,128]{3,0,2,1:T(8,128)}, f32[32,16,16,128]{3,0,2,1:T(8,128)S(1)}, u32[]{:S(2)}) copy-start(f32[32,16,16,128]{3,0,2,1:T(8,128)S(1)} %fusion.39) | copy-start | bytes 12582916
  93.6 7.9 %collective-permute-start.7 = (f32[32,1,16,128]{3,0,2,1:T(8,128)S(1)}, f32[32,1,16,128]{3,0,2,1:T(8,128)S(1)}, u32[]{:S(2)}, u32[]{:S(2)}) collective-permute-start(f32[32,1,16,128]{3,0,2,1:T(8,128)S(1)} %get-tuple-element.32), channel_id=1, source_target_pairs={{32,0},{64,32},{96,64},{33,1},{65,33},{97,65},{34,2},{66,34},{98,6... | collective-permute-start | bytes 786440 | tf_op jit(solution)/shard_map/ppermute | solution.py:23
  94.9 8.0 %collective-permute-start.6 = (f32[32,1,16,128]{3,0,2,1:T(8,128)S(1)}, f32[32,1,16,128]{3,0,2,1:T(8,128)S(1)}, u32[]{:S(2)}, u32[]{:S(2)}) collective-permute-start(f32[32,1,16,128]{3,0,2,1:T(8,128)S(1)} %get-tuple-element.31), channel_id=1, source_target_pairs={{0,32},{32,64},{64,96},{1,33},{33,65},{65,97},{2,34},{34,66},{66,9... | collective-permute-start | bytes 786440 | tf_op jit(solution)/shard_map/ppermute | solution.py:21
  103.0 10.7 %collective-permute-start.9 = (f32[32,18,1,128]{3,0,2,1:T(8,128)S(1)}, f32[32,18,1,128]{3,0,2,1:T(8,128)S(1)}, u32[]{:S(2)}, u32[]{:S(2)}) collective-permute-start(f32[32,18,1,128]{3,0,2,1:T(8,128)S(1)} %get-tuple-element.26), channel_id=1, source_target_pairs={{4,0},{8,4},{12,8},{16,12},{20,16},{24,20},{28,24},{5,1},{9,5},{13... | collective-permute-start | bytes 884744 | tf_op jit(solution)/shard_map/ppermute | solution.py:23
  104.9 9.9 %collective-permute-start.8 = (f32[32,18,1,128]{3,0,2,1:T(8,128)S(1)}, f32[32,18,1,128]{3,0,2,1:T(8,128)S(1)}, u32[]{:S(2)}, u32[]{:S(2)}) collective-permute-start(f32[32,18,1,128]{3,0,2,1:T(8,128)S(1)} %get-tuple-element.25), channel_id=1, source_target_pairs={{0,4},{4,8},{8,12},{12,16},{16,20},{20,24},{24,28},{1,5},{5,9},{9,... | collective-permute-start | bytes 884744 | tf_op jit(solution)/shard_map/ppermute | solution.py:21
  126.2 24.7 %collective-permute-start.11 = (f32[32,18,18,1]{0,3,2,1:T(1,128)S(1)}, f32[32,18,18,1]{0,3,2,1:T(1,128)S(1)}, u32[]{:S(2)}, u32[]{:S(2)}) collective-permute-start(f32[32,18,18,1]{0,3,2,1:T(1,128)S(1)} %copy.118), channel_id=1, source_target_pairs={{1,0},{2,1},{3,2},{5,4},{6,5},{7,6},{9,8},{10,9},{11,10},{13,12},{... | collective-permute-start | bytes 124424 | tf_op jit(solution)/shard_map/ppermute | solution.py:23
  131.9 11.4 %copy-start.1 = (f32[32,16,16,128]{3,0,2,1:T(8,128)S(1)}, f32[32,16,16,128]{3,0,2,1:T(8,128)}, u32[]{:S(2)}) copy-start(f32[32,16,16,128]{3,0,2,1:T(8,128)} %copy-done) | copy-start | bytes 12582916
  131.9 23.2 %collective-permute-start.10 = (f32[32,18,18,1]{0,3,2,1:T(1,128)S(1)}, f32[32,18,18,1]{0,3,2,1:T(1,128)S(1)}, u32[]{:S(2)}, u32[]{:S(2)}) collective-permute-start(f32[32,18,18,1]{0,3,2,1:T(1,128)S(1)} %copy.116), channel_id=1, source_target_pairs={{0,1},{1,2},{2,3},{4,5},{5,6},{6,7},{8,9},{9,10},{10,11},{12,13},{... | collective-permute-start | bytes 124424 | tf_op jit(solution)/shard_map/ppermute | solution.py:21
  150.9 8.0 %copy-start.23 = (f32[16,16,128]{2,1,0:T(8,128)S(1)}, f32[16,16,128]{2,1,0:T(8,128)}, u32[]{:S(2)}) copy-start(f32[16,16,128]{2,1,0:T(8,128)} %copy-done.22) | copy-start | bytes 393220
  150.9 8.0 %copy-start.25 = (f32[16,16,128]{2,1,0:T(8,128)S(1)}, f32[16,16,128]{2,1,0:T(8,128)}, u32[]{:S(2)}) copy-start(f32[16,16,128]{2,1,0:T(8,128)} %copy-done.24) | copy-start | bytes 393220
  159.0 16.0 %copy-start.2 = (f32[32,16,16,128]{3,0,2,1:T(8,128)S(1)}, f32[32,16,16,128]{3,0,2,1:T(8,128)}, u32[]{:S(2)}) copy-start(f32[32,16,16,128]{3,0,2,1:T(8,128)} %copy-done) | copy-start | bytes 12582916
  356.0 20.1 %copy-start.4 = (f32[32,16,16,128]{3,0,2,1:T(8,128)}, f32[32,16,16,128]{3,0,2,1:T(8,128)S(1)}, u32[]{:S(2)}) copy-start(f32[32,16,16,128]{3,0,2,1:T(8,128)S(1)} %fusion.65) | copy-start | bytes 12582916
  356.1 9.1 %collective-permute-start.13 = (f32[32,1,16,128]{3,0,2,1:T(8,128)S(1)}, f32[32,1,16,128]{3,0,2,1:T(8,128)S(1)}, u32[]{:S(2)}, u32[]{:S(2)}) collective-permute-start(f32[32,1,16,128]{3,0,2,1:T(8,128)S(1)} %get-tuple-element.30), channel_id=1, source_target_pairs={{32,0},{64,32},{96,64},{33,1},{65,33},{97,65},{34,2},{66,34},{98,6... | collective-permute-start | bytes 786440 | tf_op jit(solution)/shard_map/ppermute | solution.py:23
  357.4 8.7 %collective-permute-start.12 = (f32[32,1,16,128]{3,0,2,1:T(8,128)S(1)}, f32[32,1,16,128]{3,0,2,1:T(8,128)S(1)}, u32[]{:S(2)}, u32[]{:S(2)}) collective-permute-start(f32[32,1,16,128]{3,0,2,1:T(8,128)S(1)} %get-tuple-element.29), channel_id=1, source_target_pairs={{0,32},{32,64},{64,96},{1,33},{33,65},{65,97},{2,34},{34,66},{66,9... | collective-permute-start | bytes 786440 | tf_op jit(solution)/shard_map/ppermute | solution.py:21
  366.1 8.8 %collective-permute-start.15 = (f32[32,18,1,128]{3,0,2,1:T(8,128)S(1)}, f32[32,18,1,128]{3,0,2,1:T(8,128)S(1)}, u32[]{:S(2)}, u32[]{:S(2)}) collective-permute-start(f32[32,18,1,128]{3,0,2,1:T(8,128)S(1)} %get-tuple-element.24), channel_id=1, source_target_pairs={{4,0},{8,4},{12,8},{16,12},{20,16},{24,20},{28,24},{5,1},{9,5},{13... | collective-permute-start | bytes 884744 | tf_op jit(solution)/shard_map/ppermute | solution.py:23
  369.8 6.2 %collective-permute-start.14 = (f32[32,18,1,128]{3,0,2,1:T(8,128)S(1)}, f32[32,18,1,128]{3,0,2,1:T(8,128)S(1)}, u32[]{:S(2)}, u32[]{:S(2)}) collective-permute-start(f32[32,18,1,128]{3,0,2,1:T(8,128)S(1)} %get-tuple-element.23), channel_id=1, source_target_pairs={{0,4},{4,8},{8,12},{12,16},{16,20},{20,24},{24,28},{1,5},{5,9},{9,... | collective-permute-start | bytes 884744 | tf_op jit(solution)/shard_map/ppermute | solution.py:21
  387.6 27.8 %collective-permute-start.17 = (f32[32,18,18,1]{0,3,2,1:T(1,128)S(1)}, f32[32,18,18,1]{0,3,2,1:T(1,128)S(1)}, u32[]{:S(2)}, u32[]{:S(2)}) collective-permute-start(f32[32,18,18,1]{0,3,2,1:T(1,128)S(1)} %copy.135), channel_id=1, source_target_pairs={{1,0},{2,1},{3,2},{5,4},{6,5},{7,6},{9,8},{10,9},{11,10},{13,12},{... | collective-permute-start | bytes 124424 | tf_op jit(solution)/shard_map/ppermute | solution.py:23
  393.3 14.5 %copy-start.5 = (f32[32,16,16,128]{3,0,2,1:T(8,128)S(1)}, f32[32,16,16,128]{3,0,2,1:T(8,128)}, u32[]{:S(2)}) copy-start(f32[32,16,16,128]{3,0,2,1:T(8,128)} %copy-done.4) | copy-start | bytes 12582916
  393.3 26.4 %collective-permute-start.16 = (f32[32,18,18,1]{0,3,2,1:T(1,128)S(1)}, f32[32,18,18,1]{0,3,2,1:T(1,128)S(1)}, u32[]{:S(2)}, u32[]{:S(2)}) collective-permute-start(f32[32,18,18,1]{0,3,2,1:T(1,128)S(1)} %copy.133), channel_id=1, source_target_pairs={{0,1},{1,2},{2,3},{4,5},{5,6},{6,7},{8,9},{9,10},{10,11},{12,13},{... | collective-permute-start | bytes 124424 | tf_op jit(solution)/shard_map/ppermute | solution.py:21
  423.6 16.4 %copy-start.6 = (f32[32,16,16,128]{3,0,2,1:T(8,128)S(1)}, f32[32,16,16,128]{3,0,2,1:T(8,128)}, u32[]{:S(2)}) copy-start(f32[32,16,16,128]{3,0,2,1:T(8,128)} %copy-done.4) | copy-start | bytes 12582916
  (18 other events, 81.9 us)
where the time goes:
time: 565 us; the launch traced here: 554 us
  blocking collectives  197 us (35%)
  local copies, waits for them, and re-layouts  132 us (23%)
  other arithmetic  79.3 us (14%)
  matrix products  63.1 us (11%)
  starting transfers between devices  56.2 us (10%)
  waiting for transfers between devices  24.4 us (4%)
    psum x2, blocking collectives, shards(): lax.psum(products(residual, residual), ('strike', 'dip', 'layer'))  131 us
    psum x1, blocking collectives, shards(): lax.psum(products(direction, applied), ('strike', 'dip', 'layer'))  65.9 us
    dot_general x5, matrix products, combine(): lax.dot_general(mixing, rows, (((0,), (0,)), ((), ())), precision=highest...  44.2 us
    unnamed x76, local copies, waits for them, and re-layouts  42.1 us
    ppermute x9, starting transfers between devices, padded_2(): lax.ppermute(tail, axis, [(i, (i + 1) % count) for i in range(ends)])  38.8 us
    slice x8, local copies, waits for them, and re-layouts, padded_2(): lax.slice_in_dim(cells, cells.shape[dim] - width, cells.shape[dim], axis=...  37.5 us
    add x2, other arithmetic, operate(): result = result + weights[5][None] * (center - padded[:, 1:-1, 1:-1, 2:])  32.4 us
    ppermute x9, waiting for transfers between devices, padded_2(): lax.ppermute(head, axis, [((i + 1) % count, i) for i in range(ends)])  17.6 us
  transfers between devices with their start and end apart: 18, of which 12 were waited for; matrix products, arithmetic and copies ran while one was open for 11% of the time, Pallas kernels for 0%

commit v1 on v0

v1 whole, which is shorter than its diff:
```python
import functools

import jax
import jax.numpy as jnp
from jax import lax
from jax.experimental import pallas as pl
from jax.experimental.pallas import tpu as pltpu
from jax.sharding import PartitionSpec as P

LEAKAGE = 0.01
HIGHEST = lax.Precision.HIGHEST
F32 = jnp.float32
BF16 = jnp.bfloat16
VMEM_LIMIT = 24 * 1024 * 1024
AXES = ("strike", "dip", "layer")
VMEM = pl.BlockSpec(memory_space=pltpu.VMEM)
SMEM = pl.BlockSpec(memory_space=pltpu.SMEM)
HBM = pl.BlockSpec(memory_space=pltpu.HBM)


def params(**more):
    return pltpu.CompilerParams(vmem_limit_bytes=VMEM_LIMIT, **more)


def shaped(*shape):
    return jax.ShapeDtypeStruct(shape, F32)


def lanes(rows):
    return lax.broadcasted_iota(jnp.int32, (rows, 128), 1)


def rows_of(count):
    return lax.broadcasted_iota(jnp.int32, (count, 128), 0)


def packed_ends(cells, y, into):
    turned = pltpu.roll(cells, 2 * y + 1, 1)
    lane = lanes(cells.shape[0])
    return jnp.where((lane == 2 * y) | (lane == 2 * y + 1), turned, into)


def place_x(tile, x, ref, plane, rows):
    turned = pltpu.roll(tile, (x % 4) * 32, 1)
    lane = lanes(tile.shape[0])
    mine = (lane // 32) == (x % 4)
    ref[plane, rows, :] = jnp.where(mine, turned, ref[plane, rows, :])


def pack_kernel(
    class_hbm, table_hbm, guess_hbm, field_ref, perm_ref, xlo, xhi, ylo, yhi, ends_ref,
    classes, table, guess, plane_sem, class_sem, table_sem,
):
    columns, nx, ny, nz = guess_hbm.shape

    def plane(x):
        return pltpu.make_async_copy(guess_hbm.at[:, x], guess.at[x], plane_sem.at[x])

    class_copy = pltpu.make_async_copy(class_hbm, classes, class_sem)
    table_copy = pltpu.make_async_copy(table_hbm, table, table_sem)
    table_copy.start()
    class_copy.start()
    for x in range(nx):
        plane(x).start()
    ends_ref[...] = jnp.zeros_like(ends_ref)
    for ref in (xlo, xhi, ylo, yhi):
        ref[ny] = jnp.zeros((columns, nz), F32)
    table_copy.wait()
    class_copy.wait()
    lane = lanes(ny)
    row = rows_of(ny)

    def permeability(x, carry):
        perm = jnp.zeros((ny, nz), F32)
        for level in range(table.shape[0]):
            perm = jnp.where(classes[x] == level, table[level], perm)
        perm_ref[x] = perm
        ylo[ny, pl.ds(x, 1), :] = perm[0:1]
        yhi[ny, pl.ds(x, 1), :] = perm[ny - 1 : ny]
        first = jnp.broadcast_to(perm[:, 0:1], (ny, nz))
        final = jnp.broadcast_to(perm[:, nz - 1 : nz], (ny, nz))
        both = jnp.where(lane == 2 * row, final, jnp.where(lane == 2 * row + 1, first, 0.0))
        edge = jnp.sum(both, axis=0, keepdims=True)
        place_x(edge, x, ends_ref, 4, pl.ds(x // 4, 1))
        return carry

    lax.fori_loop(0, nx, permeability, 0)
    xlo[ny, 0:ny, :] = perm_ref[0]
    xhi[ny, 0:ny, :] = perm_ref[nx - 1]

    def cells_of(x, carry):
        plane(x).wait()
        flat = guess.at[x].reshape(columns * ny, nz)
        ends = jnp.zeros((columns, nz), F32)
        for y in range(ny):
            cells = flat[pl.ds(y, columns, stride=ny), :]
            field_ref[x, y] = cells
            ends = packed_ends(cells, y, ends)
            if y == 0:
                ylo[x] = cells
            if y == ny - 1:
                yhi[x] = cells
        place_x(ends, x, ends_ref, x // 4, slice(None))
        return carry

    lax.fori_loop(0, nx, cells_of, 0)
    for y in range(ny):
        xlo[y] = field_ref[0, y]
        xhi[y] = field_ref[nx - 1, y]


def pack(perm_class, perm_table, start_guess):
    columns, nx, ny, nz = start_guess.shape
    face = shaped(ny + 1, columns, nz)
    return pl.pallas_call(
        pack_kernel,
        in_specs=[HBM] * 3,
        out_specs=[VMEM] * 7,
        out_shape=[
            shaped(nx, ny, columns, nz),
            shaped(nx, ny, nz),
            face,
            face,
            shaped(nx + 1, columns, nz),
            shaped(nx + 1, columns, nz),
            shaped(5, columns, nz),
        ],
        scratch_shapes=[
            pltpu.VMEM((nx, ny, nz), jnp.int32),
            pltpu.SMEM(perm_table.shape, F32),
            pltpu.VMEM((nx, columns, ny, nz), F32),
            pltpu.SemaphoreType.DMA((nx,)),
            pltpu.SemaphoreType.DMA(()),
            pltpu.SemaphoreType.DMA(()),
        ],
        compiler_params=params(),
        name="pack_guess",
    )(perm_class, perm_table, start_guess)


def face_weight(center_k, beside_k):
    summed = center_k + beside_k
    divisor = jnp.where(summed > 0.0, summed, 1.0)
    return jnp.where(summed > 0.0, 2.0 * center_k * beside_k / divisor, 0.0)


def arrived(left, right, left_scale=None, right_scale=None):
    after = pltpu.roll(right, 127, 1)
    before = pltpu.roll(left, 1, 1)
    if left_scale is not None:
        after, before = after * right_scale, before * left_scale
    return jnp.where(lanes(left.shape[0]) % 2 == 0, after, before)


def inner_weights(perm_ref, inside, hz, wx, wy, wzm, wzp):
    nx, ny, nz = perm_ref.shape
    lane = lanes(ny)
    row = rows_of(ny)

    def at_x(x, carry):
        center = perm_ref[x]
        wx[x] = face_weight(center, perm_ref[jnp.maximum(x - 1, 0)])
        below = jnp.concatenate([center[:1], center[: ny - 1]], axis=0)
        wy[x, 0:ny, :] = face_weight(center, below)
        ends = arrived(
            hz[0][4, pl.ds(x // 4, 1), :], hz[1][4, pl.ds(x // 4, 1), :], inside[4], inside[5]
        )
        ends = jnp.broadcast_to(ends, (ny, nz))
        offset = (x % 4) * 32 + 2 * row
        after = jnp.sum(jnp.where(lane == offset, ends, 0.0), axis=1, keepdims=True)
        ahead = jnp.sum(jnp.where(lane == offset + 1, ends, 0.0), axis=1, keepdims=True)
        wzm[x] = face_weight(center, jnp.where(lane == 0, ahead, pltpu.roll(center, 1, 1)))
        wzp[x] = face_weight(center, jnp.where(lane == nz - 1, after, pltpu.roll(center, nz - 1, 1)))
        return carry

    lax.fori_loop(0, nx, at_x, 0)


def outer_weights(perm_ref, inside, hx, hy, wx, wy):
    nx, ny, nz = perm_ref.shape
    wx[0] = face_weight(perm_ref[0], hx[0][...] * inside[0])
    wx[nx] = face_weight(perm_ref[nx - 1], hx[1][...] * inside[1])
    low = jnp.concatenate([perm_ref[x, 0:1, :] for x in range(nx)], axis=0)
    high = jnp.concatenate([perm_ref[x, ny - 1 : ny, :] for x in range(nx)], axis=0)
    low = face_weight(low, hy[0][0:nx] * inside[2])
    high = face_weight(high, hy[1][0:nx] * inside[3])
    for x in range(nx):
        wy[x, 0:1, :] = low[x : x + 1]
        wy[x, ny : ny + 1, :] = high[x : x + 1]


def local_sources(boreholes, anchors, nx, ny, nz, total_y, total_z):
    cell = jnp.broadcast_to(boreholes, (boreholes.shape[0], nz))
    along_z = cell % total_z - anchors[2]
    along_y = (cell // total_z) % total_y - anchors[1]
    along_x = cell // (total_z * total_y) - anchors[0]
    inside = (along_x >= 0) & (along_x < nx) & (along_y >= 0) & (along_y < ny)
    matched = inside & (along_z == lanes(boreholes.shape[0]))
    return jnp.where(matched, along_x * ny + along_y, -1)


def inner_kernel(first, last, totals, *refs):
    refs = list(refs)
    take = lambda count: [refs.pop(0) for _ in range(count)]
    field, hzl, hzr = take(3)
    if first:
        perm, inside, anchors, boreholes = take(4)
    else:
        wx, wy, wzm, wzp = take(4)
    (out,) = take(1)
    if not last:
        (ends,) = take(1)
    if first:
        wx, wy, wzm, wzp = take(4)
    else:
        (total,) = take(1)
    (flux,) = take(1)
    nx, ny, columns, nz = field.shape
    if not last:
        ends[...] = jnp.zeros_like(ends)
    if first:
        inner_weights(perm, inside, (hzl, hzr), wx, wy, wzm, wzp)
        code = local_sources(boreholes[...], anchors, nx, ny, nz, totals[1], totals[2])
    else:
        total[...] = jnp.zeros_like(total)
    flux[...] = jnp.zeros_like(flux)
    lane = lanes(columns)

    def at_x(x, beside):
        block = lax.div(x, 4)
        beyond = arrived(hzl[block], hzr[block])
        beyond = pltpu.roll(beyond, lax.rem(128 - lax.rem(x, 4) * 32, 128), 1)
        center = field[x, 0]
        flux_y = None
        mine = jnp.zeros((columns, nz), F32)
        for y in range(ny):
            applied = LEAKAGE * center - flux[y]
            if beside is not None:
                flux_x = wx[x + 1, y : y + 1, :] * (center - beside[y])
                applied = applied + flux_x
                flux[y] = flux_x
            if flux_y is not None:
                applied = applied - flux_y
            if y + 1 < ny:
                following = field[x, y + 1]
                flux_y = wy[x, y + 1 : y + 2, :] * (center - following)
                applied = applied + flux_y
            edge = pltpu.roll(beyond, (128 - (2 * y + 1)) % 128, 1)
            after = jnp.where(lane == nz - 1, edge, pltpu.roll(center, nz - 1, 1))
            before = jnp.where(lane == 0, edge, pltpu.roll(center, 1, 1))
            applied = applied + wzp[x, y : y + 1, :] * (center - after)
            applied = applied + wzm[x, y : y + 1, :] * (center - before)
            if first:
                applied = jnp.where(code == x * ny + y, 1.0, 0.0) - applied
            out[x, y] = applied
            if not last:
                mine = packed_ends(applied, y, mine)
            center = following
        if not last:
            place_x(mine, x, ends, block, slice(None))
        if not first:
            left = split([jnp.concatenate([field[x, y] for y in range(ny)], axis=1)])
            right = split([jnp.concatenate([out[x, y] for y in range(ny)], axis=1)])
            total[...] += gram(left, jnp.concatenate([left, right], axis=0))

    def inner(x, carry):
        at_x(x, field.at[x + 1])
        return carry

    lax.fori_loop(0, nx - 1, inner, 0)
    at_x(jnp.int32(nx - 1), None)


def sides_kernel(first, last, *refs):
    refs = list(refs)
    take = lambda count: [refs.pop(0) for _ in range(count)]
    _, field, hxl, hxr, hyl, hyr = take(6)
    if not last:
        take(1)
    if first:
        take(2)
        perm, inside = take(2)
    else:
        wx, wy, total = take(3)
    if last:
        (earlier,) = take(1)
    (out,) = take(1)
    if not last:
        (ends,) = take(1)
    if first:
        wx, wy = take(2)
    else:
        (sums,) = take(1)
    if not last:
        xlo, xhi, ylo, yhi = take(4)
    nx, ny, columns, nz = field.shape
    lane = lanes(columns)
    if first:
        hx = (hxl.at[ny, 0:ny], hxr.at[ny, 0:ny])
        outer_weights(perm, inside, hx, (hyl.at[ny], hyr.at[ny]), wx, wy)

    added = None
    faces = (
        (hxl, [(0, y) for y in range(ny)], [(0, y) for y in range(ny)], wx),
        (hxr, [(nx - 1, y) for y in range(ny)], [(nx, y) for y in range(ny)], wx),
        (hyl, [(x, 0) for x in range(nx)], [(x, 0) for x in range(nx)], wy),
        (hyr, [(x, ny - 1) for x in range(nx)], [(x, ny) for x in range(nx)], wy),
    )
    for halo, rows, weight_rows, weight in faces:
        own, fluxes = [], []
        for place, ((x, y), (p, q)) in enumerate(zip(rows, weight_rows)):
            center = field[x, y]
            flux = weight[p, q : q + 1, :] * (center - halo[place])
            if first:
                out[x, y] -= flux
            else:
                out[x, y] += flux
                own.append(center)
                fluxes.append(flux)
        if not first:
            left = split([jnp.concatenate(own, axis=1)])
            right = split([jnp.concatenate(fluxes, axis=1)])
            part = gram(left, right)
            added = part if added is None else added + part
    if not last:
        for x in range(nx):
            tile = ends[x // 4]
            for y in range(ny):
                if x in (0, nx - 1) or y in (0, ny - 1):
                    tile = packed_ends(out[x, y], (x % 4) * 16 + y, tile)
            ends[x // 4] = tile
        for y in range(ny):
            xlo[y] = out[0, y]
            xhi[y] = out[nx - 1, y]
        for x in range(nx):
            ylo[x] = out[x, 0]
            yhi[x] = out[x, ny - 1]
    if not first:
        held = total[...]
        held = held[0:32] + held[32:64]
        held = held + pltpu.roll(held, 96, 1)
        held = jnp.where(lane < 32, held, pltpu.roll(held, 96, 1))
        fixed = added[0:32] + added[32:64]
        fixed = fixed[:, 0:32] + fixed[:, 32:64]
        fixed = jnp.concatenate([fixed, jnp.zeros((columns, 96), F32)], axis=1)
        held = jnp.where(lane < 32, held, held + pltpu.roll(fixed, 32, 1))
        if last:
            held = jnp.where(lane < 64, earlier[...], pltpu.roll(held, 64, 1))
        sums[...] = held


def split(fields):
    high = [field.astype(BF16) for field in fields]
    low = [(field - top.astype(F32)).astype(BF16) for field, top in zip(fields, high)]
    return jnp.concatenate(high + low, axis=0)


def gram(left, right):
    return lax.dot_general(left, right, (((1,), (1,)), ((), ())), preferred_element_type=F32)


def fold(products, fields):
    half = products.shape[0] // 2
    summed = products[:half] + products[half:]
    return summed[:, :half] + summed[:, half:]


def inner_part(field, halos, extra, first, last, totals):
    nx, ny, columns, nz = field.shape
    in_specs = [VMEM] * 3
    if first:
        in_specs += [VMEM, SMEM, SMEM, VMEM]
    else:
        in_specs += [VMEM] * 4
    out_shape = [shaped(nx, ny, columns, nz)]
    if not last:
        out_shape += [shaped(4, columns, nz)]
    if first:
        out_shape += [
            shaped(nx + 1, ny, nz),
            shaped(nx, ny + 8, nz),
            shaped(nx, ny, nz),
            shaped(nx, ny, nz),
        ]
    else:
        out_shape += [shaped(2 * columns, 4 * columns)]
    return pl.pallas_call(
        functools.partial(inner_kernel, first, last, totals),
        in_specs=in_specs,
        out_specs=[VMEM] * len(out_shape),
        out_shape=out_shape,
        scratch_shapes=[pltpu.VMEM((ny, columns, nz), F32)],
        compiler_params=params(),
        cost_estimate=pl.CostEstimate(
            flops=20 * field.size, bytes_accessed=6 * field.size * 4, transcendentals=0
        ),
        name="inner_first" if first else "inner_last" if last else "inner_next",
    )(field, *halos, *extra)


def sides_part(part, field, halos, ends, extra, first, last):
    nx, ny, columns, nz = field.shape
    operands = [part, field, *halos]
    if not last:
        operands += [ends]
    operands += extra
    in_specs = [VMEM] * len(operands)
    aliases = {0: 0}
    out_shape = [shaped(*part.shape)]
    if not last:
        aliases[6] = 1
        out_shape += [shaped(*ends.shape)]
    if first:
        in_specs[-1] = SMEM
        aliases[7] = 2
        aliases[8] = 3
        out_shape += [shaped(*extra[0].shape), shaped(*extra[1].shape)]
    else:
        out_shape += [shaped(columns, 128)]
    if not last:
        out_shape += [shaped(ny, columns, nz)] * 2 + [shaped(nx, columns, nz)] * 2
    return pl.pallas_call(
        functools.partial(sides_kernel, first, last),
        in_specs=in_specs,
        out_specs=[VMEM] * len(out_shape),
        out_shape=out_shape,
        input_output_aliases=aliases,
        compiler_params=params(),
        name="sides_first" if first else "sides_last" if last else "sides_next",
    )(*operands)


def exchanged(xlo, xhi, ylo, yhi, ends):
    ahead = lambda axis: [(i, (i + 1) % lax.axis_size(axis)) for i in range(lax.axis_size(axis))]
    back = lambda axis: [(j, i) for i, j in ahead(axis)]
    near = (
        lax.ppermute(ends, "layer", ahead("layer")),
        lax.ppermute(ends, "layer", back("layer")),
    )
    far = (
        lax.ppermute(xhi, "strike", ahead("strike")),
        lax.ppermute(xlo, "strike", back("strike")),
        lax.ppermute(yhi, "dip", ahead("dip")),
        lax.ppermute(ylo, "dip", back("dip")),
    )
    return near, far


def dot(left, right, contract=(1, 0)):
    dims = (((contract[0],), (contract[1],)), ((), ()))
    return lax.dot_general(left, right, dims, precision=HIGHEST, preferred_element_type=F32)


def eliminate(tables):
    row = rows_of(32)
    for k in range(32):
        done = []
        for table in tables:
            column = jnp.broadcast_to(table[:, k : k + 1], table.shape)
            scaled = table[k : k + 1, :] / column[k : k + 1, :]
            done.append(jnp.where(row == k, scaled, table - column * scaled))
        tables = done
    return tables


def solve_kernel(own_ref, other_ref, out_ref):
    sums = own_ref[...] + other_ref[...]
    lane = lanes(32)
    row = rows_of(32)
    unit = jnp.where(lane == row + 32, 1.0, 0.0)
    advance_table = jnp.where(lane < 32, pltpu.roll(sums, 96, 1), pltpu.roll(sums, 32, 1))
    norm_table = jnp.where(lane < 32, sums, unit)
    advance_table, norm_table = eliminate([advance_table, norm_table])
    norm = sums[:, 0:32]
    moment = sums[:, 32:64]
    square = sums[:, 64:96]
    cube = sums[:, 96:128]
    advance = advance_table[:, 32:64]
    inverse = norm_table[:, 32:64]
    turned = dot(square, advance)
    tripled = dot(dot(advance, cube, (0, 0)), advance)
    norm_next = dot(advance, turned, (0, 0)) - norm
    eye = jnp.where(lane[:, 0:32] == row[:, 0:32], 1.0, 0.0)
    mixing = eye + dot(inverse, norm_next)
    curvature = dot(mixing, dot(moment, mixing) - turned, (0, 0))
    curvature = curvature - dot(turned, mixing, (0, 0)) + tripled
    wide = jnp.concatenate([curvature, norm_next, jnp.zeros((32, 64), F32)], axis=1)
    (wide,) = eliminate([wide])
    later = wide[:, 32:64]
    taken = advance + dot(mixing, later)
    beyond = dot(advance, later)
    taken_t = taken.T
    beyond_t = beyond.T
    nothing = jnp.zeros((32, 32), F32)
    out_ref[0:32, :] = jnp.concatenate([taken_t, -beyond_t, nothing, nothing], axis=1)
    out_ref[32:64, :] = jnp.concatenate([nothing, -taken_t, beyond_t, nothing], axis=1)


def solve(own, other):
    return pl.pallas_call(
        solve_kernel,
        in_specs=[VMEM] * 2,
        out_specs=VMEM,
        out_shape=shaped(64, 128),
        compiler_params=params(),
        name="solve_small",
    )(own, other)


def combine_kernel(
    mix_ref, guess_ref, one_ref, two_ref, three_ref, solution_hbm, residual_hbm,
    solution, residual, sem,
):
    nx, ny, columns, nz = guess_ref.shape
    slots = solution.shape[0]
    mix = mix_ref[...]
    high = mix.astype(BF16)
    low = (mix - high.astype(F32)).astype(BF16)
    mixing = jnp.concatenate(
        [jnp.concatenate([high, high], axis=1), jnp.concatenate([low, low], axis=1)], axis=0
    )
    nothing = jnp.zeros((columns, 2 * nz), F32)

    def leaving(x):
        slot = lax.rem(x, slots)
        return (
            pltpu.make_async_copy(solution.at[slot], solution_hbm.at[:, x], sem.at[0, slot]),
            pltpu.make_async_copy(residual.at[slot], residual_hbm.at[:, x], sem.at[1, slot]),
        )

    def at_x(x, carry):
        slot = lax.rem(x, slots)

        @pl.when(x >= slots)
        def _():
            for copy in leaving(x - slots):
                copy.wait()

        solution_rows = solution.at[slot].reshape(columns * ny, nz)
        residual_rows = residual.at[slot].reshape(columns * ny, nz)
        for y in range(0, ny, 2):
            fields = [
                jnp.concatenate([ref[x, y], ref[x, y + 1]], axis=1)
                for ref in (one_ref, two_ref, three_ref)
            ]
            halves = split(fields + [nothing])
            mixed = jnp.dot(mixing, halves, preferred_element_type=F32)
            mixed = mixed[0:64] + mixed[64:128]
            for step in range(2):
                rows = pl.ds(y + step, columns, stride=ny)
                part = mixed[:, step * nz : (step + 1) * nz]
                solution_rows[rows, :] = guess_ref[x, y + step] + part[0:32]
                residual_rows[rows, :] = one_ref[x, y + step] + part[32:64]
        for copy in leaving(x):
            copy.start()
        return carry

    lax.fori_loop(0, nx, at_x, 0)
    for x in range(nx - slots, nx):
        for copy in leaving(jnp.int32(x)):
            copy.wait()


def combine(mix, guess, one, two, three):
    nx, ny, columns, nz = guess.shape
    return pl.pallas_call(
        combine_kernel,
        in_specs=[VMEM] * 5,
        out_specs=[HBM] * 2,
        out_shape=[shaped(columns, nx, ny, nz)] * 2,
        scratch_shapes=[
            pltpu.VMEM((8, columns, ny, nz), F32),
            pltpu.VMEM((8, columns, ny, nz), F32),
            pltpu.SemaphoreType.DMA((2, 8)),
        ],
        compiler_params=params(),
        name="combine_fields",
    )(mix, guess, one, two, three)


def summed_but_last(values):
    steps = []
    for axis in AXES[1:] + AXES[:1]:
        size, mask = lax.axis_size(axis), 1
        while mask < size:
            steps.append((axis, [(i, i ^ mask) for i in range(size)]))
            mask *= 2
    for axis, pairs in steps[:-1]:
        values = values + lax.ppermute(values, axis, pairs)
    axis, pairs = steps[-1]
    return values, lax.ppermute(values, axis, pairs)


def shards(perm_class, perm_table, boreholes, start_guess):
    columns, nx, ny, nz = start_guess.shape
    places = [lax.axis_index(axis) for axis in AXES]
    sizes = [lax.axis_size(axis) for axis in AXES]
    anchors = jnp.stack([place * size for place, size in zip(places, (nx, ny, nz))])
    totals = tuple(size * count for size, count in zip((nx, ny, nz), sizes))
    inside = []
    for place, size in zip(places, sizes):
        inside += [place > 0, place < size - 1]
    inside = jnp.stack(inside).astype(F32)

    guess, perm, *faces = pack(perm_class, perm_table, start_guess)
    near, far = exchanged(*faces)
    extra = (perm, inside, anchors.astype(jnp.int32), boreholes[:, None])
    part, ends, wx, wy, *along_z = inner_part(guess, near, extra, True, False, totals)
    residual, ends, wx, wy, *faces = sides_part(
        part, guess, far, ends, [wx, wy, perm, inside], True, False
    )
    weights = (wx, wy, *along_z)
    near, far = exchanged(*faces, ends)
    part, ends, total = inner_part(residual, near, weights, False, False, totals)
    once, ends, sums, *faces = sides_part(
        part, residual, far, ends, [wx, wy, total], False, False
    )
    near, far = exchanged(*faces, ends)
    part, total = inner_part(once, near, weights, False, True, totals)
    twice, sums = sides_part(part, once, far, None, [wx, wy, total, sums], False, True)
    mix = solve(*summed_but_last(sums))
    return tuple(combine(mix, guess, residual, once, twice))


def solution(mesh):
    placed = (P("strike", "dip", "layer"), P(), P(), P(None, "strike", "dip", "layer"))
    return jax.shard_map(
        shards,
        mesh=mesh,
        in_specs=placed,
        out_specs=(P(None, "strike", "dip", "layer"), P(None, "strike", "dip", "layer")),
        check_vma=False,
    )
```

time: 565 us -> 139 us (0.25)
  the two profiles are of different devices: /device:TPU:1 before, /device:TPU:0 now
where the time goes in v1:
time: 139 us
  Pallas kernels  51.4 us (37%)
  waiting for transfers between devices  49.6 us (36%)
  starting transfers between devices  28.6 us (21%)
  local copies, waits for them, and re-layouts  8.14 us (6%)
    pallas_call x3, Pallas kernels, inner_part(): pl.pallas_call(functools.partial(inner_kernel, first, last, totals), in_s...  28.6 us
    ppermute x6, waiting for transfers between devices, summed_but_last(): values = values + lax.ppermute(values, axis, pairs)  21.4 us
    ppermute x3, waiting for transfers between devices, exchanged(): lax.ppermute(ends, 'layer', ahead('layer'))  16.6 us
    ppermute x3, starting transfers between devices, exchanged(): lax.ppermute(ylo, 'dip', back('dip'))  8.86 us
    ppermute x3, starting transfers between devices, exchanged(): lax.ppermute(ends, 'layer', back('layer'))  8.17 us
    unnamed x14, local copies, waits for them, and re-layouts  7.95 us
    ppermute x3, starting transfers between devices, exchanged(): lax.ppermute(xlo, 'strike', back('strike'))  7.84 us
    pallas_call x1, Pallas kernels, solve(): pl.pallas_call(solve_kernel, in_specs=[VMEM] * 2, out_specs=VMEM, out_sha...  7.05 us
  transfers between devices with their start and end apart: 25, of which 13 were waited for; matrix products, arithmetic and copies ran while one was open for 0% of the time, Pallas kernels for 21%

profile of v1, /device:TPU:0, one launch (start us, length us, event | category | flops | bytes accessed | tf_op | source)
XLA Modules:
  0.0 138.7 jit_solution(9186209632425714590)
XLA Ops:
  0.6 2.2 %copy-done.3 = f32[32,16,16,128]{3,2,1,0:T(8,128)S(1)} copy-done((f32[32,16,16,128]{3,2,1,0:T(8,128)S(1)}, f32[32,16,16,128]{3,2,1,0:T(8,128)}, u32[]{:S(2)}) %copy-start.3) | copy-done | bytes 4194328
  4.4 6.8 %pack_guess.1 = (f32[16,16,32,128]{3,2,1,0:T(8,128)S(1)}, f32[16,16,128]{2,1,0:T(8,128)S(1)}, f32[17,32,128]{2,1,0:T(8,128)S(1)}, f32[17,32,128]{2,1,0:T(8,128)S...) custom-call(s32[16,16,128]{2,1,0:T(8,128)S(1)} %copy-done.4, ...), custom_call_target="tpu_custom_call" | custom-call | tf_op jit(solution)/shard_map/pack_guess/pallas_call | solution.py:115
  11.2 2.0 %copy-done = f32[16,16,32,128]{3,2,1,0:T(8,128)} copy-done((f32[16,16,32,128]{3,2,1,0:T(8,128)}, f32[16,16,32,128]{3,2,1,0:T(8,128)S(1)}, u32[]{:S(2)}) %copy-start) | copy-done | bytes 4194328
  13.2 1.6 %collective-permute-start.2 = (f32[17,32,128]{2,1,0:T(8,128)S(1)}, f32[17,32,128]{2,1,0:T(8,128)S(1)}, u32[]{:S(2)}, u32[]{:S(2)}) collective-permute-start(f32[17,32,128]{2,1,0:T(8,128)S(1)} %get-tuple-element.41), channel_id=1, source_target_pairs={{0,32},{32,64},{64,96},{96,0},{1,33},{33,65},{65,97},{97,1},{2,34}... | collective-permute-start | bytes 835592 | tf_op jit(solution)/shard_map/ppermute | solution.py:441
  14.8 1.7 %collective-permute-start.3 = (f32[17,32,128]{2,1,0:T(8,128)S(1)}, f32[17,32,128]{2,1,0:T(8,128)S(1)}, u32[]{:S(2)}, u32[]{:S(2)}) collective-permute-start(f32[17,32,128]{2,1,0:T(8,128)S(1)} %get-tuple-element.42), channel_id=1, source_target_pairs={{32,0},{64,32},{96,64},{0,96},{33,1},{65,33},{97,65},{1,97},{34,2}... | collective-permute-start | bytes 835592 | tf_op jit(solution)/shard_map/ppermute | solution.py:442
  16.5 3.0 %collective-permute-start.5 = (f32[17,32,128]{2,1,0:T(8,128)S(1)}, f32[17,32,128]{2,1,0:T(8,128)S(1)}, u32[]{:S(2)}, u32[]{:S(2)}) collective-permute-start(f32[17,32,128]{2,1,0:T(8,128)S(1)} %get-tuple-element.44), channel_id=1, source_target_pairs={{4,0},{8,4},{12,8},{16,12},{20,16},{24,20},{28,24},{0,28},{5,1},{9... | collective-permute-start | bytes 835592 | tf_op jit(solution)/shard_map/ppermute | solution.py:444
  19.4 4.1 %collective-permute-start.1 = (f32[5,32,128]{2,1,0:T(8,128)S(1)}, f32[5,32,128]{2,1,0:T(8,128)S(1)}, u32[]{:S(2)}, u32[]{:S(2)}) collective-permute-start(f32[5,32,128]{2,1,0:T(8,128)S(1)} %get-tuple-element.38), channel_id=1, source_target_pairs={{1,0},{2,1},{3,2},{0,3},{5,4},{6,5},{7,6},{4,7},{9,8},{10,9},{11,1... | collective-permute-start | bytes 245768 | tf_op jit(solution)/shard_map/ppermute | solution.py:438
  23.7 1.9 %collective-permute-done.1.refs_2_ = f32[5,32,128]{2,1,0:T(8,128)S(1)} collective-permute-done((f32[5,32,128]{2,1,0:T(8,128)S(1)}, f32[5,32,128]{2,1,0:T(8,128)S(1)}, u32[]{:S(2)}, u32[]{:S(2)}) %collective-permute-start.1) | collective-permute-done | bytes 81952 | tf_op jit(solution)/shard_map/ppermute | solution.py:438
  25.9 5.7 %collective-permute-done.refs_1_ = f32[5,32,128]{2,1,0:T(8,128)S(1)} collective-permute-done((f32[5,32,128]{2,1,0:T(8,128)S(1)}, f32[5,32,128]{2,1,0:T(8,128)S(1)}, u32[]{:S(2)}, u32[]{:S(2)}) %collective-permute-start) | collective-permute-done | bytes 81952 | tf_op jit(solution)/shard_map/ppermute | solution.py:437
  31.6 2.2 %copy-done.1 = f32[16,16,32,128]{3,2,1,0:T(8,128)S(1)} copy-done((f32[16,16,32,128]{3,2,1,0:T(8,128)S(1)}, f32[16,16,32,128]{3,2,1,0:T(8,128)}, u32[]{:S(2)}) %copy-start.1) | copy-done | bytes 4194328
  33.8 12.0 %inner_first.1 = (f32[16,16,32,128]{3,2,1,0:T(8,128)S(1)}, f32[4,32,128]{2,1,0:T(8,128)S(1)}, f32[17,16,128]{2,1,0:T(8,128)S(1)}, f32[16,24,128]{2,1,0:T(8,128)S...) custom-call(f32[16,16,32,128]{3,2,1,0:T(8,128)S(1)} %copy-done.1, ...), custom_call_target="tpu_custom_call" | custom-call | flops 20971520 | bytes 25165824 | tf_op jit(solution)/shard_map/inner_first/pallas_call | solution.py:387
  47.2 3.0 %collective-permute-start.9 = (f32[16,32,128]{2,1,0:T(8,128)S(1)}, f32[16,32,128]{2,1,0:T(8,128)S(1)}, u32[]{:S(2)}, u32[]{:S(2)}) collective-permute-start(f32[16,32,128]{2,1,0:T(8,128)S(1)} %get-tuple-element.56), channel_id=1, source_target_pairs={{32,0},{64,32},{96,64},{0,96},{33,1},{65,33},{97,65},{1,97},{34,2}... | collective-permute-start | bytes 786440 | tf_op jit(solution)/shard_map/ppermute | solution.py:442
  50.1 3.0 %collective-permute-start.11 = (f32[16,32,128]{2,1,0:T(8,128)S(1)}, f32[16,32,128]{2,1,0:T(8,128)S(1)}, u32[]{:S(2)}, u32[]{:S(2)}) collective-permute-start(f32[16,32,128]{2,1,0:T(8,128)S(1)} %get-tuple-element.58), channel_id=1, source_target_pairs={{4,0},{8,4},{12,8},{16,12},{20,16},{24,20},{28,24},{0,28},{5,1},{9... | collective-permute-start | bytes 786440 | tf_op jit(solution)/shard_map/ppermute | solution.py:444
  53.1 2.0 %collective-permute-start.7 = (f32[4,32,128]{2,1,0:T(8,128)S(1)}, f32[4,32,128]{2,1,0:T(8,128)S(1)}, u32[]{:S(2)}, u32[]{:S(2)}) collective-permute-start(f32[4,32,128]{2,1,0:T(8,128)S(1)} %get-tuple-element.49), channel_id=1, source_target_pairs={{1,0},{2,1},{3,2},{0,3},{5,4},{6,5},{7,6},{4,7},{9,8},{10,9},{11,1... | collective-permute-start | bytes 196616 | tf_op jit(solution)/shard_map/ppermute | solution.py:438
  55.1 2.2 %collective-permute-done.7.refs_2_ = f32[4,32,128]{2,1,0:T(8,128)S(1)} collective-permute-done((f32[4,32,128]{2,1,0:T(8,128)S(1)}, f32[4,32,128]{2,1,0:T(8,128)S(1)}, u32[]{:S(2)}, u32[]{:S(2)}) %collective-permute-start.7) | collective-permute-done | bytes 65568 | tf_op jit(solution)/shard_map/ppermute | solution.py:438
  57.3 5.5 %collective-permute-done.6.refs_1_ = f32[4,32,128]{2,1,0:T(8,128)S(1)} collective-permute-done((f32[4,32,128]{2,1,0:T(8,128)S(1)}, f32[4,32,128]{2,1,0:T(8,128)S(1)}, u32[]{:S(2)}, u32[]{:S(2)}) %collective-permute-start.6) | collective-permute-done | bytes 65568 | tf_op jit(solution)/shard_map/ppermute | solution.py:437
  62.8 8.4 %inner_next.1 = (f32[16,16,32,128]{3,2,1,0:T(8,128)S(1)}, f32[4,32,128]{2,1,0:T(8,128)S(1)}, f32[64,128]{1,0:T(8,128)S(1)}) custom-call(f32[16,16,32,128]{3,2,1,0:T(8,128)S(1)} %get-tuple-element.48.refs_0_.refs_1_.one_ref, f32[4,32,128]{2,1,0:T(8,128)S(1)} %collective-permute-done.6.refs_1_, f32[4,32,128]{2,1,0:T(8,128)S(1)} %collective-permute-done.7.refs_2_, ...), custom_call_target="tpu_custom_call" | custom-call | flops 20971520 | bytes 25165824 | tf_op jit(solution)/shard_map/inner_next/pallas_call | solution.py:387
  72.0 3.2 %collective-permute-start.15 = (f32[16,32,128]{2,1,0:T(8,128)S(1)}, f32[16,32,128]{2,1,0:T(8,128)S(1)}, u32[]{:S(2)}, u32[]{:S(2)}) collective-permute-start(f32[16,32,128]{2,1,0:T(8,128)S(1)} %get-tuple-element.65), channel_id=1, source_target_pairs={{32,0},{64,32},{96,64},{0,96},{33,1},{65,33},{97,65},{1,97},{34,2}... | collective-permute-start | bytes 786440 | tf_op jit(solution)/shard_map/ppermute | solution.py:442
  75.2 3.0 %collective-permute-start.17 = (f32[16,32,128]{2,1,0:T(8,128)S(1)}, f32[16,32,128]{2,1,0:T(8,128)S(1)}, u32[]{:S(2)}, u32[]{:S(2)}) collective-permute-start(f32[16,32,128]{2,1,0:T(8,128)S(1)} %get-tuple-element.67), channel_id=1, source_target_pairs={{4,0},{8,4},{12,8},{16,12},{20,16},{24,20},{28,24},{0,28},{5,1},{9... | collective-permute-start | bytes 786440 | tf_op jit(solution)/shard_map/ppermute | solution.py:444
  78.2 2.0 %collective-permute-start.13 = (f32[4,32,128]{2,1,0:T(8,128)S(1)}, f32[4,32,128]{2,1,0:T(8,128)S(1)}, u32[]{:S(2)}, u32[]{:S(2)}) collective-permute-start(f32[4,32,128]{2,1,0:T(8,128)S(1)} %get-tuple-element.62), channel_id=1, source_target_pairs={{1,0},{2,1},{3,2},{0,3},{5,4},{6,5},{7,6},{4,7},{9,8},{10,9},{11,1... | collective-permute-start | bytes 196616 | tf_op jit(solution)/shard_map/ppermute | solution.py:438
  80.2 2.2 %collective-permute-done.13.refs_2_ = f32[4,32,128]{2,1,0:T(8,128)S(1)} collective-permute-done((f32[4,32,128]{2,1,0:T(8,128)S(1)}, f32[4,32,128]{2,1,0:T(8,128)S(1)}, u32[]{:S(2)}, u32[]{:S(2)}) %collective-permute-start.13) | collective-permute-done | bytes 65568 | tf_op jit(solution)/shard_map/ppermute | solution.py:438
  82.4 5.5 %collective-permute-done.12.refs_1_ = f32[4,32,128]{2,1,0:T(8,128)S(1)} collective-permute-done((f32[4,32,128]{2,1,0:T(8,128)S(1)}, f32[4,32,128]{2,1,0:T(8,128)S(1)}, u32[]{:S(2)}, u32[]{:S(2)}) %collective-permute-start.12) | collective-permute-done | bytes 65568 | tf_op jit(solution)/shard_map/ppermute | solution.py:437
  87.9 8.2 %inner_last.1 = (f32[16,16,32,128]{3,2,1,0:T(8,128)S(1)}, f32[64,128]{1,0:T(8,128)S(1)}) custom-call(f32[16,16,32,128]{3,2,1,0:T(8,128)S(1)} %get-tuple-element.61.refs_0_.refs_1_.two_ref, f32[4,32,128]{2,1,0:T(8,128)S(1)} %collective-permute-done.12.refs_1_, f32[4,32,128]{2,1,0:T(8,128)S(1)} %collective-permute-done.13.refs_2_, ...), custom_call_target="tpu_custom_call" | custom-call | flops 20971520 | bytes 25165824 | tf_op jit(solution)/shard_map/inner_last/pallas_call | solution.py:387
  98.1 3.7 %collective-permute-done.19 = f32[32,128]{1,0:T(8,128)S(1)} collective-permute-done((f32[32,128]{1,0:T(8,128)S(1)}, f32[32,128]{1,0:T(8,128)S(1)}, u32[]{:S(2)}, u32[]{:S(2)}) %collective-permute-start.19) | collective-permute-done | bytes 16416 | tf_op jit(solution)/shard_map/ppermute | solution.py:589
  101.9 5.2 %collective-permute-done.20 = f32[32,128]{1,0:T(8,128)S(1)} collective-permute-done((f32[32,128]{1,0:T(8,128)S(1)}, f32[32,128]{1,0:T(8,128)S(1)}, u32[]{:S(2)}, u32[]{:S(2)}) %collective-permute-start.20) | collective-permute-done | bytes 16416 | tf_op jit(solution)/shard_map/ppermute | solution.py:589
  107.1 3.7 %collective-permute-done.21 = f32[32,128]{1,0:T(8,128)S(1)} collective-permute-done((f32[32,128]{1,0:T(8,128)S(1)}, f32[32,128]{1,0:T(8,128)S(1)}, u32[]{:S(2)}, u32[]{:S(2)}) %collective-permute-start.21) | collective-permute-done | bytes 16416 | tf_op jit(solution)/shard_map/ppermute | solution.py:589
  110.9 1.5 %collective-permute-start.22 = (f32[32,128]{1,0:T(8,128)S(1)}, f32[32,128]{1,0:T(8,128)S(1)}, u32[]{:S(2)}, u32[]{:S(2)}) collective-permute-start(f32[32,128]{1,0:T(8,128)S(1)} %add.21), channel_id=1, source_target_pairs={{0,2},{1,3},{2,0},{3,1},{4,6},{5,7},{6,4},{7,5},{8,10},{9,11},{10,... | collective-permute-start | bytes 49160 | tf_op jit(solution)/shard_map/ppermute | solution.py:589
  112.3 3.8 %collective-permute-done.22 = f32[32,128]{1,0:T(8,128)S(1)} collective-permute-done((f32[32,128]{1,0:T(8,128)S(1)}, f32[32,128]{1,0:T(8,128)S(1)}, u32[]{:S(2)}, u32[]{:S(2)}) %collective-permute-start.22) | collective-permute-done | bytes 16416 | tf_op jit(solution)/shard_map/ppermute | solution.py:589
  116.1 3.7 %collective-permute-done.23 = f32[32,128]{1,0:T(8,128)S(1)} collective-permute-done((f32[32,128]{1,0:T(8,128)S(1)}, f32[32,128]{1,0:T(8,128)S(1)}, u32[]{:S(2)}, u32[]{:S(2)}) %collective-permute-start.23) | collective-permute-done | bytes 16416 | tf_op jit(solution)/shard_map/ppermute | solution.py:589
  119.9 5.2 %collective-permute-done.24.other_ref = f32[32,128]{1,0:T(8,128)S(1)} collective-permute-done((f32[32,128]{1,0:T(8,128)S(1)}, f32[32,128]{1,0:T(8,128)S(1)}, u32[]{:S(2)}, u32[]{:S(2)}) %collective-permute-start.24) | collective-permute-done | bytes 16416 | tf_op jit(solution)/shard_map/ppermute | solution.py:591
  125.1 7.1 %solve_small.1.mix_ref = f32[64,128]{1,0:T(8,128)S(1)} custom-call(f32[32,128]{1,0:T(8,128)S(1)} %add.23.own_ref, f32[32,128]{1,0:T(8,128)S(1)} %collective-permute-done.24.other_ref), custom_call_target="tpu_custom_call" | custom-call | tf_op jit(solution)/shard_map/solve_small/pallas_call | solution.py:500
  132.2 6.5 %combine_fields.1 = (f32[32,16,16,128]{3,2,1,0:T(8,128)}, f32[32,16,16,128]{3,2,1,0:T(8,128)}) custom-call(f32[64,128]{1,0:T(8,128)S(1)} %solve_small.1.mix_ref, f32[16,16,32,128]{3,2,1,0:T(8,128)S(1)} %copy-done.2, f32[16,16,32,128]{3,2,1,0:T(8,128)S(1)} %get-tuple-element.48.refs_0_.refs_1_.one_ref, ...), custom_call_target="tpu_custom_call" | custom-call | tf_op jit(solution)/shard_map/combine_fields/pallas_call | solution.py:566
  (51 shorter events, 6.1 us)
Async XLA Ops:
  0.6 2.2 %copy-start.3 = (f32[32,16,16,128]{3,2,1,0:T(8,128)S(1)}, f32[32,16,16,128]{3,2,1,0:T(8,128)}, u32[]{:S(2)}) copy-start(f32[32,16,16,128]{3,2,1,0:T(8,128)} %guess_hbm.1) | copy-start | bytes 12582916
  2.8 0.9 copy-start.4
  3.7 0.7 copy-start.5
  4.4 19.3 %copy-start.6 = (s32[32]{0:T(128)S(1)}, s32[32]{0:T(128)}, u32[]{:S(2)}) copy-start(s32[32]{0:T(128)} %param.6) | copy-start | bytes 388
  11.2 2.0 %copy-start = (f32[16,16,32,128]{3,2,1,0:T(8,128)}, f32[16,16,32,128]{3,2,1,0:T(8,128)S(1)}, u32[]{:S(2)}) copy-start(f32[16,16,32,128]{3,2,1,0:T(8,128)S(1)} %get-tuple-element.37.refs_0_.refs_1_.guess_ref) | copy-start | bytes 12582916
  13.2 32.6 %collective-permute-start.2 = (f32[17,32,128]{2,1,0:T(8,128)S(1)}, f32[17,32,128]{2,1,0:T(8,128)S(1)}, u32[]{:S(2)}, u32[]{:S(2)}) collective-permute-start(f32[17,32,128]{2,1,0:T(8,128)S(1)} %get-tuple-element.41), channel_id=1, source_target_pairs={{0,32},{32,64},{64,96},{96,0},{1,33},{33,65},{65,97},{97,1},{2,34}... | collective-permute-start | bytes 835592 | tf_op jit(solution)/shard_map/ppermute | solution.py:441
  14.8 31.0 %collective-permute-start.3 = (f32[17,32,128]{2,1,0:T(8,128)S(1)}, f32[17,32,128]{2,1,0:T(8,128)S(1)}, u32[]{:S(2)}, u32[]{:S(2)}) collective-permute-start(f32[17,32,128]{2,1,0:T(8,128)S(1)} %get-tuple-element.42), channel_id=1, source_target_pairs={{32,0},{64,32},{96,64},{0,96},{33,1},{65,33},{97,65},{1,97},{34,2}... | collective-permute-start | bytes 835592 | tf_op jit(solution)/shard_map/ppermute | solution.py:442
  16.5 29.4 %collective-permute-start.4 = (f32[17,32,128]{2,1,0:T(8,128)S(1)}, f32[17,32,128]{2,1,0:T(8,128)S(1)}, u32[]{:S(2)}, u32[]{:S(2)}) collective-permute-start(f32[17,32,128]{2,1,0:T(8,128)S(1)} %get-tuple-element.43), channel_id=1, source_target_pairs={{0,4},{4,8},{8,12},{12,16},{16,20},{20,24},{24,28},{28,0},{1,5},{5... | collective-permute-start | bytes 835592 | tf_op jit(solution)/shard_map/ppermute | solution.py:443
  16.5 29.4 %collective-permute-start.5 = (f32[17,32,128]{2,1,0:T(8,128)S(1)}, f32[17,32,128]{2,1,0:T(8,128)S(1)}, u32[]{:S(2)}, u32[]{:S(2)}) collective-permute-start(f32[17,32,128]{2,1,0:T(8,128)S(1)} %get-tuple-element.44), channel_id=1, source_target_pairs={{4,0},{8,4},{12,8},{16,12},{20,16},{24,20},{28,24},{0,28},{5,1},{9... | collective-permute-start | bytes 835592 | tf_op jit(solution)/shard_map/ppermute | solution.py:444
  19.4 6.2 %collective-permute-start.1 = (f32[5,32,128]{2,1,0:T(8,128)S(1)}, f32[5,32,128]{2,1,0:T(8,128)S(1)}, u32[]{:S(2)}, u32[]{:S(2)}) collective-permute-start(f32[5,32,128]{2,1,0:T(8,128)S(1)} %get-tuple-element.38), channel_id=1, source_target_pairs={{1,0},{2,1},{3,2},{0,3},{5,4},{6,5},{7,6},{4,7},{9,8},{10,9},{11,1... | collective-permute-start | bytes 245768 | tf_op jit(solution)/shard_map/ppermute | solution.py:438
  25.6 6.0 %collective-permute-start = (f32[5,32,128]{2,1,0:T(8,128)S(1)}, f32[5,32,128]{2,1,0:T(8,128)S(1)}, u32[]{:S(2)}, u32[]{:S(2)}) collective-permute-start(f32[5,32,128]{2,1,0:T(8,128)S(1)} %get-tuple-element.38), channel_id=1, source_target_pairs={{0,1},{1,2},{2,3},{3,0},{4,5},{5,6},{6,7},{7,4},{8,9},{9,10},{10,1... | collective-permute-start | bytes 245768 | tf_op jit(solution)/shard_map/ppermute | solution.py:437
  31.6 2.2 %copy-start.1 = (f32[16,16,32,128]{3,2,1,0:T(8,128)S(1)}, f32[16,16,32,128]{3,2,1,0:T(8,128)}, u32[]{:S(2)}) copy-start(f32[16,16,32,128]{3,2,1,0:T(8,128)} %copy-done) | copy-start | bytes 12582916
  46.8 24.4 %collective-permute-start.8 = (f32[16,32,128]{2,1,0:T(8,128)S(1)}, f32[16,32,128]{2,1,0:T(8,128)S(1)}, u32[]{:S(2)}, u32[]{:S(2)}) collective-permute-start(f32[16,32,128]{2,1,0:T(8,128)S(1)} %get-tuple-element.55), channel_id=1, source_target_pairs={{0,32},{32,64},{64,96},{96,0},{1,33},{33,65},{65,97},{97,1},{2,34}... | collective-permute-start | bytes 786440 | tf_op jit(solution)/shard_map/ppermute | solution.py:441
  47.2 24.0 %collective-permute-start.9 = (f32[16,32,128]{2,1,0:T(8,128)S(1)}, f32[16,32,128]{2,1,0:T(8,128)S(1)}, u32[]{:S(2)}, u32[]{:S(2)}) collective-permute-start(f32[16,32,128]{2,1,0:T(8,128)S(1)} %get-tuple-element.56), channel_id=1, source_target_pairs={{32,0},{64,32},{96,64},{0,96},{33,1},{65,33},{97,65},{1,97},{34,2}... | collective-permute-start | bytes 786440 | tf_op jit(solution)/shard_map/ppermute | solution.py:442
  50.1 21.1 %collective-permute-start.10 = (f32[16,32,128]{2,1,0:T(8,128)S(1)}, f32[16,32,128]{2,1,0:T(8,128)S(1)}, u32[]{:S(2)}, u32[]{:S(2)}) collective-permute-start(f32[16,32,128]{2,1,0:T(8,128)S(1)} %get-tuple-element.57), channel_id=1, source_target_pairs={{0,4},{4,8},{8,12},{12,16},{16,20},{20,24},{24,28},{28,0},{1,5},{5... | collective-permute-start | bytes 786440 | tf_op jit(solution)/shard_map/ppermute | solution.py:443
  50.1 21.1 %collective-permute-start.11 = (f32[16,32,128]{2,1,0:T(8,128)S(1)}, f32[16,32,128]{2,1,0:T(8,128)S(1)}, u32[]{:S(2)}, u32[]{:S(2)}) collective-permute-start(f32[16,32,128]{2,1,0:T(8,128)S(1)} %get-tuple-element.58), channel_id=1, source_target_pairs={{4,0},{8,4},{12,8},{16,12},{20,16},{24,20},{28,24},{0,28},{5,1},{9... | collective-permute-start | bytes 786440 | tf_op jit(solution)/shard_map/ppermute | solution.py:444
  53.1 4.3 %collective-permute-start.7 = (f32[4,32,128]{2,1,0:T(8,128)S(1)}, f32[4,32,128]{2,1,0:T(8,128)S(1)}, u32[]{:S(2)}, u32[]{:S(2)}) collective-permute-start(f32[4,32,128]{2,1,0:T(8,128)S(1)} %get-tuple-element.49), channel_id=1, source_target_pairs={{1,0},{2,1},{3,2},{0,3},{5,4},{6,5},{7,6},{4,7},{9,8},{10,9},{11,1... | collective-permute-start | bytes 196616 | tf_op jit(solution)/shard_map/ppermute | solution.py:438
  57.3 5.5 %collective-permute-start.6 = (f32[4,32,128]{2,1,0:T(8,128)S(1)}, f32[4,32,128]{2,1,0:T(8,128)S(1)}, u32[]{:S(2)}, u32[]{:S(2)}) collective-permute-start(f32[4,32,128]{2,1,0:T(8,128)S(1)} %get-tuple-element.49), channel_id=1, source_target_pairs={{0,1},{1,2},{2,3},{3,0},{4,5},{5,6},{6,7},{7,4},{8,9},{9,10},{10,1... | collective-permute-start | bytes 196616 | tf_op jit(solution)/shard_map/ppermute | solution.py:437
  71.9 24.2 %collective-permute-start.14 = (f32[16,32,128]{2,1,0:T(8,128)S(1)}, f32[16,32,128]{2,1,0:T(8,128)S(1)}, u32[]{:S(2)}, u32[]{:S(2)}) collective-permute-start(f32[16,32,128]{2,1,0:T(8,128)S(1)} %get-tuple-element.64), channel_id=1, source_target_pairs={{0,32},{32,64},{64,96},{96,0},{1,33},{33,65},{65,97},{97,1},{2,34}... | collective-permute-start | bytes 786440 | tf_op jit(solution)/shard_map/ppermute | solution.py:441
  72.0 24.2 %collective-permute-start.15 = (f32[16,32,128]{2,1,0:T(8,128)S(1)}, f32[16,32,128]{2,1,0:T(8,128)S(1)}, u32[]{:S(2)}, u32[]{:S(2)}) collective-permute-start(f32[16,32,128]{2,1,0:T(8,128)S(1)} %get-tuple-element.65), channel_id=1, source_target_pairs={{32,0},{64,32},{96,64},{0,96},{33,1},{65,33},{97,65},{1,97},{34,2}... | collective-permute-start | bytes 786440 | tf_op jit(solution)/shard_map/ppermute | solution.py:442
  75.2 21.0 %collective-permute-start.16 = (f32[16,32,128]{2,1,0:T(8,128)S(1)}, f32[16,32,128]{2,1,0:T(8,128)S(1)}, u32[]{:S(2)}, u32[]{:S(2)}) collective-permute-start(f32[16,32,128]{2,1,0:T(8,128)S(1)} %get-tuple-element.66), channel_id=1, source_target_pairs={{0,4},{4,8},{8,12},{12,16},{16,20},{20,24},{24,28},{28,0},{1,5},{5... | collective-permute-start | bytes 786440 | tf_op jit(solution)/shard_map/ppermute | solution.py:443
  75.2 21.0 %collective-permute-start.17 = (f32[16,32,128]{2,1,0:T(8,128)S(1)}, f32[16,32,128]{2,1,0:T(8,128)S(1)}, u32[]{:S(2)}, u32[]{:S(2)}) collective-permute-start(f32[16,32,128]{2,1,0:T(8,128)S(1)} %get-tuple-element.67), channel_id=1, source_target_pairs={{4,0},{8,4},{12,8},{16,12},{20,16},{24,20},{28,24},{0,28},{5,1},{9... | collective-permute-start | bytes 786440 | tf_op jit(solution)/shard_map/ppermute | solution.py:444
  78.2 4.3 %collective-permute-start.13 = (f32[4,32,128]{2,1,0:T(8,128)S(1)}, f32[4,32,128]{2,1,0:T(8,128)S(1)}, u32[]{:S(2)}, u32[]{:S(2)}) collective-permute-start(f32[4,32,128]{2,1,0:T(8,128)S(1)} %get-tuple-element.62), channel_id=1, source_target_pairs={{1,0},{2,1},{3,2},{0,3},{5,4},{6,5},{7,6},{4,7},{9,8},{10,9},{11,1... | collective-permute-start | bytes 196616 | tf_op jit(solution)/shard_map/ppermute | solution.py:438
  82.4 5.5 %collective-permute-start.12 = (f32[4,32,128]{2,1,0:T(8,128)S(1)}, f32[4,32,128]{2,1,0:T(8,128)S(1)}, u32[]{:S(2)}, u32[]{:S(2)}) collective-permute-start(f32[4,32,128]{2,1,0:T(8,128)S(1)} %get-tuple-element.62), channel_id=1, source_target_pairs={{0,1},{1,2},{2,3},{3,0},{4,5},{5,6},{6,7},{7,4},{8,9},{9,10},{10,1... | collective-permute-start | bytes 196616 | tf_op jit(solution)/shard_map/ppermute | solution.py:437
  96.2 36.0 %copy-start.2 = (f32[16,16,32,128]{3,2,1,0:T(8,128)S(1)}, f32[16,16,32,128]{3,2,1,0:T(8,128)}, u32[]{:S(2)}) copy-start(f32[16,16,32,128]{3,2,1,0:T(8,128)} %copy-done) | copy-start | bytes 12582916
  96.9 1.2 collective-permute-start.18
  98.1 3.7 %collective-permute-start.19 = (f32[32,128]{1,0:T(8,128)S(1)}, f32[32,128]{1,0:T(8,128)S(1)}, u32[]{:S(2)}, u32[]{:S(2)}) collective-permute-start(f32[32,128]{1,0:T(8,128)S(1)} %add.18), channel_id=1, source_target_pairs={{0,8},{4,12},{8,0},{12,4},{16,24},{20,28},{24,16},{28,20},{1,9},{5... | collective-permute-start | bytes 49160 | tf_op jit(solution)/shard_map/ppermute | solution.py:589
  101.9 5.2 %collective-permute-start.20 = (f32[32,128]{1,0:T(8,128)S(1)}, f32[32,128]{1,0:T(8,128)S(1)}, u32[]{:S(2)}, u32[]{:S(2)}) collective-permute-start(f32[32,128]{1,0:T(8,128)S(1)} %add.19), channel_id=1, source_target_pairs={{0,16},{4,20},{8,24},{12,28},{16,0},{20,4},{24,8},{28,12},{1,17},{... | collective-permute-start | bytes 49160 | tf_op jit(solution)/shard_map/ppermute | solution.py:589
  107.1 3.7 %collective-permute-start.21 = (f32[32,128]{1,0:T(8,128)S(1)}, f32[32,128]{1,0:T(8,128)S(1)}, u32[]{:S(2)}, u32[]{:S(2)}) collective-permute-start(f32[32,128]{1,0:T(8,128)S(1)} %add.20), channel_id=1, source_target_pairs={{0,1},{1,0},{2,3},{3,2},{4,5},{5,4},{6,7},{7,6},{8,9},{9,8},{10,11... | collective-permute-start | bytes 49160 | tf_op jit(solution)/shard_map/ppermute | solution.py:589
  110.9 5.2 %collective-permute-start.22 = (f32[32,128]{1,0:T(8,128)S(1)}, f32[32,128]{1,0:T(8,128)S(1)}, u32[]{:S(2)}, u32[]{:S(2)}) collective-permute-start(f32[32,128]{1,0:T(8,128)S(1)} %add.21), channel_id=1, source_target_pairs={{0,2},{1,3},{2,0},{3,1},{4,6},{5,7},{6,4},{7,5},{8,10},{9,11},{10,... | collective-permute-start | bytes 49160 | tf_op jit(solution)/shard_map/ppermute | solution.py:589
  116.1 3.7 %collective-permute-start.23 = (f32[32,128]{1,0:T(8,128)S(1)}, f32[32,128]{1,0:T(8,128)S(1)}, u32[]{:S(2)}, u32[]{:S(2)}) collective-permute-start(f32[32,128]{1,0:T(8,128)S(1)} %add.22), channel_id=1, source_target_pairs={{0,32},{32,0},{64,96},{96,64},{1,33},{33,1},{65,97},{97,65},{2,34}... | collective-permute-start | bytes 49160 | tf_op jit(solution)/shard_map/ppermute | solution.py:589
  119.9 5.2 %collective-permute-start.24 = (f32[32,128]{1,0:T(8,128)S(1)}, f32[32,128]{1,0:T(8,128)S(1)}, u32[]{:S(2)}, u32[]{:S(2)}) collective-permute-start(f32[32,128]{1,0:T(8,128)S(1)} %add.23.own_ref), channel_id=1, source_target_pairs={{0,64},{32,96},{64,0},{96,32},{1,65},{33,97},{65,1},{97,33},{2,66}... | collective-permute-start | bytes 49160 | tf_op jit(solution)/shard_map/ppermute | solution.py:591

commit v2 on v1

--- a/solution.py
+++ b/solution.py
@@ -23,7 +23,7 @@
 
 
 def shaped(*shape):
-    return jax.ShapeDtypeStruct(shape, F32)
+    return pltpu.VMEM(shape, F32)
 
 
 def lanes(rows):
@@ -133,7 +133,7 @@
             pltpu.SemaphoreType.DMA(()),
             pltpu.SemaphoreType.DMA(()),
         ],
-        compiler_params=params(),
+        compiler_params=pltpu.CompilerParams(vmem_limit_bytes=VMEM_LIMIT),
         name="pack_guess",
     )(perm_class, perm_table, start_guess)
 
@@ -437,6 +437,7 @@
         lax.ppermute(ends, "layer", ahead("layer")),
         lax.ppermute(ends, "layer", back("layer")),
     )
+    near, ylo, yhi = lax.optimization_barrier((near, ylo, yhi))
     far = (
         lax.ppermute(xhi, "strike", ahead("strike")),
         lax.ppermute(xlo, "strike", back("strike")),
@@ -453,18 +454,28 @@
 
 def eliminate(tables):
     row = rows_of(32)
-    for k in range(32):
+    for k in range(0, 32, 2):
         done = []
         for table in tables:
-            column = jnp.broadcast_to(table[:, k : k + 1], table.shape)
-            scaled = table[k : k + 1, :] / column[k : k + 1, :]
-            done.append(jnp.where(row == k, scaled, table - column * scaled))
+            one = jnp.broadcast_to(table[:, k : k + 1], table.shape)
+            two = jnp.broadcast_to(table[:, k + 1 : k + 2], table.shape)
+            a, b = one[k : k + 1], two[k : k + 1]
+            c, d = one[k + 1 : k + 2], two[k + 1 : k + 2]
+            scale = 1.0 / (a * d - b * c)
+            upper, lower = table[k : k + 1], table[k + 1 : k + 2]
+            first = (d * upper - b * lower) * scale
+            second = (a * lower - c * upper) * scale
+            rest = (table - one * first) - two * second
+            done.append(jnp.where(row == k, first, jnp.where(row == k + 1, second, rest)))
         tables = done
     return tables
 
 
-def solve_kernel(own_ref, other_ref, out_ref):
-    sums = own_ref[...] + other_ref[...]
+def solve_kernel(*refs):
+    out_ref = refs[-1]
+    sums = refs[0][...]
+    for ref in refs[1:-1]:
+        sums = sums + ref[...]
     lane = lanes(32)
     row = rows_of(32)
     unit = jnp.where(lane == row + 32, 1.0, 0.0)
@@ -496,30 +507,26 @@
     out_ref[32:64, :] = jnp.concatenate([nothing, -taken_t, beyond_t, nothing], axis=1)
 
 
-def solve(own, other):
+def solve(parts):
     return pl.pallas_call(
         solve_kernel,
-        in_specs=[VMEM] * 2,
+        in_specs=[VMEM] * len(parts),
         out_specs=VMEM,
         out_shape=shaped(64, 128),
         compiler_params=params(),
         name="solve_small",
-    )(own, other)
+    )(*parts)
 
 
 def combine_kernel(
-    mix_ref, guess_ref, one_ref, two_ref, three_ref, solution_hbm, residual_hbm,
-    solution, residual, sem,
+    mix_ref, guess_hbm, one_ref, two_ref, three_ref, solution_hbm, residual_hbm,
+    guess, solution, residual, sem, guess_sem,
 ):
-    nx, ny, columns, nz = guess_ref.shape
+    nx, ny, columns, nz = one_ref.shape
     slots = solution.shape[0]
-    mix = mix_ref[...]
-    high = mix.astype(BF16)
-    low = (mix - high.astype(F32)).astype(BF16)
-    mixing = jnp.concatenate(
-        [jnp.concatenate([high, high], axis=1), jnp.concatenate([low, low], axis=1)], axis=0
-    )
-    nothing = jnp.zeros((columns, 2 * nz), F32)
+
+    def arriving(x):
+        return pltpu.make_async_copy(guess_hbm.at[:, x], guess.at[x], guess_sem.at[x])
 
     def leaving(x):
         slot = lax.rem(x, slots)
@@ -528,6 +535,16 @@
             pltpu.make_async_copy(residual.at[slot], residual_hbm.at[:, x], sem.at[1, slot]),
         )
 
+    for x in range(nx):
+        arriving(x).start()
+    mix = mix_ref[...]
+    high = mix.astype(BF16)
+    low = (mix - high.astype(F32)).astype(BF16)
+    mixing = jnp.concatenate(
+        [jnp.concatenate([high, high], axis=1), jnp.concatenate([low, low], axis=1)], axis=0
+    )
+    nothing = jnp.zeros((columns, 2 * nz), F32)
+
     def at_x(x, carry):
         slot = lax.rem(x, slots)
 
@@ -536,6 +553,8 @@
             for copy in leaving(x - slots):
                 copy.wait()
 
+        arriving(x).wait()
+        guess_rows = guess.at[x].reshape(columns * ny, nz)
         solution_rows = solution.at[slot].reshape(columns * ny, nz)
         residual_rows = residual.at[slot].reshape(columns * ny, nz)
         for y in range(0, ny, 2):
@@ -549,7 +568,7 @@
             for step in range(2):
                 rows = pl.ds(y + step, columns, stride=ny)
                 part = mixed[:, step * nz : (step + 1) * nz]
-                solution_rows[rows, :] = guess_ref[x, y + step] + part[0:32]
+                solution_rows[rows, :] = guess_rows[rows, :] + part[0:32]
                 residual_rows[rows, :] = one_ref[x, y + step] + part[32:64]
         for copy in leaving(x):
             copy.start()
@@ -562,33 +581,46 @@
 
 
 def combine(mix, guess, one, two, three):
-    nx, ny, columns, nz = guess.shape
+    nx, ny, columns, nz = one.shape
     return pl.pallas_call(
         combine_kernel,
-        in_specs=[VMEM] * 5,
+        in_specs=[VMEM, HBM, VMEM, VMEM, VMEM],
         out_specs=[HBM] * 2,
-        out_shape=[shaped(columns, nx, ny, nz)] * 2,
+        out_shape=[jax.ShapeDtypeStruct((columns, nx, ny, nz), F32)] * 2,
         scratch_shapes=[
+            pltpu.VMEM((nx, columns, ny, nz), F32),
             pltpu.VMEM((8, columns, ny, nz), F32),
             pltpu.VMEM((8, columns, ny, nz), F32),
             pltpu.SemaphoreType.DMA((2, 8)),
+            pltpu.SemaphoreType.DMA((nx,)),
         ],
-        compiler_params=params(),
+        compiler_params=pltpu.CompilerParams(vmem_limit_bytes=VMEM_LIMIT),
         name="combine_fields",
     )(mix, guess, one, two, three)
 
 
+def swaps(axis, mask, stride=1):
+    return [(i, i ^ (mask * stride)) for i in range(lax.axis_size(axis))]
+
+
 def summed_but_last(values):
-    steps = []
-    for axis in AXES[1:] + AXES[:1]:
-        size, mask = lax.axis_size(axis), 1
-        while mask < size:
-            steps.append((axis, [(i, i ^ mask) for i in range(size)]))
-            mask *= 2
-    for axis, pairs in steps[:-1]:
-        values = values + lax.ppermute(values, axis, pairs)
-    axis, pairs = steps[-1]
-    return values, lax.ppermute(values, axis, pairs)
+    groups = []
+    for axis in AXES[::-1]:
+        size, stride = lax.axis_size(axis), 1
+        while size // stride > 4:
+            values = values + lax.ppermute(values, axis, swaps(axis, 1, stride))
+            stride *= 2
+        groups.append((axis, stride))
+    for place, (axis, stride) in enumerate(groups):
+        others = [
+            lax.ppermute(values, axis, swaps(axis, mask, stride))
+            for mask in (1, 3, 2)
+            if mask * stride < lax.axis_size(axis)
+        ]
+        if place + 1 < len(groups):
+            for other in others:
+                values = values + other
+    return [values, *others]
 
 
 def shards(perm_class, perm_table, boreholes, start_guess):
@@ -602,6 +634,10 @@
         inside += [place > 0, place < size - 1]
     inside = jnp.stack(inside).astype(F32)
 
+    perm_class, perm_table, start_guess = (
+        pltpu.with_memory_space_constraint(held, pltpu.HBM)
+        for held in (perm_class, perm_table, start_guess)
+    )
     guess, perm, *faces = pack(perm_class, perm_table, start_guess)
     near, far = exchanged(*faces)
     extra = (perm, inside, anchors.astype(jnp.int32), boreholes[:, None])
@@ -618,8 +654,8 @@
     near, far = exchanged(*faces, ends)
     part, total = inner_part(once, near, weights, False, True, totals)
     twice, sums = sides_part(part, once, far, None, [wx, wy, total, sums], False, True)
-    mix = solve(*summed_but_last(sums))
-    return tuple(combine(mix, guess, residual, once, twice))
+    mix = solve(summed_but_last(sums))
+    return tuple(combine(mix, start_guess, residual, once, twice))
 
 
 def solution(mesh):

time: 139 us -> 110 us (0.79)
  waiting for transfers between devices: 49.6 us -> 14.1 us
  starting transfers between devices: 28.6 us -> 37.4 us
  local copies, waits for them, and re-layouts: 8.14 us -> 4.39 us
    ppermute x7 -> x10, waiting for transfers between devices: 26.6 us -> 9.4 us  [the longest x9 8.23 us: summed_but_last(): lax.ppermute(values, axis, swaps(axis, mask, stride))]
    ppermute x3, waiting for transfers between devices: 16.6 us -> 4.66 us  [exchanged(): lax.ppermute(ends, 'layer', ahead('layer'))]
    ppermute x7 -> x10, starting transfers between devices: 1.51 us -> 10.6 us  [the longest x9 10.5 us: summed_but_last(): lax.ppermute(values, axis, swaps(axis, mask, stride))]
    ppermute x3, waiting for transfers between devices: 6.34 us -> 0.01 us  [exchanged(): lax.ppermute(ends, 'layer', back('layer'))]
    unnamed x14 -> x6, local copies, waits for them, and re-layouts: 7.95 us -> 4.2 us
    ppermute x3, starting transfers between devices: 8.17 us -> 6.08 us  [exchanged(): lax.ppermute(ends, 'layer', back('layer'))]
    ppermute x3, starting transfers between devices: 0.27 us -> 2.22 us  [exchanged(): lax.ppermute(ends, 'layer', ahead('layer'))]
    ppermute x3, starting transfers between devices: 7.84 us -> 5.98 us  [exchanged(): lax.ppermute(xlo, 'strike', back('strike'))]
  transfers between devices with their start and end apart: 25 -> 28, of which waited for: 13 -> 9; matrix products, arithmetic and copies ran while one was open for 0% -> 0% of each run, Pallas kernels for 21% -> 26%
where the time goes in v2:
time: 110 us; the launch traced here: 109 us
  Pallas kernels  52.5 us (48%)
  starting transfers between devices  37.4 us (34%)
  waiting for transfers between devices  14.1 us (13%)
  local copies, waits for them, and re-layouts  4.39 us (4%)
    pallas_call x3, Pallas kernels, inner_part(): pl.pallas_call(functools.partial(inner_kernel, first, last, totals), in_s...  28.6 us
    ppermute x9, starting transfers between devices, summed_but_last(): lax.ppermute(values, axis, swaps(axis, mask, stride))  10.5 us
    ppermute x3, starting transfers between devices, exchanged(): lax.ppermute(ylo, 'dip', back('dip'))  8.86 us
    pallas_call x1, Pallas kernels, pack(): pl.pallas_call(pack_kernel, in_specs=[HBM] * 3, out_specs=[VMEM] * 7, out...  8.4 us
    pallas_call x1, Pallas kernels, combine(): pl.pallas_call(combine_kernel, in_specs=[VMEM, HBM, VMEM, VMEM, VMEM], ou...  8.37 us
    ppermute x9, waiting for transfers between devices, summed_but_last(): lax.ppermute(values, axis, swaps(axis, mask, stride))  8.23 us
    ppermute x3, starting transfers between devices, exchanged(): lax.ppermute(ends, 'layer', back('layer'))  6.08 us
    ppermute x3, starting transfers between devices, exchanged(): lax.ppermute(xlo, 'strike', back('strike'))  5.98 us
  transfers between devices with their start and end apart: 28, of which 9 were waited for; matrix products, arithmetic and copies ran while one was open for 0% of the time, Pallas kernels for 26%

profile of v2, /device:TPU:0, one launch (start us, length us, event | category | flops | bytes accessed | tf_op | source)
XLA Modules:
  0.0 109.4 jit_solution(832630791282242779)
XLA Ops:
  0.6 8.4 %pack_guess.1 = (f32[16,16,32,128]{3,2,1,0:T(8,128)S(1)}, f32[16,16,128]{2,1,0:T(8,128)S(1)}, f32[17,32,128]{2,1,0:T(8,128)S(1)}, f32[17,32,128]{2,1,0:T(8,128)S...) custom-call(s32[16,16,128]{2,1,0:T(8,128)} %class_hbm.1, f32[16]{0:T(128)} %table_hbm.1, ...), custom_call_target="tpu_custom_call" | custom-call | tf_op jit(solution)/shard_map/pack_guess/pallas_call | solution.py:115
  9.1 2.0 %copy-done = f32[16,16,32,128]{3,2,1,0:T(8,128)} copy-done((f32[16,16,32,128]{3,2,1,0:T(8,128)}, f32[16,16,32,128]{3,2,1,0:T(8,128)S(1)}, u32[]{:S(2)}) %copy-start) | copy-done | bytes 4194328
  11.1 4.1 %collective-permute-start.1 = (f32[5,32,128]{2,1,0:T(8,128)S(1)}, f32[5,32,128]{2,1,0:T(8,128)S(1)}, u32[]{:S(2)}, u32[]{:S(2)}) collective-permute-start(f32[5,32,128]{2,1,0:T(8,128)S(1)} %get-tuple-element.50), channel_id=1, source_target_pairs={{1,0},{2,1},{3,2},{0,3},{5,4},{6,5},{7,6},{4,7},{9,8},{10,9},{11,1... | collective-permute-start | bytes 245768 | tf_op jit(solution)/shard_map/ppermute | solution.py:438
  15.2 1.5 %collective-permute-start.2 = (f32[17,32,128]{2,1,0:T(8,128)S(1)}, f32[17,32,128]{2,1,0:T(8,128)S(1)}, u32[]{:S(2)}, u32[]{:S(2)}) collective-permute-start(f32[17,32,128]{2,1,0:T(8,128)S(1)} %get-tuple-element.57), channel_id=1, source_target_pairs={{0,32},{32,64},{64,96},{96,0},{1,33},{33,65},{65,97},{97,1},{2,34}... | collective-permute-start | bytes 835592 | tf_op jit(solution)/shard_map/ppermute | solution.py:442
  16.7 1.7 %collective-permute-start.3 = (f32[17,32,128]{2,1,0:T(8,128)S(1)}, f32[17,32,128]{2,1,0:T(8,128)S(1)}, u32[]{:S(2)}, u32[]{:S(2)}) collective-permute-start(f32[17,32,128]{2,1,0:T(8,128)S(1)} %get-tuple-element.58), channel_id=1, source_target_pairs={{32,0},{64,32},{96,64},{0,96},{33,1},{65,33},{97,65},{1,97},{34,2}... | collective-permute-start | bytes 835592 | tf_op jit(solution)/shard_map/ppermute | solution.py:443
  18.4 2.4 %collective-permute-done.refs_1_ = f32[5,32,128]{2,1,0:T(8,128)S(1)} collective-permute-done((f32[5,32,128]{2,1,0:T(8,128)S(1)}, f32[5,32,128]{2,1,0:T(8,128)S(1)}, u32[]{:S(2)}, u32[]{:S(2)}) %collective-permute-start) | collective-permute-done | bytes 81952 | tf_op jit(solution)/shard_map/ppermute | solution.py:437
  20.8 3.0 %collective-permute-start.5 = (f32[17,32,128]{2,1,0:T(8,128)S(1)}, f32[17,32,128]{2,1,0:T(8,128)S(1)}, u32[]{:S(2)}, u32[]{:S(2)}) collective-permute-start(f32[17,32,128]{2,1,0:T(8,128)S(1)} %get-tuple-element.60), channel_id=1, source_target_pairs={{4,0},{8,4},{12,8},{16,12},{20,16},{24,20},{28,24},{0,28},{5,1},{9... | collective-permute-start | bytes 835592 | tf_op jit(solution)/shard_map/ppermute | solution.py:445
  24.1 2.2 %copy-done.1 = f32[16,16,32,128]{3,2,1,0:T(8,128)S(1)} copy-done((f32[16,16,32,128]{3,2,1,0:T(8,128)S(1)}, f32[16,16,32,128]{3,2,1,0:T(8,128)}, u32[]{:S(2)}) %copy-start.1) | copy-done | bytes 4194328
  26.3 12.0 %inner_first.1 = (f32[16,16,32,128]{3,2,1,0:T(8,128)S(1)}, f32[4,32,128]{2,1,0:T(8,128)S(1)}, f32[17,16,128]{2,1,0:T(8,128)S(1)}, f32[16,24,128]{2,1,0:T(8,128)S...) custom-call(f32[16,16,32,128]{3,2,1,0:T(8,128)S(1)} %copy-done.1, ...), custom_call_target="tpu_custom_call" | custom-call | flops 20971520 | bytes 25165824 | tf_op jit(solution)/shard_map/inner_first/pallas_call | solution.py:387
  40.2 1.2 %collective-permute-start.6 = (f32[4,32,128]{2,1,0:T(8,128)S(1)}, f32[4,32,128]{2,1,0:T(8,128)S(1)}, u32[]{:S(2)}, u32[]{:S(2)}) collective-permute-start(f32[4,32,128]{2,1,0:T(8,128)S(1)} %get-tuple-element.65), channel_id=1, source_target_pairs={{0,1},{1,2},{2,3},{3,0},{4,5},{5,6},{6,7},{7,4},{8,9},{9,10},{10,1... | collective-permute-start | bytes 196616 | tf_op jit(solution)/shard_map/ppermute | solution.py:437
  41.4 1.5 %collective-permute-start.8 = (f32[16,32,128]{2,1,0:T(8,128)S(1)}, f32[16,32,128]{2,1,0:T(8,128)S(1)}, u32[]{:S(2)}, u32[]{:S(2)}) collective-permute-start(f32[16,32,128]{2,1,0:T(8,128)S(1)} %get-tuple-element.75), channel_id=1, source_target_pairs={{0,32},{32,64},{64,96},{96,0},{1,33},{33,65},{65,97},{97,1},{2,34}... | collective-permute-start | bytes 786440 | tf_op jit(solution)/shard_map/ppermute | solution.py:442
  42.9 1.7 %collective-permute-start.9 = (f32[16,32,128]{2,1,0:T(8,128)S(1)}, f32[16,32,128]{2,1,0:T(8,128)S(1)}, u32[]{:S(2)}, u32[]{:S(2)}) collective-permute-start(f32[16,32,128]{2,1,0:T(8,128)S(1)} %get-tuple-element.76), channel_id=1, source_target_pairs={{32,0},{64,32},{96,64},{0,96},{33,1},{65,33},{97,65},{1,97},{34,2}... | collective-permute-start | bytes 786440 | tf_op jit(solution)/shard_map/ppermute | solution.py:443
  44.6 1.0 collective-permute-done.6.refs_1_
  45.6 3.0 %collective-permute-start.11 = (f32[16,32,128]{2,1,0:T(8,128)S(1)}, f32[16,32,128]{2,1,0:T(8,128)S(1)}, u32[]{:S(2)}, u32[]{:S(2)}) collective-permute-start(f32[16,32,128]{2,1,0:T(8,128)S(1)} %get-tuple-element.78), channel_id=1, source_target_pairs={{4,0},{8,4},{12,8},{16,12},{20,16},{24,20},{28,24},{0,28},{5,1},{9... | collective-permute-start | bytes 786440 | tf_op jit(solution)/shard_map/ppermute | solution.py:445
  48.6 8.4 %inner_next.1 = (f32[16,16,32,128]{3,2,1,0:T(8,128)S(1)}, f32[4,32,128]{2,1,0:T(8,128)S(1)}, f32[64,128]{1,0:T(8,128)S(1)}) custom-call(f32[16,16,32,128]{3,2,1,0:T(8,128)S(1)} %get-tuple-element.64.refs_0_.refs_1_.one_ref, f32[4,32,128]{2,1,0:T(8,128)S(1)} %collective-permute-done.6.refs_1_, f32[4,32,128]{2,1,0:T(8,128)S(1)} %collective-permute-done.7.refs_2_, ...), custom_call_target="tpu_custom_call" | custom-call | flops 20971520 | bytes 25165824 | tf_op jit(solution)/shard_map/inner_next/pallas_call | solution.py:387
  57.7 1.1 collective-permute-start.13
  58.8 1.0 collective-permute-start.12
  60.6 2.5 %collective-permute-start.15 = (f32[16,32,128]{2,1,0:T(8,128)S(1)}, f32[16,32,128]{2,1,0:T(8,128)S(1)}, u32[]{:S(2)}, u32[]{:S(2)}) collective-permute-start(f32[16,32,128]{2,1,0:T(8,128)S(1)} %get-tuple-element.89), channel_id=1, source_target_pairs={{32,0},{64,32},{96,64},{0,96},{33,1},{65,33},{97,65},{1,97},{34,2}... | collective-permute-start | bytes 786440 | tf_op jit(solution)/shard_map/ppermute | solution.py:443
  63.1 1.2 %collective-permute-done.12.refs_1_ = f32[4,32,128]{2,1,0:T(8,128)S(1)} collective-permute-done((f32[4,32,128]{2,1,0:T(8,128)S(1)}, f32[4,32,128]{2,1,0:T(8,128)S(1)}, u32[]{:S(2)}, u32[]{:S(2)}) %collective-permute-start.12) | collective-permute-done | bytes 65568 | tf_op jit(solution)/shard_map/ppermute | solution.py:437
  64.3 3.0 %collective-permute-start.17 = (f32[16,32,128]{2,1,0:T(8,128)S(1)}, f32[16,32,128]{2,1,0:T(8,128)S(1)}, u32[]{:S(2)}, u32[]{:S(2)}) collective-permute-start(f32[16,32,128]{2,1,0:T(8,128)S(1)} %get-tuple-element.91), channel_id=1, source_target_pairs={{4,0},{8,4},{12,8},{16,12},{20,16},{24,20},{28,24},{0,28},{5,1},{9... | collective-permute-start | bytes 786440 | tf_op jit(solution)/shard_map/ppermute | solution.py:445
  67.2 8.2 %inner_last.1 = (f32[16,16,32,128]{3,2,1,0:T(8,128)S(1)}, f32[64,128]{1,0:T(8,128)S(1)}) custom-call(f32[16,16,32,128]{3,2,1,0:T(8,128)S(1)} %get-tuple-element.81.refs_0_.refs_1_.two_ref, f32[4,32,128]{2,1,0:T(8,128)S(1)} %collective-permute-done.12.refs_1_, f32[4,32,128]{2,1,0:T(8,128)S(1)} %collective-permute-done.13.refs_2_, ...), custom_call_target="tpu_custom_call" | custom-call | flops 20971520 | bytes 25165824 | tf_op jit(solution)/shard_map/inner_last/pallas_call | solution.py:387
  76.3 1.2 %collective-permute-done.18 = f32[32,128]{1,0:T(8,128)S(1)} collective-permute-done((f32[32,128]{1,0:T(8,128)S(1)}, f32[32,128]{1,0:T(8,128)S(1)}, u32[]{:S(2)}, u32[]{:S(2)}) %collective-permute-start.18) | collective-permute-done | bytes 16416 | tf_op jit(solution)/shard_map/ppermute | solution.py:611
  77.5 2.5 %collective-permute-start.20 = (f32[32,128]{1,0:T(8,128)S(1)}, f32[32,128]{1,0:T(8,128)S(1)}, u32[]{:S(2)}, u32[]{:S(2)}) collective-permute-start(f32[32,128]{1,0:T(8,128)S(1)} %add.21), channel_id=1, source_target_pairs={{0,3},{1,2},{2,1},{3,0},{4,7},{5,6},{6,5},{7,4},{8,11},{9,10},{10,... | collective-permute-start | bytes 49160 | tf_op jit(solution)/shard_map/ppermute | solution.py:616
  80.9 1.8 %collective-permute-done.21 = f32[32,128]{1,0:T(8,128)S(1)} collective-permute-done((f32[32,128]{1,0:T(8,128)S(1)}, f32[32,128]{1,0:T(8,128)S(1)}, u32[]{:S(2)}, u32[]{:S(2)}) %collective-permute-start.21) | collective-permute-done | bytes 16416 | tf_op jit(solution)/shard_map/ppermute | solution.py:616
  84.3 2.9 %collective-permute-start.22 = (f32[32,128]{1,0:T(8,128)S(1)}, f32[32,128]{1,0:T(8,128)S(1)}, u32[]{:S(2)}, u32[]{:S(2)}) collective-permute-start(f32[32,128]{1,0:T(8,128)S(1)} %add_add_fusion.1), channel_id=1, source_target_pairs={{0,8},{4,12},{8,0},{12,4},{16,24},{20,28},{24,16},{28,20},{1,9},{5... | collective-permute-start | bytes 49160 | tf_op jit(solution)/shard_map/ppermute | solution.py:616
  87.2 1.8 %collective-permute-done.24 = f32[32,128]{1,0:T(8,128)S(1)} collective-permute-done((f32[32,128]{1,0:T(8,128)S(1)}, f32[32,128]{1,0:T(8,128)S(1)}, u32[]{:S(2)}, u32[]{:S(2)}) %collective-permute-start.24) | collective-permute-done | bytes 16416 | tf_op jit(solution)/shard_map/ppermute | solution.py:616
  88.9 2.4 %collective-permute-start.27 = (f32[32,128]{1,0:T(8,128)S(1)}, f32[32,128]{1,0:T(8,128)S(1)}, u32[]{:S(2)}, u32[]{:S(2)}) collective-permute-start(f32[32,128]{1,0:T(8,128)S(1)} %add_add_fusion.refs_0_), channel_id=1, source_target_pairs={{0,64},{32,96},{64,0},{96,32},{1,65},{33,97},{65,1},{97,33},{2,66}... | collective-permute-start | bytes 49160 | tf_op jit(solution)/shard_map/ppermute | solution.py:616
  91.3 1.1 %collective-permute-start.26 = (f32[32,128]{1,0:T(8,128)S(1)}, f32[32,128]{1,0:T(8,128)S(1)}, u32[]{:S(2)}, u32[]{:S(2)}) collective-permute-start(f32[32,128]{1,0:T(8,128)S(1)} %add_add_fusion.refs_0_), channel_id=1, source_target_pairs={{0,96},{32,64},{64,32},{96,0},{1,97},{33,65},{65,33},{97,1},{2,98}... | collective-permute-start | bytes 49160 | tf_op jit(solution)/shard_map/ppermute | solution.py:616
  92.5 1.8 %collective-permute-done.27.refs_3_ = f32[32,128]{1,0:T(8,128)S(1)} collective-permute-done((f32[32,128]{1,0:T(8,128)S(1)}, f32[32,128]{1,0:T(8,128)S(1)}, u32[]{:S(2)}, u32[]{:S(2)}) %collective-permute-start.27) | collective-permute-done | bytes 16416 | tf_op jit(solution)/shard_map/ppermute | solution.py:616
  94.3 2.0 %collective-permute-done.26.refs_2_ = f32[32,128]{1,0:T(8,128)S(1)} collective-permute-done((f32[32,128]{1,0:T(8,128)S(1)}, f32[32,128]{1,0:T(8,128)S(1)}, u32[]{:S(2)}, u32[]{:S(2)}) %collective-permute-start.26) | collective-permute-done | bytes 16416 | tf_op jit(solution)/shard_map/ppermute | solution.py:616
  96.3 4.8 %solve_small.1.mix_ref = f32[64,128]{1,0:T(8,128)S(1)} custom-call(f32[32,128]{1,0:T(8,128)S(1)} %add_add_fusion.refs_0_, f32[32,128]{1,0:T(8,128)S(1)} %collective-permute-done.25.refs_1_, f32[32,128]{1,0:T(8,128)S(1)} %collective-permute-done.26.refs_2_, f32[32,128]{1,0:T(8,128)S(1)} %collective-permute-done.27.refs_3_), custom_call_target="tpu_custom_call" | custom-call | tf_op jit(solution)/shard_map/solve_small/pallas_call | solution.py:511
  101.0 8.4 %combine_fields.1 = (f32[32,16,16,128]{3,2,1,0:T(8,128)}, f32[32,16,16,128]{3,2,1,0:T(8,128)}) custom-call(f32[64,128]{1,0:T(8,128)S(1)} %solve_small.1.mix_ref, f32[32,16,16,128]{3,2,1,0:T(8,128)} %guess_hbm.3, f32[16,16,32,128]{3,2,1,0:T(8,128)S(1)} %get-tuple-element.64.refs_0_.refs_1_.one_ref, ...), custom_call_target="tpu_custom_call" | custom-call | tf_op jit(solution)/shard_map/combine_fields/pallas_call | solution.py:585
  (46 shorter events, 7.0 us)
Async XLA Ops:
  0.6 23.3 %copy-start.2 = (s32[32]{0:T(128)S(1)}, s32[32]{0:T(128)}, u32[]{:S(2)}) copy-start(s32[32]{0:T(128)} %param.6) | copy-start | bytes 388
  9.0 2.0 %copy-start = (f32[16,16,32,128]{3,2,1,0:T(8,128)}, f32[16,16,32,128]{3,2,1,0:T(8,128)S(1)}, u32[]{:S(2)}) copy-start(f32[16,16,32,128]{3,2,1,0:T(8,128)S(1)} %get-tuple-element.49.refs_0_.refs_1_) | copy-start | bytes 12582916
  11.1 7.4 %collective-permute-start.1 = (f32[5,32,128]{2,1,0:T(8,128)S(1)}, f32[5,32,128]{2,1,0:T(8,128)S(1)}, u32[]{:S(2)}, u32[]{:S(2)}) collective-permute-start(f32[5,32,128]{2,1,0:T(8,128)S(1)} %get-tuple-element.50), channel_id=1, source_target_pairs={{1,0},{2,1},{3,2},{0,3},{5,4},{6,5},{7,6},{4,7},{9,8},{10,9},{11,1... | collective-permute-start | bytes 245768 | tf_op jit(solution)/shard_map/ppermute | solution.py:438
  15.2 5.7 %collective-permute-start = (f32[5,32,128]{2,1,0:T(8,128)S(1)}, f32[5,32,128]{2,1,0:T(8,128)S(1)}, u32[]{:S(2)}, u32[]{:S(2)}) collective-permute-start(f32[5,32,128]{2,1,0:T(8,128)S(1)} %get-tuple-element.50), channel_id=1, source_target_pairs={{0,1},{1,2},{2,3},{3,0},{4,5},{5,6},{6,7},{7,4},{8,9},{9,10},{10,1... | collective-permute-start | bytes 245768 | tf_op jit(solution)/shard_map/ppermute | solution.py:437
  15.2 23.1 %collective-permute-start.2 = (f32[17,32,128]{2,1,0:T(8,128)S(1)}, f32[17,32,128]{2,1,0:T(8,128)S(1)}, u32[]{:S(2)}, u32[]{:S(2)}) collective-permute-start(f32[17,32,128]{2,1,0:T(8,128)S(1)} %get-tuple-element.57), channel_id=1, source_target_pairs={{0,32},{32,64},{64,96},{96,0},{1,33},{33,65},{65,97},{97,1},{2,34}... | collective-permute-start | bytes 835592 | tf_op jit(solution)/shard_map/ppermute | solution.py:442
  16.7 21.6 %collective-permute-start.3 = (f32[17,32,128]{2,1,0:T(8,128)S(1)}, f32[17,32,128]{2,1,0:T(8,128)S(1)}, u32[]{:S(2)}, u32[]{:S(2)}) collective-permute-start(f32[17,32,128]{2,1,0:T(8,128)S(1)} %get-tuple-element.58), channel_id=1, source_target_pairs={{32,0},{64,32},{96,64},{0,96},{33,1},{65,33},{97,65},{1,97},{34,2}... | collective-permute-start | bytes 835592 | tf_op jit(solution)/shard_map/ppermute | solution.py:443
  20.8 17.5 %collective-permute-start.4 = (f32[17,32,128]{2,1,0:T(8,128)S(1)}, f32[17,32,128]{2,1,0:T(8,128)S(1)}, u32[]{:S(2)}, u32[]{:S(2)}) collective-permute-start(f32[17,32,128]{2,1,0:T(8,128)S(1)} %get-tuple-element.59), channel_id=1, source_target_pairs={{0,4},{4,8},{8,12},{12,16},{16,20},{20,24},{24,28},{28,0},{1,5},{5... | collective-permute-start | bytes 835592 | tf_op jit(solution)/shard_map/ppermute | solution.py:444
  20.8 17.5 %collective-permute-start.5 = (f32[17,32,128]{2,1,0:T(8,128)S(1)}, f32[17,32,128]{2,1,0:T(8,128)S(1)}, u32[]{:S(2)}, u32[]{:S(2)}) collective-permute-start(f32[17,32,128]{2,1,0:T(8,128)S(1)} %get-tuple-element.60), channel_id=1, source_target_pairs={{4,0},{8,4},{12,8},{16,12},{20,16},{24,20},{28,24},{0,28},{5,1},{9... | collective-permute-start | bytes 835592 | tf_op jit(solution)/shard_map/ppermute | solution.py:445
  24.1 2.2 %copy-start.1 = (f32[16,16,32,128]{3,2,1,0:T(8,128)S(1)}, f32[16,16,32,128]{3,2,1,0:T(8,128)}, u32[]{:S(2)}) copy-start(f32[16,16,32,128]{3,2,1,0:T(8,128)} %copy-done) | copy-start | bytes 12582916
  39.3 5.3 %collective-permute-start.7 = (f32[4,32,128]{2,1,0:T(8,128)S(1)}, f32[4,32,128]{2,1,0:T(8,128)S(1)}, u32[]{:S(2)}, u32[]{:S(2)}) collective-permute-start(f32[4,32,128]{2,1,0:T(8,128)S(1)} %get-tuple-element.65), channel_id=1, source_target_pairs={{1,0},{2,1},{3,2},{0,3},{5,4},{6,5},{7,6},{4,7},{9,8},{10,9},{11,1... | collective-permute-start | bytes 196616 | tf_op jit(solution)/shard_map/ppermute | solution.py:438
  40.2 5.5 %collective-permute-start.6 = (f32[4,32,128]{2,1,0:T(8,128)S(1)}, f32[4,32,128]{2,1,0:T(8,128)S(1)}, u32[]{:S(2)}, u32[]{:S(2)}) collective-permute-start(f32[4,32,128]{2,1,0:T(8,128)S(1)} %get-tuple-element.65), channel_id=1, source_target_pairs={{0,1},{1,2},{2,3},{3,0},{4,5},{5,6},{6,7},{7,4},{8,9},{9,10},{10,1... | collective-permute-start | bytes 196616 | tf_op jit(solution)/shard_map/ppermute | solution.py:437
  41.4 15.6 %collective-permute-start.8 = (f32[16,32,128]{2,1,0:T(8,128)S(1)}, f32[16,32,128]{2,1,0:T(8,128)S(1)}, u32[]{:S(2)}, u32[]{:S(2)}) collective-permute-start(f32[16,32,128]{2,1,0:T(8,128)S(1)} %get-tuple-element.75), channel_id=1, source_target_pairs={{0,32},{32,64},{64,96},{96,0},{1,33},{33,65},{65,97},{97,1},{2,34}... | collective-permute-start | bytes 786440 | tf_op jit(solution)/shard_map/ppermute | solution.py:442
  42.9 14.1 %collective-permute-start.9 = (f32[16,32,128]{2,1,0:T(8,128)S(1)}, f32[16,32,128]{2,1,0:T(8,128)S(1)}, u32[]{:S(2)}, u32[]{:S(2)}) collective-permute-start(f32[16,32,128]{2,1,0:T(8,128)S(1)} %get-tuple-element.76), channel_id=1, source_target_pairs={{32,0},{64,32},{96,64},{0,96},{33,1},{65,33},{97,65},{1,97},{34,2}... | collective-permute-start | bytes 786440 | tf_op jit(solution)/shard_map/ppermute | solution.py:443
  45.6 11.4 %collective-permute-start.10 = (f32[16,32,128]{2,1,0:T(8,128)S(1)}, f32[16,32,128]{2,1,0:T(8,128)S(1)}, u32[]{:S(2)}, u32[]{:S(2)}) collective-permute-start(f32[16,32,128]{2,1,0:T(8,128)S(1)} %get-tuple-element.77), channel_id=1, source_target_pairs={{0,4},{4,8},{8,12},{12,16},{16,20},{20,24},{24,28},{28,0},{1,5},{5... | collective-permute-start | bytes 786440 | tf_op jit(solution)/shard_map/ppermute | solution.py:444
  45.6 11.4 %collective-permute-start.11 = (f32[16,32,128]{2,1,0:T(8,128)S(1)}, f32[16,32,128]{2,1,0:T(8,128)S(1)}, u32[]{:S(2)}, u32[]{:S(2)}) collective-permute-start(f32[16,32,128]{2,1,0:T(8,128)S(1)} %get-tuple-element.78), channel_id=1, source_target_pairs={{4,0},{8,4},{12,8},{16,12},{20,16},{24,20},{28,24},{0,28},{5,1},{9... | collective-permute-start | bytes 786440 | tf_op jit(solution)/shard_map/ppermute | solution.py:445
  57.7 5.3 %collective-permute-start.13 = (f32[4,32,128]{2,1,0:T(8,128)S(1)}, f32[4,32,128]{2,1,0:T(8,128)S(1)}, u32[]{:S(2)}, u32[]{:S(2)}) collective-permute-start(f32[4,32,128]{2,1,0:T(8,128)S(1)} %get-tuple-element.82), channel_id=1, source_target_pairs={{1,0},{2,1},{3,2},{0,3},{5,4},{6,5},{7,6},{4,7},{9,8},{10,9},{11,1... | collective-permute-start | bytes 196616 | tf_op jit(solution)/shard_map/ppermute | solution.py:438
  58.8 5.5 %collective-permute-start.12 = (f32[4,32,128]{2,1,0:T(8,128)S(1)}, f32[4,32,128]{2,1,0:T(8,128)S(1)}, u32[]{:S(2)}, u32[]{:S(2)}) collective-permute-start(f32[4,32,128]{2,1,0:T(8,128)S(1)} %get-tuple-element.82), channel_id=1, source_target_pairs={{0,1},{1,2},{2,3},{3,0},{4,5},{5,6},{6,7},{7,4},{8,9},{9,10},{10,1... | collective-permute-start | bytes 196616 | tf_op jit(solution)/shard_map/ppermute | solution.py:437
  59.8 15.7 %collective-permute-start.14 = (f32[16,32,128]{2,1,0:T(8,128)S(1)}, f32[16,32,128]{2,1,0:T(8,128)S(1)}, u32[]{:S(2)}, u32[]{:S(2)}) collective-permute-start(f32[16,32,128]{2,1,0:T(8,128)S(1)} %get-tuple-element.88), channel_id=1, source_target_pairs={{0,32},{32,64},{64,96},{96,0},{1,33},{33,65},{65,97},{97,1},{2,34}... | collective-permute-start | bytes 786440 | tf_op jit(solution)/shard_map/ppermute | solution.py:442
  60.6 14.9 %collective-permute-start.15 = (f32[16,32,128]{2,1,0:T(8,128)S(1)}, f32[16,32,128]{2,1,0:T(8,128)S(1)}, u32[]{:S(2)}, u32[]{:S(2)}) collective-permute-start(f32[16,32,128]{2,1,0:T(8,128)S(1)} %get-tuple-element.89), channel_id=1, source_target_pairs={{32,0},{64,32},{96,64},{0,96},{33,1},{65,33},{97,65},{1,97},{34,2}... | collective-permute-start | bytes 786440 | tf_op jit(solution)/shard_map/ppermute | solution.py:443
  64.3 11.2 %collective-permute-start.16 = (f32[16,32,128]{2,1,0:T(8,128)S(1)}, f32[16,32,128]{2,1,0:T(8,128)S(1)}, u32[]{:S(2)}, u32[]{:S(2)}) collective-permute-start(f32[16,32,128]{2,1,0:T(8,128)S(1)} %get-tuple-element.90), channel_id=1, source_target_pairs={{0,4},{4,8},{8,12},{12,16},{16,20},{20,24},{24,28},{28,0},{1,5},{5... | collective-permute-start | bytes 786440 | tf_op jit(solution)/shard_map/ppermute | solution.py:444
  64.3 11.2 %collective-permute-start.17 = (f32[16,32,128]{2,1,0:T(8,128)S(1)}, f32[16,32,128]{2,1,0:T(8,128)S(1)}, u32[]{:S(2)}, u32[]{:S(2)}) collective-permute-start(f32[16,32,128]{2,1,0:T(8,128)S(1)} %get-tuple-element.91), channel_id=1, source_target_pairs={{4,0},{8,4},{12,8},{16,12},{20,16},{24,20},{28,24},{0,28},{5,1},{9... | collective-permute-start | bytes 786440 | tf_op jit(solution)/shard_map/ppermute | solution.py:445
  76.2 1.2 %collective-permute-start.18 = (f32[32,128]{1,0:T(8,128)S(1)}, f32[32,128]{1,0:T(8,128)S(1)}, u32[]{:S(2)}, u32[]{:S(2)}) collective-permute-start(f32[32,128]{1,0:T(8,128)S(1)} %get-tuple-element.94), channel_id=1, source_target_pairs={{0,4},{4,0},{8,12},{12,8},{16,20},{20,16},{24,28},{28,24},{1,5},{5... | collective-permute-start | bytes 49160 | tf_op jit(solution)/shard_map/ppermute | solution.py:611
  77.5 5.3 %collective-permute-start.21 = (f32[32,128]{1,0:T(8,128)S(1)}, f32[32,128]{1,0:T(8,128)S(1)}, u32[]{:S(2)}, u32[]{:S(2)}) collective-permute-start(f32[32,128]{1,0:T(8,128)S(1)} %add.21), channel_id=1, source_target_pairs={{0,2},{1,3},{2,0},{3,1},{4,6},{5,7},{6,4},{7,5},{8,10},{9,11},{10,... | collective-permute-start | bytes 49160 | tf_op jit(solution)/shard_map/ppermute | solution.py:616
  77.5 5.3 %collective-permute-start.20 = (f32[32,128]{1,0:T(8,128)S(1)}, f32[32,128]{1,0:T(8,128)S(1)}, u32[]{:S(2)}, u32[]{:S(2)}) collective-permute-start(f32[32,128]{1,0:T(8,128)S(1)} %add.21), channel_id=1, source_target_pairs={{0,3},{1,2},{2,1},{3,0},{4,7},{5,6},{6,5},{7,4},{8,11},{9,10},{10,... | collective-permute-start | bytes 49160 | tf_op jit(solution)/shard_map/ppermute | solution.py:616
  79.9 3.7 %collective-permute-start.19 = (f32[32,128]{1,0:T(8,128)S(1)}, f32[32,128]{1,0:T(8,128)S(1)}, u32[]{:S(2)}, u32[]{:S(2)}) collective-permute-start(f32[32,128]{1,0:T(8,128)S(1)} %add.21), channel_id=1, source_target_pairs={{0,1},{1,0},{2,3},{3,2},{4,5},{5,4},{6,7},{7,6},{8,9},{9,8},{10,11... | collective-permute-start | bytes 49160 | tf_op jit(solution)/shard_map/ppermute | solution.py:616
  83.7 5.2 %collective-permute-start.24 = (f32[32,128]{1,0:T(8,128)S(1)}, f32[32,128]{1,0:T(8,128)S(1)}, u32[]{:S(2)}, u32[]{:S(2)}) collective-permute-start(f32[32,128]{1,0:T(8,128)S(1)} %add_add_fusion.1), channel_id=1, source_target_pairs={{0,16},{4,20},{8,24},{12,28},{16,0},{20,4},{24,8},{28,12},{1,17},{... | collective-permute-start | bytes 49160 | tf_op jit(solution)/shard_map/ppermute | solution.py:616
  83.7 5.2 %collective-permute-start.23 = (f32[32,128]{1,0:T(8,128)S(1)}, f32[32,128]{1,0:T(8,128)S(1)}, u32[]{:S(2)}, u32[]{:S(2)}) collective-permute-start(f32[32,128]{1,0:T(8,128)S(1)} %add_add_fusion.1), channel_id=1, source_target_pairs={{0,24},{4,28},{8,16},{12,20},{16,8},{20,12},{24,0},{28,4},{1,25},{... | collective-permute-start | bytes 49160 | tf_op jit(solution)/shard_map/ppermute | solution.py:616
  84.3 4.6 %collective-permute-start.22 = (f32[32,128]{1,0:T(8,128)S(1)}, f32[32,128]{1,0:T(8,128)S(1)}, u32[]{:S(2)}, u32[]{:S(2)}) collective-permute-start(f32[32,128]{1,0:T(8,128)S(1)} %add_add_fusion.1), channel_id=1, source_target_pairs={{0,8},{4,12},{8,0},{12,4},{16,24},{20,28},{24,16},{28,20},{1,9},{5... | collective-permute-start | bytes 49160 | tf_op jit(solution)/shard_map/ppermute | solution.py:616
  88.9 5.3 %collective-permute-start.27 = (f32[32,128]{1,0:T(8,128)S(1)}, f32[32,128]{1,0:T(8,128)S(1)}, u32[]{:S(2)}, u32[]{:S(2)}) collective-permute-start(f32[32,128]{1,0:T(8,128)S(1)} %add_add_fusion.refs_0_), channel_id=1, source_target_pairs={{0,64},{32,96},{64,0},{96,32},{1,65},{33,97},{65,1},{97,33},{2,66}... | collective-permute-start | bytes 49160 | tf_op jit(solution)/shard_map/ppermute | solution.py:616
  91.3 4.9 %collective-permute-start.26 = (f32[32,128]{1,0:T(8,128)S(1)}, f32[32,128]{1,0:T(8,128)S(1)}, u32[]{:S(2)}, u32[]{:S(2)}) collective-permute-start(f32[32,128]{1,0:T(8,128)S(1)} %add_add_fusion.refs_0_), channel_id=1, source_target_pairs={{0,96},{32,64},{64,32},{96,0},{1,97},{33,65},{65,33},{97,1},{2,98}... | collective-permute-start | bytes 49160 | tf_op jit(solution)/shard_map/ppermute | solution.py:616
  92.4 3.8 %collective-permute-start.25 = (f32[32,128]{1,0:T(8,128)S(1)}, f32[32,128]{1,0:T(8,128)S(1)}, u32[]{:S(2)}, u32[]{:S(2)}) collective-permute-start(f32[32,128]{1,0:T(8,128)S(1)} %add_add_fusion.refs_0_), channel_id=1, source_target_pairs={{0,32},{32,0},{64,96},{96,64},{1,33},{33,1},{65,97},{97,65},{2,34}... | collective-permute-start | bytes 49160 | tf_op jit(solution)/shard_map/ppermute | solution.py:616

commit v3 on v2

--- a/solution.py
+++ b/solution.py
@@ -48,13 +48,16 @@
 
 
 def pack_kernel(
-    class_hbm, table_hbm, guess_hbm, field_ref, perm_ref, xlo, xhi, ylo, yhi, ends_ref,
-    classes, table, guess, plane_sem, class_sem, table_sem,
+    class_hbm, table_hbm, guess_hbm, field_hbm, perm_ref, xlo, xhi, ylo, yhi, ends_ref,
+    classes, table, guess, field_ref, plane_sem, field_sem, class_sem, table_sem,
 ):
     columns, nx, ny, nz = guess_hbm.shape
 
     def plane(x):
         return pltpu.make_async_copy(guess_hbm.at[:, x], guess.at[x], plane_sem.at[x])
+
+    def leaving(x):
+        return pltpu.make_async_copy(field_ref.at[x], field_hbm.at[x], field_sem.at[x])
 
     class_copy = pltpu.make_async_copy(class_hbm, classes, class_sem)
     table_copy = pltpu.make_async_copy(table_hbm, table, table_sem)
@@ -70,7 +73,7 @@
     lane = lanes(ny)
     row = rows_of(ny)
 
-    def permeability(x, carry):
+    def permeability(x):
         perm = jnp.zeros((ny, nz), F32)
         for level in range(table.shape[0]):
             perm = jnp.where(classes[x] == level, table[level], perm)
@@ -81,32 +84,42 @@
         final = jnp.broadcast_to(perm[:, nz - 1 : nz], (ny, nz))
         both = jnp.where(lane == 2 * row, final, jnp.where(lane == 2 * row + 1, first, 0.0))
         edge = jnp.sum(both, axis=0, keepdims=True)
-        place_x(edge, x, ends_ref, 4, pl.ds(x // 4, 1))
+        return jnp.where((lanes(1) // 32) == x % 4, pltpu.roll(edge, (x % 4) * 32, 1), 0.0)
+
+    def four(block, carry):
+        edges = [permeability(4 * block + step) for step in range(4)]
+        ends_ref[4, pl.ds(block, 1), :] = (edges[0] + edges[1]) + (edges[2] + edges[3])
         return carry
 
-    lax.fori_loop(0, nx, permeability, 0)
+    lax.fori_loop(0, nx // 4, four, 0)
     xlo[ny, 0:ny, :] = perm_ref[0]
     xhi[ny, 0:ny, :] = perm_ref[nx - 1]
 
-    def cells_of(x, carry):
-        plane(x).wait()
-        flat = guess.at[x].reshape(columns * ny, nz)
-        ends = jnp.zeros((columns, nz), F32)
-        for y in range(ny):
-            cells = flat[pl.ds(y, columns, stride=ny), :]
-            field_ref[x, y] = cells
-            ends = packed_ends(cells, y, ends)
-            if y == 0:
-                ylo[x] = cells
-            if y == ny - 1:
-                yhi[x] = cells
-        place_x(ends, x, ends_ref, x // 4, slice(None))
+    def cells_of(pair, carry):
+        for step in range(2):
+            plane(2 * pair + step).wait()
+        for step in range(2):
+            x = 2 * pair + step
+            flat = guess.at[x].reshape(columns * ny, nz)
+            ends = jnp.zeros((columns, nz), F32)
+            for y in range(ny):
+                cells = flat[pl.ds(y, columns, stride=ny), :]
+                field_ref[x, y] = cells
+                ends = packed_ends(cells, y, ends)
+                if y == 0:
+                    ylo[x] = cells
+                if y == ny - 1:
+                    yhi[x] = cells
+            place_x(ends, x, ends_ref, x // 4, slice(None))
+            leaving(x).start()
         return carry
 
-    lax.fori_loop(0, nx, cells_of, 0)
+    lax.fori_loop(0, nx // 2, cells_of, 0)
     for y in range(ny):
         xlo[y] = field_ref[0, y]
         xhi[y] = field_ref[nx - 1, y]
+    for x in range(nx):
+        leaving(x).wait()
 
 
 def pack(perm_class, perm_table, start_guess):
@@ -115,9 +128,9 @@
     return pl.pallas_call(
         pack_kernel,
         in_specs=[HBM] * 3,
-        out_specs=[VMEM] * 7,
+        out_specs=[HBM] + [VMEM] * 6,
         out_shape=[
-            shaped(nx, ny, columns, nz),
+            pltpu.HBM((nx, ny, columns, nz), F32),
             shaped(nx, ny, nz),
             face,
             face,
@@ -129,6 +142,8 @@
             pltpu.VMEM((nx, ny, nz), jnp.int32),
             pltpu.SMEM(perm_table.shape, F32),
             pltpu.VMEM((nx, columns, ny, nz), F32),
+            pltpu.VMEM((nx, ny, columns, nz), F32),
+            pltpu.SemaphoreType.DMA((nx,)),
             pltpu.SemaphoreType.DMA((nx,)),
             pltpu.SemaphoreType.DMA(()),
             pltpu.SemaphoreType.DMA(()),
@@ -152,38 +167,49 @@
     return jnp.where(lanes(left.shape[0]) % 2 == 0, after, before)
 
 
-def inner_weights(perm_ref, inside, hz, wx, wy, wzm, wzp):
+def inner_weights(perm_ref, inside, hz, wx, wy, wzm, wzp, wze):
     nx, ny, nz = perm_ref.shape
     lane = lanes(ny)
     row = rows_of(ny)
 
-    def at_x(x, carry):
+    def at_x(x):
         center = perm_ref[x]
         wx[x] = face_weight(center, perm_ref[jnp.maximum(x - 1, 0)])
         below = jnp.concatenate([center[:1], center[: ny - 1]], axis=0)
         wy[x, 0:ny, :] = face_weight(center, below)
         ends = arrived(
-            hz[0][4, pl.ds(x // 4, 1), :], hz[1][4, pl.ds(x // 4, 1), :], inside[4], inside[5]
+            hz[0][4, pl.ds(x // 4, 1), :], hz[1][4, pl.ds(x // 4, 1), :], inside[4:5], inside[5:6]
         )
         ends = jnp.broadcast_to(ends, (ny, nz))
         offset = (x % 4) * 32 + 2 * row
         after = jnp.sum(jnp.where(lane == offset, ends, 0.0), axis=1, keepdims=True)
         ahead = jnp.sum(jnp.where(lane == offset + 1, ends, 0.0), axis=1, keepdims=True)
-        wzm[x] = face_weight(center, jnp.where(lane == 0, ahead, pltpu.roll(center, 1, 1)))
-        wzp[x] = face_weight(center, jnp.where(lane == nz - 1, after, pltpu.roll(center, nz - 1, 1)))
+        down = face_weight(center, jnp.where(lane == 0, ahead, pltpu.roll(center, 1, 1)))
+        up = face_weight(center, jnp.where(lane == nz - 1, after, pltpu.roll(center, nz - 1, 1)))
+        wzm[x] = down
+        wzp[x] = up
+        first = jnp.broadcast_to(down[:, 0:1], (ny, nz))
+        final = jnp.broadcast_to(up[:, nz - 1 : nz], (ny, nz))
+        both = jnp.where(lane == 2 * row, final, jnp.where(lane == 2 * row + 1, first, 0.0))
+        return jnp.sum(both, axis=0, keepdims=True)
+
+    def at_four(block, carry):
+        edges = [at_x(4 * block + step) for step in range(4)]
+        for step in range(4):
+            wze[pl.ds(4 * block + step, 1), :] = edges[step]
         return carry
 
-    lax.fori_loop(0, nx, at_x, 0)
+    lax.fori_loop(0, nx // 4, at_four, 0)
 
 
 def outer_weights(perm_ref, inside, hx, hy, wx, wy):
     nx, ny, nz = perm_ref.shape
-    wx[0] = face_weight(perm_ref[0], hx[0][...] * inside[0])
-    wx[nx] = face_weight(perm_ref[nx - 1], hx[1][...] * inside[1])
+    wx[0] = face_weight(perm_ref[0], hx[0][...] * inside[0:1])
+    wx[nx] = face_weight(perm_ref[nx - 1], hx[1][...] * inside[1:2])
     low = jnp.concatenate([perm_ref[x, 0:1, :] for x in range(nx)], axis=0)
     high = jnp.concatenate([perm_ref[x, ny - 1 : ny, :] for x in range(nx)], axis=0)
-    low = face_weight(low, hy[0][0:nx] * inside[2])
-    high = face_weight(high, hy[1][0:nx] * inside[3])
+    low = face_weight(low, hy[0][0:nx] * inside[2:3])
+    high = face_weight(high, hy[1][0:nx] * inside[3:4])
     for x in range(nx):
         wy[x, 0:1, :] = low[x : x + 1]
         wy[x, ny : ny + 1, :] = high[x : x + 1]
@@ -199,37 +225,35 @@
     return jnp.where(matched, along_x * ny + along_y, -1)
 
 
-def inner_kernel(first, last, totals, *refs):
-    refs = list(refs)
-    take = lambda count: [refs.pop(0) for _ in range(count)]
-    field, hzl, hzr = take(3)
-    if first:
-        perm, inside, anchors, boreholes = take(4)
-    else:
-        wx, wy, wzm, wzp = take(4)
-    (out,) = take(1)
-    if not last:
-        (ends,) = take(1)
-    if first:
-        wx, wy, wzm, wzp = take(4)
-    else:
-        (total,) = take(1)
-    (flux,) = take(1)
+def difference_matrix(matrix):
+    size = matrix.shape[0] // 2
+    source = lax.broadcasted_iota(jnp.int32, matrix.shape, 0) % size
+    target = lax.broadcasted_iota(jnp.int32, matrix.shape, 1)
+    beside = jnp.where(target < size, target + 1, target - size - 1)
+    same = jnp.where(source == target % size, 1.0, 0.0)
+    matrix[...] = (same - jnp.where(source == beside, 1.0, 0.0)).astype(BF16)
+
+
+def first_kernel(
+    away, hzl, hzr, perm, inside, code, out, ends, wx, wy, wzm, wzp, wze, flux, field, plane_sem
+):
     nx, ny, columns, nz = field.shape
-    if not last:
-        ends[...] = jnp.zeros_like(ends)
-    if first:
-        inner_weights(perm, inside, (hzl, hzr), wx, wy, wzm, wzp)
-        code = local_sources(boreholes[...], anchors, nx, ny, nz, totals[1], totals[2])
-    else:
-        total[...] = jnp.zeros_like(total)
+
+    def plane(x):
+        return pltpu.make_async_copy(away.at[x], field.at[x], plane_sem.at[x])
+
+    for x in range(nx):
+        plane(x).start()
+    ends[...] = jnp.zeros_like(ends)
+    inner_weights(perm, inside, (hzl, hzr), wx, wy, wzm, wzp, wze)
     flux[...] = jnp.zeros_like(flux)
-    lane = lanes(columns)
+    plane(0).wait()
 
     def at_x(x, beside):
-        block = lax.div(x, 4)
+        block = x // 4
         beyond = arrived(hzl[block], hzr[block])
-        beyond = pltpu.roll(beyond, lax.rem(128 - lax.rem(x, 4) * 32, 128), 1)
+        beyond = pltpu.roll(beyond, (128 - (x % 4) * 32) % 128, 1)
+        lane = lanes(columns)
         center = field[x, 0]
         flux_y = None
         mine = jnp.zeros((columns, nz), F32)
@@ -250,31 +274,118 @@
             before = jnp.where(lane == 0, edge, pltpu.roll(center, 1, 1))
             applied = applied + wzp[x, y : y + 1, :] * (center - after)
             applied = applied + wzm[x, y : y + 1, :] * (center - before)
-            if first:
-                applied = jnp.where(code == x * ny + y, 1.0, 0.0) - applied
+            applied = jnp.where(code[...] == x * ny + y, 1.0, 0.0) - applied
+            out[x, y] = applied
+            mine = packed_ends(applied, y, mine)
+            center = following
+        place_x(mine, x, ends, block, slice(None))
+
+    def inner(x, carry):
+        plane(x + 1).wait()
+        at_x(x, field.at[x + 1])
+        return carry
+
+    lax.fori_loop(0, nx - 1, inner, 0)
+    at_x(nx - 1, None)
+
+
+def inner_kernel(last, *refs):
+    refs = list(refs)
+    take = lambda count: [refs.pop(0) for _ in range(count)]
+    field, hzl, hzr, wx, wy, wzm, wzp, wze, out = take(9)
+    if not last:
+        (ends,) = take(1)
+    total, flux, matrix, even, odd, even_halves, odd_halves = take(7)
+    nx, ny, columns, nz = field.shape
+    if not last:
+        ends[...] = jnp.zeros_like(ends)
+    difference_matrix(matrix)
+    total[...] = jnp.zeros_like(total)
+    flux[...] = jnp.zeros_like(flux)
+
+    def differences(x, across, halves):
+        plane = field[x].reshape(ny * columns, nz)
+        high = plane.astype(BF16)
+        low = (plane - high.astype(F32)).astype(BF16)
+        both = jnp.concatenate([high, low], axis=1)
+        halves[...] = both
+        across[...] = jnp.dot(both, matrix[...], preferred_element_type=F32)
+
+    def products(x, halves):
+        left = jnp.concatenate(
+            [
+                jnp.concatenate(
+                    [halves[y * columns : (y + 1) * columns, half] for y in range(ny)], axis=1
+                )
+                for half in (slice(0, nz), slice(nz, 2 * nz))
+            ],
+            axis=0,
+        )
+        right = split([jnp.concatenate([out[x, y] for y in range(ny)], axis=1)])
+        total[...] += gram(left, jnp.concatenate([left, right], axis=0))
+
+    def stencil(x, across, beside):
+        block = x // 4
+        beyond = arrived(hzl[block], hzr[block])
+        beyond = pltpu.roll(beyond, (128 - (x % 4) * 32) % 128, 1)
+        beyond = beyond * wze[pl.ds(x, 1), :]
+        lane = lanes(columns)
+        outer = (lane == 0) | (lane == nz - 1)
+        center = field[x, 0]
+        flux_y = None
+        mine = jnp.zeros((columns, nz), F32)
+        for y in range(ny):
+            rows = slice(y * columns, (y + 1) * columns)
+            applied = LEAKAGE * center - flux[y]
+            if beside is not None:
+                flux_x = wx[x + 1, y : y + 1, :] * (center - beside[y])
+                applied = applied + flux_x
+                flux[y] = flux_x
+            if flux_y is not None:
+                applied = applied - flux_y
+            if y + 1 < ny:
+                following = field[x, y + 1]
+                flux_y = wy[x, y + 1 : y + 2, :] * (center - following)
+                applied = applied + flux_y
+            applied = applied + wzp[x, y : y + 1, :] * across[rows, 0:nz]
+            applied = applied + wzm[x, y : y + 1, :] * across[rows, nz : 2 * nz]
+            edge = pltpu.roll(beyond, (128 - (2 * y + 1)) % 128, 1)
+            applied = applied - jnp.where(outer, edge, 0.0)
             out[x, y] = applied
             if not last:
                 mine = packed_ends(applied, y, mine)
             center = following
         if not last:
             place_x(mine, x, ends, block, slice(None))
-        if not first:
-            left = split([jnp.concatenate([field[x, y] for y in range(ny)], axis=1)])
-            right = split([jnp.concatenate([out[x, y] for y in range(ny)], axis=1)])
-            total[...] += gram(left, jnp.concatenate([left, right], axis=0))
-
-    def inner(x, carry):
-        at_x(x, field.at[x + 1])
+
+    def step(x, here, there, halves):
+        products(x - 1, halves)
+        differences(x + 1, there, halves)
+        stencil(x, here, field.at[x + 1])
+
+    def pair(place, carry):
+        step(2 * place + 1, odd, even, even_halves)
+        step(2 * place + 2, even, odd, odd_halves)
         return carry
 
-    lax.fori_loop(0, nx - 1, inner, 0)
-    at_x(jnp.int32(nx - 1), None)
+    differences(0, even, even_halves)
+    differences(1, odd, odd_halves)
+    stencil(0, even, field.at[1])
+    lax.fori_loop(0, nx // 2 - 1, pair, 0)
+    products(nx - 2, even_halves)
+    stencil(nx - 1, odd, None)
+    products(nx - 1, odd_halves)
 
 
 def sides_kernel(first, last, *refs):
     refs = list(refs)
     take = lambda count: [refs.pop(0) for _ in range(count)]
-    _, field, hxl, hxr, hyl, hyr = take(6)
+    part = take(1)[0]
+    if first:
+        own_faces = take(4)
+    else:
+        (field,) = take(1)
+    hxl, hxr, hyl, hyr = take(4)
     if not last:
         take(1)
     if first:
@@ -293,7 +404,7 @@
         (sums,) = take(1)
     if not last:
         xlo, xhi, ylo, yhi = take(4)
-    nx, ny, columns, nz = field.shape
+    nx, ny, columns, nz = part.shape
     lane = lanes(columns)
     if first:
         hx = (hxl.at[ny, 0:ny], hxr.at[ny, 0:ny])
@@ -306,10 +417,10 @@
         (hyl, [(x, 0) for x in range(nx)], [(x, 0) for x in range(nx)], wy),
         (hyr, [(x, ny - 1) for x in range(nx)], [(x, ny) for x in range(nx)], wy),
     )
-    for halo, rows, weight_rows, weight in faces:
+    for side, (halo, rows, weight_rows, weight) in enumerate(faces):
         own, fluxes = [], []
         for place, ((x, y), (p, q)) in enumerate(zip(rows, weight_rows)):
-            center = field[x, y]
+            center = own_faces[side][place] if first else field[x, y]
             flux = weight[p, q : q + 1, :] * (center - halo[place])
             if first:
                 out[x, y] -= flux
@@ -365,31 +476,33 @@
     return summed[:, :half] + summed[:, half:]
 
 
-def inner_part(field, halos, extra, first, last, totals):
+def inner_part(field, halos, extra, first, last):
     nx, ny, columns, nz = field.shape
-    in_specs = [VMEM] * 3
-    if first:
-        in_specs += [VMEM, SMEM, SMEM, VMEM]
-    else:
-        in_specs += [VMEM] * 4
+    in_specs = [HBM if first else VMEM] + [VMEM] * (len(halos) + len(extra))
+    scratch = [pltpu.VMEM((ny, columns, nz), F32)]
     out_shape = [shaped(nx, ny, columns, nz)]
     if not last:
         out_shape += [shaped(4, columns, nz)]
     if first:
+        scratch += [pltpu.VMEM(field.shape, F32), pltpu.SemaphoreType.DMA((nx,))]
         out_shape += [
             shaped(nx + 1, ny, nz),
             shaped(nx, ny + 8, nz),
             shaped(nx, ny, nz),
             shaped(nx, ny, nz),
+            shaped(nx, nz),
         ]
     else:
+        scratch += [pltpu.VMEM((2 * nz, 2 * nz), BF16)]
+        scratch += [pltpu.VMEM((ny * columns, 2 * nz), F32)] * 2
+        scratch += [pltpu.VMEM((ny * columns, 2 * nz), BF16)] * 2
         out_shape += [shaped(2 * columns, 4 * columns)]
     return pl.pallas_call(
-        functools.partial(inner_kernel, first, last, totals),
+        first_kernel if first else functools.partial(inner_kernel, last),
         in_specs=in_specs,
         out_specs=[VMEM] * len(out_shape),
         out_shape=out_shape,
-        scratch_shapes=[pltpu.VMEM((ny, columns, nz), F32)],
+        scratch_shapes=scratch,
         compiler_params=params(),
         cost_estimate=pl.CostEstimate(
             flops=20 * field.size, bytes_accessed=6 * field.size * 4, transcendentals=0
@@ -398,9 +511,10 @@
     )(field, *halos, *extra)
 
 
-def sides_part(part, field, halos, ends, extra, first, last):
-    nx, ny, columns, nz = field.shape
-    operands = [part, field, *halos]
+def sides_part(part, own, halos, ends, extra, first, last):
+    nx, ny, columns, nz = part.shape
+    operands = [part, *own, *halos]
+    place = len(operands)
     if not last:
         operands += [ends]
     operands += extra
@@ -408,12 +522,11 @@
     aliases = {0: 0}
     out_shape = [shaped(*part.shape)]
     if not last:
-        aliases[6] = 1
+        aliases[place] = 1
         out_shape += [shaped(*ends.shape)]
     if first:
-        in_specs[-1] = SMEM
-        aliases[7] = 2
-        aliases[8] = 3
+        aliases[place + 1] = 2
+        aliases[place + 2] = 3
         out_shape += [shaped(*extra[0].shape), shaped(*extra[1].shape)]
     else:
         out_shape += [shaped(columns, 128)]
@@ -520,20 +633,13 @@
 
 def combine_kernel(
     mix_ref, guess_hbm, one_ref, two_ref, three_ref, solution_hbm, residual_hbm,
-    guess, solution, residual, sem, guess_sem,
+    guess_ref, solution, residual, sem, guess_sem,
 ):
-    nx, ny, columns, nz = one_ref.shape
+    nx, ny, columns, nz = guess_ref.shape
     slots = solution.shape[0]
 
     def arriving(x):
-        return pltpu.make_async_copy(guess_hbm.at[:, x], guess.at[x], guess_sem.at[x])
-
-    def leaving(x):
-        slot = lax.rem(x, slots)
-        return (
-            pltpu.make_async_copy(solution.at[slot], solution_hbm.at[:, x], sem.at[0, slot]),
-            pltpu.make_async_copy(residual.at[slot], residual_hbm.at[:, x], sem.at[1, slot]),
-        )
+        return pltpu.make_async_copy(guess_hbm.at[x], guess_ref.at[x], guess_sem.at[x])
 
     for x in range(nx):
         arriving(x).start()
@@ -545,6 +651,13 @@
     )
     nothing = jnp.zeros((columns, 2 * nz), F32)
 
+    def leaving(x):
+        slot = lax.rem(x, slots)
+        return (
+            pltpu.make_async_copy(solution.at[slot], solution_hbm.at[:, x], sem.at[0, slot]),
+            pltpu.make_async_copy(residual.at[slot], residual_hbm.at[:, x], sem.at[1, slot]),
+        )
+
     def at_x(x, carry):
         slot = lax.rem(x, slots)
 
@@ -554,7 +667,6 @@
                 copy.wait()
 
         arriving(x).wait()
-        guess_rows = guess.at[x].reshape(columns * ny, nz)
         solution_rows = solution.at[slot].reshape(columns * ny, nz)
         residual_rows = residual.at[slot].reshape(columns * ny, nz)
         for y in range(0, ny, 2):
@@ -568,7 +680,7 @@
             for step in range(2):
                 rows = pl.ds(y + step, columns, stride=ny)
                 part = mixed[:, step * nz : (step + 1) * nz]
-                solution_rows[rows, :] = guess_rows[rows, :] + part[0:32]
+                solution_rows[rows, :] = guess_ref[x, y + step] + part[0:32]
                 residual_rows[rows, :] = one_ref[x, y + step] + part[32:64]
         for copy in leaving(x):
             copy.start()
@@ -581,20 +693,20 @@
 
 
 def combine(mix, guess, one, two, three):
-    nx, ny, columns, nz = one.shape
+    nx, ny, columns, nz = guess.shape
     return pl.pallas_call(
         combine_kernel,
-        in_specs=[VMEM, HBM, VMEM, VMEM, VMEM],
+        in_specs=[VMEM, HBM] + [VMEM] * 3,
         out_specs=[HBM] * 2,
         out_shape=[jax.ShapeDtypeStruct((columns, nx, ny, nz), F32)] * 2,
         scratch_shapes=[
-            pltpu.VMEM((nx, columns, ny, nz), F32),
+            pltpu.VMEM(guess.shape, F32),
             pltpu.VMEM((8, columns, ny, nz), F32),
             pltpu.VMEM((8, columns, ny, nz), F32),
             pltpu.SemaphoreType.DMA((2, 8)),
             pltpu.SemaphoreType.DMA((nx,)),
         ],
-        compiler_params=pltpu.CompilerParams(vmem_limit_bytes=VMEM_LIMIT),
+        compiler_params=params(),
         name="combine_fields",
     )(mix, guess, one, two, three)
 
@@ -627,35 +739,37 @@
     columns, nx, ny, nz = start_guess.shape
     places = [lax.axis_index(axis) for axis in AXES]
     sizes = [lax.axis_size(axis) for axis in AXES]
-    anchors = jnp.stack([place * size for place, size in zip(places, (nx, ny, nz))])
+    anchors = [place * size for place, size in zip(places, (nx, ny, nz))]
     totals = tuple(size * count for size, count in zip((nx, ny, nz), sizes))
     inside = []
     for place, size in zip(places, sizes):
         inside += [place > 0, place < size - 1]
-    inside = jnp.stack(inside).astype(F32)
-
-    perm_class, perm_table, start_guess = (
+    inside = jnp.broadcast_to(jnp.stack(inside + inside[:2]).astype(F32)[:, None], (8, nz))
+
+    in_hbm = [
         pltpu.with_memory_space_constraint(held, pltpu.HBM)
         for held in (perm_class, perm_table, start_guess)
-    )
-    guess, perm, *faces = pack(perm_class, perm_table, start_guess)
+    ]
+    guess, perm, *faces = pack(*in_hbm)
+    guess = pltpu.with_memory_space_constraint(guess, pltpu.HBM)
     near, far = exchanged(*faces)
-    extra = (perm, inside, anchors.astype(jnp.int32), boreholes[:, None])
-    part, ends, wx, wy, *along_z = inner_part(guess, near, extra, True, False, totals)
+    code = local_sources(boreholes[:, None], anchors, nx, ny, nz, totals[1], totals[2])
+    extra = (perm, inside, code)
+    part, ends, wx, wy, *along_z = inner_part(guess, near, extra, True, False)
     residual, ends, wx, wy, *faces = sides_part(
-        part, guess, far, ends, [wx, wy, perm, inside], True, False
+        part, faces[:4], far, ends, [wx, wy, perm, inside], True, False
     )
     weights = (wx, wy, *along_z)
     near, far = exchanged(*faces, ends)
-    part, ends, total = inner_part(residual, near, weights, False, False, totals)
+    part, ends, total = inner_part(residual, near, weights, False, False)
     once, ends, sums, *faces = sides_part(
-        part, residual, far, ends, [wx, wy, total], False, False
+        part, [residual], far, ends, [wx, wy, total], False, False
     )
     near, far = exchanged(*faces, ends)
-    part, total = inner_part(once, near, weights, False, True, totals)
-    twice, sums = sides_part(part, once, far, None, [wx, wy, total, sums], False, True)
+    part, total = inner_part(once, near, weights, False, True)
+    twice, sums = sides_part(part, [once], far, None, [wx, wy, total, sums], False, True)
     mix = solve(summed_but_last(sums))
-    return tuple(combine(mix, start_guess, residual, once, twice))
+    return tuple(combine(mix, guess, residual, once, twice))
 
 
 def solution(mesh):

time: 110 us -> 96.3 us (0.88)
  Pallas kernels: 52.5 us -> 43 us
  local copies, waits for them, and re-layouts: 4.39 us -> 0.18 us
    pallas_call x5, Pallas kernels: 45.4 us -> 36.4 us  [the longest x3 22.4 us: inner_part(): pl.pallas_call(first_kernel if first else functools.partial(inner_kernel,...]
    unnamed x6 -> x2, local copies, waits for them, and re-layouts: 4.2 us -> 0.01 us
  transfers between devices with their start and end apart: 28 -> 28, of which waited for: 9 -> 9; matrix products, arithmetic and copies ran while one was open for 0% -> 0% of each run, Pallas kernels for 26% -> 23%
where the time goes in v3:
time: 96.3 us; the launch traced here: 96.1 us
  Pallas kernels  43 us (45%)
  starting transfers between devices  37.6 us (39%)
  waiting for transfers between devices  14.1 us (15%)
  between operations  1.02 us (1%)
    pallas_call x3, Pallas kernels, inner_part(): pl.pallas_call(first_kernel if first else functools.partial(inner_kernel,...  22.4 us
    ppermute x9, starting transfers between devices, summed_but_last(): lax.ppermute(values, axis, swaps(axis, mask, stride))  11.1 us
    ppermute x3, starting transfers between devices, exchanged(): lax.ppermute(ylo, 'dip', back('dip'))  8.86 us
    ppermute x9, waiting for transfers between devices, summed_but_last(): lax.ppermute(values, axis, swaps(axis, mask, stride))  8.2 us
    pallas_call x1, Pallas kernels, combine(): pl.pallas_call(combine_kernel, in_specs=[VMEM, HBM] + [VMEM] * 3, out_spe...  7.61 us
    ppermute x3, starting transfers between devices, exchanged(): lax.ppermute(xlo, 'strike', back('strike'))  6.59 us
    pallas_call x1, Pallas kernels, pack(): pl.pallas_call(pack_kernel, in_specs=[HBM] * 3, out_specs=[HBM] + [VMEM]...  6.41 us
    ppermute x3, starting transfers between devices, exchanged(): lax.ppermute(ends, 'layer', back('layer'))  5.74 us
  transfers between devices with their start and end apart: 28, of which 9 were waited for; matrix products, arithmetic and copies ran while one was open for 0% of the time, Pallas kernels for 23%

profile of v3, /device:TPU:0, one launch (start us, length us, event | category | flops | bytes accessed | tf_op | source)
XLA Modules:
  0.0 96.1 jit_solution(16508733912040697551)
XLA Ops:
  0.6 6.4 %pack_guess.1 = (f32[16,16,32,128]{3,2,1,0:T(8,128)}, f32[16,16,128]{2,1,0:T(8,128)S(1)}, f32[17,32,128]{2,1,0:T(8,128)S(1)}, f32[17,32,128]{2,1,0:T(8,128)S(1)}...) custom-call(s32[16,16,128]{2,1,0:T(8,128)} %class_hbm.1, f32[16]{0:T(128)} %table_hbm.1, ...), custom_call_target="tpu_custom_call" | custom-call | tf_op jit(solution)/shard_map/pack_guess/pallas_call | solution.py:128
  7.1 4.2 %collective-permute-start.1 = (f32[5,32,128]{2,1,0:T(8,128)S(1)}, f32[5,32,128]{2,1,0:T(8,128)S(1)}, u32[]{:S(2)}, u32[]{:S(2)}) collective-permute-start(f32[5,32,128]{2,1,0:T(8,128)S(1)} %get-tuple-element.51), channel_id=1, source_target_pairs={{1,0},{2,1},{3,2},{0,3},{5,4},{6,5},{7,6},{4,7},{9,8},{10,9},{11,1... | collective-permute-start | bytes 245768 | tf_op jit(solution)/shard_map/ppermute | solution.py:551
  11.2 2.8 %collective-permute-start.3 = (f32[17,32,128]{2,1,0:T(8,128)S(1)}, f32[17,32,128]{2,1,0:T(8,128)S(1)}, u32[]{:S(2)}, u32[]{:S(2)}) collective-permute-start(f32[17,32,128]{2,1,0:T(8,128)S(1)} %get-tuple-element.58.refs_1_), channel_id=1, source_target_pairs={{32,0},{64,32},{96,64},{0,96},{33,1},{65,33},{97,65},{1,97},{34,2}... | collective-permute-start | bytes 835592 | tf_op jit(solution)/shard_map/ppermute | solution.py:556
  14.1 2.8 %collective-permute-done.hzl = f32[5,32,128]{2,1,0:T(8,128)S(1)} collective-permute-done((f32[5,32,128]{2,1,0:T(8,128)S(1)}, f32[5,32,128]{2,1,0:T(8,128)S(1)}, u32[]{:S(2)}, u32[]{:S(2)}) %collective-permute-start) | collective-permute-done | bytes 81952 | tf_op jit(solution)/shard_map/ppermute | solution.py:550
  16.9 3.0 %collective-permute-start.5 = (f32[17,32,128]{2,1,0:T(8,128)S(1)}, f32[17,32,128]{2,1,0:T(8,128)S(1)}, u32[]{:S(2)}, u32[]{:S(2)}) collective-permute-start(f32[17,32,128]{2,1,0:T(8,128)S(1)} %get-tuple-element.61.refs_3_), channel_id=1, source_target_pairs={{4,0},{8,4},{12,8},{16,12},{20,16},{24,20},{28,24},{0,28},{5,1},{9... | collective-permute-start | bytes 835592 | tf_op jit(solution)/shard_map/ppermute | solution.py:558
  20.2 9.7 %inner_first.1 = (f32[16,16,32,128]{3,2,1,0:T(8,128)S(1)}, f32[4,32,128]{2,1,0:T(8,128)S(1)}, f32[17,16,128]{2,1,0:T(8,128)S(1)}, f32[16,24,128]{2,1,0:T(8,128)S...) custom-call(f32[16,16,32,128]{3,2,1,0:T(8,128)} %get-tuple-element.50.away.guess_hbm, ...), custom_call_target="tpu_custom_call" | custom-call | flops 20971520 | bytes 25165824 | tf_op jit(solution)/shard_map/inner_first/pallas_call | solution.py:500
  30.8 1.6 %collective-permute-start.6 = (f32[4,32,128]{2,1,0:T(8,128)S(1)}, f32[4,32,128]{2,1,0:T(8,128)S(1)}, u32[]{:S(2)}, u32[]{:S(2)}) collective-permute-start(f32[4,32,128]{2,1,0:T(8,128)S(1)} %get-tuple-element.66), channel_id=1, source_target_pairs={{0,1},{1,2},{2,3},{3,0},{4,5},{5,6},{6,7},{7,4},{8,9},{9,10},{10,1... | collective-permute-start | bytes 196616 | tf_op jit(solution)/shard_map/ppermute | solution.py:550
  32.4 1.5 %collective-permute-start.8 = (f32[16,32,128]{2,1,0:T(8,128)S(1)}, f32[16,32,128]{2,1,0:T(8,128)S(1)}, u32[]{:S(2)}, u32[]{:S(2)}) collective-permute-start(f32[16,32,128]{2,1,0:T(8,128)S(1)} %get-tuple-element.77), channel_id=1, source_target_pairs={{0,32},{32,64},{64,96},{96,0},{1,33},{33,65},{65,97},{97,1},{2,34}... | collective-permute-start | bytes 786440 | tf_op jit(solution)/shard_map/ppermute | solution.py:555
  33.9 1.7 %collective-permute-start.9 = (f32[16,32,128]{2,1,0:T(8,128)S(1)}, f32[16,32,128]{2,1,0:T(8,128)S(1)}, u32[]{:S(2)}, u32[]{:S(2)}) collective-permute-start(f32[16,32,128]{2,1,0:T(8,128)S(1)} %get-tuple-element.78), channel_id=1, source_target_pairs={{32,0},{64,32},{96,64},{0,96},{33,1},{65,33},{97,65},{1,97},{34,2}... | collective-permute-start | bytes 786440 | tf_op jit(solution)/shard_map/ppermute | solution.py:556
  36.3 3.0 %collective-permute-start.11 = (f32[16,32,128]{2,1,0:T(8,128)S(1)}, f32[16,32,128]{2,1,0:T(8,128)S(1)}, u32[]{:S(2)}, u32[]{:S(2)}) collective-permute-start(f32[16,32,128]{2,1,0:T(8,128)S(1)} %get-tuple-element.80), channel_id=1, source_target_pairs={{4,0},{8,4},{12,8},{16,12},{20,16},{24,20},{28,24},{0,28},{5,1},{9... | collective-permute-start | bytes 786440 | tf_op jit(solution)/shard_map/ppermute | solution.py:558
  39.3 6.8 %inner_next.1 = (f32[16,16,32,128]{3,2,1,0:T(8,128)S(1)}, f32[4,32,128]{2,1,0:T(8,128)S(1)}, f32[64,128]{1,0:T(8,128)S(1)}) custom-call(f32[16,16,32,128]{3,2,1,0:T(8,128)S(1)} %get-tuple-element.65.refs_0_.refs_1_.one_ref, f32[4,32,128]{2,1,0:T(8,128)S(1)} %collective-permute-done.6.refs_1_, f32[4,32,128]{2,1,0:T(8,128)S(1)} %collective-permute-done.7.refs_2_, ...), custom_call_target="tpu_custom_call" | custom-call | flops 20971520 | bytes 25165824 | tf_op jit(solution)/shard_map/inner_next/pallas_call | solution.py:500
  46.8 1.1 %collective-permute-start.13 = (f32[4,32,128]{2,1,0:T(8,128)S(1)}, f32[4,32,128]{2,1,0:T(8,128)S(1)}, u32[]{:S(2)}, u32[]{:S(2)}) collective-permute-start(f32[4,32,128]{2,1,0:T(8,128)S(1)} %get-tuple-element.84), channel_id=1, source_target_pairs={{1,0},{2,1},{3,2},{0,3},{5,4},{6,5},{7,6},{4,7},{9,8},{10,9},{11,1... | collective-permute-start | bytes 196616 | tf_op jit(solution)/shard_map/ppermute | solution.py:551
  47.9 1.0 %collective-permute-start.12 = (f32[4,32,128]{2,1,0:T(8,128)S(1)}, f32[4,32,128]{2,1,0:T(8,128)S(1)}, u32[]{:S(2)}, u32[]{:S(2)}) collective-permute-start(f32[4,32,128]{2,1,0:T(8,128)S(1)} %get-tuple-element.84), channel_id=1, source_target_pairs={{0,1},{1,2},{2,3},{3,0},{4,5},{5,6},{6,7},{7,4},{8,9},{9,10},{10,1... | collective-permute-start | bytes 196616 | tf_op jit(solution)/shard_map/ppermute | solution.py:550
  48.9 1.2 %collective-permute-start.14 = (f32[16,32,128]{2,1,0:T(8,128)S(1)}, f32[16,32,128]{2,1,0:T(8,128)S(1)}, u32[]{:S(2)}, u32[]{:S(2)}) collective-permute-start(f32[16,32,128]{2,1,0:T(8,128)S(1)} %get-tuple-element.90), channel_id=1, source_target_pairs={{0,32},{32,64},{64,96},{96,0},{1,33},{33,65},{65,97},{97,1},{2,34}... | collective-permute-start | bytes 786440 | tf_op jit(solution)/shard_map/ppermute | solution.py:555
  50.0 2.1 %collective-permute-start.15 = (f32[16,32,128]{2,1,0:T(8,128)S(1)}, f32[16,32,128]{2,1,0:T(8,128)S(1)}, u32[]{:S(2)}, u32[]{:S(2)}) collective-permute-start(f32[16,32,128]{2,1,0:T(8,128)S(1)} %get-tuple-element.91), channel_id=1, source_target_pairs={{32,0},{64,32},{96,64},{0,96},{33,1},{65,33},{97,65},{1,97},{34,2}... | collective-permute-start | bytes 786440 | tf_op jit(solution)/shard_map/ppermute | solution.py:556
  52.1 1.2 %collective-permute-done.12.refs_1_ = f32[4,32,128]{2,1,0:T(8,128)S(1)} collective-permute-done((f32[4,32,128]{2,1,0:T(8,128)S(1)}, f32[4,32,128]{2,1,0:T(8,128)S(1)}, u32[]{:S(2)}, u32[]{:S(2)}) %collective-permute-start.12) | collective-permute-done | bytes 65568 | tf_op jit(solution)/shard_map/ppermute | solution.py:550
  53.4 3.0 %collective-permute-start.17 = (f32[16,32,128]{2,1,0:T(8,128)S(1)}, f32[16,32,128]{2,1,0:T(8,128)S(1)}, u32[]{:S(2)}, u32[]{:S(2)}) collective-permute-start(f32[16,32,128]{2,1,0:T(8,128)S(1)} %get-tuple-element.93), channel_id=1, source_target_pairs={{4,0},{8,4},{12,8},{16,12},{20,16},{24,20},{28,24},{0,28},{5,1},{9... | collective-permute-start | bytes 786440 | tf_op jit(solution)/shard_map/ppermute | solution.py:558
  56.3 5.9 %inner_last.1 = (f32[16,16,32,128]{3,2,1,0:T(8,128)S(1)}, f32[64,128]{1,0:T(8,128)S(1)}) custom-call(f32[16,16,32,128]{3,2,1,0:T(8,128)S(1)} %get-tuple-element.83.refs_0_.refs_1_.two_ref, f32[4,32,128]{2,1,0:T(8,128)S(1)} %collective-permute-done.12.refs_1_, f32[4,32,128]{2,1,0:T(8,128)S(1)} %collective-permute-done.13.refs_2_, ...), custom_call_target="tpu_custom_call" | custom-call | flops 20971520 | bytes 25165824 | tf_op jit(solution)/shard_map/inner_last/pallas_call | solution.py:500
  63.0 1.2 %collective-permute-done.18 = f32[32,128]{1,0:T(8,128)S(1)} collective-permute-done((f32[32,128]{1,0:T(8,128)S(1)}, f32[32,128]{1,0:T(8,128)S(1)}, u32[]{:S(2)}, u32[]{:S(2)}) %collective-permute-start.18) | collective-permute-done | bytes 16416 | tf_op jit(solution)/shard_map/ppermute | solution.py:723
  64.4 2.2 %collective-permute-start.20 = (f32[32,128]{1,0:T(8,128)S(1)}, f32[32,128]{1,0:T(8,128)S(1)}, u32[]{:S(2)}, u32[]{:S(2)}) collective-permute-start(f32[32,128]{1,0:T(8,128)S(1)} %add.42), channel_id=1, source_target_pairs={{0,3},{1,2},{2,1},{3,0},{4,7},{5,6},{6,5},{7,4},{8,11},{9,10},{10,... | collective-permute-start | bytes 49160 | tf_op jit(solution)/shard_map/ppermute | solution.py:728
  66.6 1.0 %collective-permute-start.19 = (f32[32,128]{1,0:T(8,128)S(1)}, f32[32,128]{1,0:T(8,128)S(1)}, u32[]{:S(2)}, u32[]{:S(2)}) collective-permute-start(f32[32,128]{1,0:T(8,128)S(1)} %add.42), channel_id=1, source_target_pairs={{0,1},{1,0},{2,3},{3,2},{4,5},{5,4},{6,7},{7,6},{8,9},{9,8},{10,11... | collective-permute-start | bytes 49160 | tf_op jit(solution)/shard_map/ppermute | solution.py:728
  67.6 1.9 %collective-permute-done.21 = f32[32,128]{1,0:T(8,128)S(1)} collective-permute-done((f32[32,128]{1,0:T(8,128)S(1)}, f32[32,128]{1,0:T(8,128)S(1)}, u32[]{:S(2)}, u32[]{:S(2)}) %collective-permute-start.21) | collective-permute-done | bytes 16416 | tf_op jit(solution)/shard_map/ppermute | solution.py:728
  69.5 0.8 collective-permute-done.19
  70.4 1.4 %collective-permute-start.23 = (f32[32,128]{1,0:T(8,128)S(1)}, f32[32,128]{1,0:T(8,128)S(1)}, u32[]{:S(2)}, u32[]{:S(2)}) collective-permute-start(f32[32,128]{1,0:T(8,128)S(1)} %add_add_fusion.1), channel_id=1, source_target_pairs={{0,24},{4,28},{8,16},{12,20},{16,8},{20,12},{24,0},{28,4},{1,25},{... | collective-permute-start | bytes 49160 | tf_op jit(solution)/shard_map/ppermute | solution.py:728
  71.8 2.1 %collective-permute-start.22 = (f32[32,128]{1,0:T(8,128)S(1)}, f32[32,128]{1,0:T(8,128)S(1)}, u32[]{:S(2)}, u32[]{:S(2)}) collective-permute-start(f32[32,128]{1,0:T(8,128)S(1)} %add_add_fusion.1), channel_id=1, source_target_pairs={{0,8},{4,12},{8,0},{12,4},{16,24},{20,28},{24,16},{28,20},{1,9},{5... | collective-permute-start | bytes 49160 | tf_op jit(solution)/shard_map/ppermute | solution.py:728
  73.9 1.9 %collective-permute-done.24 = f32[32,128]{1,0:T(8,128)S(1)} collective-permute-done((f32[32,128]{1,0:T(8,128)S(1)}, f32[32,128]{1,0:T(8,128)S(1)}, u32[]{:S(2)}, u32[]{:S(2)}) %collective-permute-start.24) | collective-permute-done | bytes 16416 | tf_op jit(solution)/shard_map/ppermute | solution.py:728
  75.8 2.8 %collective-permute-start.27 = (f32[32,128]{1,0:T(8,128)S(1)}, f32[32,128]{1,0:T(8,128)S(1)}, u32[]{:S(2)}, u32[]{:S(2)}) collective-permute-start(f32[32,128]{1,0:T(8,128)S(1)} %add_add_fusion.refs_0_), channel_id=1, source_target_pairs={{0,64},{32,96},{64,0},{96,32},{1,65},{33,97},{65,1},{97,33},{2,66}... | collective-permute-start | bytes 49160 | tf_op jit(solution)/shard_map/ppermute | solution.py:728
  78.6 1.1 %collective-permute-start.26 = (f32[32,128]{1,0:T(8,128)S(1)}, f32[32,128]{1,0:T(8,128)S(1)}, u32[]{:S(2)}, u32[]{:S(2)}) collective-permute-start(f32[32,128]{1,0:T(8,128)S(1)} %add_add_fusion.refs_0_), channel_id=1, source_target_pairs={{0,96},{32,64},{64,32},{96,0},{1,97},{33,65},{65,33},{97,1},{2,98}... | collective-permute-start | bytes 49160 | tf_op jit(solution)/shard_map/ppermute | solution.py:728
  80.0 1.2 %collective-permute-done.27.refs_3_ = f32[32,128]{1,0:T(8,128)S(1)} collective-permute-done((f32[32,128]{1,0:T(8,128)S(1)}, f32[32,128]{1,0:T(8,128)S(1)}, u32[]{:S(2)}, u32[]{:S(2)}) %collective-permute-start.27) | collective-permute-done | bytes 16416 | tf_op jit(solution)/shard_map/ppermute | solution.py:728
  81.1 2.4 %collective-permute-done.26.refs_2_ = f32[32,128]{1,0:T(8,128)S(1)} collective-permute-done((f32[32,128]{1,0:T(8,128)S(1)}, f32[32,128]{1,0:T(8,128)S(1)}, u32[]{:S(2)}, u32[]{:S(2)}) %collective-permute-start.26) | collective-permute-done | bytes 16416 | tf_op jit(solution)/shard_map/ppermute | solution.py:728
  83.5 4.7 %solve_small.1.mix_ref = f32[64,128]{1,0:T(8,128)S(1)} custom-call(f32[32,128]{1,0:T(8,128)S(1)} %add_add_fusion.refs_0_, f32[32,128]{1,0:T(8,128)S(1)} %collective-permute-done.25.refs_1_, f32[32,128]{1,0:T(8,128)S(1)} %collective-permute-done.26.refs_2_, f32[32,128]{1,0:T(8,128)S(1)} %collective-permute-done.27.refs_3_), custom_call_target="tpu_custom_call" | custom-call | tf_op jit(solution)/shard_map/solve_small/pallas_call | solution.py:624
  88.3 7.6 %combine_fields.1 = (f32[32,16,16,128]{3,2,1,0:T(8,128)}, f32[32,16,16,128]{3,2,1,0:T(8,128)}) custom-call(f32[64,128]{1,0:T(8,128)S(1)} %solve_small.1.mix_ref, f32[16,16,32,128]{3,2,1,0:T(8,128)} %get-tuple-element.50.away.guess_hbm, f32[16,16,32,128]{3,2,1,0:T(8,128)S(1)} %get-tuple-element.65.refs_0_.refs_1_.one_ref, ...), custom_call_target="tpu_custom_call" | custom-call | tf_op jit(solution)/shard_map/combine_fields/pallas_call | solution.py:697
  (46 shorter events, 4.0 us)
Async XLA Ops:
  0.6 13.4 %copy-start = (s32[32]{0:T(128)S(1)}, s32[32]{0:T(128)}, u32[]{:S(2)}) copy-start(s32[32]{0:T(128)} %param.6) | copy-start | bytes 388
  7.1 7.0 %collective-permute-start.1 = (f32[5,32,128]{2,1,0:T(8,128)S(1)}, f32[5,32,128]{2,1,0:T(8,128)S(1)}, u32[]{:S(2)}, u32[]{:S(2)}) collective-permute-start(f32[5,32,128]{2,1,0:T(8,128)S(1)} %get-tuple-element.51), channel_id=1, source_target_pairs={{1,0},{2,1},{3,2},{0,3},{5,4},{6,5},{7,6},{4,7},{9,8},{10,9},{11,1... | collective-permute-start | bytes 245768 | tf_op jit(solution)/shard_map/ppermute | solution.py:551
  11.2 5.7 %collective-permute-start = (f32[5,32,128]{2,1,0:T(8,128)S(1)}, f32[5,32,128]{2,1,0:T(8,128)S(1)}, u32[]{:S(2)}, u32[]{:S(2)}) collective-permute-start(f32[5,32,128]{2,1,0:T(8,128)S(1)} %get-tuple-element.51), channel_id=1, source_target_pairs={{0,1},{1,2},{2,3},{3,0},{4,5},{5,6},{6,7},{7,4},{8,9},{9,10},{10,1... | collective-permute-start | bytes 245768 | tf_op jit(solution)/shard_map/ppermute | solution.py:550
  11.2 18.6 %collective-permute-start.3 = (f32[17,32,128]{2,1,0:T(8,128)S(1)}, f32[17,32,128]{2,1,0:T(8,128)S(1)}, u32[]{:S(2)}, u32[]{:S(2)}) collective-permute-start(f32[17,32,128]{2,1,0:T(8,128)S(1)} %get-tuple-element.58.refs_1_), channel_id=1, source_target_pairs={{32,0},{64,32},{96,64},{0,96},{33,1},{65,33},{97,65},{1,97},{34,2}... | collective-permute-start | bytes 835592 | tf_op jit(solution)/shard_map/ppermute | solution.py:556
  14.0 15.9 %collective-permute-start.2 = (f32[17,32,128]{2,1,0:T(8,128)S(1)}, f32[17,32,128]{2,1,0:T(8,128)S(1)}, u32[]{:S(2)}, u32[]{:S(2)}) collective-permute-start(f32[17,32,128]{2,1,0:T(8,128)S(1)} %get-tuple-element.59.refs_2_), channel_id=1, source_target_pairs={{0,32},{32,64},{64,96},{96,0},{1,33},{33,65},{65,97},{97,1},{2,34}... | collective-permute-start | bytes 835592 | tf_op jit(solution)/shard_map/ppermute | solution.py:555
  16.9 13.0 %collective-permute-start.4 = (f32[17,32,128]{2,1,0:T(8,128)S(1)}, f32[17,32,128]{2,1,0:T(8,128)S(1)}, u32[]{:S(2)}, u32[]{:S(2)}) collective-permute-start(f32[17,32,128]{2,1,0:T(8,128)S(1)} %get-tuple-element.60.refs_4_), channel_id=1, source_target_pairs={{0,4},{4,8},{8,12},{12,16},{16,20},{20,24},{24,28},{28,0},{1,5},{5... | collective-permute-start | bytes 835592 | tf_op jit(solution)/shard_map/ppermute | solution.py:557
  16.9 13.0 %collective-permute-start.5 = (f32[17,32,128]{2,1,0:T(8,128)S(1)}, f32[17,32,128]{2,1,0:T(8,128)S(1)}, u32[]{:S(2)}, u32[]{:S(2)}) collective-permute-start(f32[17,32,128]{2,1,0:T(8,128)S(1)} %get-tuple-element.61.refs_3_), channel_id=1, source_target_pairs={{4,0},{8,4},{12,8},{16,12},{20,16},{24,20},{28,24},{0,28},{5,1},{9... | collective-permute-start | bytes 835592 | tf_op jit(solution)/shard_map/ppermute | solution.py:558
  30.3 5.3 %collective-permute-start.7 = (f32[4,32,128]{2,1,0:T(8,128)S(1)}, f32[4,32,128]{2,1,0:T(8,128)S(1)}, u32[]{:S(2)}, u32[]{:S(2)}) collective-permute-start(f32[4,32,128]{2,1,0:T(8,128)S(1)} %get-tuple-element.66), channel_id=1, source_target_pairs={{1,0},{2,1},{3,2},{0,3},{5,4},{6,5},{7,6},{4,7},{9,8},{10,9},{11,1... | collective-permute-start | bytes 196616 | tf_op jit(solution)/shard_map/ppermute | solution.py:551
  30.8 5.5 %collective-permute-start.6 = (f32[4,32,128]{2,1,0:T(8,128)S(1)}, f32[4,32,128]{2,1,0:T(8,128)S(1)}, u32[]{:S(2)}, u32[]{:S(2)}) collective-permute-start(f32[4,32,128]{2,1,0:T(8,128)S(1)} %get-tuple-element.66), channel_id=1, source_target_pairs={{0,1},{1,2},{2,3},{3,0},{4,5},{5,6},{6,7},{7,4},{8,9},{9,10},{10,1... | collective-permute-start | bytes 196616 | tf_op jit(solution)/shard_map/ppermute | solution.py:550
  32.4 13.6 %collective-permute-start.8 = (f32[16,32,128]{2,1,0:T(8,128)S(1)}, f32[16,32,128]{2,1,0:T(8,128)S(1)}, u32[]{:S(2)}, u32[]{:S(2)}) collective-permute-start(f32[16,32,128]{2,1,0:T(8,128)S(1)} %get-tuple-element.77), channel_id=1, source_target_pairs={{0,32},{32,64},{64,96},{96,0},{1,33},{33,65},{65,97},{97,1},{2,34}... | collective-permute-start | bytes 786440 | tf_op jit(solution)/shard_map/ppermute | solution.py:555
  33.9 12.2 %collective-permute-start.9 = (f32[16,32,128]{2,1,0:T(8,128)S(1)}, f32[16,32,128]{2,1,0:T(8,128)S(1)}, u32[]{:S(2)}, u32[]{:S(2)}) collective-permute-start(f32[16,32,128]{2,1,0:T(8,128)S(1)} %get-tuple-element.78), channel_id=1, source_target_pairs={{32,0},{64,32},{96,64},{0,96},{33,1},{65,33},{97,65},{1,97},{34,2}... | collective-permute-start | bytes 786440 | tf_op jit(solution)/shard_map/ppermute | solution.py:556
  36.3 9.8 %collective-permute-start.10 = (f32[16,32,128]{2,1,0:T(8,128)S(1)}, f32[16,32,128]{2,1,0:T(8,128)S(1)}, u32[]{:S(2)}, u32[]{:S(2)}) collective-permute-start(f32[16,32,128]{2,1,0:T(8,128)S(1)} %get-tuple-element.79), channel_id=1, source_target_pairs={{0,4},{4,8},{8,12},{12,16},{16,20},{20,24},{24,28},{28,0},{1,5},{5... | collective-permute-start | bytes 786440 | tf_op jit(solution)/shard_map/ppermute | solution.py:557
  36.3 9.8 %collective-permute-start.11 = (f32[16,32,128]{2,1,0:T(8,128)S(1)}, f32[16,32,128]{2,1,0:T(8,128)S(1)}, u32[]{:S(2)}, u32[]{:S(2)}) collective-permute-start(f32[16,32,128]{2,1,0:T(8,128)S(1)} %get-tuple-element.80), channel_id=1, source_target_pairs={{4,0},{8,4},{12,8},{16,12},{20,16},{24,20},{28,24},{0,28},{5,1},{9... | collective-permute-start | bytes 786440 | tf_op jit(solution)/shard_map/ppermute | solution.py:558
  46.8 5.3 %collective-permute-start.13 = (f32[4,32,128]{2,1,0:T(8,128)S(1)}, f32[4,32,128]{2,1,0:T(8,128)S(1)}, u32[]{:S(2)}, u32[]{:S(2)}) collective-permute-start(f32[4,32,128]{2,1,0:T(8,128)S(1)} %get-tuple-element.84), channel_id=1, source_target_pairs={{1,0},{2,1},{3,2},{0,3},{5,4},{6,5},{7,6},{4,7},{9,8},{10,9},{11,1... | collective-permute-start | bytes 196616 | tf_op jit(solution)/shard_map/ppermute | solution.py:551
  47.9 5.5 %collective-permute-start.12 = (f32[4,32,128]{2,1,0:T(8,128)S(1)}, f32[4,32,128]{2,1,0:T(8,128)S(1)}, u32[]{:S(2)}, u32[]{:S(2)}) collective-permute-start(f32[4,32,128]{2,1,0:T(8,128)S(1)} %get-tuple-element.84), channel_id=1, source_target_pairs={{0,1},{1,2},{2,3},{3,0},{4,5},{5,6},{6,7},{7,4},{8,9},{9,10},{10,1... | collective-permute-start | bytes 196616 | tf_op jit(solution)/shard_map/ppermute | solution.py:550
  48.9 13.3 %collective-permute-start.14 = (f32[16,32,128]{2,1,0:T(8,128)S(1)}, f32[16,32,128]{2,1,0:T(8,128)S(1)}, u32[]{:S(2)}, u32[]{:S(2)}) collective-permute-start(f32[16,32,128]{2,1,0:T(8,128)S(1)} %get-tuple-element.90), channel_id=1, source_target_pairs={{0,32},{32,64},{64,96},{96,0},{1,33},{33,65},{65,97},{97,1},{2,34}... | collective-permute-start | bytes 786440 | tf_op jit(solution)/shard_map/ppermute | solution.py:555
  50.0 12.1 %collective-permute-start.15 = (f32[16,32,128]{2,1,0:T(8,128)S(1)}, f32[16,32,128]{2,1,0:T(8,128)S(1)}, u32[]{:S(2)}, u32[]{:S(2)}) collective-permute-start(f32[16,32,128]{2,1,0:T(8,128)S(1)} %get-tuple-element.91), channel_id=1, source_target_pairs={{32,0},{64,32},{96,64},{0,96},{33,1},{65,33},{97,65},{1,97},{34,2}... | collective-permute-start | bytes 786440 | tf_op jit(solution)/shard_map/ppermute | solution.py:556
  53.3 8.9 %collective-permute-start.16 = (f32[16,32,128]{2,1,0:T(8,128)S(1)}, f32[16,32,128]{2,1,0:T(8,128)S(1)}, u32[]{:S(2)}, u32[]{:S(2)}) collective-permute-start(f32[16,32,128]{2,1,0:T(8,128)S(1)} %get-tuple-element.92), channel_id=1, source_target_pairs={{0,4},{4,8},{8,12},{12,16},{16,20},{20,24},{24,28},{28,0},{1,5},{5... | collective-permute-start | bytes 786440 | tf_op jit(solution)/shard_map/ppermute | solution.py:557
  53.4 8.9 %collective-permute-start.17 = (f32[16,32,128]{2,1,0:T(8,128)S(1)}, f32[16,32,128]{2,1,0:T(8,128)S(1)}, u32[]{:S(2)}, u32[]{:S(2)}) collective-permute-start(f32[16,32,128]{2,1,0:T(8,128)S(1)} %get-tuple-element.93), channel_id=1, source_target_pairs={{4,0},{8,4},{12,8},{16,12},{20,16},{24,20},{28,24},{0,28},{5,1},{9... | collective-permute-start | bytes 786440 | tf_op jit(solution)/shard_map/ppermute | solution.py:558
  62.9 1.2 %collective-permute-start.18 = (f32[32,128]{1,0:T(8,128)S(1)}, f32[32,128]{1,0:T(8,128)S(1)}, u32[]{:S(2)}, u32[]{:S(2)}) collective-permute-start(f32[32,128]{1,0:T(8,128)S(1)} %get-tuple-element.96), channel_id=1, source_target_pairs={{0,4},{4,0},{8,12},{12,8},{16,20},{20,16},{24,28},{28,24},{1,5},{5... | collective-permute-start | bytes 49160 | tf_op jit(solution)/shard_map/ppermute | solution.py:723
  64.1 5.4 %collective-permute-start.21 = (f32[32,128]{1,0:T(8,128)S(1)}, f32[32,128]{1,0:T(8,128)S(1)}, u32[]{:S(2)}, u32[]{:S(2)}) collective-permute-start(f32[32,128]{1,0:T(8,128)S(1)} %add.42), channel_id=1, source_target_pairs={{0,2},{1,3},{2,0},{3,1},{4,6},{5,7},{6,4},{7,5},{8,10},{9,11},{10,... | collective-permute-start | bytes 49160 | tf_op jit(solution)/shard_map/ppermute | solution.py:728
  64.4 5.1 %collective-permute-start.20 = (f32[32,128]{1,0:T(8,128)S(1)}, f32[32,128]{1,0:T(8,128)S(1)}, u32[]{:S(2)}, u32[]{:S(2)}) collective-permute-start(f32[32,128]{1,0:T(8,128)S(1)} %add.42), channel_id=1, source_target_pairs={{0,3},{1,2},{2,1},{3,0},{4,7},{5,6},{6,5},{7,4},{8,11},{9,10},{10,... | collective-permute-start | bytes 49160 | tf_op jit(solution)/shard_map/ppermute | solution.py:728
  66.6 3.7 %collective-permute-start.19 = (f32[32,128]{1,0:T(8,128)S(1)}, f32[32,128]{1,0:T(8,128)S(1)}, u32[]{:S(2)}, u32[]{:S(2)}) collective-permute-start(f32[32,128]{1,0:T(8,128)S(1)} %add.42), channel_id=1, source_target_pairs={{0,1},{1,0},{2,3},{3,2},{4,5},{5,4},{6,7},{7,6},{8,9},{9,8},{10,11... | collective-permute-start | bytes 49160 | tf_op jit(solution)/shard_map/ppermute | solution.py:728
  70.4 5.3 %collective-permute-start.24 = (f32[32,128]{1,0:T(8,128)S(1)}, f32[32,128]{1,0:T(8,128)S(1)}, u32[]{:S(2)}, u32[]{:S(2)}) collective-permute-start(f32[32,128]{1,0:T(8,128)S(1)} %add_add_fusion.1), channel_id=1, source_target_pairs={{0,16},{4,20},{8,24},{12,28},{16,0},{20,4},{24,8},{28,12},{1,17},{... | collective-permute-start | bytes 49160 | tf_op jit(solution)/shard_map/ppermute | solution.py:728
  70.4 5.4 %collective-permute-start.23 = (f32[32,128]{1,0:T(8,128)S(1)}, f32[32,128]{1,0:T(8,128)S(1)}, u32[]{:S(2)}, u32[]{:S(2)}) collective-permute-start(f32[32,128]{1,0:T(8,128)S(1)} %add_add_fusion.1), channel_id=1, source_target_pairs={{0,24},{4,28},{8,16},{12,20},{16,8},{20,12},{24,0},{28,4},{1,25},{... | collective-permute-start | bytes 49160 | tf_op jit(solution)/shard_map/ppermute | solution.py:728
  71.8 4.0 %collective-permute-start.22 = (f32[32,128]{1,0:T(8,128)S(1)}, f32[32,128]{1,0:T(8,128)S(1)}, u32[]{:S(2)}, u32[]{:S(2)}) collective-permute-start(f32[32,128]{1,0:T(8,128)S(1)} %add_add_fusion.1), channel_id=1, source_target_pairs={{0,8},{4,12},{8,0},{12,4},{16,24},{20,28},{24,16},{28,20},{1,9},{5... | collective-permute-start | bytes 49160 | tf_op jit(solution)/shard_map/ppermute | solution.py:728
  75.8 5.3 %collective-permute-start.27 = (f32[32,128]{1,0:T(8,128)S(1)}, f32[32,128]{1,0:T(8,128)S(1)}, u32[]{:S(2)}, u32[]{:S(2)}) collective-permute-start(f32[32,128]{1,0:T(8,128)S(1)} %add_add_fusion.refs_0_), channel_id=1, source_target_pairs={{0,64},{32,96},{64,0},{96,32},{1,65},{33,97},{65,1},{97,33},{2,66}... | collective-permute-start | bytes 49160 | tf_op jit(solution)/shard_map/ppermute | solution.py:728
  78.6 4.9 %collective-permute-start.26 = (f32[32,128]{1,0:T(8,128)S(1)}, f32[32,128]{1,0:T(8,128)S(1)}, u32[]{:S(2)}, u32[]{:S(2)}) collective-permute-start(f32[32,128]{1,0:T(8,128)S(1)} %add_add_fusion.refs_0_), channel_id=1, source_target_pairs={{0,96},{32,64},{64,32},{96,0},{1,97},{33,65},{65,33},{97,1},{2,98}... | collective-permute-start | bytes 49160 | tf_op jit(solution)/shard_map/ppermute | solution.py:728
  79.7 3.8 %collective-permute-start.25 = (f32[32,128]{1,0:T(8,128)S(1)}, f32[32,128]{1,0:T(8,128)S(1)}, u32[]{:S(2)}, u32[]{:S(2)}) collective-permute-start(f32[32,128]{1,0:T(8,128)S(1)} %add_add_fusion.refs_0_), channel_id=1, source_target_pairs={{0,32},{32,0},{64,96},{96,64},{1,33},{33,1},{65,97},{97,65},{2,34}... | collective-permute-start | bytes 49160 | tf_op jit(solution)/shard_map/ppermute | solution.py:728

commit v4 on v3

--- a/solution.py
+++ b/solution.py
@@ -591,30 +591,25 @@
         sums = sums + ref[...]
     lane = lanes(32)
     row = rows_of(32)
-    unit = jnp.where(lane == row + 32, 1.0, 0.0)
-    advance_table = jnp.where(lane < 32, pltpu.roll(sums, 96, 1), pltpu.roll(sums, 32, 1))
-    norm_table = jnp.where(lane < 32, sums, unit)
-    advance_table, norm_table = eliminate([advance_table, norm_table])
+    table = jnp.where(lane < 32, pltpu.roll(sums, 96, 1), pltpu.roll(sums, 32, 1))
+    table = jnp.where(lane < 64, table, jnp.where(lane == row + 64, 1.0, 0.0))
+    (table,) = eliminate([table])
     norm = sums[:, 0:32]
-    moment = sums[:, 32:64]
     square = sums[:, 64:96]
     cube = sums[:, 96:128]
-    advance = advance_table[:, 32:64]
-    inverse = norm_table[:, 32:64]
+    advance = table[:, 32:64]
+    inverse = table[:, 64:96]
+    advance_t = advance.T
     turned = dot(square, advance)
-    tripled = dot(dot(advance, cube, (0, 0)), advance)
+    tripled = dot(advance, dot(cube, advance), (0, 0))
+    mixing = dot(inverse, turned)
     norm_next = dot(advance, turned, (0, 0)) - norm
-    eye = jnp.where(lane[:, 0:32] == row[:, 0:32], 1.0, 0.0)
-    mixing = eye + dot(inverse, norm_next)
-    curvature = dot(mixing, dot(moment, mixing) - turned, (0, 0))
-    curvature = curvature - dot(turned, mixing, (0, 0)) + tripled
+    curvature = tripled - dot(turned, mixing, (0, 0))
     wide = jnp.concatenate([curvature, norm_next, jnp.zeros((32, 64), F32)], axis=1)
     (wide,) = eliminate([wide])
     later = wide[:, 32:64]
-    taken = advance + dot(mixing, later)
-    beyond = dot(advance, later)
-    taken_t = taken.T
-    beyond_t = beyond.T
+    taken_t = advance_t + dot(later, mixing, (0, 1))
+    beyond_t = dot(later, advance, (0, 1))
     nothing = jnp.zeros((32, 32), F32)
     out_ref[0:32, :] = jnp.concatenate([taken_t, -beyond_t, nothing, nothing], axis=1)
     out_ref[32:64, :] = jnp.concatenate([nothing, -taken_t, beyond_t, nothing], axis=1)
@@ -647,48 +642,73 @@
     high = mix.astype(BF16)
     low = (mix - high.astype(F32)).astype(BF16)
     mixing = jnp.concatenate(
-        [jnp.concatenate([high, high], axis=1), jnp.concatenate([low, low], axis=1)], axis=0
+        [
+            jnp.concatenate([half[:, : 3 * columns], half[:, : 3 * columns]], axis=1)
+            for half in (high, low)
+        ],
+        axis=0,
     )
-    nothing = jnp.zeros((columns, 2 * nz), F32)
 
     def leaving(x):
-        slot = lax.rem(x, slots)
-        return (
-            pltpu.make_async_copy(solution.at[slot], solution_hbm.at[:, x], sem.at[0, slot]),
-            pltpu.make_async_copy(residual.at[slot], residual_hbm.at[:, x], sem.at[1, slot]),
-        )
-
-    def at_x(x, carry):
-        slot = lax.rem(x, slots)
-
-        @pl.when(x >= slots)
+        slot = x % slots
+        copies = []
+        for place, (held, away) in enumerate(((solution, solution_hbm), (residual, residual_hbm))):
+            for half in range(ny // 8):
+                copies.append(
+                    pltpu.make_async_copy(
+                        held.at[slot, half],
+                        away.at[:, x, 8 * half : 8 * half + 8],
+                        sem.at[place, half, slot],
+                    )
+                )
+        return copies
+
+    mix = mix_ref[...]
+    high = mix.astype(BF16)
+    low = (mix - high.astype(F32)).astype(BF16)
+    mixing = jnp.concatenate(
+        [
+            jnp.concatenate([half[:, : 3 * columns], half[:, : 3 * columns]], axis=1)
+            for half in (high, low)
+        ],
+        axis=0,
+    )
+
+    def at_pair(pair, carry):
+        @pl.when(2 * pair >= slots)
         def _():
-            for copy in leaving(x - slots):
-                copy.wait()
-
-        arriving(x).wait()
-        solution_rows = solution.at[slot].reshape(columns * ny, nz)
-        residual_rows = residual.at[slot].reshape(columns * ny, nz)
-        for y in range(0, ny, 2):
-            fields = [
-                jnp.concatenate([ref[x, y], ref[x, y + 1]], axis=1)
-                for ref in (one_ref, two_ref, three_ref)
-            ]
-            halves = split(fields + [nothing])
-            mixed = jnp.dot(mixing, halves, preferred_element_type=F32)
-            mixed = mixed[0:64] + mixed[64:128]
             for step in range(2):
-                rows = pl.ds(y + step, columns, stride=ny)
-                part = mixed[:, step * nz : (step + 1) * nz]
-                solution_rows[rows, :] = guess_ref[x, y + step] + part[0:32]
-                residual_rows[rows, :] = one_ref[x, y + step] + part[32:64]
+                for copy in leaving(2 * pair + step - slots):
+                    copy.wait()
+
+        for step in range(2):
+            arriving(2 * pair + step).wait()
+        for step in range(2):
+            x = 2 * pair + step
+            slot = lax.rem(x, slots)
+            solution_rows = solution.at[slot].reshape(columns * ny, nz)
+            residual_rows = residual.at[slot].reshape(columns * ny, nz)
+            for y in range(0, ny, 2):
+                fields = [
+                    jnp.concatenate([ref[x, y], ref[x, y + 1]], axis=1)
+                    for ref in (one_ref, two_ref, three_ref)
+                ]
+                mixed = jnp.dot(mixing, split(fields), preferred_element_type=F32)
+                mixed = mixed[0:64] + mixed[64:128]
+                for z in range(2):
+                    own = y + z
+                    rows = pl.ds((own // 8) * 8 * columns + own % 8, columns, stride=8)
+                    part = mixed[:, z * nz : (z + 1) * nz]
+                    solution_rows[rows, :] = guess_ref[x, own] + part[0:32]
+                    residual_rows[rows, :] = one_ref[x, own] + part[32:64]
+        for step in range(2):
+            for copy in leaving(2 * pair + step):
+                copy.start()
+        return carry
+
+    lax.fori_loop(0, nx // 2, at_pair, 0)
+    for x in range(nx - slots, nx):
         for copy in leaving(x):
-            copy.start()
-        return carry
-
-    lax.fori_loop(0, nx, at_x, 0)
-    for x in range(nx - slots, nx):
-        for copy in leaving(jnp.int32(x)):
             copy.wait()
 
 
@@ -701,9 +721,9 @@
         out_shape=[jax.ShapeDtypeStruct((columns, nx, ny, nz), F32)] * 2,
         scratch_shapes=[
             pltpu.VMEM(guess.shape, F32),
-            pltpu.VMEM((8, columns, ny, nz), F32),
-            pltpu.VMEM((8, columns, ny, nz), F32),
-            pltpu.SemaphoreType.DMA((2, 8)),
+            pltpu.VMEM((8, ny // 8, columns, 8, nz), F32),
+            pltpu.VMEM((8, ny // 8, columns, 8, nz), F32),
+            pltpu.SemaphoreType.DMA((2, ny // 8, 8)),
             pltpu.SemaphoreType.DMA((nx,)),
         ],
         compiler_params=params(),

time: 96.3 us -> 94.1 us (0.977)
  Pallas kernels: 43 us -> 40.9 us
    pallas_call x1, Pallas kernels: 7.61 us -> 6.24 us  [combine(): pl.pallas_call(combine_kernel, in_specs=[VMEM, HBM] + [VMEM] * 3, out_spe...]
  transfers between devices with their start and end apart: 28 -> 28, of which waited for: 9 -> 9; matrix products, arithmetic and copies ran while one was open for 0% -> 0% of each run, Pallas kernels for 23% -> 24%
where the time goes in v4:
time: 94.1 us; the launch traced here: 93.9 us
  Pallas kernels  40.9 us (43%)
  starting transfers between devices  37.6 us (40%)
  waiting for transfers between devices  14.1 us (15%)
  between operations  1.01 us (1%)
    pallas_call x3, Pallas kernels, inner_part(): pl.pallas_call(first_kernel if first else functools.partial(inner_kernel,...  22.4 us
    ppermute x9, starting transfers between devices, summed_but_last(): lax.ppermute(values, axis, swaps(axis, mask, stride))  11.1 us
    ppermute x3, starting transfers between devices, exchanged(): lax.ppermute(ylo, 'dip', back('dip'))  8.86 us
    ppermute x9, waiting for transfers between devices, summed_but_last(): lax.ppermute(values, axis, swaps(axis, mask, stride))  8.2 us
    ppermute x3, starting transfers between devices, exchanged(): lax.ppermute(xlo, 'strike', back('strike'))  6.59 us
    pallas_call x1, Pallas kernels, pack(): pl.pallas_call(pack_kernel, in_specs=[HBM] * 3, out_specs=[HBM] + [VMEM]...  6.41 us
    pallas_call x1, Pallas kernels, combine(): pl.pallas_call(combine_kernel, in_specs=[VMEM, HBM] + [VMEM] * 3, out_spe...  6.24 us
    ppermute x3, starting transfers between devices, exchanged(): lax.ppermute(ends, 'layer', back('layer'))  5.74 us
  transfers between devices with their start and end apart: 28, of which 9 were waited for; matrix products, arithmetic and copies ran while one was open for 0% of the time, Pallas kernels for 24%

profile of v4, /device:TPU:0, one launch (start us, length us, event | category | flops | bytes accessed | tf_op | source)
XLA Modules:
  0.0 93.9 jit_solution(8880695368196918767)
XLA Ops:
  0.6 6.4 %pack_guess.1 = (f32[16,16,32,128]{3,2,1,0:T(8,128)}, f32[16,16,128]{2,1,0:T(8,128)S(1)}, f32[17,32,128]{2,1,0:T(8,128)S(1)}, f32[17,32,128]{2,1,0:T(8,128)S(1)}...) custom-call(s32[16,16,128]{2,1,0:T(8,128)} %class_hbm.1, f32[16]{0:T(128)} %table_hbm.1, ...), custom_call_target="tpu_custom_call" | custom-call | tf_op jit(solution)/shard_map/pack_guess/pallas_call | solution.py:128
  7.1 4.2 %collective-permute-start.1 = (f32[5,32,128]{2,1,0:T(8,128)S(1)}, f32[5,32,128]{2,1,0:T(8,128)S(1)}, u32[]{:S(2)}, u32[]{:S(2)}) collective-permute-start(f32[5,32,128]{2,1,0:T(8,128)S(1)} %get-tuple-element.51), channel_id=1, source_target_pairs={{1,0},{2,1},{3,2},{0,3},{5,4},{6,5},{7,6},{4,7},{9,8},{10,9},{11,1... | collective-permute-start | bytes 245768 | tf_op jit(solution)/shard_map/ppermute | solution.py:551
  11.2 2.8 %collective-permute-start.3 = (f32[17,32,128]{2,1,0:T(8,128)S(1)}, f32[17,32,128]{2,1,0:T(8,128)S(1)}, u32[]{:S(2)}, u32[]{:S(2)}) collective-permute-start(f32[17,32,128]{2,1,0:T(8,128)S(1)} %get-tuple-element.58.refs_1_), channel_id=1, source_target_pairs={{32,0},{64,32},{96,64},{0,96},{33,1},{65,33},{97,65},{1,97},{34,2}... | collective-permute-start | bytes 835592 | tf_op jit(solution)/shard_map/ppermute | solution.py:556
  14.1 2.8 %collective-permute-done.hzl = f32[5,32,128]{2,1,0:T(8,128)S(1)} collective-permute-done((f32[5,32,128]{2,1,0:T(8,128)S(1)}, f32[5,32,128]{2,1,0:T(8,128)S(1)}, u32[]{:S(2)}, u32[]{:S(2)}) %collective-permute-start) | collective-permute-done | bytes 81952 | tf_op jit(solution)/shard_map/ppermute | solution.py:550
  16.9 3.0 %collective-permute-start.5 = (f32[17,32,128]{2,1,0:T(8,128)S(1)}, f32[17,32,128]{2,1,0:T(8,128)S(1)}, u32[]{:S(2)}, u32[]{:S(2)}) collective-permute-start(f32[17,32,128]{2,1,0:T(8,128)S(1)} %get-tuple-element.61.refs_3_), channel_id=1, source_target_pairs={{4,0},{8,4},{12,8},{16,12},{20,16},{24,20},{28,24},{0,28},{5,1},{9... | collective-permute-start | bytes 835592 | tf_op jit(solution)/shard_map/ppermute | solution.py:558
  20.2 9.7 %inner_first.1 = (f32[16,16,32,128]{3,2,1,0:T(8,128)S(1)}, f32[4,32,128]{2,1,0:T(8,128)S(1)}, f32[17,16,128]{2,1,0:T(8,128)S(1)}, f32[16,24,128]{2,1,0:T(8,128)S...) custom-call(f32[16,16,32,128]{3,2,1,0:T(8,128)} %get-tuple-element.50.away.guess_hbm, ...), custom_call_target="tpu_custom_call" | custom-call | flops 20971520 | bytes 25165824 | tf_op jit(solution)/shard_map/inner_first/pallas_call | solution.py:500
  30.8 1.6 %collective-permute-start.6 = (f32[4,32,128]{2,1,0:T(8,128)S(1)}, f32[4,32,128]{2,1,0:T(8,128)S(1)}, u32[]{:S(2)}, u32[]{:S(2)}) collective-permute-start(f32[4,32,128]{2,1,0:T(8,128)S(1)} %get-tuple-element.66), channel_id=1, source_target_pairs={{0,1},{1,2},{2,3},{3,0},{4,5},{5,6},{6,7},{7,4},{8,9},{9,10},{10,1... | collective-permute-start | bytes 196616 | tf_op jit(solution)/shard_map/ppermute | solution.py:550
  32.4 1.5 %collective-permute-start.8 = (f32[16,32,128]{2,1,0:T(8,128)S(1)}, f32[16,32,128]{2,1,0:T(8,128)S(1)}, u32[]{:S(2)}, u32[]{:S(2)}) collective-permute-start(f32[16,32,128]{2,1,0:T(8,128)S(1)} %get-tuple-element.77), channel_id=1, source_target_pairs={{0,32},{32,64},{64,96},{96,0},{1,33},{33,65},{65,97},{97,1},{2,34}... | collective-permute-start | bytes 786440 | tf_op jit(solution)/shard_map/ppermute | solution.py:555
  33.9 1.7 %collective-permute-start.9 = (f32[16,32,128]{2,1,0:T(8,128)S(1)}, f32[16,32,128]{2,1,0:T(8,128)S(1)}, u32[]{:S(2)}, u32[]{:S(2)}) collective-permute-start(f32[16,32,128]{2,1,0:T(8,128)S(1)} %get-tuple-element.78), channel_id=1, source_target_pairs={{32,0},{64,32},{96,64},{0,96},{33,1},{65,33},{97,65},{1,97},{34,2}... | collective-permute-start | bytes 786440 | tf_op jit(solution)/shard_map/ppermute | solution.py:556
  36.3 3.0 %collective-permute-start.11 = (f32[16,32,128]{2,1,0:T(8,128)S(1)}, f32[16,32,128]{2,1,0:T(8,128)S(1)}, u32[]{:S(2)}, u32[]{:S(2)}) collective-permute-start(f32[16,32,128]{2,1,0:T(8,128)S(1)} %get-tuple-element.80), channel_id=1, source_target_pairs={{4,0},{8,4},{12,8},{16,12},{20,16},{24,20},{28,24},{0,28},{5,1},{9... | collective-permute-start | bytes 786440 | tf_op jit(solution)/shard_map/ppermute | solution.py:558
  39.3 6.8 %inner_next.1 = (f32[16,16,32,128]{3,2,1,0:T(8,128)S(1)}, f32[4,32,128]{2,1,0:T(8,128)S(1)}, f32[64,128]{1,0:T(8,128)S(1)}) custom-call(f32[16,16,32,128]{3,2,1,0:T(8,128)S(1)} %get-tuple-element.65.refs_0_.refs_1_.one_ref, f32[4,32,128]{2,1,0:T(8,128)S(1)} %collective-permute-done.6.refs_1_, f32[4,32,128]{2,1,0:T(8,128)S(1)} %collective-permute-done.7.refs_2_, ...), custom_call_target="tpu_custom_call" | custom-call | flops 20971520 | bytes 25165824 | tf_op jit(solution)/shard_map/inner_next/pallas_call | solution.py:500
  46.8 1.1 %collective-permute-start.13 = (f32[4,32,128]{2,1,0:T(8,128)S(1)}, f32[4,32,128]{2,1,0:T(8,128)S(1)}, u32[]{:S(2)}, u32[]{:S(2)}) collective-permute-start(f32[4,32,128]{2,1,0:T(8,128)S(1)} %get-tuple-element.84), channel_id=1, source_target_pairs={{1,0},{2,1},{3,2},{0,3},{5,4},{6,5},{7,6},{4,7},{9,8},{10,9},{11,1... | collective-permute-start | bytes 196616 | tf_op jit(solution)/shard_map/ppermute | solution.py:551
  47.9 1.0 %collective-permute-start.12 = (f32[4,32,128]{2,1,0:T(8,128)S(1)}, f32[4,32,128]{2,1,0:T(8,128)S(1)}, u32[]{:S(2)}, u32[]{:S(2)}) collective-permute-start(f32[4,32,128]{2,1,0:T(8,128)S(1)} %get-tuple-element.84), channel_id=1, source_target_pairs={{0,1},{1,2},{2,3},{3,0},{4,5},{5,6},{6,7},{7,4},{8,9},{9,10},{10,1... | collective-permute-start | bytes 196616 | tf_op jit(solution)/shard_map/ppermute | solution.py:550
  48.9 1.2 %collective-permute-start.14 = (f32[16,32,128]{2,1,0:T(8,128)S(1)}, f32[16,32,128]{2,1,0:T(8,128)S(1)}, u32[]{:S(2)}, u32[]{:S(2)}) collective-permute-start(f32[16,32,128]{2,1,0:T(8,128)S(1)} %get-tuple-element.90), channel_id=1, source_target_pairs={{0,32},{32,64},{64,96},{96,0},{1,33},{33,65},{65,97},{97,1},{2,34}... | collective-permute-start | bytes 786440 | tf_op jit(solution)/shard_map/ppermute | solution.py:555
  50.0 2.1 %collective-permute-start.15 = (f32[16,32,128]{2,1,0:T(8,128)S(1)}, f32[16,32,128]{2,1,0:T(8,128)S(1)}, u32[]{:S(2)}, u32[]{:S(2)}) collective-permute-start(f32[16,32,128]{2,1,0:T(8,128)S(1)} %get-tuple-element.91), channel_id=1, source_target_pairs={{32,0},{64,32},{96,64},{0,96},{33,1},{65,33},{97,65},{1,97},{34,2}... | collective-permute-start | bytes 786440 | tf_op jit(solution)/shard_map/ppermute | solution.py:556
  52.1 1.2 %collective-permute-done.12.refs_1_ = f32[4,32,128]{2,1,0:T(8,128)S(1)} collective-permute-done((f32[4,32,128]{2,1,0:T(8,128)S(1)}, f32[4,32,128]{2,1,0:T(8,128)S(1)}, u32[]{:S(2)}, u32[]{:S(2)}) %collective-permute-start.12) | collective-permute-done | bytes 65568 | tf_op jit(solution)/shard_map/ppermute | solution.py:550
  53.4 3.0 %collective-permute-start.17 = (f32[16,32,128]{2,1,0:T(8,128)S(1)}, f32[16,32,128]{2,1,0:T(8,128)S(1)}, u32[]{:S(2)}, u32[]{:S(2)}) collective-permute-start(f32[16,32,128]{2,1,0:T(8,128)S(1)} %get-tuple-element.93), channel_id=1, source_target_pairs={{4,0},{8,4},{12,8},{16,12},{20,16},{24,20},{28,24},{0,28},{5,1},{9... | collective-permute-start | bytes 786440 | tf_op jit(solution)/shard_map/ppermute | solution.py:558
  56.3 5.9 %inner_last.1 = (f32[16,16,32,128]{3,2,1,0:T(8,128)S(1)}, f32[64,128]{1,0:T(8,128)S(1)}) custom-call(f32[16,16,32,128]{3,2,1,0:T(8,128)S(1)} %get-tuple-element.83.refs_0_.refs_1_.two_ref, f32[4,32,128]{2,1,0:T(8,128)S(1)} %collective-permute-done.12.refs_1_, f32[4,32,128]{2,1,0:T(8,128)S(1)} %collective-permute-done.13.refs_2_, ...), custom_call_target="tpu_custom_call" | custom-call | flops 20971520 | bytes 25165824 | tf_op jit(solution)/shard_map/inner_last/pallas_call | solution.py:500
  63.0 1.2 %collective-permute-done.18 = f32[32,128]{1,0:T(8,128)S(1)} collective-permute-done((f32[32,128]{1,0:T(8,128)S(1)}, f32[32,128]{1,0:T(8,128)S(1)}, u32[]{:S(2)}, u32[]{:S(2)}) %collective-permute-start.18) | collective-permute-done | bytes 16416 | tf_op jit(solution)/shard_map/ppermute | solution.py:743
  64.4 2.2 %collective-permute-start.20 = (f32[32,128]{1,0:T(8,128)S(1)}, f32[32,128]{1,0:T(8,128)S(1)}, u32[]{:S(2)}, u32[]{:S(2)}) collective-permute-start(f32[32,128]{1,0:T(8,128)S(1)} %add.42), channel_id=1, source_target_pairs={{0,3},{1,2},{2,1},{3,0},{4,7},{5,6},{6,5},{7,4},{8,11},{9,10},{10,... | collective-permute-start | bytes 49160 | tf_op jit(solution)/shard_map/ppermute | solution.py:748
  66.6 1.0 %collective-permute-start.19 = (f32[32,128]{1,0:T(8,128)S(1)}, f32[32,128]{1,0:T(8,128)S(1)}, u32[]{:S(2)}, u32[]{:S(2)}) collective-permute-start(f32[32,128]{1,0:T(8,128)S(1)} %add.42), channel_id=1, source_target_pairs={{0,1},{1,0},{2,3},{3,2},{4,5},{5,4},{6,7},{7,6},{8,9},{9,8},{10,11... | collective-permute-start | bytes 49160 | tf_op jit(solution)/shard_map/ppermute | solution.py:748
  67.6 1.9 %collective-permute-done.21 = f32[32,128]{1,0:T(8,128)S(1)} collective-permute-done((f32[32,128]{1,0:T(8,128)S(1)}, f32[32,128]{1,0:T(8,128)S(1)}, u32[]{:S(2)}, u32[]{:S(2)}) %collective-permute-start.21) | collective-permute-done | bytes 16416 | tf_op jit(solution)/shard_map/ppermute | solution.py:748
  69.5 0.8 collective-permute-done.19
  70.4 1.4 %collective-permute-start.23 = (f32[32,128]{1,0:T(8,128)S(1)}, f32[32,128]{1,0:T(8,128)S(1)}, u32[]{:S(2)}, u32[]{:S(2)}) collective-permute-start(f32[32,128]{1,0:T(8,128)S(1)} %add_add_fusion.1), channel_id=1, source_target_pairs={{0,24},{4,28},{8,16},{12,20},{16,8},{20,12},{24,0},{28,4},{1,25},{... | collective-permute-start | bytes 49160 | tf_op jit(solution)/shard_map/ppermute | solution.py:748
  71.8 2.1 %collective-permute-start.22 = (f32[32,128]{1,0:T(8,128)S(1)}, f32[32,128]{1,0:T(8,128)S(1)}, u32[]{:S(2)}, u32[]{:S(2)}) collective-permute-start(f32[32,128]{1,0:T(8,128)S(1)} %add_add_fusion.1), channel_id=1, source_target_pairs={{0,8},{4,12},{8,0},{12,4},{16,24},{20,28},{24,16},{28,20},{1,9},{5... | collective-permute-start | bytes 49160 | tf_op jit(solution)/shard_map/ppermute | solution.py:748
  73.9 1.9 %collective-permute-done.24 = f32[32,128]{1,0:T(8,128)S(1)} collective-permute-done((f32[32,128]{1,0:T(8,128)S(1)}, f32[32,128]{1,0:T(8,128)S(1)}, u32[]{:S(2)}, u32[]{:S(2)}) %collective-permute-start.24) | collective-permute-done | bytes 16416 | tf_op jit(solution)/shard_map/ppermute | solution.py:748
  75.8 2.8 %collective-permute-start.27 = (f32[32,128]{1,0:T(8,128)S(1)}, f32[32,128]{1,0:T(8,128)S(1)}, u32[]{:S(2)}, u32[]{:S(2)}) collective-permute-start(f32[32,128]{1,0:T(8,128)S(1)} %add_add_fusion.refs_0_), channel_id=1, source_target_pairs={{0,64},{32,96},{64,0},{96,32},{1,65},{33,97},{65,1},{97,33},{2,66}... | collective-permute-start | bytes 49160 | tf_op jit(solution)/shard_map/ppermute | solution.py:748
  78.6 1.1 %collective-permute-start.26 = (f32[32,128]{1,0:T(8,128)S(1)}, f32[32,128]{1,0:T(8,128)S(1)}, u32[]{:S(2)}, u32[]{:S(2)}) collective-permute-start(f32[32,128]{1,0:T(8,128)S(1)} %add_add_fusion.refs_0_), channel_id=1, source_target_pairs={{0,96},{32,64},{64,32},{96,0},{1,97},{33,65},{65,33},{97,1},{2,98}... | collective-permute-start | bytes 49160 | tf_op jit(solution)/shard_map/ppermute | solution.py:748
  80.0 1.2 %collective-permute-done.27.refs_3_ = f32[32,128]{1,0:T(8,128)S(1)} collective-permute-done((f32[32,128]{1,0:T(8,128)S(1)}, f32[32,128]{1,0:T(8,128)S(1)}, u32[]{:S(2)}, u32[]{:S(2)}) %collective-permute-start.27) | collective-permute-done | bytes 16416 | tf_op jit(solution)/shard_map/ppermute | solution.py:748
  81.1 2.4 %collective-permute-done.26.refs_2_ = f32[32,128]{1,0:T(8,128)S(1)} collective-permute-done((f32[32,128]{1,0:T(8,128)S(1)}, f32[32,128]{1,0:T(8,128)S(1)}, u32[]{:S(2)}, u32[]{:S(2)}) %collective-permute-start.26) | collective-permute-done | bytes 16416 | tf_op jit(solution)/shard_map/ppermute | solution.py:748
  83.5 4.0 %solve_small.1.mix_ref = f32[64,128]{1,0:T(8,128)S(1)} custom-call(f32[32,128]{1,0:T(8,128)S(1)} %add_add_fusion.refs_0_, f32[32,128]{1,0:T(8,128)S(1)} %collective-permute-done.25.refs_1_, f32[32,128]{1,0:T(8,128)S(1)} %collective-permute-done.26.refs_2_, f32[32,128]{1,0:T(8,128)S(1)} %collective-permute-done.27.refs_3_), custom_call_target="tpu_custom_call" | custom-call | tf_op jit(solution)/shard_map/solve_small/pallas_call | solution.py:619
  87.5 6.2 %combine_fields.1 = (f32[32,16,16,128]{3,2,1,0:T(8,128)}, f32[32,16,16,128]{3,2,1,0:T(8,128)}) custom-call(f32[64,128]{1,0:T(8,128)S(1)} %solve_small.1.mix_ref, f32[16,16,32,128]{3,2,1,0:T(8,128)} %get-tuple-element.50.away.guess_hbm, f32[16,16,32,128]{3,2,1,0:T(8,128)S(1)} %get-tuple-element.65.refs_0_.refs_1_.one_ref, ...), custom_call_target="tpu_custom_call" | custom-call | tf_op jit(solution)/shard_map/combine_fields/pallas_call | solution.py:717
  (46 shorter events, 4.0 us)
Async XLA Ops:
  0.6 13.4 %copy-start = (s32[32]{0:T(128)S(1)}, s32[32]{0:T(128)}, u32[]{:S(2)}) copy-start(s32[32]{0:T(128)} %param.6) | copy-start | bytes 388
  7.1 7.0 %collective-permute-start.1 = (f32[5,32,128]{2,1,0:T(8,128)S(1)}, f32[5,32,128]{2,1,0:T(8,128)S(1)}, u32[]{:S(2)}, u32[]{:S(2)}) collective-permute-start(f32[5,32,128]{2,1,0:T(8,128)S(1)} %get-tuple-element.51), channel_id=1, source_target_pairs={{1,0},{2,1},{3,2},{0,3},{5,4},{6,5},{7,6},{4,7},{9,8},{10,9},{11,1... | collective-permute-start | bytes 245768 | tf_op jit(solution)/shard_map/ppermute | solution.py:551
  11.2 5.7 %collective-permute-start = (f32[5,32,128]{2,1,0:T(8,128)S(1)}, f32[5,32,128]{2,1,0:T(8,128)S(1)}, u32[]{:S(2)}, u32[]{:S(2)}) collective-permute-start(f32[5,32,128]{2,1,0:T(8,128)S(1)} %get-tuple-element.51), channel_id=1, source_target_pairs={{0,1},{1,2},{2,3},{3,0},{4,5},{5,6},{6,7},{7,4},{8,9},{9,10},{10,1... | collective-permute-start | bytes 245768 | tf_op jit(solution)/shard_map/ppermute | solution.py:550
  11.2 18.6 %collective-permute-start.3 = (f32[17,32,128]{2,1,0:T(8,128)S(1)}, f32[17,32,128]{2,1,0:T(8,128)S(1)}, u32[]{:S(2)}, u32[]{:S(2)}) collective-permute-start(f32[17,32,128]{2,1,0:T(8,128)S(1)} %get-tuple-element.58.refs_1_), channel_id=1, source_target_pairs={{32,0},{64,32},{96,64},{0,96},{33,1},{65,33},{97,65},{1,97},{34,2}... | collective-permute-start | bytes 835592 | tf_op jit(solution)/shard_map/ppermute | solution.py:556
  14.0 15.9 %collective-permute-start.2 = (f32[17,32,128]{2,1,0:T(8,128)S(1)}, f32[17,32,128]{2,1,0:T(8,128)S(1)}, u32[]{:S(2)}, u32[]{:S(2)}) collective-permute-start(f32[17,32,128]{2,1,0:T(8,128)S(1)} %get-tuple-element.59.refs_2_), channel_id=1, source_target_pairs={{0,32},{32,64},{64,96},{96,0},{1,33},{33,65},{65,97},{97,1},{2,34}... | collective-permute-start | bytes 835592 | tf_op jit(solution)/shard_map/ppermute | solution.py:555
  16.9 13.0 %collective-permute-start.4 = (f32[17,32,128]{2,1,0:T(8,128)S(1)}, f32[17,32,128]{2,1,0:T(8,128)S(1)}, u32[]{:S(2)}, u32[]{:S(2)}) collective-permute-start(f32[17,32,128]{2,1,0:T(8,128)S(1)} %get-tuple-element.60.refs_4_), channel_id=1, source_target_pairs={{0,4},{4,8},{8,12},{12,16},{16,20},{20,24},{24,28},{28,0},{1,5},{5... | collective-permute-start | bytes 835592 | tf_op jit(solution)/shard_map/ppermute | solution.py:557
  16.9 13.0 %collective-permute-start.5 = (f32[17,32,128]{2,1,0:T(8,128)S(1)}, f32[17,32,128]{2,1,0:T(8,128)S(1)}, u32[]{:S(2)}, u32[]{:S(2)}) collective-permute-start(f32[17,32,128]{2,1,0:T(8,128)S(1)} %get-tuple-element.61.refs_3_), channel_id=1, source_target_pairs={{4,0},{8,4},{12,8},{16,12},{20,16},{24,20},{28,24},{0,28},{5,1},{9... | collective-permute-start | bytes 835592 | tf_op jit(solution)/shard_map/ppermute | solution.py:558
  30.3 5.3 %collective-permute-start.7 = (f32[4,32,128]{2,1,0:T(8,128)S(1)}, f32[4,32,128]{2,1,0:T(8,128)S(1)}, u32[]{:S(2)}, u32[]{:S(2)}) collective-permute-start(f32[4,32,128]{2,1,0:T(8,128)S(1)} %get-tuple-element.66), channel_id=1, source_target_pairs={{1,0},{2,1},{3,2},{0,3},{5,4},{6,5},{7,6},{4,7},{9,8},{10,9},{11,1... | collective-permute-start | bytes 196616 | tf_op jit(solution)/shard_map/ppermute | solution.py:551
  30.8 5.5 %collective-permute-start.6 = (f32[4,32,128]{2,1,0:T(8,128)S(1)}, f32[4,32,128]{2,1,0:T(8,128)S(1)}, u32[]{:S(2)}, u32[]{:S(2)}) collective-permute-start(f32[4,32,128]{2,1,0:T(8,128)S(1)} %get-tuple-element.66), channel_id=1, source_target_pairs={{0,1},{1,2},{2,3},{3,0},{4,5},{5,6},{6,7},{7,4},{8,9},{9,10},{10,1... | collective-permute-start | bytes 196616 | tf_op jit(solution)/shard_map/ppermute | solution.py:550
  32.4 13.6 %collective-permute-start.8 = (f32[16,32,128]{2,1,0:T(8,128)S(1)}, f32[16,32,128]{2,1,0:T(8,128)S(1)}, u32[]{:S(2)}, u32[]{:S(2)}) collective-permute-start(f32[16,32,128]{2,1,0:T(8,128)S(1)} %get-tuple-element.77), channel_id=1, source_target_pairs={{0,32},{32,64},{64,96},{96,0},{1,33},{33,65},{65,97},{97,1},{2,34}... | collective-permute-start | bytes 786440 | tf_op jit(solution)/shard_map/ppermute | solution.py:555
  33.9 12.2 %collective-permute-start.9 = (f32[16,32,128]{2,1,0:T(8,128)S(1)}, f32[16,32,128]{2,1,0:T(8,128)S(1)}, u32[]{:S(2)}, u32[]{:S(2)}) collective-permute-start(f32[16,32,128]{2,1,0:T(8,128)S(1)} %get-tuple-element.78), channel_id=1, source_target_pairs={{32,0},{64,32},{96,64},{0,96},{33,1},{65,33},{97,65},{1,97},{34,2}... | collective-permute-start | bytes 786440 | tf_op jit(solution)/shard_map/ppermute | solution.py:556
  36.3 9.8 %collective-permute-start.10 = (f32[16,32,128]{2,1,0:T(8,128)S(1)}, f32[16,32,128]{2,1,0:T(8,128)S(1)}, u32[]{:S(2)}, u32[]{:S(2)}) collective-permute-start(f32[16,32,128]{2,1,0:T(8,128)S(1)} %get-tuple-element.79), channel_id=1, source_target_pairs={{0,4},{4,8},{8,12},{12,16},{16,20},{20,24},{24,28},{28,0},{1,5},{5... | collective-permute-start | bytes 786440 | tf_op jit(solution)/shard_map/ppermute | solution.py:557
  36.3 9.8 %collective-permute-start.11 = (f32[16,32,128]{2,1,0:T(8,128)S(1)}, f32[16,32,128]{2,1,0:T(8,128)S(1)}, u32[]{:S(2)}, u32[]{:S(2)}) collective-permute-start(f32[16,32,128]{2,1,0:T(8,128)S(1)} %get-tuple-element.80), channel_id=1, source_target_pairs={{4,0},{8,4},{12,8},{16,12},{20,16},{24,20},{28,24},{0,28},{5,1},{9... | collective-permute-start | bytes 786440 | tf_op jit(solution)/shard_map/ppermute | solution.py:558
  46.8 5.3 %collective-permute-start.13 = (f32[4,32,128]{2,1,0:T(8,128)S(1)}, f32[4,32,128]{2,1,0:T(8,128)S(1)}, u32[]{:S(2)}, u32[]{:S(2)}) collective-permute-start(f32[4,32,128]{2,1,0:T(8,128)S(1)} %get-tuple-element.84), channel_id=1, source_target_pairs={{1,0},{2,1},{3,2},{0,3},{5,4},{6,5},{7,6},{4,7},{9,8},{10,9},{11,1... | collective-permute-start | bytes 196616 | tf_op jit(solution)/shard_map/ppermute | solution.py:551
  47.9 5.5 %collective-permute-start.12 = (f32[4,32,128]{2,1,0:T(8,128)S(1)}, f32[4,32,128]{2,1,0:T(8,128)S(1)}, u32[]{:S(2)}, u32[]{:S(2)}) collective-permute-start(f32[4,32,128]{2,1,0:T(8,128)S(1)} %get-tuple-element.84), channel_id=1, source_target_pairs={{0,1},{1,2},{2,3},{3,0},{4,5},{5,6},{6,7},{7,4},{8,9},{9,10},{10,1... | collective-permute-start | bytes 196616 | tf_op jit(solution)/shard_map/ppermute | solution.py:550
  48.9 13.3 %collective-permute-start.14 = (f32[16,32,128]{2,1,0:T(8,128)S(1)}, f32[16,32,128]{2,1,0:T(8,128)S(1)}, u32[]{:S(2)}, u32[]{:S(2)}) collective-permute-start(f32[16,32,128]{2,1,0:T(8,128)S(1)} %get-tuple-element.90), channel_id=1, source_target_pairs={{0,32},{32,64},{64,96},{96,0},{1,33},{33,65},{65,97},{97,1},{2,34}... | collective-permute-start | bytes 786440 | tf_op jit(solution)/shard_map/ppermute | solution.py:555
  50.0 12.1 %collective-permute-start.15 = (f32[16,32,128]{2,1,0:T(8,128)S(1)}, f32[16,32,128]{2,1,0:T(8,128)S(1)}, u32[]{:S(2)}, u32[]{:S(2)}) collective-permute-start(f32[16,32,128]{2,1,0:T(8,128)S(1)} %get-tuple-element.91), channel_id=1, source_target_pairs={{32,0},{64,32},{96,64},{0,96},{33,1},{65,33},{97,65},{1,97},{34,2}... | collective-permute-start | bytes 786440 | tf_op jit(solution)/shard_map/ppermute | solution.py:556
  53.3 8.9 %collective-permute-start.16 = (f32[16,32,128]{2,1,0:T(8,128)S(1)}, f32[16,32,128]{2,1,0:T(8,128)S(1)}, u32[]{:S(2)}, u32[]{:S(2)}) collective-permute-start(f32[16,32,128]{2,1,0:T(8,128)S(1)} %get-tuple-element.92), channel_id=1, source_target_pairs={{0,4},{4,8},{8,12},{12,16},{16,20},{20,24},{24,28},{28,0},{1,5},{5... | collective-permute-start | bytes 786440 | tf_op jit(solution)/shard_map/ppermute | solution.py:557
  53.4 8.9 %collective-permute-start.17 = (f32[16,32,128]{2,1,0:T(8,128)S(1)}, f32[16,32,128]{2,1,0:T(8,128)S(1)}, u32[]{:S(2)}, u32[]{:S(2)}) collective-permute-start(f32[16,32,128]{2,1,0:T(8,128)S(1)} %get-tuple-element.93), channel_id=1, source_target_pairs={{4,0},{8,4},{12,8},{16,12},{20,16},{24,20},{28,24},{0,28},{5,1},{9... | collective-permute-start | bytes 786440 | tf_op jit(solution)/shard_map/ppermute | solution.py:558
  62.9 1.2 %collective-permute-start.18 = (f32[32,128]{1,0:T(8,128)S(1)}, f32[32,128]{1,0:T(8,128)S(1)}, u32[]{:S(2)}, u32[]{:S(2)}) collective-permute-start(f32[32,128]{1,0:T(8,128)S(1)} %get-tuple-element.96), channel_id=1, source_target_pairs={{0,4},{4,0},{8,12},{12,8},{16,20},{20,16},{24,28},{28,24},{1,5},{5... | collective-permute-start | bytes 49160 | tf_op jit(solution)/shard_map/ppermute | solution.py:743
  64.1 5.4 %collective-permute-start.21 = (f32[32,128]{1,0:T(8,128)S(1)}, f32[32,128]{1,0:T(8,128)S(1)}, u32[]{:S(2)}, u32[]{:S(2)}) collective-permute-start(f32[32,128]{1,0:T(8,128)S(1)} %add.42), channel_id=1, source_target_pairs={{0,2},{1,3},{2,0},{3,1},{4,6},{5,7},{6,4},{7,5},{8,10},{9,11},{10,... | collective-permute-start | bytes 49160 | tf_op jit(solution)/shard_map/ppermute | solution.py:748
  64.4 5.1 %collective-permute-start.20 = (f32[32,128]{1,0:T(8,128)S(1)}, f32[32,128]{1,0:T(8,128)S(1)}, u32[]{:S(2)}, u32[]{:S(2)}) collective-permute-start(f32[32,128]{1,0:T(8,128)S(1)} %add.42), channel_id=1, source_target_pairs={{0,3},{1,2},{2,1},{3,0},{4,7},{5,6},{6,5},{7,4},{8,11},{9,10},{10,... | collective-permute-start | bytes 49160 | tf_op jit(solution)/shard_map/ppermute | solution.py:748
  66.6 3.7 %collective-permute-start.19 = (f32[32,128]{1,0:T(8,128)S(1)}, f32[32,128]{1,0:T(8,128)S(1)}, u32[]{:S(2)}, u32[]{:S(2)}) collective-permute-start(f32[32,128]{1,0:T(8,128)S(1)} %add.42), channel_id=1, source_target_pairs={{0,1},{1,0},{2,3},{3,2},{4,5},{5,4},{6,7},{7,6},{8,9},{9,8},{10,11... | collective-permute-start | bytes 49160 | tf_op jit(solution)/shard_map/ppermute | solution.py:748
  70.4 5.3 %collective-permute-start.24 = (f32[32,128]{1,0:T(8,128)S(1)}, f32[32,128]{1,0:T(8,128)S(1)}, u32[]{:S(2)}, u32[]{:S(2)}) collective-permute-start(f32[32,128]{1,0:T(8,128)S(1)} %add_add_fusion.1), channel_id=1, source_target_pairs={{0,16},{4,20},{8,24},{12,28},{16,0},{20,4},{24,8},{28,12},{1,17},{... | collective-permute-start | bytes 49160 | tf_op jit(solution)/shard_map/ppermute | solution.py:748
  70.4 5.4 %collective-permute-start.23 = (f32[32,128]{1,0:T(8,128)S(1)}, f32[32,128]{1,0:T(8,128)S(1)}, u32[]{:S(2)}, u32[]{:S(2)}) collective-permute-start(f32[32,128]{1,0:T(8,128)S(1)} %add_add_fusion.1), channel_id=1, source_target_pairs={{0,24},{4,28},{8,16},{12,20},{16,8},{20,12},{24,0},{28,4},{1,25},{... | collective-permute-start | bytes 49160 | tf_op jit(solution)/shard_map/ppermute | solution.py:748
  71.8 4.0 %collective-permute-start.22 = (f32[32,128]{1,0:T(8,128)S(1)}, f32[32,128]{1,0:T(8,128)S(1)}, u32[]{:S(2)}, u32[]{:S(2)}) collective-permute-start(f32[32,128]{1,0:T(8,128)S(1)} %add_add_fusion.1), channel_id=1, source_target_pairs={{0,8},{4,12},{8,0},{12,4},{16,24},{20,28},{24,16},{28,20},{1,9},{5... | collective-permute-start | bytes 49160 | tf_op jit(solution)/shard_map/ppermute | solution.py:748
  75.8 5.3 %collective-permute-start.27 = (f32[32,128]{1,0:T(8,128)S(1)}, f32[32,128]{1,0:T(8,128)S(1)}, u32[]{:S(2)}, u32[]{:S(2)}) collective-permute-start(f32[32,128]{1,0:T(8,128)S(1)} %add_add_fusion.refs_0_), channel_id=1, source_target_pairs={{0,64},{32,96},{64,0},{96,32},{1,65},{33,97},{65,1},{97,33},{2,66}... | collective-permute-start | bytes 49160 | tf_op jit(solution)/shard_map/ppermute | solution.py:748
  78.6 4.9 %collective-permute-start.26 = (f32[32,128]{1,0:T(8,128)S(1)}, f32[32,128]{1,0:T(8,128)S(1)}, u32[]{:S(2)}, u32[]{:S(2)}) collective-permute-start(f32[32,128]{1,0:T(8,128)S(1)} %add_add_fusion.refs_0_), channel_id=1, source_target_pairs={{0,96},{32,64},{64,32},{96,0},{1,97},{33,65},{65,33},{97,1},{2,98}... | collective-permute-start | bytes 49160 | tf_op jit(solution)/shard_map/ppermute | solution.py:748
  79.7 3.8 %collective-permute-start.25 = (f32[32,128]{1,0:T(8,128)S(1)}, f32[32,128]{1,0:T(8,128)S(1)}, u32[]{:S(2)}, u32[]{:S(2)}) collective-permute-start(f32[32,128]{1,0:T(8,128)S(1)} %add_add_fusion.refs_0_), channel_id=1, source_target_pairs={{0,32},{32,0},{64,96},{96,64},{1,33},{33,1},{65,97},{97,65},{2,34}... | collective-permute-start | bytes 49160 | tf_op jit(solution)/shard_map/ppermute | solution.py:748

commit v5 on v4

--- a/solution.py
+++ b/solution.py
@@ -550,7 +550,7 @@
         lax.ppermute(ends, "layer", ahead("layer")),
         lax.ppermute(ends, "layer", back("layer")),
     )
-    near, ylo, yhi = lax.optimization_barrier((near, ylo, yhi))
+    near, ylo = lax.optimization_barrier((near, ylo))
     far = (
         lax.ppermute(xhi, "strike", ahead("strike")),
         lax.ppermute(xlo, "strike", back("strike")),

time: 94.1 us -> 90.8 us (0.965)
  starting transfers between devices: 37.6 us -> 32.8 us
  waiting for transfers between devices: 14.1 us -> 15.2 us
    ppermute x3, starting transfers between devices: 8.86 us -> 2.48 us  [exchanged(): lax.ppermute(ylo, 'dip', back('dip'))]
    ppermute x3, starting transfers between devices: 5.74 us -> 9.89 us  [exchanged(): lax.ppermute(ends, 'layer', back('layer'))]
    ppermute x3, starting transfers between devices: 2.63 us -> 0.01 us  [exchanged(): lax.ppermute(ends, 'layer', ahead('layer'))]
    ppermute x3, waiting for transfers between devices: 4.68 us -> 7.28 us  [exchanged(): lax.ppermute(ends, 'layer', ahead('layer'))]
    ppermute x3, starting transfers between devices: 6.59 us -> 8.07 us  [exchanged(): lax.ppermute(xlo, 'strike', back('strike'))]
    ppermute x3, starting transfers between devices: 2.65 us -> 1.17 us  [exchanged(): lax.ppermute(xhi, 'strike', ahead('strike'))]
    ppermute x9, waiting for transfers between devices: 8.2 us -> 6.75 us  [summed_but_last(): lax.ppermute(values, axis, swaps(axis, mask, stride))]
  transfers between devices with their start and end apart: 28 -> 28, of which waited for: 9 -> 9; matrix products, arithmetic and copies ran while one was open for 0% -> 0% of each run, Pallas kernels for 24% -> 25%
where the time goes in v5:
time: 90.8 us; the launch traced here: 90.3 us
  Pallas kernels  40.9 us (45%)
  starting transfers between devices  32.8 us (36%)
  waiting for transfers between devices  15.2 us (17%)
  between operations  1.02 us (1%)
    pallas_call x3, Pallas kernels, inner_part(): pl.pallas_call(first_kernel if first else functools.partial(inner_kernel,...  22.4 us
    ppermute x9, starting transfers between devices, summed_but_last(): lax.ppermute(values, axis, swaps(axis, mask, stride))  11.1 us
    ppermute x3, starting transfers between devices, exchanged(): lax.ppermute(ends, 'layer', back('layer'))  9.89 us
    ppermute x3, starting transfers between devices, exchanged(): lax.ppermute(xlo, 'strike', back('strike'))  8.07 us
    ppermute x3, waiting for transfers between devices, exchanged(): lax.ppermute(ends, 'layer', ahead('layer'))  7.28 us
    ppermute x9, waiting for transfers between devices, summed_but_last(): lax.ppermute(values, axis, swaps(axis, mask, stride))  6.75 us
    pallas_call x1, Pallas kernels, pack(): pl.pallas_call(pack_kernel, in_specs=[HBM] * 3, out_specs=[HBM] + [VMEM]...  6.41 us
    pallas_call x1, Pallas kernels, combine(): pl.pallas_call(combine_kernel, in_specs=[VMEM, HBM] + [VMEM] * 3, out_spe...  6.24 us
  transfers between devices with their start and end apart: 28, of which 9 were waited for; matrix products, arithmetic and copies ran while one was open for 0% of the time, Pallas kernels for 25%

profile of v5, /device:TPU:0, one launch (start us, length us, event | category | flops | bytes accessed | tf_op | source)
XLA Modules:
  0.0 90.3 jit_solution(6782145135193405695)
XLA Ops:
  0.6 6.4 %pack_guess.1 = (f32[16,16,32,128]{3,2,1,0:T(8,128)}, f32[16,16,128]{2,1,0:T(8,128)S(1)}, f32[17,32,128]{2,1,0:T(8,128)S(1)}, f32[17,32,128]{2,1,0:T(8,128)S(1)}...) custom-call(s32[16,16,128]{2,1,0:T(8,128)} %class_hbm.1, f32[16]{0:T(128)} %table_hbm.1, ...), custom_call_target="tpu_custom_call" | custom-call | tf_op jit(solution)/shard_map/pack_guess/pallas_call | solution.py:128
  7.1 4.2 %collective-permute-start.1 = (f32[5,32,128]{2,1,0:T(8,128)S(1)}, f32[5,32,128]{2,1,0:T(8,128)S(1)}, u32[]{:S(2)}, u32[]{:S(2)}) collective-permute-start(f32[5,32,128]{2,1,0:T(8,128)S(1)} %get-tuple-element.48), channel_id=1, source_target_pairs={{1,0},{2,1},{3,2},{0,3},{5,4},{6,5},{7,6},{4,7},{9,8},{10,9},{11,1... | collective-permute-start | bytes 245768 | tf_op jit(solution)/shard_map/ppermute | solution.py:551
  11.2 2.8 %collective-permute-start.3 = (f32[17,32,128]{2,1,0:T(8,128)S(1)}, f32[17,32,128]{2,1,0:T(8,128)S(1)}, u32[]{:S(2)}, u32[]{:S(2)}) collective-permute-start(f32[17,32,128]{2,1,0:T(8,128)S(1)} %get-tuple-element.54.refs_1_), channel_id=1, source_target_pairs={{32,0},{64,32},{96,64},{0,96},{33,1},{65,33},{97,65},{1,97},{34,2}... | collective-permute-start | bytes 835592 | tf_op jit(solution)/shard_map/ppermute | solution.py:556
  14.1 2.8 %collective-permute-done.hzl = f32[5,32,128]{2,1,0:T(8,128)S(1)} collective-permute-done((f32[5,32,128]{2,1,0:T(8,128)S(1)}, f32[5,32,128]{2,1,0:T(8,128)S(1)}, u32[]{:S(2)}, u32[]{:S(2)}) %collective-permute-start) | collective-permute-done | bytes 81952 | tf_op jit(solution)/shard_map/ppermute | solution.py:550
  16.9 1.0 %collective-permute-start.5 = (f32[17,32,128]{2,1,0:T(8,128)S(1)}, f32[17,32,128]{2,1,0:T(8,128)S(1)}, u32[]{:S(2)}, u32[]{:S(2)}) collective-permute-start(f32[17,32,128]{2,1,0:T(8,128)S(1)} %get-tuple-element.57.refs_3_), channel_id=1, source_target_pairs={{4,0},{8,4},{12,8},{16,12},{20,16},{24,20},{28,24},{0,28},{5,1},{9... | collective-permute-start | bytes 835592 | tf_op jit(solution)/shard_map/ppermute | solution.py:558
  18.2 9.7 %inner_first.1 = (f32[16,16,32,128]{3,2,1,0:T(8,128)S(1)}, f32[4,32,128]{2,1,0:T(8,128)S(1)}, f32[17,16,128]{2,1,0:T(8,128)S(1)}, f32[16,24,128]{2,1,0:T(8,128)S...) custom-call(f32[16,16,32,128]{3,2,1,0:T(8,128)} %get-tuple-element.47.away.guess_hbm, ...), custom_call_target="tpu_custom_call" | custom-call | flops 20971520 | bytes 25165824 | tf_op jit(solution)/shard_map/inner_first/pallas_call | solution.py:500
  28.4 2.4 %collective-permute-start.7 = (f32[4,32,128]{2,1,0:T(8,128)S(1)}, f32[4,32,128]{2,1,0:T(8,128)S(1)}, u32[]{:S(2)}, u32[]{:S(2)}) collective-permute-start(f32[4,32,128]{2,1,0:T(8,128)S(1)} %get-tuple-element.62), channel_id=1, source_target_pairs={{1,0},{2,1},{3,2},{0,3},{5,4},{6,5},{7,6},{4,7},{9,8},{10,9},{11,1... | collective-permute-start | bytes 196616 | tf_op jit(solution)/shard_map/ppermute | solution.py:551
  30.8 1.2 %collective-permute-start.8 = (f32[16,32,128]{2,1,0:T(8,128)S(1)}, f32[16,32,128]{2,1,0:T(8,128)S(1)}, u32[]{:S(2)}, u32[]{:S(2)}) collective-permute-start(f32[16,32,128]{2,1,0:T(8,128)S(1)} %get-tuple-element.72), channel_id=1, source_target_pairs={{0,32},{32,64},{64,96},{96,0},{1,33},{33,65},{65,97},{97,1},{2,34}... | collective-permute-start | bytes 786440 | tf_op jit(solution)/shard_map/ppermute | solution.py:555
  32.0 2.1 %collective-permute-start.9 = (f32[16,32,128]{2,1,0:T(8,128)S(1)}, f32[16,32,128]{2,1,0:T(8,128)S(1)}, u32[]{:S(2)}, u32[]{:S(2)}) collective-permute-start(f32[16,32,128]{2,1,0:T(8,128)S(1)} %get-tuple-element.73), channel_id=1, source_target_pairs={{32,0},{64,32},{96,64},{0,96},{33,1},{65,33},{97,65},{1,97},{34,2}... | collective-permute-start | bytes 786440 | tf_op jit(solution)/shard_map/ppermute | solution.py:556
  34.1 2.2 %collective-permute-done.6.refs_1_ = f32[4,32,128]{2,1,0:T(8,128)S(1)} collective-permute-done((f32[4,32,128]{2,1,0:T(8,128)S(1)}, f32[4,32,128]{2,1,0:T(8,128)S(1)}, u32[]{:S(2)}, u32[]{:S(2)}) %collective-permute-start.6) | collective-permute-done | bytes 65568 | tf_op jit(solution)/shard_map/ppermute | solution.py:550
  36.3 0.7 collective-permute-start.11
  37.0 6.8 %inner_next.1 = (f32[16,16,32,128]{3,2,1,0:T(8,128)S(1)}, f32[4,32,128]{2,1,0:T(8,128)S(1)}, f32[64,128]{1,0:T(8,128)S(1)}) custom-call(f32[16,16,32,128]{3,2,1,0:T(8,128)S(1)} %get-tuple-element.61.refs_0_.refs_1_.one_ref, f32[4,32,128]{2,1,0:T(8,128)S(1)} %collective-permute-done.6.refs_1_, f32[4,32,128]{2,1,0:T(8,128)S(1)} %collective-permute-done.7.refs_2_, ...), custom_call_target="tpu_custom_call" | custom-call | flops 20971520 | bytes 25165824 | tf_op jit(solution)/shard_map/inner_next/pallas_call | solution.py:500
  44.6 3.3 %collective-permute-start.13 = (f32[4,32,128]{2,1,0:T(8,128)S(1)}, f32[4,32,128]{2,1,0:T(8,128)S(1)}, u32[]{:S(2)}, u32[]{:S(2)}) collective-permute-start(f32[4,32,128]{2,1,0:T(8,128)S(1)} %get-tuple-element.79), channel_id=1, source_target_pairs={{1,0},{2,1},{3,2},{0,3},{5,4},{6,5},{7,6},{4,7},{9,8},{10,9},{11,1... | collective-permute-start | bytes 196616 | tf_op jit(solution)/shard_map/ppermute | solution.py:551
  47.9 3.2 %collective-permute-start.15 = (f32[16,32,128]{2,1,0:T(8,128)S(1)}, f32[16,32,128]{2,1,0:T(8,128)S(1)}, u32[]{:S(2)}, u32[]{:S(2)}) collective-permute-start(f32[16,32,128]{2,1,0:T(8,128)S(1)} %get-tuple-element.85), channel_id=1, source_target_pairs={{32,0},{64,32},{96,64},{0,96},{33,1},{65,33},{97,65},{1,97},{34,2}... | collective-permute-start | bytes 786440 | tf_op jit(solution)/shard_map/ppermute | solution.py:556
  51.1 2.2 %collective-permute-done.12.refs_1_ = f32[4,32,128]{2,1,0:T(8,128)S(1)} collective-permute-done((f32[4,32,128]{2,1,0:T(8,128)S(1)}, f32[4,32,128]{2,1,0:T(8,128)S(1)}, u32[]{:S(2)}, u32[]{:S(2)}) %collective-permute-start.12) | collective-permute-done | bytes 65568 | tf_op jit(solution)/shard_map/ppermute | solution.py:550
  53.3 0.7 collective-permute-start.17
  54.1 5.9 %inner_last.1 = (f32[16,16,32,128]{3,2,1,0:T(8,128)S(1)}, f32[64,128]{1,0:T(8,128)S(1)}) custom-call(f32[16,16,32,128]{3,2,1,0:T(8,128)S(1)} %get-tuple-element.78.refs_0_.refs_1_.two_ref, f32[4,32,128]{2,1,0:T(8,128)S(1)} %collective-permute-done.12.refs_1_, f32[4,32,128]{2,1,0:T(8,128)S(1)} %collective-permute-done.13.refs_2_, ...), custom_call_target="tpu_custom_call" | custom-call | flops 20971520 | bytes 25165824 | tf_op jit(solution)/shard_map/inner_last/pallas_call | solution.py:500
  60.0 0.7 sides_last.1
  60.7 1.2 %collective-permute-done.18 = f32[32,128]{1,0:T(8,128)S(1)} collective-permute-done((f32[32,128]{1,0:T(8,128)S(1)}, f32[32,128]{1,0:T(8,128)S(1)}, u32[]{:S(2)}, u32[]{:S(2)}) %collective-permute-start.18) | collective-permute-done | bytes 16416 | tf_op jit(solution)/shard_map/ppermute | solution.py:743
  61.9 1.5 %collective-permute-start.21 = (f32[32,128]{1,0:T(8,128)S(1)}, f32[32,128]{1,0:T(8,128)S(1)}, u32[]{:S(2)}, u32[]{:S(2)}) collective-permute-start(f32[32,128]{1,0:T(8,128)S(1)} %add.42), channel_id=1, source_target_pairs={{0,2},{1,3},{2,0},{3,1},{4,6},{5,7},{6,4},{7,5},{8,10},{9,11},{10,... | collective-permute-start | bytes 49160 | tf_op jit(solution)/shard_map/ppermute | solution.py:748
  63.5 1.8 %collective-permute-start.20 = (f32[32,128]{1,0:T(8,128)S(1)}, f32[32,128]{1,0:T(8,128)S(1)}, u32[]{:S(2)}, u32[]{:S(2)}) collective-permute-start(f32[32,128]{1,0:T(8,128)S(1)} %add.42), channel_id=1, source_target_pairs={{0,3},{1,2},{2,1},{3,0},{4,7},{5,6},{6,5},{7,4},{8,11},{9,10},{10,... | collective-permute-start | bytes 49160 | tf_op jit(solution)/shard_map/ppermute | solution.py:748
  65.2 0.8 collective-permute-start.19
  66.0 1.1 %collective-permute-done.21 = f32[32,128]{1,0:T(8,128)S(1)} collective-permute-done((f32[32,128]{1,0:T(8,128)S(1)}, f32[32,128]{1,0:T(8,128)S(1)}, u32[]{:S(2)}, u32[]{:S(2)}) %collective-permute-start.21) | collective-permute-done | bytes 16416 | tf_op jit(solution)/shard_map/ppermute | solution.py:748
  67.2 1.2 %collective-permute-done.20 = f32[32,128]{1,0:T(8,128)S(1)} collective-permute-done((f32[32,128]{1,0:T(8,128)S(1)}, f32[32,128]{1,0:T(8,128)S(1)}, u32[]{:S(2)}, u32[]{:S(2)}) %collective-permute-start.20) | collective-permute-done | bytes 16416 | tf_op jit(solution)/shard_map/ppermute | solution.py:748
  69.0 1.4 %collective-permute-start.23 = (f32[32,128]{1,0:T(8,128)S(1)}, f32[32,128]{1,0:T(8,128)S(1)}, u32[]{:S(2)}, u32[]{:S(2)}) collective-permute-start(f32[32,128]{1,0:T(8,128)S(1)} %add_add_fusion.1), channel_id=1, source_target_pairs={{0,24},{4,28},{8,16},{12,20},{16,8},{20,12},{24,0},{28,4},{1,25},{... | collective-permute-start | bytes 49160 | tf_op jit(solution)/shard_map/ppermute | solution.py:748
  70.4 2.1 %collective-permute-start.22 = (f32[32,128]{1,0:T(8,128)S(1)}, f32[32,128]{1,0:T(8,128)S(1)}, u32[]{:S(2)}, u32[]{:S(2)}) collective-permute-start(f32[32,128]{1,0:T(8,128)S(1)} %add_add_fusion.1), channel_id=1, source_target_pairs={{0,8},{4,12},{8,0},{12,4},{16,24},{20,28},{24,16},{28,20},{1,9},{5... | collective-permute-start | bytes 49160 | tf_op jit(solution)/shard_map/ppermute | solution.py:748
  72.5 1.9 %collective-permute-done.24 = f32[32,128]{1,0:T(8,128)S(1)} collective-permute-done((f32[32,128]{1,0:T(8,128)S(1)}, f32[32,128]{1,0:T(8,128)S(1)}, u32[]{:S(2)}, u32[]{:S(2)}) %collective-permute-start.24) | collective-permute-done | bytes 16416 | tf_op jit(solution)/shard_map/ppermute | solution.py:748
  74.7 1.2 %collective-permute-start.26 = (f32[32,128]{1,0:T(8,128)S(1)}, f32[32,128]{1,0:T(8,128)S(1)}, u32[]{:S(2)}, u32[]{:S(2)}) collective-permute-start(f32[32,128]{1,0:T(8,128)S(1)} %add_add_fusion.refs_0_), channel_id=1, source_target_pairs={{0,96},{32,64},{64,32},{96,0},{1,97},{33,65},{65,33},{97,1},{2,98}... | collective-permute-start | bytes 49160 | tf_op jit(solution)/shard_map/ppermute | solution.py:748
  75.9 2.0 %collective-permute-start.25 = (f32[32,128]{1,0:T(8,128)S(1)}, f32[32,128]{1,0:T(8,128)S(1)}, u32[]{:S(2)}, u32[]{:S(2)}) collective-permute-start(f32[32,128]{1,0:T(8,128)S(1)} %add_add_fusion.refs_0_), channel_id=1, source_target_pairs={{0,32},{32,0},{64,96},{96,64},{1,33},{33,1},{65,97},{97,65},{2,34}... | collective-permute-start | bytes 49160 | tf_op jit(solution)/shard_map/ppermute | solution.py:748
  78.0 1.9 %collective-permute-done.27.refs_3_ = f32[32,128]{1,0:T(8,128)S(1)} collective-permute-done((f32[32,128]{1,0:T(8,128)S(1)}, f32[32,128]{1,0:T(8,128)S(1)}, u32[]{:S(2)}, u32[]{:S(2)}) %collective-permute-start.27) | collective-permute-done | bytes 16416 | tf_op jit(solution)/shard_map/ppermute | solution.py:748
  79.9 4.0 %solve_small.1.mix_ref = f32[64,128]{1,0:T(8,128)S(1)} custom-call(f32[32,128]{1,0:T(8,128)S(1)} %add_add_fusion.refs_0_, f32[32,128]{1,0:T(8,128)S(1)} %collective-permute-done.25.refs_1_, f32[32,128]{1,0:T(8,128)S(1)} %collective-permute-done.26.refs_2_, f32[32,128]{1,0:T(8,128)S(1)} %collective-permute-done.27.refs_3_), custom_call_target="tpu_custom_call" | custom-call | tf_op jit(solution)/shard_map/solve_small/pallas_call | solution.py:619
  83.9 6.2 %combine_fields.1 = (f32[32,16,16,128]{3,2,1,0:T(8,128)}, f32[32,16,16,128]{3,2,1,0:T(8,128)}) custom-call(f32[64,128]{1,0:T(8,128)S(1)} %solve_small.1.mix_ref, f32[16,16,32,128]{3,2,1,0:T(8,128)} %get-tuple-element.47.away.guess_hbm, f32[16,16,32,128]{3,2,1,0:T(8,128)S(1)} %get-tuple-element.61.refs_0_.refs_1_.one_ref, ...), custom_call_target="tpu_custom_call" | custom-call | tf_op jit(solution)/shard_map/combine_fields/pallas_call | solution.py:717
  (46 shorter events, 2.5 us)
Async XLA Ops:
  0.6 13.4 %copy-start = (s32[32]{0:T(128)S(1)}, s32[32]{0:T(128)}, u32[]{:S(2)}) copy-start(s32[32]{0:T(128)} %param.6) | copy-start | bytes 388
  7.1 7.0 %collective-permute-start.1 = (f32[5,32,128]{2,1,0:T(8,128)S(1)}, f32[5,32,128]{2,1,0:T(8,128)S(1)}, u32[]{:S(2)}, u32[]{:S(2)}) collective-permute-start(f32[5,32,128]{2,1,0:T(8,128)S(1)} %get-tuple-element.48), channel_id=1, source_target_pairs={{1,0},{2,1},{3,2},{0,3},{5,4},{6,5},{7,6},{4,7},{9,8},{10,9},{11,1... | collective-permute-start | bytes 245768 | tf_op jit(solution)/shard_map/ppermute | solution.py:551
  11.2 5.7 %collective-permute-start = (f32[5,32,128]{2,1,0:T(8,128)S(1)}, f32[5,32,128]{2,1,0:T(8,128)S(1)}, u32[]{:S(2)}, u32[]{:S(2)}) collective-permute-start(f32[5,32,128]{2,1,0:T(8,128)S(1)} %get-tuple-element.48), channel_id=1, source_target_pairs={{0,1},{1,2},{2,3},{3,0},{4,5},{5,6},{6,7},{7,4},{8,9},{9,10},{10,1... | collective-permute-start | bytes 245768 | tf_op jit(solution)/shard_map/ppermute | solution.py:550
  11.2 16.7 %collective-permute-start.3 = (f32[17,32,128]{2,1,0:T(8,128)S(1)}, f32[17,32,128]{2,1,0:T(8,128)S(1)}, u32[]{:S(2)}, u32[]{:S(2)}) collective-permute-start(f32[17,32,128]{2,1,0:T(8,128)S(1)} %get-tuple-element.54.refs_1_), channel_id=1, source_target_pairs={{32,0},{64,32},{96,64},{0,96},{33,1},{65,33},{97,65},{1,97},{34,2}... | collective-permute-start | bytes 835592 | tf_op jit(solution)/shard_map/ppermute | solution.py:556
  14.0 14.0 %collective-permute-start.2 = (f32[17,32,128]{2,1,0:T(8,128)S(1)}, f32[17,32,128]{2,1,0:T(8,128)S(1)}, u32[]{:S(2)}, u32[]{:S(2)}) collective-permute-start(f32[17,32,128]{2,1,0:T(8,128)S(1)} %get-tuple-element.55.refs_2_), channel_id=1, source_target_pairs={{0,32},{32,64},{64,96},{96,0},{1,33},{33,65},{65,97},{97,1},{2,34}... | collective-permute-start | bytes 835592 | tf_op jit(solution)/shard_map/ppermute | solution.py:555
  14.0 14.0 %collective-permute-start.4 = (f32[17,32,128]{2,1,0:T(8,128)S(1)}, f32[17,32,128]{2,1,0:T(8,128)S(1)}, u32[]{:S(2)}, u32[]{:S(2)}) collective-permute-start(f32[17,32,128]{2,1,0:T(8,128)S(1)} %get-tuple-element.56.refs_4_), channel_id=1, source_target_pairs={{0,4},{4,8},{8,12},{12,16},{16,20},{20,24},{24,28},{28,0},{1,5},{5... | collective-permute-start | bytes 835592 | tf_op jit(solution)/shard_map/ppermute | solution.py:557
  16.9 11.1 %collective-permute-start.5 = (f32[17,32,128]{2,1,0:T(8,128)S(1)}, f32[17,32,128]{2,1,0:T(8,128)S(1)}, u32[]{:S(2)}, u32[]{:S(2)}) collective-permute-start(f32[17,32,128]{2,1,0:T(8,128)S(1)} %get-tuple-element.57.refs_3_), channel_id=1, source_target_pairs={{4,0},{8,4},{12,8},{16,12},{20,16},{24,20},{28,24},{0,28},{5,1},{9... | collective-permute-start | bytes 835592 | tf_op jit(solution)/shard_map/ppermute | solution.py:558
  28.4 5.7 %collective-permute-start.7 = (f32[4,32,128]{2,1,0:T(8,128)S(1)}, f32[4,32,128]{2,1,0:T(8,128)S(1)}, u32[]{:S(2)}, u32[]{:S(2)}) collective-permute-start(f32[4,32,128]{2,1,0:T(8,128)S(1)} %get-tuple-element.62), channel_id=1, source_target_pairs={{1,0},{2,1},{3,2},{0,3},{5,4},{6,5},{7,6},{4,7},{9,8},{10,9},{11,1... | collective-permute-start | bytes 196616 | tf_op jit(solution)/shard_map/ppermute | solution.py:551
  30.8 5.5 %collective-permute-start.6 = (f32[4,32,128]{2,1,0:T(8,128)S(1)}, f32[4,32,128]{2,1,0:T(8,128)S(1)}, u32[]{:S(2)}, u32[]{:S(2)}) collective-permute-start(f32[4,32,128]{2,1,0:T(8,128)S(1)} %get-tuple-element.62), channel_id=1, source_target_pairs={{0,1},{1,2},{2,3},{3,0},{4,5},{5,6},{6,7},{7,4},{8,9},{9,10},{10,1... | collective-permute-start | bytes 196616 | tf_op jit(solution)/shard_map/ppermute | solution.py:550
  30.8 13.0 %collective-permute-start.8 = (f32[16,32,128]{2,1,0:T(8,128)S(1)}, f32[16,32,128]{2,1,0:T(8,128)S(1)}, u32[]{:S(2)}, u32[]{:S(2)}) collective-permute-start(f32[16,32,128]{2,1,0:T(8,128)S(1)} %get-tuple-element.72), channel_id=1, source_target_pairs={{0,32},{32,64},{64,96},{96,0},{1,33},{33,65},{65,97},{97,1},{2,34}... | collective-permute-start | bytes 786440 | tf_op jit(solution)/shard_map/ppermute | solution.py:555
  32.0 11.9 %collective-permute-start.9 = (f32[16,32,128]{2,1,0:T(8,128)S(1)}, f32[16,32,128]{2,1,0:T(8,128)S(1)}, u32[]{:S(2)}, u32[]{:S(2)}) collective-permute-start(f32[16,32,128]{2,1,0:T(8,128)S(1)} %get-tuple-element.73), channel_id=1, source_target_pairs={{32,0},{64,32},{96,64},{0,96},{33,1},{65,33},{97,65},{1,97},{34,2}... | collective-permute-start | bytes 786440 | tf_op jit(solution)/shard_map/ppermute | solution.py:556
  34.1 9.8 %collective-permute-start.10 = (f32[16,32,128]{2,1,0:T(8,128)S(1)}, f32[16,32,128]{2,1,0:T(8,128)S(1)}, u32[]{:S(2)}, u32[]{:S(2)}) collective-permute-start(f32[16,32,128]{2,1,0:T(8,128)S(1)} %get-tuple-element.74), channel_id=1, source_target_pairs={{0,4},{4,8},{8,12},{12,16},{16,20},{20,24},{24,28},{28,0},{1,5},{5... | collective-permute-start | bytes 786440 | tf_op jit(solution)/shard_map/ppermute | solution.py:557
  36.3 7.6 %collective-permute-start.11 = (f32[16,32,128]{2,1,0:T(8,128)S(1)}, f32[16,32,128]{2,1,0:T(8,128)S(1)}, u32[]{:S(2)}, u32[]{:S(2)}) collective-permute-start(f32[16,32,128]{2,1,0:T(8,128)S(1)} %get-tuple-element.75), channel_id=1, source_target_pairs={{4,0},{8,4},{12,8},{16,12},{20,16},{24,20},{28,24},{0,28},{5,1},{9... | collective-permute-start | bytes 786440 | tf_op jit(solution)/shard_map/ppermute | solution.py:558
  44.6 6.5 %collective-permute-start.13 = (f32[4,32,128]{2,1,0:T(8,128)S(1)}, f32[4,32,128]{2,1,0:T(8,128)S(1)}, u32[]{:S(2)}, u32[]{:S(2)}) collective-permute-start(f32[4,32,128]{2,1,0:T(8,128)S(1)} %get-tuple-element.79), channel_id=1, source_target_pairs={{1,0},{2,1},{3,2},{0,3},{5,4},{6,5},{7,6},{4,7},{9,8},{10,9},{11,1... | collective-permute-start | bytes 196616 | tf_op jit(solution)/shard_map/ppermute | solution.py:551
  47.9 5.5 %collective-permute-start.12 = (f32[4,32,128]{2,1,0:T(8,128)S(1)}, f32[4,32,128]{2,1,0:T(8,128)S(1)}, u32[]{:S(2)}, u32[]{:S(2)}) collective-permute-start(f32[4,32,128]{2,1,0:T(8,128)S(1)} %get-tuple-element.79), channel_id=1, source_target_pairs={{0,1},{1,2},{2,3},{3,0},{4,5},{5,6},{6,7},{7,4},{8,9},{9,10},{10,1... | collective-permute-start | bytes 196616 | tf_op jit(solution)/shard_map/ppermute | solution.py:550
  47.9 12.1 %collective-permute-start.14 = (f32[16,32,128]{2,1,0:T(8,128)S(1)}, f32[16,32,128]{2,1,0:T(8,128)S(1)}, u32[]{:S(2)}, u32[]{:S(2)}) collective-permute-start(f32[16,32,128]{2,1,0:T(8,128)S(1)} %get-tuple-element.84), channel_id=1, source_target_pairs={{0,32},{32,64},{64,96},{96,0},{1,33},{33,65},{65,97},{97,1},{2,34}... | collective-permute-start | bytes 786440 | tf_op jit(solution)/shard_map/ppermute | solution.py:555
  47.9 12.1 %collective-permute-start.15 = (f32[16,32,128]{2,1,0:T(8,128)S(1)}, f32[16,32,128]{2,1,0:T(8,128)S(1)}, u32[]{:S(2)}, u32[]{:S(2)}) collective-permute-start(f32[16,32,128]{2,1,0:T(8,128)S(1)} %get-tuple-element.85), channel_id=1, source_target_pairs={{32,0},{64,32},{96,64},{0,96},{33,1},{65,33},{97,65},{1,97},{34,2}... | collective-permute-start | bytes 786440 | tf_op jit(solution)/shard_map/ppermute | solution.py:556
  51.1 8.9 %collective-permute-start.16 = (f32[16,32,128]{2,1,0:T(8,128)S(1)}, f32[16,32,128]{2,1,0:T(8,128)S(1)}, u32[]{:S(2)}, u32[]{:S(2)}) collective-permute-start(f32[16,32,128]{2,1,0:T(8,128)S(1)} %get-tuple-element.86), channel_id=1, source_target_pairs={{0,4},{4,8},{8,12},{12,16},{16,20},{20,24},{24,28},{28,0},{1,5},{5... | collective-permute-start | bytes 786440 | tf_op jit(solution)/shard_map/ppermute | solution.py:557
  53.3 6.6 %collective-permute-start.17 = (f32[16,32,128]{2,1,0:T(8,128)S(1)}, f32[16,32,128]{2,1,0:T(8,128)S(1)}, u32[]{:S(2)}, u32[]{:S(2)}) collective-permute-start(f32[16,32,128]{2,1,0:T(8,128)S(1)} %get-tuple-element.87), channel_id=1, source_target_pairs={{4,0},{8,4},{12,8},{16,12},{20,16},{24,20},{28,24},{0,28},{5,1},{9... | collective-permute-start | bytes 786440 | tf_op jit(solution)/shard_map/ppermute | solution.py:558
  60.7 1.2 %collective-permute-start.18 = (f32[32,128]{1,0:T(8,128)S(1)}, f32[32,128]{1,0:T(8,128)S(1)}, u32[]{:S(2)}, u32[]{:S(2)}) collective-permute-start(f32[32,128]{1,0:T(8,128)S(1)} %get-tuple-element.90), channel_id=1, source_target_pairs={{0,4},{4,0},{8,12},{12,8},{16,20},{20,16},{24,28},{28,24},{1,5},{5... | collective-permute-start | bytes 49160 | tf_op jit(solution)/shard_map/ppermute | solution.py:743
  61.9 5.2 %collective-permute-start.21 = (f32[32,128]{1,0:T(8,128)S(1)}, f32[32,128]{1,0:T(8,128)S(1)}, u32[]{:S(2)}, u32[]{:S(2)}) collective-permute-start(f32[32,128]{1,0:T(8,128)S(1)} %add.42), channel_id=1, source_target_pairs={{0,2},{1,3},{2,0},{3,1},{4,6},{5,7},{6,4},{7,5},{8,10},{9,11},{10,... | collective-permute-start | bytes 49160 | tf_op jit(solution)/shard_map/ppermute | solution.py:748
  63.5 4.9 %collective-permute-start.20 = (f32[32,128]{1,0:T(8,128)S(1)}, f32[32,128]{1,0:T(8,128)S(1)}, u32[]{:S(2)}, u32[]{:S(2)}) collective-permute-start(f32[32,128]{1,0:T(8,128)S(1)} %add.42), channel_id=1, source_target_pairs={{0,3},{1,2},{2,1},{3,0},{4,7},{5,6},{6,5},{7,4},{8,11},{9,10},{10,... | collective-permute-start | bytes 49160 | tf_op jit(solution)/shard_map/ppermute | solution.py:748
  65.2 3.7 %collective-permute-start.19 = (f32[32,128]{1,0:T(8,128)S(1)}, f32[32,128]{1,0:T(8,128)S(1)}, u32[]{:S(2)}, u32[]{:S(2)}) collective-permute-start(f32[32,128]{1,0:T(8,128)S(1)} %add.42), channel_id=1, source_target_pairs={{0,1},{1,0},{2,3},{3,2},{4,5},{5,4},{6,7},{7,6},{8,9},{9,8},{10,11... | collective-permute-start | bytes 49160 | tf_op jit(solution)/shard_map/ppermute | solution.py:748
  69.0 5.3 %collective-permute-start.24 = (f32[32,128]{1,0:T(8,128)S(1)}, f32[32,128]{1,0:T(8,128)S(1)}, u32[]{:S(2)}, u32[]{:S(2)}) collective-permute-start(f32[32,128]{1,0:T(8,128)S(1)} %add_add_fusion.1), channel_id=1, source_target_pairs={{0,16},{4,20},{8,24},{12,28},{16,0},{20,4},{24,8},{28,12},{1,17},{... | collective-permute-start | bytes 49160 | tf_op jit(solution)/shard_map/ppermute | solution.py:748
  69.0 5.4 %collective-permute-start.23 = (f32[32,128]{1,0:T(8,128)S(1)}, f32[32,128]{1,0:T(8,128)S(1)}, u32[]{:S(2)}, u32[]{:S(2)}) collective-permute-start(f32[32,128]{1,0:T(8,128)S(1)} %add_add_fusion.1), channel_id=1, source_target_pairs={{0,24},{4,28},{8,16},{12,20},{16,8},{20,12},{24,0},{28,4},{1,25},{... | collective-permute-start | bytes 49160 | tf_op jit(solution)/shard_map/ppermute | solution.py:748
  70.4 4.0 %collective-permute-start.22 = (f32[32,128]{1,0:T(8,128)S(1)}, f32[32,128]{1,0:T(8,128)S(1)}, u32[]{:S(2)}, u32[]{:S(2)}) collective-permute-start(f32[32,128]{1,0:T(8,128)S(1)} %add_add_fusion.1), channel_id=1, source_target_pairs={{0,8},{4,12},{8,0},{12,4},{16,24},{20,28},{24,16},{28,20},{1,9},{5... | collective-permute-start | bytes 49160 | tf_op jit(solution)/shard_map/ppermute | solution.py:748
  74.4 5.4 %collective-permute-start.27 = (f32[32,128]{1,0:T(8,128)S(1)}, f32[32,128]{1,0:T(8,128)S(1)}, u32[]{:S(2)}, u32[]{:S(2)}) collective-permute-start(f32[32,128]{1,0:T(8,128)S(1)} %add_add_fusion.refs_0_), channel_id=1, source_target_pairs={{0,64},{32,96},{64,0},{96,32},{1,65},{33,97},{65,1},{97,33},{2,66}... | collective-permute-start | bytes 49160 | tf_op jit(solution)/shard_map/ppermute | solution.py:748
  74.7 5.1 %collective-permute-start.26 = (f32[32,128]{1,0:T(8,128)S(1)}, f32[32,128]{1,0:T(8,128)S(1)}, u32[]{:S(2)}, u32[]{:S(2)}) collective-permute-start(f32[32,128]{1,0:T(8,128)S(1)} %add_add_fusion.refs_0_), channel_id=1, source_target_pairs={{0,96},{32,64},{64,32},{96,0},{1,97},{33,65},{65,33},{97,1},{2,98}... | collective-permute-start | bytes 49160 | tf_op jit(solution)/shard_map/ppermute | solution.py:748
  75.9 3.9 %collective-permute-start.25 = (f32[32,128]{1,0:T(8,128)S(1)}, f32[32,128]{1,0:T(8,128)S(1)}, u32[]{:S(2)}, u32[]{:S(2)}) collective-permute-start(f32[32,128]{1,0:T(8,128)S(1)} %add_add_fusion.refs_0_), channel_id=1, source_target_pairs={{0,32},{32,0},{64,96},{96,64},{1,33},{33,1},{65,97},{97,65},{2,34}... | collective-permute-start | bytes 49160 | tf_op jit(solution)/shard_map/ppermute | solution.py:748

commit v6 on v5

--- a/solution.py
+++ b/solution.py
@@ -550,7 +550,7 @@
         lax.ppermute(ends, "layer", ahead("layer")),
         lax.ppermute(ends, "layer", back("layer")),
     )
-    near, ylo = lax.optimization_barrier((near, ylo))
+    near, yhi = lax.optimization_barrier((near, yhi))
     far = (
         lax.ppermute(xhi, "strike", ahead("strike")),
         lax.ppermute(xlo, "strike", back("strike")),

time: 90.8 us -> 90.3 us (level)
  waiting for transfers between devices: 15.2 us -> 12.7 us
  starting transfers between devices: 32.8 us -> 35.2 us
    ppermute x3, waiting for transfers between devices: 7.28 us -> 1.37 us  [exchanged(): lax.ppermute(ends, 'layer', ahead('layer'))]
    ppermute x3, starting transfers between devices: 2.48 us -> 5.93 us  [exchanged(): lax.ppermute(ylo, 'dip', back('dip'))]
    ppermute x9, waiting for transfers between devices: 6.75 us -> 8.91 us  [summed_but_last(): lax.ppermute(values, axis, swaps(axis, mask, stride))]
    ppermute x3, waiting for transfers between devices: 0.01 us -> 1.26 us  [exchanged(): lax.ppermute(yhi, 'dip', ahead('dip'))]
  transfers between devices with their start and end apart: 28 -> 28, of which waited for: 9 -> 13; matrix products, arithmetic and copies ran while one was open for 0% -> 0% of each run, Pallas kernels for 25% -> 25%
where the time goes in v6:
time: 90.3 us; the launch traced here: 90.2 us
  Pallas kernels  40.9 us (45%)
  starting transfers between devices  35.2 us (39%)
  waiting for transfers between devices  12.7 us (14%)
  between operations  1.01 us (1%)
    pallas_call x3, Pallas kernels, inner_part(): pl.pallas_call(first_kernel if first else functools.partial(inner_kernel,...  22.4 us
    ppermute x9, starting transfers between devices, summed_but_last(): lax.ppermute(values, axis, swaps(axis, mask, stride))  10.8 us
    ppermute x3, starting transfers between devices, exchanged(): lax.ppermute(ends, 'layer', back('layer'))  9.17 us
    ppermute x9, waiting for transfers between devices, summed_but_last(): lax.ppermute(values, axis, swaps(axis, mask, stride))  8.91 us
    ppermute x3, starting transfers between devices, exchanged(): lax.ppermute(xlo, 'strike', back('strike'))  7.61 us
    pallas_call x1, Pallas kernels, pack(): pl.pallas_call(pack_kernel, in_specs=[HBM] * 3, out_specs=[HBM] + [VMEM]...  6.41 us
    pallas_call x1, Pallas kernels, combine(): pl.pallas_call(combine_kernel, in_specs=[VMEM, HBM] + [VMEM] * 3, out_spe...  6.24 us
    ppermute x3, starting transfers between devices, exchanged(): lax.ppermute(ylo, 'dip', back('dip'))  5.93 us
  transfers between devices with their start and end apart: 28, of which 13 were waited for; matrix products, arithmetic and copies ran while one was open for 0% of the time, Pallas kernels for 25%

profile of v6, /device:TPU:0, one launch (start us, length us, event | category | flops | bytes accessed | tf_op | source)
XLA Modules:
  0.0 90.2 jit_solution(6191761712376438372)
XLA Ops:
  0.6 6.4 %pack_guess.1 = (f32[16,16,32,128]{3,2,1,0:T(8,128)}, f32[16,16,128]{2,1,0:T(8,128)S(1)}, f32[17,32,128]{2,1,0:T(8,128)S(1)}, f32[17,32,128]{2,1,0:T(8,128)S(1)}...) custom-call(s32[16,16,128]{2,1,0:T(8,128)} %class_hbm.1, f32[16]{0:T(128)} %table_hbm.1, ...), custom_call_target="tpu_custom_call" | custom-call | tf_op jit(solution)/shard_map/pack_guess/pallas_call | solution.py:128
  7.1 4.2 %collective-permute-start.1 = (f32[5,32,128]{2,1,0:T(8,128)S(1)}, f32[5,32,128]{2,1,0:T(8,128)S(1)}, u32[]{:S(2)}, u32[]{:S(2)}) collective-permute-start(f32[5,32,128]{2,1,0:T(8,128)S(1)} %get-tuple-element.48), channel_id=1, source_target_pairs={{1,0},{2,1},{3,2},{0,3},{5,4},{6,5},{7,6},{4,7},{9,8},{10,9},{11,1... | collective-permute-start | bytes 245768 | tf_op jit(solution)/shard_map/ppermute | solution.py:551
  11.2 2.8 %collective-permute-start.3 = (f32[17,32,128]{2,1,0:T(8,128)S(1)}, f32[17,32,128]{2,1,0:T(8,128)S(1)}, u32[]{:S(2)}, u32[]{:S(2)}) collective-permute-start(f32[17,32,128]{2,1,0:T(8,128)S(1)} %get-tuple-element.54.refs_1_), channel_id=1, source_target_pairs={{32,0},{64,32},{96,64},{0,96},{33,1},{65,33},{97,65},{1,97},{34,2}... | collective-permute-start | bytes 835592 | tf_op jit(solution)/shard_map/ppermute | solution.py:556
  14.0 1.9 %collective-permute-start.5 = (f32[17,32,128]{2,1,0:T(8,128)S(1)}, f32[17,32,128]{2,1,0:T(8,128)S(1)}, u32[]{:S(2)}, u32[]{:S(2)}) collective-permute-start(f32[17,32,128]{2,1,0:T(8,128)S(1)} %get-tuple-element.56.refs_3_), channel_id=1, source_target_pairs={{4,0},{8,4},{12,8},{16,12},{20,16},{24,20},{28,24},{0,28},{5,1},{9... | collective-permute-start | bytes 835592 | tf_op jit(solution)/shard_map/ppermute | solution.py:558
  16.0 0.9 %collective-permute-done.hzl = f32[5,32,128]{2,1,0:T(8,128)S(1)} collective-permute-done((f32[5,32,128]{2,1,0:T(8,128)S(1)}, f32[5,32,128]{2,1,0:T(8,128)S(1)}, u32[]{:S(2)}, u32[]{:S(2)}) %collective-permute-start) | collective-permute-done | bytes 81952 | tf_op jit(solution)/shard_map/ppermute | solution.py:550
  17.2 9.7 %inner_first.1 = (f32[16,16,32,128]{3,2,1,0:T(8,128)S(1)}, f32[4,32,128]{2,1,0:T(8,128)S(1)}, f32[17,16,128]{2,1,0:T(8,128)S(1)}, f32[16,24,128]{2,1,0:T(8,128)S...) custom-call(f32[16,16,32,128]{3,2,1,0:T(8,128)} %get-tuple-element.47.away.guess_hbm, ...), custom_call_target="tpu_custom_call" | custom-call | flops 20971520 | bytes 25165824 | tf_op jit(solution)/shard_map/inner_first/pallas_call | solution.py:500
  27.4 2.1 %collective-permute-start.7 = (f32[4,32,128]{2,1,0:T(8,128)S(1)}, f32[4,32,128]{2,1,0:T(8,128)S(1)}, u32[]{:S(2)}, u32[]{:S(2)}) collective-permute-start(f32[4,32,128]{2,1,0:T(8,128)S(1)} %get-tuple-element.62), channel_id=1, source_target_pairs={{1,0},{2,1},{3,2},{0,3},{5,4},{6,5},{7,6},{4,7},{9,8},{10,9},{11,1... | collective-permute-start | bytes 196616 | tf_op jit(solution)/shard_map/ppermute | solution.py:551
  29.5 1.5 %collective-permute-start.8 = (f32[16,32,128]{2,1,0:T(8,128)S(1)}, f32[16,32,128]{2,1,0:T(8,128)S(1)}, u32[]{:S(2)}, u32[]{:S(2)}) collective-permute-start(f32[16,32,128]{2,1,0:T(8,128)S(1)} %get-tuple-element.72), channel_id=1, source_target_pairs={{0,32},{32,64},{64,96},{96,0},{1,33},{33,65},{65,97},{97,1},{2,34}... | collective-permute-start | bytes 786440 | tf_op jit(solution)/shard_map/ppermute | solution.py:555
  31.0 1.8 %collective-permute-start.9 = (f32[16,32,128]{2,1,0:T(8,128)S(1)}, f32[16,32,128]{2,1,0:T(8,128)S(1)}, u32[]{:S(2)}, u32[]{:S(2)}) collective-permute-start(f32[16,32,128]{2,1,0:T(8,128)S(1)} %get-tuple-element.73), channel_id=1, source_target_pairs={{32,0},{64,32},{96,64},{0,96},{33,1},{65,33},{97,65},{1,97},{34,2}... | collective-permute-start | bytes 786440 | tf_op jit(solution)/shard_map/ppermute | solution.py:556
  32.8 2.1 %collective-permute-start.11 = (f32[16,32,128]{2,1,0:T(8,128)S(1)}, f32[16,32,128]{2,1,0:T(8,128)S(1)}, u32[]{:S(2)}, u32[]{:S(2)}) collective-permute-start(f32[16,32,128]{2,1,0:T(8,128)S(1)} %get-tuple-element.75), channel_id=1, source_target_pairs={{4,0},{8,4},{12,8},{16,12},{20,16},{24,20},{28,24},{0,28},{5,1},{9... | collective-permute-start | bytes 786440 | tf_op jit(solution)/shard_map/ppermute | solution.py:558
  35.0 6.8 %inner_next.1 = (f32[16,16,32,128]{3,2,1,0:T(8,128)S(1)}, f32[4,32,128]{2,1,0:T(8,128)S(1)}, f32[64,128]{1,0:T(8,128)S(1)}) custom-call(f32[16,16,32,128]{3,2,1,0:T(8,128)S(1)} %get-tuple-element.61.refs_0_.refs_1_.one_ref, f32[4,32,128]{2,1,0:T(8,128)S(1)} %collective-permute-done.6.refs_1_, f32[4,32,128]{2,1,0:T(8,128)S(1)} %collective-permute-done.7.refs_2_, ...), custom_call_target="tpu_custom_call" | custom-call | flops 20971520 | bytes 25165824 | tf_op jit(solution)/shard_map/inner_next/pallas_call | solution.py:500
  42.7 2.9 %collective-permute-start.13 = (f32[4,32,128]{2,1,0:T(8,128)S(1)}, f32[4,32,128]{2,1,0:T(8,128)S(1)}, u32[]{:S(2)}, u32[]{:S(2)}) collective-permute-start(f32[4,32,128]{2,1,0:T(8,128)S(1)} %get-tuple-element.79), channel_id=1, source_target_pairs={{1,0},{2,1},{3,2},{0,3},{5,4},{6,5},{7,6},{4,7},{9,8},{10,9},{11,1... | collective-permute-start | bytes 196616 | tf_op jit(solution)/shard_map/ppermute | solution.py:551
  45.7 3.1 %collective-permute-start.15 = (f32[16,32,128]{2,1,0:T(8,128)S(1)}, f32[16,32,128]{2,1,0:T(8,128)S(1)}, u32[]{:S(2)}, u32[]{:S(2)}) collective-permute-start(f32[16,32,128]{2,1,0:T(8,128)S(1)} %get-tuple-element.85), channel_id=1, source_target_pairs={{32,0},{64,32},{96,64},{0,96},{33,1},{65,33},{97,65},{1,97},{34,2}... | collective-permute-start | bytes 786440 | tf_op jit(solution)/shard_map/ppermute | solution.py:556
  48.8 2.0 %collective-permute-start.17 = (f32[16,32,128]{2,1,0:T(8,128)S(1)}, f32[16,32,128]{2,1,0:T(8,128)S(1)}, u32[]{:S(2)}, u32[]{:S(2)}) collective-permute-start(f32[16,32,128]{2,1,0:T(8,128)S(1)} %get-tuple-element.87), channel_id=1, source_target_pairs={{4,0},{8,4},{12,8},{16,12},{20,16},{24,20},{28,24},{0,28},{5,1},{9... | collective-permute-start | bytes 786440 | tf_op jit(solution)/shard_map/ppermute | solution.py:558
  51.1 5.9 %inner_last.1 = (f32[16,16,32,128]{3,2,1,0:T(8,128)S(1)}, f32[64,128]{1,0:T(8,128)S(1)}) custom-call(f32[16,16,32,128]{3,2,1,0:T(8,128)S(1)} %get-tuple-element.78.refs_0_.refs_1_.two_ref, f32[4,32,128]{2,1,0:T(8,128)S(1)} %collective-permute-done.12.refs_1_, f32[4,32,128]{2,1,0:T(8,128)S(1)} %collective-permute-done.13.refs_2_, ...), custom_call_target="tpu_custom_call" | custom-call | flops 20971520 | bytes 25165824 | tf_op jit(solution)/shard_map/inner_last/pallas_call | solution.py:500
  57.0 1.1 %collective-permute-done.16.refs_4_ = f32[16,32,128]{2,1,0:T(8,128)S(1)} collective-permute-done((f32[16,32,128]{2,1,0:T(8,128)S(1)}, f32[16,32,128]{2,1,0:T(8,128)S(1)}, u32[]{:S(2)}, u32[]{:S(2)}) %collective-permute-start.16) | collective-permute-done | bytes 262176 | tf_op jit(solution)/shard_map/ppermute | solution.py:557
  58.8 1.2 %collective-permute-done.18 = f32[32,128]{1,0:T(8,128)S(1)} collective-permute-done((f32[32,128]{1,0:T(8,128)S(1)}, f32[32,128]{1,0:T(8,128)S(1)}, u32[]{:S(2)}, u32[]{:S(2)}) %collective-permute-start.18) | collective-permute-done | bytes 16416 | tf_op jit(solution)/shard_map/ppermute | solution.py:743
  60.0 1.3 %collective-permute-start.21 = (f32[32,128]{1,0:T(8,128)S(1)}, f32[32,128]{1,0:T(8,128)S(1)}, u32[]{:S(2)}, u32[]{:S(2)}) collective-permute-start(f32[32,128]{1,0:T(8,128)S(1)} %add.42), channel_id=1, source_target_pairs={{0,2},{1,3},{2,0},{3,1},{4,6},{5,7},{6,4},{7,5},{8,10},{9,11},{10,... | collective-permute-start | bytes 49160 | tf_op jit(solution)/shard_map/ppermute | solution.py:748
  61.3 1.5 %collective-permute-start.20 = (f32[32,128]{1,0:T(8,128)S(1)}, f32[32,128]{1,0:T(8,128)S(1)}, u32[]{:S(2)}, u32[]{:S(2)}) collective-permute-start(f32[32,128]{1,0:T(8,128)S(1)} %add.42), channel_id=1, source_target_pairs={{0,3},{1,2},{2,1},{3,0},{4,7},{5,6},{6,5},{7,4},{8,11},{9,10},{10,... | collective-permute-start | bytes 49160 | tf_op jit(solution)/shard_map/ppermute | solution.py:748
  62.8 0.8 collective-permute-start.19
  63.5 1.8 %collective-permute-done.21 = f32[32,128]{1,0:T(8,128)S(1)} collective-permute-done((f32[32,128]{1,0:T(8,128)S(1)}, f32[32,128]{1,0:T(8,128)S(1)}, u32[]{:S(2)}, u32[]{:S(2)}) %collective-permute-start.21) | collective-permute-done | bytes 16416 | tf_op jit(solution)/shard_map/ppermute | solution.py:748
  65.3 0.9 %collective-permute-done.20 = f32[32,128]{1,0:T(8,128)S(1)} collective-permute-done((f32[32,128]{1,0:T(8,128)S(1)}, f32[32,128]{1,0:T(8,128)S(1)}, u32[]{:S(2)}, u32[]{:S(2)}) %collective-permute-start.20) | collective-permute-done | bytes 16416 | tf_op jit(solution)/shard_map/ppermute | solution.py:748
  66.5 0.9 %collective-permute-start.24 = (f32[32,128]{1,0:T(8,128)S(1)}, f32[32,128]{1,0:T(8,128)S(1)}, u32[]{:S(2)}, u32[]{:S(2)}) collective-permute-start(f32[32,128]{1,0:T(8,128)S(1)} %add_add_fusion.1), channel_id=1, source_target_pairs={{0,16},{4,20},{8,24},{12,28},{16,0},{20,4},{24,8},{28,12},{1,17},{... | collective-permute-start | bytes 49160 | tf_op jit(solution)/shard_map/ppermute | solution.py:748
  67.4 1.2 %collective-permute-start.23 = (f32[32,128]{1,0:T(8,128)S(1)}, f32[32,128]{1,0:T(8,128)S(1)}, u32[]{:S(2)}, u32[]{:S(2)}) collective-permute-start(f32[32,128]{1,0:T(8,128)S(1)} %add_add_fusion.1), channel_id=1, source_target_pairs={{0,24},{4,28},{8,16},{12,20},{16,8},{20,12},{24,0},{28,4},{1,25},{... | collective-permute-start | bytes 49160 | tf_op jit(solution)/shard_map/ppermute | solution.py:748
  68.7 1.3 %collective-permute-start.22 = (f32[32,128]{1,0:T(8,128)S(1)}, f32[32,128]{1,0:T(8,128)S(1)}, u32[]{:S(2)}, u32[]{:S(2)}) collective-permute-start(f32[32,128]{1,0:T(8,128)S(1)} %add_add_fusion.1), channel_id=1, source_target_pairs={{0,8},{4,12},{8,0},{12,4},{16,24},{20,28},{24,16},{28,20},{1,9},{5... | collective-permute-start | bytes 49160 | tf_op jit(solution)/shard_map/ppermute | solution.py:748
  70.0 1.8 %collective-permute-done.24 = f32[32,128]{1,0:T(8,128)S(1)} collective-permute-done((f32[32,128]{1,0:T(8,128)S(1)}, f32[32,128]{1,0:T(8,128)S(1)}, u32[]{:S(2)}, u32[]{:S(2)}) %collective-permute-start.24) | collective-permute-done | bytes 16416 | tf_op jit(solution)/shard_map/ppermute | solution.py:748
  72.4 2.3 %collective-permute-start.27 = (f32[32,128]{1,0:T(8,128)S(1)}, f32[32,128]{1,0:T(8,128)S(1)}, u32[]{:S(2)}, u32[]{:S(2)}) collective-permute-start(f32[32,128]{1,0:T(8,128)S(1)} %add_add_fusion.refs_0_), channel_id=1, source_target_pairs={{0,64},{32,96},{64,0},{96,32},{1,65},{33,97},{65,1},{97,33},{2,66}... | collective-permute-start | bytes 49160 | tf_op jit(solution)/shard_map/ppermute | solution.py:748
  74.8 1.1 %collective-permute-start.26 = (f32[32,128]{1,0:T(8,128)S(1)}, f32[32,128]{1,0:T(8,128)S(1)}, u32[]{:S(2)}, u32[]{:S(2)}) collective-permute-start(f32[32,128]{1,0:T(8,128)S(1)} %add_add_fusion.refs_0_), channel_id=1, source_target_pairs={{0,96},{32,64},{64,32},{96,0},{1,97},{33,65},{65,33},{97,1},{2,98}... | collective-permute-start | bytes 49160 | tf_op jit(solution)/shard_map/ppermute | solution.py:748
  76.2 1.5 %collective-permute-done.27.refs_3_ = f32[32,128]{1,0:T(8,128)S(1)} collective-permute-done((f32[32,128]{1,0:T(8,128)S(1)}, f32[32,128]{1,0:T(8,128)S(1)}, u32[]{:S(2)}, u32[]{:S(2)}) %collective-permute-start.27) | collective-permute-done | bytes 16416 | tf_op jit(solution)/shard_map/ppermute | solution.py:748
  77.7 2.0 %collective-permute-done.26.refs_2_ = f32[32,128]{1,0:T(8,128)S(1)} collective-permute-done((f32[32,128]{1,0:T(8,128)S(1)}, f32[32,128]{1,0:T(8,128)S(1)}, u32[]{:S(2)}, u32[]{:S(2)}) %collective-permute-start.26) | collective-permute-done | bytes 16416 | tf_op jit(solution)/shard_map/ppermute | solution.py:748
  79.7 4.0 %solve_small.1.mix_ref = f32[64,128]{1,0:T(8,128)S(1)} custom-call(f32[32,128]{1,0:T(8,128)S(1)} %add_add_fusion.refs_0_, f32[32,128]{1,0:T(8,128)S(1)} %collective-permute-done.25.refs_1_, f32[32,128]{1,0:T(8,128)S(1)} %collective-permute-done.26.refs_2_, f32[32,128]{1,0:T(8,128)S(1)} %collective-permute-done.27.refs_3_), custom_call_target="tpu_custom_call" | custom-call | tf_op jit(solution)/shard_map/solve_small/pallas_call | solution.py:619
  83.8 6.2 %combine_fields.1 = (f32[32,16,16,128]{3,2,1,0:T(8,128)}, f32[32,16,16,128]{3,2,1,0:T(8,128)}) custom-call(f32[64,128]{1,0:T(8,128)S(1)} %solve_small.1.mix_ref, f32[16,16,32,128]{3,2,1,0:T(8,128)} %get-tuple-element.47.away.guess_hbm, f32[16,16,32,128]{3,2,1,0:T(8,128)S(1)} %get-tuple-element.61.refs_0_.refs_1_.one_ref, ...), custom_call_target="tpu_custom_call" | custom-call | tf_op jit(solution)/shard_map/combine_fields/pallas_call | solution.py:717
  (46 shorter events, 4.3 us)
Async XLA Ops:
  0.6 15.3 %copy-start = (s32[32]{0:T(128)S(1)}, s32[32]{0:T(128)}, u32[]{:S(2)}) copy-start(s32[32]{0:T(128)} %param.6) | copy-start | bytes 388
  7.1 8.9 %collective-permute-start.1 = (f32[5,32,128]{2,1,0:T(8,128)S(1)}, f32[5,32,128]{2,1,0:T(8,128)S(1)}, u32[]{:S(2)}, u32[]{:S(2)}) collective-permute-start(f32[5,32,128]{2,1,0:T(8,128)S(1)} %get-tuple-element.48), channel_id=1, source_target_pairs={{1,0},{2,1},{3,2},{0,3},{5,4},{6,5},{7,6},{4,7},{9,8},{10,9},{11,1... | collective-permute-start | bytes 245768 | tf_op jit(solution)/shard_map/ppermute | solution.py:551
  11.2 5.7 %collective-permute-start = (f32[5,32,128]{2,1,0:T(8,128)S(1)}, f32[5,32,128]{2,1,0:T(8,128)S(1)}, u32[]{:S(2)}, u32[]{:S(2)}) collective-permute-start(f32[5,32,128]{2,1,0:T(8,128)S(1)} %get-tuple-element.48), channel_id=1, source_target_pairs={{0,1},{1,2},{2,3},{3,0},{4,5},{5,6},{6,7},{7,4},{8,9},{9,10},{10,1... | collective-permute-start | bytes 245768 | tf_op jit(solution)/shard_map/ppermute | solution.py:550
  11.2 15.7 %collective-permute-start.3 = (f32[17,32,128]{2,1,0:T(8,128)S(1)}, f32[17,32,128]{2,1,0:T(8,128)S(1)}, u32[]{:S(2)}, u32[]{:S(2)}) collective-permute-start(f32[17,32,128]{2,1,0:T(8,128)S(1)} %get-tuple-element.54.refs_1_), channel_id=1, source_target_pairs={{32,0},{64,32},{96,64},{0,96},{33,1},{65,33},{97,65},{1,97},{34,2}... | collective-permute-start | bytes 835592 | tf_op jit(solution)/shard_map/ppermute | solution.py:556
  14.0 13.0 %collective-permute-start.2 = (f32[17,32,128]{2,1,0:T(8,128)S(1)}, f32[17,32,128]{2,1,0:T(8,128)S(1)}, u32[]{:S(2)}, u32[]{:S(2)}) collective-permute-start(f32[17,32,128]{2,1,0:T(8,128)S(1)} %get-tuple-element.55.refs_2_), channel_id=1, source_target_pairs={{0,32},{32,64},{64,96},{96,0},{1,33},{33,65},{65,97},{97,1},{2,34}... | collective-permute-start | bytes 835592 | tf_op jit(solution)/shard_map/ppermute | solution.py:555
  14.0 13.0 %collective-permute-start.5 = (f32[17,32,128]{2,1,0:T(8,128)S(1)}, f32[17,32,128]{2,1,0:T(8,128)S(1)}, u32[]{:S(2)}, u32[]{:S(2)}) collective-permute-start(f32[17,32,128]{2,1,0:T(8,128)S(1)} %get-tuple-element.56.refs_3_), channel_id=1, source_target_pairs={{4,0},{8,4},{12,8},{16,12},{20,16},{24,20},{28,24},{0,28},{5,1},{9... | collective-permute-start | bytes 835592 | tf_op jit(solution)/shard_map/ppermute | solution.py:558
  16.9 10.1 %collective-permute-start.4 = (f32[17,32,128]{2,1,0:T(8,128)S(1)}, f32[17,32,128]{2,1,0:T(8,128)S(1)}, u32[]{:S(2)}, u32[]{:S(2)}) collective-permute-start(f32[17,32,128]{2,1,0:T(8,128)S(1)} %get-tuple-element.57.refs_4_), channel_id=1, source_target_pairs={{0,4},{4,8},{8,12},{12,16},{16,20},{20,24},{24,28},{28,0},{1,5},{5... | collective-permute-start | bytes 835592 | tf_op jit(solution)/shard_map/ppermute | solution.py:557
  27.4 7.4 %collective-permute-start.7 = (f32[4,32,128]{2,1,0:T(8,128)S(1)}, f32[4,32,128]{2,1,0:T(8,128)S(1)}, u32[]{:S(2)}, u32[]{:S(2)}) collective-permute-start(f32[4,32,128]{2,1,0:T(8,128)S(1)} %get-tuple-element.62), channel_id=1, source_target_pairs={{1,0},{2,1},{3,2},{0,3},{5,4},{6,5},{7,6},{4,7},{9,8},{10,9},{11,1... | collective-permute-start | bytes 196616 | tf_op jit(solution)/shard_map/ppermute | solution.py:551
  29.5 5.5 %collective-permute-start.6 = (f32[4,32,128]{2,1,0:T(8,128)S(1)}, f32[4,32,128]{2,1,0:T(8,128)S(1)}, u32[]{:S(2)}, u32[]{:S(2)}) collective-permute-start(f32[4,32,128]{2,1,0:T(8,128)S(1)} %get-tuple-element.62), channel_id=1, source_target_pairs={{0,1},{1,2},{2,3},{3,0},{4,5},{5,6},{6,7},{7,4},{8,9},{9,10},{10,1... | collective-permute-start | bytes 196616 | tf_op jit(solution)/shard_map/ppermute | solution.py:550
  29.5 12.3 %collective-permute-start.8 = (f32[16,32,128]{2,1,0:T(8,128)S(1)}, f32[16,32,128]{2,1,0:T(8,128)S(1)}, u32[]{:S(2)}, u32[]{:S(2)}) collective-permute-start(f32[16,32,128]{2,1,0:T(8,128)S(1)} %get-tuple-element.72), channel_id=1, source_target_pairs={{0,32},{32,64},{64,96},{96,0},{1,33},{33,65},{65,97},{97,1},{2,34}... | collective-permute-start | bytes 786440 | tf_op jit(solution)/shard_map/ppermute | solution.py:555
  31.0 10.8 %collective-permute-start.9 = (f32[16,32,128]{2,1,0:T(8,128)S(1)}, f32[16,32,128]{2,1,0:T(8,128)S(1)}, u32[]{:S(2)}, u32[]{:S(2)}) collective-permute-start(f32[16,32,128]{2,1,0:T(8,128)S(1)} %get-tuple-element.73), channel_id=1, source_target_pairs={{32,0},{64,32},{96,64},{0,96},{33,1},{65,33},{97,65},{1,97},{34,2}... | collective-permute-start | bytes 786440 | tf_op jit(solution)/shard_map/ppermute | solution.py:556
  32.8 9.1 %collective-permute-start.11 = (f32[16,32,128]{2,1,0:T(8,128)S(1)}, f32[16,32,128]{2,1,0:T(8,128)S(1)}, u32[]{:S(2)}, u32[]{:S(2)}) collective-permute-start(f32[16,32,128]{2,1,0:T(8,128)S(1)} %get-tuple-element.75), channel_id=1, source_target_pairs={{4,0},{8,4},{12,8},{16,12},{20,16},{24,20},{28,24},{0,28},{5,1},{9... | collective-permute-start | bytes 786440 | tf_op jit(solution)/shard_map/ppermute | solution.py:558
  35.0 7.0 %collective-permute-start.10 = (f32[16,32,128]{2,1,0:T(8,128)S(1)}, f32[16,32,128]{2,1,0:T(8,128)S(1)}, u32[]{:S(2)}, u32[]{:S(2)}) collective-permute-start(f32[16,32,128]{2,1,0:T(8,128)S(1)} %get-tuple-element.74), channel_id=1, source_target_pairs={{0,4},{4,8},{8,12},{12,16},{16,20},{20,24},{24,28},{28,0},{1,5},{5... | collective-permute-start | bytes 786440 | tf_op jit(solution)/shard_map/ppermute | solution.py:557
  42.7 8.1 %collective-permute-start.13 = (f32[4,32,128]{2,1,0:T(8,128)S(1)}, f32[4,32,128]{2,1,0:T(8,128)S(1)}, u32[]{:S(2)}, u32[]{:S(2)}) collective-permute-start(f32[4,32,128]{2,1,0:T(8,128)S(1)} %get-tuple-element.79), channel_id=1, source_target_pairs={{1,0},{2,1},{3,2},{0,3},{5,4},{6,5},{7,6},{4,7},{9,8},{10,9},{11,1... | collective-permute-start | bytes 196616 | tf_op jit(solution)/shard_map/ppermute | solution.py:551
  45.6 5.5 %collective-permute-start.12 = (f32[4,32,128]{2,1,0:T(8,128)S(1)}, f32[4,32,128]{2,1,0:T(8,128)S(1)}, u32[]{:S(2)}, u32[]{:S(2)}) collective-permute-start(f32[4,32,128]{2,1,0:T(8,128)S(1)} %get-tuple-element.79), channel_id=1, source_target_pairs={{0,1},{1,2},{2,3},{3,0},{4,5},{5,6},{6,7},{7,4},{8,9},{9,10},{10,1... | collective-permute-start | bytes 196616 | tf_op jit(solution)/shard_map/ppermute | solution.py:550
  45.6 11.4 %collective-permute-start.14 = (f32[16,32,128]{2,1,0:T(8,128)S(1)}, f32[16,32,128]{2,1,0:T(8,128)S(1)}, u32[]{:S(2)}, u32[]{:S(2)}) collective-permute-start(f32[16,32,128]{2,1,0:T(8,128)S(1)} %get-tuple-element.84), channel_id=1, source_target_pairs={{0,32},{32,64},{64,96},{96,0},{1,33},{33,65},{65,97},{97,1},{2,34}... | collective-permute-start | bytes 786440 | tf_op jit(solution)/shard_map/ppermute | solution.py:555
  45.7 11.2 %collective-permute-start.15 = (f32[16,32,128]{2,1,0:T(8,128)S(1)}, f32[16,32,128]{2,1,0:T(8,128)S(1)}, u32[]{:S(2)}, u32[]{:S(2)}) collective-permute-start(f32[16,32,128]{2,1,0:T(8,128)S(1)} %get-tuple-element.85), channel_id=1, source_target_pairs={{32,0},{64,32},{96,64},{0,96},{33,1},{65,33},{97,65},{1,97},{34,2}... | collective-permute-start | bytes 786440 | tf_op jit(solution)/shard_map/ppermute | solution.py:556
  48.8 8.1 %collective-permute-start.17 = (f32[16,32,128]{2,1,0:T(8,128)S(1)}, f32[16,32,128]{2,1,0:T(8,128)S(1)}, u32[]{:S(2)}, u32[]{:S(2)}) collective-permute-start(f32[16,32,128]{2,1,0:T(8,128)S(1)} %get-tuple-element.87), channel_id=1, source_target_pairs={{4,0},{8,4},{12,8},{16,12},{20,16},{24,20},{28,24},{0,28},{5,1},{9... | collective-permute-start | bytes 786440 | tf_op jit(solution)/shard_map/ppermute | solution.py:558
  51.0 7.0 %collective-permute-start.16 = (f32[16,32,128]{2,1,0:T(8,128)S(1)}, f32[16,32,128]{2,1,0:T(8,128)S(1)}, u32[]{:S(2)}, u32[]{:S(2)}) collective-permute-start(f32[16,32,128]{2,1,0:T(8,128)S(1)} %get-tuple-element.86), channel_id=1, source_target_pairs={{0,4},{4,8},{8,12},{12,16},{16,20},{20,24},{24,28},{28,0},{1,5},{5... | collective-permute-start | bytes 786440 | tf_op jit(solution)/shard_map/ppermute | solution.py:557
  58.8 1.2 %collective-permute-start.18 = (f32[32,128]{1,0:T(8,128)S(1)}, f32[32,128]{1,0:T(8,128)S(1)}, u32[]{:S(2)}, u32[]{:S(2)}) collective-permute-start(f32[32,128]{1,0:T(8,128)S(1)} %get-tuple-element.90), channel_id=1, source_target_pairs={{0,4},{4,0},{8,12},{12,8},{16,20},{20,16},{24,28},{28,24},{1,5},{5... | collective-permute-start | bytes 49160 | tf_op jit(solution)/shard_map/ppermute | solution.py:743
  60.0 5.3 %collective-permute-start.21 = (f32[32,128]{1,0:T(8,128)S(1)}, f32[32,128]{1,0:T(8,128)S(1)}, u32[]{:S(2)}, u32[]{:S(2)}) collective-permute-start(f32[32,128]{1,0:T(8,128)S(1)} %add.42), channel_id=1, source_target_pairs={{0,2},{1,3},{2,0},{3,1},{4,6},{5,7},{6,4},{7,5},{8,10},{9,11},{10,... | collective-permute-start | bytes 49160 | tf_op jit(solution)/shard_map/ppermute | solution.py:748
  61.3 4.9 %collective-permute-start.20 = (f32[32,128]{1,0:T(8,128)S(1)}, f32[32,128]{1,0:T(8,128)S(1)}, u32[]{:S(2)}, u32[]{:S(2)}) collective-permute-start(f32[32,128]{1,0:T(8,128)S(1)} %add.42), channel_id=1, source_target_pairs={{0,3},{1,2},{2,1},{3,0},{4,7},{5,6},{6,5},{7,4},{8,11},{9,10},{10,... | collective-permute-start | bytes 49160 | tf_op jit(solution)/shard_map/ppermute | solution.py:748
  62.8 3.7 %collective-permute-start.19 = (f32[32,128]{1,0:T(8,128)S(1)}, f32[32,128]{1,0:T(8,128)S(1)}, u32[]{:S(2)}, u32[]{:S(2)}) collective-permute-start(f32[32,128]{1,0:T(8,128)S(1)} %add.42), channel_id=1, source_target_pairs={{0,1},{1,0},{2,3},{3,2},{4,5},{5,4},{6,7},{7,6},{8,9},{9,8},{10,11... | collective-permute-start | bytes 49160 | tf_op jit(solution)/shard_map/ppermute | solution.py:748
  66.5 5.2 %collective-permute-start.24 = (f32[32,128]{1,0:T(8,128)S(1)}, f32[32,128]{1,0:T(8,128)S(1)}, u32[]{:S(2)}, u32[]{:S(2)}) collective-permute-start(f32[32,128]{1,0:T(8,128)S(1)} %add_add_fusion.1), channel_id=1, source_target_pairs={{0,16},{4,20},{8,24},{12,28},{16,0},{20,4},{24,8},{28,12},{1,17},{... | collective-permute-start | bytes 49160 | tf_op jit(solution)/shard_map/ppermute | solution.py:748
  67.4 5.0 %collective-permute-start.23 = (f32[32,128]{1,0:T(8,128)S(1)}, f32[32,128]{1,0:T(8,128)S(1)}, u32[]{:S(2)}, u32[]{:S(2)}) collective-permute-start(f32[32,128]{1,0:T(8,128)S(1)} %add_add_fusion.1), channel_id=1, source_target_pairs={{0,24},{4,28},{8,16},{12,20},{16,8},{20,12},{24,0},{28,4},{1,25},{... | collective-permute-start | bytes 49160 | tf_op jit(solution)/shard_map/ppermute | solution.py:748
  68.7 3.7 %collective-permute-start.22 = (f32[32,128]{1,0:T(8,128)S(1)}, f32[32,128]{1,0:T(8,128)S(1)}, u32[]{:S(2)}, u32[]{:S(2)}) collective-permute-start(f32[32,128]{1,0:T(8,128)S(1)} %add_add_fusion.1), channel_id=1, source_target_pairs={{0,8},{4,12},{8,0},{12,4},{16,24},{20,28},{24,16},{28,20},{1,9},{5... | collective-permute-start | bytes 49160 | tf_op jit(solution)/shard_map/ppermute | solution.py:748
  72.4 5.3 %collective-permute-start.27 = (f32[32,128]{1,0:T(8,128)S(1)}, f32[32,128]{1,0:T(8,128)S(1)}, u32[]{:S(2)}, u32[]{:S(2)}) collective-permute-start(f32[32,128]{1,0:T(8,128)S(1)} %add_add_fusion.refs_0_), channel_id=1, source_target_pairs={{0,64},{32,96},{64,0},{96,32},{1,65},{33,97},{65,1},{97,33},{2,66}... | collective-permute-start | bytes 49160 | tf_op jit(solution)/shard_map/ppermute | solution.py:748
  74.8 4.9 %collective-permute-start.26 = (f32[32,128]{1,0:T(8,128)S(1)}, f32[32,128]{1,0:T(8,128)S(1)}, u32[]{:S(2)}, u32[]{:S(2)}) collective-permute-start(f32[32,128]{1,0:T(8,128)S(1)} %add_add_fusion.refs_0_), channel_id=1, source_target_pairs={{0,96},{32,64},{64,32},{96,0},{1,97},{33,65},{65,33},{97,1},{2,98}... | collective-permute-start | bytes 49160 | tf_op jit(solution)/shard_map/ppermute | solution.py:748
  75.9 3.9 %collective-permute-start.25 = (f32[32,128]{1,0:T(8,128)S(1)}, f32[32,128]{1,0:T(8,128)S(1)}, u32[]{:S(2)}, u32[]{:S(2)}) collective-permute-start(f32[32,128]{1,0:T(8,128)S(1)} %add_add_fusion.refs_0_), channel_id=1, source_target_pairs={{0,32},{32,0},{64,96},{96,64},{1,33},{33,1},{65,97},{97,65},{2,34}... | collective-permute-start | bytes 49160 | tf_op jit(solution)/shard_map/ppermute | solution.py:748

commit v7 on v6

--- a/solution.py
+++ b/solution.py
@@ -61,15 +61,13 @@
 
     class_copy = pltpu.make_async_copy(class_hbm, classes, class_sem)
     table_copy = pltpu.make_async_copy(table_hbm, table, table_sem)
+    for x in range(nx):
+        plane(x).start()
     table_copy.start()
     class_copy.start()
-    for x in range(nx):
-        plane(x).start()
     ends_ref[...] = jnp.zeros_like(ends_ref)
     for ref in (xlo, xhi, ylo, yhi):
         ref[ny] = jnp.zeros((columns, nz), F32)
-    table_copy.wait()
-    class_copy.wait()
     lane = lanes(ny)
     row = rows_of(ny)
 
@@ -90,10 +88,6 @@
         edges = [permeability(4 * block + step) for step in range(4)]
         ends_ref[4, pl.ds(block, 1), :] = (edges[0] + edges[1]) + (edges[2] + edges[3])
         return carry
-
-    lax.fori_loop(0, nx // 4, four, 0)
-    xlo[ny, 0:ny, :] = perm_ref[0]
-    xhi[ny, 0:ny, :] = perm_ref[nx - 1]
 
     def cells_of(pair, carry):
         for step in range(2):
@@ -115,6 +109,11 @@
         return carry
 
     lax.fori_loop(0, nx // 2, cells_of, 0)
+    table_copy.wait()
+    class_copy.wait()
+    lax.fori_loop(0, nx // 4, four, 0)
+    xlo[ny, 0:ny, :] = perm_ref[0]
+    xhi[ny, 0:ny, :] = perm_ref[nx - 1]
     for y in range(ny):
         xlo[y] = field_ref[0, y]
         xhi[y] = field_ref[nx - 1, y]
@@ -627,17 +626,12 @@
 
 
 def combine_kernel(
-    mix_ref, guess_hbm, one_ref, two_ref, three_ref, solution_hbm, residual_hbm,
-    guess_ref, solution, residual, sem, guess_sem,
+    mix_ref, guess_ref, one_ref, two_ref, three_ref, solution_hbm, residual_hbm,
+    solution, residual, sem,
 ):
     nx, ny, columns, nz = guess_ref.shape
     slots = solution.shape[0]
 
-    def arriving(x):
-        return pltpu.make_async_copy(guess_hbm.at[x], guess_ref.at[x], guess_sem.at[x])
-
-    for x in range(nx):
-        arriving(x).start()
     mix = mix_ref[...]
     high = mix.astype(BF16)
     low = (mix - high.astype(F32)).astype(BF16)
@@ -681,8 +675,6 @@
                 for copy in leaving(2 * pair + step - slots):
                     copy.wait()
 
-        for step in range(2):
-            arriving(2 * pair + step).wait()
         for step in range(2):
             x = 2 * pair + step
             slot = lax.rem(x, slots)
@@ -716,15 +708,13 @@
     nx, ny, columns, nz = guess.shape
     return pl.pallas_call(
         combine_kernel,
-        in_specs=[VMEM, HBM] + [VMEM] * 3,
+        in_specs=[VMEM] * 5,
         out_specs=[HBM] * 2,
         out_shape=[jax.ShapeDtypeStruct((columns, nx, ny, nz), F32)] * 2,
         scratch_shapes=[
-            pltpu.VMEM(guess.shape, F32),
             pltpu.VMEM((8, ny // 8, columns, 8, nz), F32),
             pltpu.VMEM((8, ny // 8, columns, 8, nz), F32),
             pltpu.SemaphoreType.DMA((2, ny // 8, 8)),
-            pltpu.SemaphoreType.DMA((nx,)),
         ],
         compiler_params=params(),
         name="combine_fields",
@@ -789,6 +779,7 @@
     part, total = inner_part(once, near, weights, False, True)
     twice, sums = sides_part(part, [once], far, None, [wx, wy, total, sums], False, True)
     mix = solve(summed_but_last(sums))
+    guess = pltpu.with_memory_space_constraint(guess, pltpu.VMEM)
     return tuple(combine(mix, guess, residual, once, twice))
 
 

time: 90.3 us -> 87.5 us (0.969)
  Pallas kernels: 40.9 us -> 38.1 us
    pallas_call x1, Pallas kernels: 6.41 us -> 4.64 us  [pack(): pl.pallas_call(pack_kernel, in_specs=[HBM] * 3, out_specs=[HBM] + [VMEM]...]
    pallas_call x1, Pallas kernels: 6.24 us -> 5.2 us  [combine(): pl.pallas_call(combine_kernel, in_specs=[VMEM] * 5, out_specs=[HBM] * 2,...]
  transfers between devices with their start and end apart: 28 -> 28, of which waited for: 13 -> 13; matrix products, arithmetic and copies ran while one was open for 0% -> 0% of each run, Pallas kernels for 25% -> 26%
where the time goes in v7:
time: 87.5 us; the launch traced here: 87.4 us
  Pallas kernels  38.1 us (44%)
  starting transfers between devices  35.2 us (40%)
  waiting for transfers between devices  12.8 us (15%)
  between operations  1.01 us (1%)
    pallas_call x3, Pallas kernels, inner_part(): pl.pallas_call(first_kernel if first else functools.partial(inner_kernel,...  22.4 us
    ppermute x9, starting transfers between devices, summed_but_last(): lax.ppermute(values, axis, swaps(axis, mask, stride))  10.8 us
    ppermute x3, starting transfers between devices, exchanged(): lax.ppermute(ends, 'layer', back('layer'))  9.16 us
    ppermute x9, waiting for transfers between devices, summed_but_last(): lax.ppermute(values, axis, swaps(axis, mask, stride))  8.92 us
    ppermute x3, starting transfers between devices, exchanged(): lax.ppermute(xlo, 'strike', back('strike'))  7.6 us
    ppermute x3, starting transfers between devices, exchanged(): lax.ppermute(ylo, 'dip', back('dip'))  5.93 us
    pallas_call x1, Pallas kernels, combine(): pl.pallas_call(combine_kernel, in_specs=[VMEM] * 5, out_specs=[HBM] * 2,...  5.2 us
    pallas_call x1, Pallas kernels, pack(): pl.pallas_call(pack_kernel, in_specs=[HBM] * 3, out_specs=[HBM] + [VMEM]...  4.64 us
  transfers between devices with their start and end apart: 28, of which 13 were waited for; matrix products, arithmetic and copies ran while one was open for 0% of the time, Pallas kernels for 26%

profile of v7, /device:TPU:0, one launch (start us, length us, event | category | flops | bytes accessed | tf_op | source)
XLA Modules:
  0.0 87.4 jit_solution(14862272178272478509)
XLA Ops:
  0.6 4.6 %pack_guess.1 = (f32[16,16,32,128]{3,2,1,0:T(8,128)}, f32[16,16,128]{2,1,0:T(8,128)S(1)}, f32[17,32,128]{2,1,0:T(8,128)S(1)}, f32[17,32,128]{2,1,0:T(8,128)S(1)}...) custom-call(s32[16,16,128]{2,1,0:T(8,128)} %class_hbm.1, f32[16]{0:T(128)} %table_hbm.1, ...), custom_call_target="tpu_custom_call" | custom-call | tf_op jit(solution)/shard_map/pack_guess/pallas_call | solution.py:127
  5.3 4.2 %collective-permute-start.1 = (f32[5,32,128]{2,1,0:T(8,128)S(1)}, f32[5,32,128]{2,1,0:T(8,128)S(1)}, u32[]{:S(2)}, u32[]{:S(2)}) collective-permute-start(f32[5,32,128]{2,1,0:T(8,128)S(1)} %get-tuple-element.48), channel_id=1, source_target_pairs={{1,0},{2,1},{3,2},{0,3},{5,4},{6,5},{7,6},{4,7},{9,8},{10,9},{11,1... | collective-permute-start | bytes 245768 | tf_op jit(solution)/shard_map/ppermute | solution.py:550
  9.5 2.8 %collective-permute-start.3 = (f32[17,32,128]{2,1,0:T(8,128)S(1)}, f32[17,32,128]{2,1,0:T(8,128)S(1)}, u32[]{:S(2)}, u32[]{:S(2)}) collective-permute-start(f32[17,32,128]{2,1,0:T(8,128)S(1)} %get-tuple-element.54.refs_1_), channel_id=1, source_target_pairs={{32,0},{64,32},{96,64},{0,96},{33,1},{65,33},{97,65},{1,97},{34,2}... | collective-permute-start | bytes 835592 | tf_op jit(solution)/shard_map/ppermute | solution.py:555
  12.2 1.9 %collective-permute-start.5 = (f32[17,32,128]{2,1,0:T(8,128)S(1)}, f32[17,32,128]{2,1,0:T(8,128)S(1)}, u32[]{:S(2)}, u32[]{:S(2)}) collective-permute-start(f32[17,32,128]{2,1,0:T(8,128)S(1)} %get-tuple-element.56.refs_3_), channel_id=1, source_target_pairs={{4,0},{8,4},{12,8},{16,12},{20,16},{24,20},{28,24},{0,28},{5,1},{9... | collective-permute-start | bytes 835592 | tf_op jit(solution)/shard_map/ppermute | solution.py:557
  14.2 0.9 %collective-permute-done.hzl = f32[5,32,128]{2,1,0:T(8,128)S(1)} collective-permute-done((f32[5,32,128]{2,1,0:T(8,128)S(1)}, f32[5,32,128]{2,1,0:T(8,128)S(1)}, u32[]{:S(2)}, u32[]{:S(2)}) %collective-permute-start) | collective-permute-done | bytes 81952 | tf_op jit(solution)/shard_map/ppermute | solution.py:549
  15.5 9.7 %inner_first.1 = (f32[16,16,32,128]{3,2,1,0:T(8,128)S(1)}, f32[4,32,128]{2,1,0:T(8,128)S(1)}, f32[17,16,128]{2,1,0:T(8,128)S(1)}, f32[16,24,128]{2,1,0:T(8,128)S...) custom-call(f32[16,16,32,128]{3,2,1,0:T(8,128)} %get-tuple-element.47.away.guess_ref, ...), custom_call_target="tpu_custom_call" | custom-call | flops 20971520 | bytes 25165824 | tf_op jit(solution)/shard_map/inner_first/pallas_call | solution.py:499
  25.6 2.1 %collective-permute-start.7 = (f32[4,32,128]{2,1,0:T(8,128)S(1)}, f32[4,32,128]{2,1,0:T(8,128)S(1)}, u32[]{:S(2)}, u32[]{:S(2)}) collective-permute-start(f32[4,32,128]{2,1,0:T(8,128)S(1)} %get-tuple-element.62), channel_id=1, source_target_pairs={{1,0},{2,1},{3,2},{0,3},{5,4},{6,5},{7,6},{4,7},{9,8},{10,9},{11,1... | collective-permute-start | bytes 196616 | tf_op jit(solution)/shard_map/ppermute | solution.py:550
  27.8 1.5 %collective-permute-start.8 = (f32[16,32,128]{2,1,0:T(8,128)S(1)}, f32[16,32,128]{2,1,0:T(8,128)S(1)}, u32[]{:S(2)}, u32[]{:S(2)}) collective-permute-start(f32[16,32,128]{2,1,0:T(8,128)S(1)} %get-tuple-element.72), channel_id=1, source_target_pairs={{0,32},{32,64},{64,96},{96,0},{1,33},{33,65},{65,97},{97,1},{2,34}... | collective-permute-start | bytes 786440 | tf_op jit(solution)/shard_map/ppermute | solution.py:554
  29.2 1.8 %collective-permute-start.9 = (f32[16,32,128]{2,1,0:T(8,128)S(1)}, f32[16,32,128]{2,1,0:T(8,128)S(1)}, u32[]{:S(2)}, u32[]{:S(2)}) collective-permute-start(f32[16,32,128]{2,1,0:T(8,128)S(1)} %get-tuple-element.73), channel_id=1, source_target_pairs={{32,0},{64,32},{96,64},{0,96},{33,1},{65,33},{97,65},{1,97},{34,2}... | collective-permute-start | bytes 786440 | tf_op jit(solution)/shard_map/ppermute | solution.py:555
  31.0 2.1 %collective-permute-start.11 = (f32[16,32,128]{2,1,0:T(8,128)S(1)}, f32[16,32,128]{2,1,0:T(8,128)S(1)}, u32[]{:S(2)}, u32[]{:S(2)}) collective-permute-start(f32[16,32,128]{2,1,0:T(8,128)S(1)} %get-tuple-element.75), channel_id=1, source_target_pairs={{4,0},{8,4},{12,8},{16,12},{20,16},{24,20},{28,24},{0,28},{5,1},{9... | collective-permute-start | bytes 786440 | tf_op jit(solution)/shard_map/ppermute | solution.py:557
  33.2 6.8 %inner_next.1 = (f32[16,16,32,128]{3,2,1,0:T(8,128)S(1)}, f32[4,32,128]{2,1,0:T(8,128)S(1)}, f32[64,128]{1,0:T(8,128)S(1)}) custom-call(f32[16,16,32,128]{3,2,1,0:T(8,128)S(1)} %get-tuple-element.61.refs_0_.refs_1_.one_ref, f32[4,32,128]{2,1,0:T(8,128)S(1)} %collective-permute-done.6.refs_1_, f32[4,32,128]{2,1,0:T(8,128)S(1)} %collective-permute-done.7.refs_2_, ...), custom_call_target="tpu_custom_call" | custom-call | flops 20971520 | bytes 25165824 | tf_op jit(solution)/shard_map/inner_next/pallas_call | solution.py:499
  41.0 2.9 %collective-permute-start.13 = (f32[4,32,128]{2,1,0:T(8,128)S(1)}, f32[4,32,128]{2,1,0:T(8,128)S(1)}, u32[]{:S(2)}, u32[]{:S(2)}) collective-permute-start(f32[4,32,128]{2,1,0:T(8,128)S(1)} %get-tuple-element.79), channel_id=1, source_target_pairs={{1,0},{2,1},{3,2},{0,3},{5,4},{6,5},{7,6},{4,7},{9,8},{10,9},{11,1... | collective-permute-start | bytes 196616 | tf_op jit(solution)/shard_map/ppermute | solution.py:550
  44.0 3.1 %collective-permute-start.15 = (f32[16,32,128]{2,1,0:T(8,128)S(1)}, f32[16,32,128]{2,1,0:T(8,128)S(1)}, u32[]{:S(2)}, u32[]{:S(2)}) collective-permute-start(f32[16,32,128]{2,1,0:T(8,128)S(1)} %get-tuple-element.85), channel_id=1, source_target_pairs={{32,0},{64,32},{96,64},{0,96},{33,1},{65,33},{97,65},{1,97},{34,2}... | collective-permute-start | bytes 786440 | tf_op jit(solution)/shard_map/ppermute | solution.py:555
  47.1 2.0 %collective-permute-start.17 = (f32[16,32,128]{2,1,0:T(8,128)S(1)}, f32[16,32,128]{2,1,0:T(8,128)S(1)}, u32[]{:S(2)}, u32[]{:S(2)}) collective-permute-start(f32[16,32,128]{2,1,0:T(8,128)S(1)} %get-tuple-element.87), channel_id=1, source_target_pairs={{4,0},{8,4},{12,8},{16,12},{20,16},{24,20},{28,24},{0,28},{5,1},{9... | collective-permute-start | bytes 786440 | tf_op jit(solution)/shard_map/ppermute | solution.py:557
  49.3 5.9 %inner_last.1 = (f32[16,16,32,128]{3,2,1,0:T(8,128)S(1)}, f32[64,128]{1,0:T(8,128)S(1)}) custom-call(f32[16,16,32,128]{3,2,1,0:T(8,128)S(1)} %get-tuple-element.78.refs_0_.refs_1_.two_ref, f32[4,32,128]{2,1,0:T(8,128)S(1)} %collective-permute-done.12.refs_1_, f32[4,32,128]{2,1,0:T(8,128)S(1)} %collective-permute-done.13.refs_2_, ...), custom_call_target="tpu_custom_call" | custom-call | flops 20971520 | bytes 25165824 | tf_op jit(solution)/shard_map/inner_last/pallas_call | solution.py:499
  55.2 1.1 %collective-permute-done.16.refs_4_ = f32[16,32,128]{2,1,0:T(8,128)S(1)} collective-permute-done((f32[16,32,128]{2,1,0:T(8,128)S(1)}, f32[16,32,128]{2,1,0:T(8,128)S(1)}, u32[]{:S(2)}, u32[]{:S(2)}) %collective-permute-start.16) | collective-permute-done | bytes 262176 | tf_op jit(solution)/shard_map/ppermute | solution.py:556
  57.1 1.2 %collective-permute-done.18 = f32[32,128]{1,0:T(8,128)S(1)} collective-permute-done((f32[32,128]{1,0:T(8,128)S(1)}, f32[32,128]{1,0:T(8,128)S(1)}, u32[]{:S(2)}, u32[]{:S(2)}) %collective-permute-start.18) | collective-permute-done | bytes 16416 | tf_op jit(solution)/shard_map/ppermute | solution.py:733
  58.2 1.3 %collective-permute-start.21 = (f32[32,128]{1,0:T(8,128)S(1)}, f32[32,128]{1,0:T(8,128)S(1)}, u32[]{:S(2)}, u32[]{:S(2)}) collective-permute-start(f32[32,128]{1,0:T(8,128)S(1)} %add.42), channel_id=1, source_target_pairs={{0,2},{1,3},{2,0},{3,1},{4,6},{5,7},{6,4},{7,5},{8,10},{9,11},{10,... | collective-permute-start | bytes 49160 | tf_op jit(solution)/shard_map/ppermute | solution.py:738
  59.5 1.5 %collective-permute-start.20 = (f32[32,128]{1,0:T(8,128)S(1)}, f32[32,128]{1,0:T(8,128)S(1)}, u32[]{:S(2)}, u32[]{:S(2)}) collective-permute-start(f32[32,128]{1,0:T(8,128)S(1)} %add.42), channel_id=1, source_target_pairs={{0,3},{1,2},{2,1},{3,0},{4,7},{5,6},{6,5},{7,4},{8,11},{9,10},{10,... | collective-permute-start | bytes 49160 | tf_op jit(solution)/shard_map/ppermute | solution.py:738
  61.0 0.8 collective-permute-start.19
  61.8 1.8 %collective-permute-done.21 = f32[32,128]{1,0:T(8,128)S(1)} collective-permute-done((f32[32,128]{1,0:T(8,128)S(1)}, f32[32,128]{1,0:T(8,128)S(1)}, u32[]{:S(2)}, u32[]{:S(2)}) %collective-permute-start.21) | collective-permute-done | bytes 16416 | tf_op jit(solution)/shard_map/ppermute | solution.py:738
  63.6 0.9 %collective-permute-done.20 = f32[32,128]{1,0:T(8,128)S(1)} collective-permute-done((f32[32,128]{1,0:T(8,128)S(1)}, f32[32,128]{1,0:T(8,128)S(1)}, u32[]{:S(2)}, u32[]{:S(2)}) %collective-permute-start.20) | collective-permute-done | bytes 16416 | tf_op jit(solution)/shard_map/ppermute | solution.py:738
  64.8 1.0 %collective-permute-start.24 = (f32[32,128]{1,0:T(8,128)S(1)}, f32[32,128]{1,0:T(8,128)S(1)}, u32[]{:S(2)}, u32[]{:S(2)}) collective-permute-start(f32[32,128]{1,0:T(8,128)S(1)} %add_add_fusion.1), channel_id=1, source_target_pairs={{0,16},{4,20},{8,24},{12,28},{16,0},{20,4},{24,8},{28,12},{1,17},{... | collective-permute-start | bytes 49160 | tf_op jit(solution)/shard_map/ppermute | solution.py:738
  65.7 1.2 %collective-permute-start.23 = (f32[32,128]{1,0:T(8,128)S(1)}, f32[32,128]{1,0:T(8,128)S(1)}, u32[]{:S(2)}, u32[]{:S(2)}) collective-permute-start(f32[32,128]{1,0:T(8,128)S(1)} %add_add_fusion.1), channel_id=1, source_target_pairs={{0,24},{4,28},{8,16},{12,20},{16,8},{20,12},{24,0},{28,4},{1,25},{... | collective-permute-start | bytes 49160 | tf_op jit(solution)/shard_map/ppermute | solution.py:738
  67.0 1.3 %collective-permute-start.22 = (f32[32,128]{1,0:T(8,128)S(1)}, f32[32,128]{1,0:T(8,128)S(1)}, u32[]{:S(2)}, u32[]{:S(2)}) collective-permute-start(f32[32,128]{1,0:T(8,128)S(1)} %add_add_fusion.1), channel_id=1, source_target_pairs={{0,8},{4,12},{8,0},{12,4},{16,24},{20,28},{24,16},{28,20},{1,9},{5... | collective-permute-start | bytes 49160 | tf_op jit(solution)/shard_map/ppermute | solution.py:738
  68.2 1.8 %collective-permute-done.24 = f32[32,128]{1,0:T(8,128)S(1)} collective-permute-done((f32[32,128]{1,0:T(8,128)S(1)}, f32[32,128]{1,0:T(8,128)S(1)}, u32[]{:S(2)}, u32[]{:S(2)}) %collective-permute-start.24) | collective-permute-done | bytes 16416 | tf_op jit(solution)/shard_map/ppermute | solution.py:738
  70.7 2.3 %collective-permute-start.27 = (f32[32,128]{1,0:T(8,128)S(1)}, f32[32,128]{1,0:T(8,128)S(1)}, u32[]{:S(2)}, u32[]{:S(2)}) collective-permute-start(f32[32,128]{1,0:T(8,128)S(1)} %add_add_fusion.refs_0_), channel_id=1, source_target_pairs={{0,64},{32,96},{64,0},{96,32},{1,65},{33,97},{65,1},{97,33},{2,66}... | collective-permute-start | bytes 49160 | tf_op jit(solution)/shard_map/ppermute | solution.py:738
  73.0 1.1 %collective-permute-start.26 = (f32[32,128]{1,0:T(8,128)S(1)}, f32[32,128]{1,0:T(8,128)S(1)}, u32[]{:S(2)}, u32[]{:S(2)}) collective-permute-start(f32[32,128]{1,0:T(8,128)S(1)} %add_add_fusion.refs_0_), channel_id=1, source_target_pairs={{0,96},{32,64},{64,32},{96,0},{1,97},{33,65},{65,33},{97,1},{2,98}... | collective-permute-start | bytes 49160 | tf_op jit(solution)/shard_map/ppermute | solution.py:738
  74.5 1.5 %collective-permute-done.27.refs_3_ = f32[32,128]{1,0:T(8,128)S(1)} collective-permute-done((f32[32,128]{1,0:T(8,128)S(1)}, f32[32,128]{1,0:T(8,128)S(1)}, u32[]{:S(2)}, u32[]{:S(2)}) %collective-permute-start.27) | collective-permute-done | bytes 16416 | tf_op jit(solution)/shard_map/ppermute | solution.py:738
  76.0 2.0 %collective-permute-done.26.refs_2_ = f32[32,128]{1,0:T(8,128)S(1)} collective-permute-done((f32[32,128]{1,0:T(8,128)S(1)}, f32[32,128]{1,0:T(8,128)S(1)}, u32[]{:S(2)}, u32[]{:S(2)}) %collective-permute-start.26) | collective-permute-done | bytes 16416 | tf_op jit(solution)/shard_map/ppermute | solution.py:738
  78.0 4.0 %solve_small.1.mix_ref = f32[64,128]{1,0:T(8,128)S(1)} custom-call(f32[32,128]{1,0:T(8,128)S(1)} %add_add_fusion.refs_0_, f32[32,128]{1,0:T(8,128)S(1)} %collective-permute-done.25.refs_1_, f32[32,128]{1,0:T(8,128)S(1)} %collective-permute-done.26.refs_2_, f32[32,128]{1,0:T(8,128)S(1)} %collective-permute-done.27.refs_3_), custom_call_target="tpu_custom_call" | custom-call | tf_op jit(solution)/shard_map/solve_small/pallas_call | solution.py:618
  82.0 5.2 %combine_fields.1 = (f32[32,16,16,128]{3,2,1,0:T(8,128)}, f32[32,16,16,128]{3,2,1,0:T(8,128)}) custom-call(f32[64,128]{1,0:T(8,128)S(1)} %solve_small.1.mix_ref, f32[16,16,32,128]{3,2,1,0:T(8,128)S(1)} %copy-done, f32[16,16,32,128]{3,2,1,0:T(8,128)S(1)} %get-tuple-element.61.refs_0_.refs_1_.one_ref, ...), custom_call_target="tpu_custom_call" | custom-call | tf_op jit(solution)/shard_map/combine_fields/pallas_call | solution.py:709
  (48 shorter events, 4.3 us)
Async XLA Ops:
  0.6 13.5 %copy-start.1 = (s32[32]{0:T(128)S(1)}, s32[32]{0:T(128)}, u32[]{:S(2)}) copy-start(s32[32]{0:T(128)} %param.6) | copy-start | bytes 388
  5.3 8.9 %collective-permute-start.1 = (f32[5,32,128]{2,1,0:T(8,128)S(1)}, f32[5,32,128]{2,1,0:T(8,128)S(1)}, u32[]{:S(2)}, u32[]{:S(2)}) collective-permute-start(f32[5,32,128]{2,1,0:T(8,128)S(1)} %get-tuple-element.48), channel_id=1, source_target_pairs={{1,0},{2,1},{3,2},{0,3},{5,4},{6,5},{7,6},{4,7},{9,8},{10,9},{11,1... | collective-permute-start | bytes 245768 | tf_op jit(solution)/shard_map/ppermute | solution.py:550
  9.5 5.7 %collective-permute-start = (f32[5,32,128]{2,1,0:T(8,128)S(1)}, f32[5,32,128]{2,1,0:T(8,128)S(1)}, u32[]{:S(2)}, u32[]{:S(2)}) collective-permute-start(f32[5,32,128]{2,1,0:T(8,128)S(1)} %get-tuple-element.48), channel_id=1, source_target_pairs={{0,1},{1,2},{2,3},{3,0},{4,5},{5,6},{6,7},{7,4},{8,9},{9,10},{10,1... | collective-permute-start | bytes 245768 | tf_op jit(solution)/shard_map/ppermute | solution.py:549
  9.5 15.7 %collective-permute-start.3 = (f32[17,32,128]{2,1,0:T(8,128)S(1)}, f32[17,32,128]{2,1,0:T(8,128)S(1)}, u32[]{:S(2)}, u32[]{:S(2)}) collective-permute-start(f32[17,32,128]{2,1,0:T(8,128)S(1)} %get-tuple-element.54.refs_1_), channel_id=1, source_target_pairs={{32,0},{64,32},{96,64},{0,96},{33,1},{65,33},{97,65},{1,97},{34,2}... | collective-permute-start | bytes 835592 | tf_op jit(solution)/shard_map/ppermute | solution.py:555
  12.2 13.0 %collective-permute-start.2 = (f32[17,32,128]{2,1,0:T(8,128)S(1)}, f32[17,32,128]{2,1,0:T(8,128)S(1)}, u32[]{:S(2)}, u32[]{:S(2)}) collective-permute-start(f32[17,32,128]{2,1,0:T(8,128)S(1)} %get-tuple-element.55.refs_2_), channel_id=1, source_target_pairs={{0,32},{32,64},{64,96},{96,0},{1,33},{33,65},{65,97},{97,1},{2,34}... | collective-permute-start | bytes 835592 | tf_op jit(solution)/shard_map/ppermute | solution.py:554
  12.2 13.0 %collective-permute-start.5 = (f32[17,32,128]{2,1,0:T(8,128)S(1)}, f32[17,32,128]{2,1,0:T(8,128)S(1)}, u32[]{:S(2)}, u32[]{:S(2)}) collective-permute-start(f32[17,32,128]{2,1,0:T(8,128)S(1)} %get-tuple-element.56.refs_3_), channel_id=1, source_target_pairs={{4,0},{8,4},{12,8},{16,12},{20,16},{24,20},{28,24},{0,28},{5,1},{9... | collective-permute-start | bytes 835592 | tf_op jit(solution)/shard_map/ppermute | solution.py:557
  15.1 10.1 %collective-permute-start.4 = (f32[17,32,128]{2,1,0:T(8,128)S(1)}, f32[17,32,128]{2,1,0:T(8,128)S(1)}, u32[]{:S(2)}, u32[]{:S(2)}) collective-permute-start(f32[17,32,128]{2,1,0:T(8,128)S(1)} %get-tuple-element.57.refs_4_), channel_id=1, source_target_pairs={{0,4},{4,8},{8,12},{12,16},{16,20},{20,24},{24,28},{28,0},{1,5},{5... | collective-permute-start | bytes 835592 | tf_op jit(solution)/shard_map/ppermute | solution.py:556
  25.6 7.4 %collective-permute-start.7 = (f32[4,32,128]{2,1,0:T(8,128)S(1)}, f32[4,32,128]{2,1,0:T(8,128)S(1)}, u32[]{:S(2)}, u32[]{:S(2)}) collective-permute-start(f32[4,32,128]{2,1,0:T(8,128)S(1)} %get-tuple-element.62), channel_id=1, source_target_pairs={{1,0},{2,1},{3,2},{0,3},{5,4},{6,5},{7,6},{4,7},{9,8},{10,9},{11,1... | collective-permute-start | bytes 196616 | tf_op jit(solution)/shard_map/ppermute | solution.py:550
  27.8 5.5 %collective-permute-start.6 = (f32[4,32,128]{2,1,0:T(8,128)S(1)}, f32[4,32,128]{2,1,0:T(8,128)S(1)}, u32[]{:S(2)}, u32[]{:S(2)}) collective-permute-start(f32[4,32,128]{2,1,0:T(8,128)S(1)} %get-tuple-element.62), channel_id=1, source_target_pairs={{0,1},{1,2},{2,3},{3,0},{4,5},{5,6},{6,7},{7,4},{8,9},{9,10},{10,1... | collective-permute-start | bytes 196616 | tf_op jit(solution)/shard_map/ppermute | solution.py:549
  27.8 12.3 %collective-permute-start.8 = (f32[16,32,128]{2,1,0:T(8,128)S(1)}, f32[16,32,128]{2,1,0:T(8,128)S(1)}, u32[]{:S(2)}, u32[]{:S(2)}) collective-permute-start(f32[16,32,128]{2,1,0:T(8,128)S(1)} %get-tuple-element.72), channel_id=1, source_target_pairs={{0,32},{32,64},{64,96},{96,0},{1,33},{33,65},{65,97},{97,1},{2,34}... | collective-permute-start | bytes 786440 | tf_op jit(solution)/shard_map/ppermute | solution.py:554
  29.2 10.8 %collective-permute-start.9 = (f32[16,32,128]{2,1,0:T(8,128)S(1)}, f32[16,32,128]{2,1,0:T(8,128)S(1)}, u32[]{:S(2)}, u32[]{:S(2)}) collective-permute-start(f32[16,32,128]{2,1,0:T(8,128)S(1)} %get-tuple-element.73), channel_id=1, source_target_pairs={{32,0},{64,32},{96,64},{0,96},{33,1},{65,33},{97,65},{1,97},{34,2}... | collective-permute-start | bytes 786440 | tf_op jit(solution)/shard_map/ppermute | solution.py:555
  31.0 9.1 %collective-permute-start.11 = (f32[16,32,128]{2,1,0:T(8,128)S(1)}, f32[16,32,128]{2,1,0:T(8,128)S(1)}, u32[]{:S(2)}, u32[]{:S(2)}) collective-permute-start(f32[16,32,128]{2,1,0:T(8,128)S(1)} %get-tuple-element.75), channel_id=1, source_target_pairs={{4,0},{8,4},{12,8},{16,12},{20,16},{24,20},{28,24},{0,28},{5,1},{9... | collective-permute-start | bytes 786440 | tf_op jit(solution)/shard_map/ppermute | solution.py:557
  33.2 7.0 %collective-permute-start.10 = (f32[16,32,128]{2,1,0:T(8,128)S(1)}, f32[16,32,128]{2,1,0:T(8,128)S(1)}, u32[]{:S(2)}, u32[]{:S(2)}) collective-permute-start(f32[16,32,128]{2,1,0:T(8,128)S(1)} %get-tuple-element.74), channel_id=1, source_target_pairs={{0,4},{4,8},{8,12},{12,16},{16,20},{20,24},{24,28},{28,0},{1,5},{5... | collective-permute-start | bytes 786440 | tf_op jit(solution)/shard_map/ppermute | solution.py:556
  41.0 8.1 %collective-permute-start.13 = (f32[4,32,128]{2,1,0:T(8,128)S(1)}, f32[4,32,128]{2,1,0:T(8,128)S(1)}, u32[]{:S(2)}, u32[]{:S(2)}) collective-permute-start(f32[4,32,128]{2,1,0:T(8,128)S(1)} %get-tuple-element.79), channel_id=1, source_target_pairs={{1,0},{2,1},{3,2},{0,3},{5,4},{6,5},{7,6},{4,7},{9,8},{10,9},{11,1... | collective-permute-start | bytes 196616 | tf_op jit(solution)/shard_map/ppermute | solution.py:550
  43.8 5.5 %collective-permute-start.12 = (f32[4,32,128]{2,1,0:T(8,128)S(1)}, f32[4,32,128]{2,1,0:T(8,128)S(1)}, u32[]{:S(2)}, u32[]{:S(2)}) collective-permute-start(f32[4,32,128]{2,1,0:T(8,128)S(1)} %get-tuple-element.79), channel_id=1, source_target_pairs={{0,1},{1,2},{2,3},{3,0},{4,5},{5,6},{6,7},{7,4},{8,9},{9,10},{10,1... | collective-permute-start | bytes 196616 | tf_op jit(solution)/shard_map/ppermute | solution.py:549
  43.8 11.4 %collective-permute-start.14 = (f32[16,32,128]{2,1,0:T(8,128)S(1)}, f32[16,32,128]{2,1,0:T(8,128)S(1)}, u32[]{:S(2)}, u32[]{:S(2)}) collective-permute-start(f32[16,32,128]{2,1,0:T(8,128)S(1)} %get-tuple-element.84), channel_id=1, source_target_pairs={{0,32},{32,64},{64,96},{96,0},{1,33},{33,65},{65,97},{97,1},{2,34}... | collective-permute-start | bytes 786440 | tf_op jit(solution)/shard_map/ppermute | solution.py:554
  44.0 11.2 %collective-permute-start.15 = (f32[16,32,128]{2,1,0:T(8,128)S(1)}, f32[16,32,128]{2,1,0:T(8,128)S(1)}, u32[]{:S(2)}, u32[]{:S(2)}) collective-permute-start(f32[16,32,128]{2,1,0:T(8,128)S(1)} %get-tuple-element.85), channel_id=1, source_target_pairs={{32,0},{64,32},{96,64},{0,96},{33,1},{65,33},{97,65},{1,97},{34,2}... | collective-permute-start | bytes 786440 | tf_op jit(solution)/shard_map/ppermute | solution.py:555
  47.1 8.1 %collective-permute-start.17 = (f32[16,32,128]{2,1,0:T(8,128)S(1)}, f32[16,32,128]{2,1,0:T(8,128)S(1)}, u32[]{:S(2)}, u32[]{:S(2)}) collective-permute-start(f32[16,32,128]{2,1,0:T(8,128)S(1)} %get-tuple-element.87), channel_id=1, source_target_pairs={{4,0},{8,4},{12,8},{16,12},{20,16},{24,20},{28,24},{0,28},{5,1},{9... | collective-permute-start | bytes 786440 | tf_op jit(solution)/shard_map/ppermute | solution.py:557
  49.3 7.0 %collective-permute-start.16 = (f32[16,32,128]{2,1,0:T(8,128)S(1)}, f32[16,32,128]{2,1,0:T(8,128)S(1)}, u32[]{:S(2)}, u32[]{:S(2)}) collective-permute-start(f32[16,32,128]{2,1,0:T(8,128)S(1)} %get-tuple-element.86), channel_id=1, source_target_pairs={{0,4},{4,8},{8,12},{12,16},{16,20},{20,24},{24,28},{28,0},{1,5},{5... | collective-permute-start | bytes 786440 | tf_op jit(solution)/shard_map/ppermute | solution.py:556
  56.3 25.7 %copy-start = (f32[16,16,32,128]{3,2,1,0:T(8,128)S(1)}, f32[16,16,32,128]{3,2,1,0:T(8,128)}, u32[]{:S(2)}) copy-start(f32[16,16,32,128]{3,2,1,0:T(8,128)} %get-tuple-element.47.away.guess_ref) | copy-start | bytes 12582916
  57.0 1.2 %collective-permute-start.18 = (f32[32,128]{1,0:T(8,128)S(1)}, f32[32,128]{1,0:T(8,128)S(1)}, u32[]{:S(2)}, u32[]{:S(2)}) collective-permute-start(f32[32,128]{1,0:T(8,128)S(1)} %get-tuple-element.90), channel_id=1, source_target_pairs={{0,4},{4,0},{8,12},{12,8},{16,20},{20,16},{24,28},{28,24},{1,5},{5... | collective-permute-start | bytes 49160 | tf_op jit(solution)/shard_map/ppermute | solution.py:733
  58.2 5.3 %collective-permute-start.21 = (f32[32,128]{1,0:T(8,128)S(1)}, f32[32,128]{1,0:T(8,128)S(1)}, u32[]{:S(2)}, u32[]{:S(2)}) collective-permute-start(f32[32,128]{1,0:T(8,128)S(1)} %add.42), channel_id=1, source_target_pairs={{0,2},{1,3},{2,0},{3,1},{4,6},{5,7},{6,4},{7,5},{8,10},{9,11},{10,... | collective-permute-start | bytes 49160 | tf_op jit(solution)/shard_map/ppermute | solution.py:738
  59.5 4.9 %collective-permute-start.20 = (f32[32,128]{1,0:T(8,128)S(1)}, f32[32,128]{1,0:T(8,128)S(1)}, u32[]{:S(2)}, u32[]{:S(2)}) collective-permute-start(f32[32,128]{1,0:T(8,128)S(1)} %add.42), channel_id=1, source_target_pairs={{0,3},{1,2},{2,1},{3,0},{4,7},{5,6},{6,5},{7,4},{8,11},{9,10},{10,... | collective-permute-start | bytes 49160 | tf_op jit(solution)/shard_map/ppermute | solution.py:738
  61.0 3.7 %collective-permute-start.19 = (f32[32,128]{1,0:T(8,128)S(1)}, f32[32,128]{1,0:T(8,128)S(1)}, u32[]{:S(2)}, u32[]{:S(2)}) collective-permute-start(f32[32,128]{1,0:T(8,128)S(1)} %add.42), channel_id=1, source_target_pairs={{0,1},{1,0},{2,3},{3,2},{4,5},{5,4},{6,7},{7,6},{8,9},{9,8},{10,11... | collective-permute-start | bytes 49160 | tf_op jit(solution)/shard_map/ppermute | solution.py:738
  64.8 5.2 %collective-permute-start.24 = (f32[32,128]{1,0:T(8,128)S(1)}, f32[32,128]{1,0:T(8,128)S(1)}, u32[]{:S(2)}, u32[]{:S(2)}) collective-permute-start(f32[32,128]{1,0:T(8,128)S(1)} %add_add_fusion.1), channel_id=1, source_target_pairs={{0,16},{4,20},{8,24},{12,28},{16,0},{20,4},{24,8},{28,12},{1,17},{... | collective-permute-start | bytes 49160 | tf_op jit(solution)/shard_map/ppermute | solution.py:738
  65.7 5.0 %collective-permute-start.23 = (f32[32,128]{1,0:T(8,128)S(1)}, f32[32,128]{1,0:T(8,128)S(1)}, u32[]{:S(2)}, u32[]{:S(2)}) collective-permute-start(f32[32,128]{1,0:T(8,128)S(1)} %add_add_fusion.1), channel_id=1, source_target_pairs={{0,24},{4,28},{8,16},{12,20},{16,8},{20,12},{24,0},{28,4},{1,25},{... | collective-permute-start | bytes 49160 | tf_op jit(solution)/shard_map/ppermute | solution.py:738
  67.0 3.7 %collective-permute-start.22 = (f32[32,128]{1,0:T(8,128)S(1)}, f32[32,128]{1,0:T(8,128)S(1)}, u32[]{:S(2)}, u32[]{:S(2)}) collective-permute-start(f32[32,128]{1,0:T(8,128)S(1)} %add_add_fusion.1), channel_id=1, source_target_pairs={{0,8},{4,12},{8,0},{12,4},{16,24},{20,28},{24,16},{28,20},{1,9},{5... | collective-permute-start | bytes 49160 | tf_op jit(solution)/shard_map/ppermute | solution.py:738
  70.7 5.3 %collective-permute-start.27 = (f32[32,128]{1,0:T(8,128)S(1)}, f32[32,128]{1,0:T(8,128)S(1)}, u32[]{:S(2)}, u32[]{:S(2)}) collective-permute-start(f32[32,128]{1,0:T(8,128)S(1)} %add_add_fusion.refs_0_), channel_id=1, source_target_pairs={{0,64},{32,96},{64,0},{96,32},{1,65},{33,97},{65,1},{97,33},{2,66}... | collective-permute-start | bytes 49160 | tf_op jit(solution)/shard_map/ppermute | solution.py:738
  73.0 4.9 %collective-permute-start.26 = (f32[32,128]{1,0:T(8,128)S(1)}, f32[32,128]{1,0:T(8,128)S(1)}, u32[]{:S(2)}, u32[]{:S(2)}) collective-permute-start(f32[32,128]{1,0:T(8,128)S(1)} %add_add_fusion.refs_0_), channel_id=1, source_target_pairs={{0,96},{32,64},{64,32},{96,0},{1,97},{33,65},{65,33},{97,1},{2,98}... | collective-permute-start | bytes 49160 | tf_op jit(solution)/shard_map/ppermute | solution.py:738
  74.1 3.9 %collective-permute-start.25 = (f32[32,128]{1,0:T(8,128)S(1)}, f32[32,128]{1,0:T(8,128)S(1)}, u32[]{:S(2)}, u32[]{:S(2)}) collective-permute-start(f32[32,128]{1,0:T(8,128)S(1)} %add_add_fusion.refs_0_), channel_id=1, source_target_pairs={{0,32},{32,0},{64,96},{96,64},{1,33},{33,1},{65,97},{97,65},{2,34}... | collective-permute-start | bytes 49160 | tf_op jit(solution)/shard_map/ppermute | solution.py:738

commit v8 on v7

--- a/solution.py
+++ b/solution.py
@@ -54,7 +54,9 @@
     columns, nx, ny, nz = guess_hbm.shape
 
     def plane(x):
-        return pltpu.make_async_copy(guess_hbm.at[:, x], guess.at[x], plane_sem.at[x])
+        return pltpu.make_async_copy(
+            guess_hbm.at[:, x], guess.at[x, 0:columns], plane_sem.at[x]
+        )
 
     def leaving(x):
         return pltpu.make_async_copy(field_ref.at[x], field_hbm.at[x], field_sem.at[x])
@@ -94,7 +96,7 @@
             plane(2 * pair + step).wait()
         for step in range(2):
             x = 2 * pair + step
-            flat = guess.at[x].reshape(columns * ny, nz)
+            flat = guess.at[x].reshape((columns + 1) * ny, nz)
             ends = jnp.zeros((columns, nz), F32)
             for y in range(ny):
                 cells = flat[pl.ds(y, columns, stride=ny), :]
@@ -140,7 +142,7 @@
         scratch_shapes=[
             pltpu.VMEM((nx, ny, nz), jnp.int32),
             pltpu.SMEM(perm_table.shape, F32),
-            pltpu.VMEM((nx, columns, ny, nz), F32),
+            pltpu.VMEM((nx, columns + 1, ny, nz), F32),
             pltpu.VMEM((nx, ny, columns, nz), F32),
             pltpu.SemaphoreType.DMA((nx,)),
             pltpu.SemaphoreType.DMA((nx,)),
@@ -650,7 +652,7 @@
             for half in range(ny // 8):
                 copies.append(
                     pltpu.make_async_copy(
-                        held.at[slot, half],
+                        held.at[slot, half, 0:columns],
                         away.at[:, x, 8 * half : 8 * half + 8],
                         sem.at[place, half, slot],
                     )
@@ -678,8 +680,8 @@
         for step in range(2):
             x = 2 * pair + step
             slot = lax.rem(x, slots)
-            solution_rows = solution.at[slot].reshape(columns * ny, nz)
-            residual_rows = residual.at[slot].reshape(columns * ny, nz)
+            solution_rows = solution.at[slot].reshape((columns + 1) * ny, nz)
+            residual_rows = residual.at[slot].reshape((columns + 1) * ny, nz)
             for y in range(0, ny, 2):
                 fields = [
                     jnp.concatenate([ref[x, y], ref[x, y + 1]], axis=1)
@@ -689,7 +691,7 @@
                 mixed = mixed[0:64] + mixed[64:128]
                 for z in range(2):
                     own = y + z
-                    rows = pl.ds((own // 8) * 8 * columns + own % 8, columns, stride=8)
+                    rows = pl.ds((own // 8) * 8 * (columns + 1) + own % 8, columns, stride=8)
                     part = mixed[:, z * nz : (z + 1) * nz]
                     solution_rows[rows, :] = guess_ref[x, own] + part[0:32]
                     residual_rows[rows, :] = one_ref[x, own] + part[32:64]
@@ -712,8 +714,8 @@
         out_specs=[HBM] * 2,
         out_shape=[jax.ShapeDtypeStruct((columns, nx, ny, nz), F32)] * 2,
         scratch_shapes=[
-            pltpu.VMEM((8, ny // 8, columns, 8, nz), F32),
-            pltpu.VMEM((8, ny // 8, columns, 8, nz), F32),
+            pltpu.VMEM((8, ny // 8, columns + 1, 8, nz), F32),
+            pltpu.VMEM((8, ny // 8, columns + 1, 8, nz), F32),
             pltpu.SemaphoreType.DMA((2, ny // 8, 8)),
         ],
         compiler_params=params(),

time: 87.5 us -> 87.5 us (level)
  no operation moved by 1% of the time
where the time goes in v8:
time: 87.5 us; the launch traced here: 87.4 us
  Pallas kernels  38.1 us (44%)
  starting transfers between devices  35.2 us (40%)
  waiting for transfers between devices  12.8 us (15%)
  between operations  1.01 us (1%)
    pallas_call x3, Pallas kernels, inner_part(): pl.pallas_call(first_kernel if first else functools.partial(inner_kernel,...  22.4 us
    ppermute x9, starting transfers between devices, summed_but_last(): lax.ppermute(values, axis, swaps(axis, mask, stride))  10.8 us
    ppermute x3, starting transfers between devices, exchanged(): lax.ppermute(ends, 'layer', back('layer'))  9.17 us
    ppermute x9, waiting for transfers between devices, summed_but_last(): lax.ppermute(values, axis, swaps(axis, mask, stride))  8.92 us
    ppermute x3, starting transfers between devices, exchanged(): lax.ppermute(xlo, 'strike', back('strike'))  7.61 us
    ppermute x3, starting transfers between devices, exchanged(): lax.ppermute(ylo, 'dip', back('dip'))  5.93 us
    pallas_call x1, Pallas kernels, combine(): pl.pallas_call(combine_kernel, in_specs=[VMEM] * 5, out_specs=[HBM] * 2,...  5.21 us
    pallas_call x1, Pallas kernels, pack(): pl.pallas_call(pack_kernel, in_specs=[HBM] * 3, out_specs=[HBM] + [VMEM]...  4.66 us
  transfers between devices with their start and end apart: 28, of which 13 were waited for; matrix products, arithmetic and copies ran while one was open for 0% of the time, Pallas kernels for 26%

profile of v8, /device:TPU:0, one launch (start us, length us, event | category | flops | bytes accessed | tf_op | source)
XLA Modules:
  0.0 87.4 jit_solution(14482828665412488070)
XLA Ops:
  0.6 4.7 %pack_guess.1 = (f32[16,16,32,128]{3,2,1,0:T(8,128)}, f32[16,16,128]{2,1,0:T(8,128)S(1)}, f32[17,32,128]{2,1,0:T(8,128)S(1)}, f32[17,32,128]{2,1,0:T(8,128)S(1)}...) custom-call(s32[16,16,128]{2,1,0:T(8,128)} %class_hbm.1, f32[16]{0:T(128)} %table_hbm.1, ...), custom_call_target="tpu_custom_call" | custom-call | tf_op jit(solution)/shard_map/pack_guess/pallas_call | solution.py:129
  5.3 4.2 %collective-permute-start.1 = (f32[5,32,128]{2,1,0:T(8,128)S(1)}, f32[5,32,128]{2,1,0:T(8,128)S(1)}, u32[]{:S(2)}, u32[]{:S(2)}) collective-permute-start(f32[5,32,128]{2,1,0:T(8,128)S(1)} %get-tuple-element.48), channel_id=1, source_target_pairs={{1,0},{2,1},{3,2},{0,3},{5,4},{6,5},{7,6},{4,7},{9,8},{10,9},{11,1... | collective-permute-start | bytes 245768 | tf_op jit(solution)/shard_map/ppermute | solution.py:552
  9.5 2.8 %collective-permute-start.3 = (f32[17,32,128]{2,1,0:T(8,128)S(1)}, f32[17,32,128]{2,1,0:T(8,128)S(1)}, u32[]{:S(2)}, u32[]{:S(2)}) collective-permute-start(f32[17,32,128]{2,1,0:T(8,128)S(1)} %get-tuple-element.54.refs_1_), channel_id=1, source_target_pairs={{32,0},{64,32},{96,64},{0,96},{33,1},{65,33},{97,65},{1,97},{34,2}... | collective-permute-start | bytes 835592 | tf_op jit(solution)/shard_map/ppermute | solution.py:557
  12.3 1.9 %collective-permute-start.5 = (f32[17,32,128]{2,1,0:T(8,128)S(1)}, f32[17,32,128]{2,1,0:T(8,128)S(1)}, u32[]{:S(2)}, u32[]{:S(2)}) collective-permute-start(f32[17,32,128]{2,1,0:T(8,128)S(1)} %get-tuple-element.56.refs_3_), channel_id=1, source_target_pairs={{4,0},{8,4},{12,8},{16,12},{20,16},{24,20},{28,24},{0,28},{5,1},{9... | collective-permute-start | bytes 835592 | tf_op jit(solution)/shard_map/ppermute | solution.py:559
  14.2 0.9 %collective-permute-done.hzl = f32[5,32,128]{2,1,0:T(8,128)S(1)} collective-permute-done((f32[5,32,128]{2,1,0:T(8,128)S(1)}, f32[5,32,128]{2,1,0:T(8,128)S(1)}, u32[]{:S(2)}, u32[]{:S(2)}) %collective-permute-start) | collective-permute-done | bytes 81952 | tf_op jit(solution)/shard_map/ppermute | solution.py:551
  15.5 9.7 %inner_first.1 = (f32[16,16,32,128]{3,2,1,0:T(8,128)S(1)}, f32[4,32,128]{2,1,0:T(8,128)S(1)}, f32[17,16,128]{2,1,0:T(8,128)S(1)}, f32[16,24,128]{2,1,0:T(8,128)S...) custom-call(f32[16,16,32,128]{3,2,1,0:T(8,128)} %get-tuple-element.47.away.guess_ref, ...), custom_call_target="tpu_custom_call" | custom-call | flops 20971520 | bytes 25165824 | tf_op jit(solution)/shard_map/inner_first/pallas_call | solution.py:501
  25.7 2.1 %collective-permute-start.7 = (f32[4,32,128]{2,1,0:T(8,128)S(1)}, f32[4,32,128]{2,1,0:T(8,128)S(1)}, u32[]{:S(2)}, u32[]{:S(2)}) collective-permute-start(f32[4,32,128]{2,1,0:T(8,128)S(1)} %get-tuple-element.62), channel_id=1, source_target_pairs={{1,0},{2,1},{3,2},{0,3},{5,4},{6,5},{7,6},{4,7},{9,8},{10,9},{11,1... | collective-permute-start | bytes 196616 | tf_op jit(solution)/shard_map/ppermute | solution.py:552
  27.8 1.5 %collective-permute-start.8 = (f32[16,32,128]{2,1,0:T(8,128)S(1)}, f32[16,32,128]{2,1,0:T(8,128)S(1)}, u32[]{:S(2)}, u32[]{:S(2)}) collective-permute-start(f32[16,32,128]{2,1,0:T(8,128)S(1)} %get-tuple-element.72), channel_id=1, source_target_pairs={{0,32},{32,64},{64,96},{96,0},{1,33},{33,65},{65,97},{97,1},{2,34}... | collective-permute-start | bytes 786440 | tf_op jit(solution)/shard_map/ppermute | solution.py:556
  29.3 1.8 %collective-permute-start.9 = (f32[16,32,128]{2,1,0:T(8,128)S(1)}, f32[16,32,128]{2,1,0:T(8,128)S(1)}, u32[]{:S(2)}, u32[]{:S(2)}) collective-permute-start(f32[16,32,128]{2,1,0:T(8,128)S(1)} %get-tuple-element.73), channel_id=1, source_target_pairs={{32,0},{64,32},{96,64},{0,96},{33,1},{65,33},{97,65},{1,97},{34,2}... | collective-permute-start | bytes 786440 | tf_op jit(solution)/shard_map/ppermute | solution.py:557
  31.0 2.1 %collective-permute-start.11 = (f32[16,32,128]{2,1,0:T(8,128)S(1)}, f32[16,32,128]{2,1,0:T(8,128)S(1)}, u32[]{:S(2)}, u32[]{:S(2)}) collective-permute-start(f32[16,32,128]{2,1,0:T(8,128)S(1)} %get-tuple-element.75), channel_id=1, source_target_pairs={{4,0},{8,4},{12,8},{16,12},{20,16},{24,20},{28,24},{0,28},{5,1},{9... | collective-permute-start | bytes 786440 | tf_op jit(solution)/shard_map/ppermute | solution.py:559
  33.3 6.8 %inner_next.1 = (f32[16,16,32,128]{3,2,1,0:T(8,128)S(1)}, f32[4,32,128]{2,1,0:T(8,128)S(1)}, f32[64,128]{1,0:T(8,128)S(1)}) custom-call(f32[16,16,32,128]{3,2,1,0:T(8,128)S(1)} %get-tuple-element.61.refs_0_.refs_1_.one_ref, f32[4,32,128]{2,1,0:T(8,128)S(1)} %collective-permute-done.6.refs_1_, f32[4,32,128]{2,1,0:T(8,128)S(1)} %collective-permute-done.7.refs_2_, ...), custom_call_target="tpu_custom_call" | custom-call | flops 20971520 | bytes 25165824 | tf_op jit(solution)/shard_map/inner_next/pallas_call | solution.py:501
  41.0 2.9 %collective-permute-start.13 = (f32[4,32,128]{2,1,0:T(8,128)S(1)}, f32[4,32,128]{2,1,0:T(8,128)S(1)}, u32[]{:S(2)}, u32[]{:S(2)}) collective-permute-start(f32[4,32,128]{2,1,0:T(8,128)S(1)} %get-tuple-element.79), channel_id=1, source_target_pairs={{1,0},{2,1},{3,2},{0,3},{5,4},{6,5},{7,6},{4,7},{9,8},{10,9},{11,1... | collective-permute-start | bytes 196616 | tf_op jit(solution)/shard_map/ppermute | solution.py:552
  44.0 3.1 %collective-permute-start.15 = (f32[16,32,128]{2,1,0:T(8,128)S(1)}, f32[16,32,128]{2,1,0:T(8,128)S(1)}, u32[]{:S(2)}, u32[]{:S(2)}) collective-permute-start(f32[16,32,128]{2,1,0:T(8,128)S(1)} %get-tuple-element.85), channel_id=1, source_target_pairs={{32,0},{64,32},{96,64},{0,96},{33,1},{65,33},{97,65},{1,97},{34,2}... | collective-permute-start | bytes 786440 | tf_op jit(solution)/shard_map/ppermute | solution.py:557
  47.1 2.0 %collective-permute-start.17 = (f32[16,32,128]{2,1,0:T(8,128)S(1)}, f32[16,32,128]{2,1,0:T(8,128)S(1)}, u32[]{:S(2)}, u32[]{:S(2)}) collective-permute-start(f32[16,32,128]{2,1,0:T(8,128)S(1)} %get-tuple-element.87), channel_id=1, source_target_pairs={{4,0},{8,4},{12,8},{16,12},{20,16},{24,20},{28,24},{0,28},{5,1},{9... | collective-permute-start | bytes 786440 | tf_op jit(solution)/shard_map/ppermute | solution.py:559
  49.3 5.9 %inner_last.1 = (f32[16,16,32,128]{3,2,1,0:T(8,128)S(1)}, f32[64,128]{1,0:T(8,128)S(1)}) custom-call(f32[16,16,32,128]{3,2,1,0:T(8,128)S(1)} %get-tuple-element.78.refs_0_.refs_1_.two_ref, f32[4,32,128]{2,1,0:T(8,128)S(1)} %collective-permute-done.12.refs_1_, f32[4,32,128]{2,1,0:T(8,128)S(1)} %collective-permute-done.13.refs_2_, ...), custom_call_target="tpu_custom_call" | custom-call | flops 20971520 | bytes 25165824 | tf_op jit(solution)/shard_map/inner_last/pallas_call | solution.py:501
  55.2 1.1 %collective-permute-done.16.refs_4_ = f32[16,32,128]{2,1,0:T(8,128)S(1)} collective-permute-done((f32[16,32,128]{2,1,0:T(8,128)S(1)}, f32[16,32,128]{2,1,0:T(8,128)S(1)}, u32[]{:S(2)}, u32[]{:S(2)}) %collective-permute-start.16) | collective-permute-done | bytes 262176 | tf_op jit(solution)/shard_map/ppermute | solution.py:558
  57.1 1.2 %collective-permute-done.18 = f32[32,128]{1,0:T(8,128)S(1)} collective-permute-done((f32[32,128]{1,0:T(8,128)S(1)}, f32[32,128]{1,0:T(8,128)S(1)}, u32[]{:S(2)}, u32[]{:S(2)}) %collective-permute-start.18) | collective-permute-done | bytes 16416 | tf_op jit(solution)/shard_map/ppermute | solution.py:735
  58.3 1.3 %collective-permute-start.21 = (f32[32,128]{1,0:T(8,128)S(1)}, f32[32,128]{1,0:T(8,128)S(1)}, u32[]{:S(2)}, u32[]{:S(2)}) collective-permute-start(f32[32,128]{1,0:T(8,128)S(1)} %add.42), channel_id=1, source_target_pairs={{0,2},{1,3},{2,0},{3,1},{4,6},{5,7},{6,4},{7,5},{8,10},{9,11},{10,... | collective-permute-start | bytes 49160 | tf_op jit(solution)/shard_map/ppermute | solution.py:740
  59.5 1.5 %collective-permute-start.20 = (f32[32,128]{1,0:T(8,128)S(1)}, f32[32,128]{1,0:T(8,128)S(1)}, u32[]{:S(2)}, u32[]{:S(2)}) collective-permute-start(f32[32,128]{1,0:T(8,128)S(1)} %add.42), channel_id=1, source_target_pairs={{0,3},{1,2},{2,1},{3,0},{4,7},{5,6},{6,5},{7,4},{8,11},{9,10},{10,... | collective-permute-start | bytes 49160 | tf_op jit(solution)/shard_map/ppermute | solution.py:740
  61.0 0.8 collective-permute-start.19
  61.8 1.8 %collective-permute-done.21 = f32[32,128]{1,0:T(8,128)S(1)} collective-permute-done((f32[32,128]{1,0:T(8,128)S(1)}, f32[32,128]{1,0:T(8,128)S(1)}, u32[]{:S(2)}, u32[]{:S(2)}) %collective-permute-start.21) | collective-permute-done | bytes 16416 | tf_op jit(solution)/shard_map/ppermute | solution.py:740
  63.6 0.9 %collective-permute-done.20 = f32[32,128]{1,0:T(8,128)S(1)} collective-permute-done((f32[32,128]{1,0:T(8,128)S(1)}, f32[32,128]{1,0:T(8,128)S(1)}, u32[]{:S(2)}, u32[]{:S(2)}) %collective-permute-start.20) | collective-permute-done | bytes 16416 | tf_op jit(solution)/shard_map/ppermute | solution.py:740
  64.8 0.9 %collective-permute-start.24 = (f32[32,128]{1,0:T(8,128)S(1)}, f32[32,128]{1,0:T(8,128)S(1)}, u32[]{:S(2)}, u32[]{:S(2)}) collective-permute-start(f32[32,128]{1,0:T(8,128)S(1)} %add_add_fusion.1), channel_id=1, source_target_pairs={{0,16},{4,20},{8,24},{12,28},{16,0},{20,4},{24,8},{28,12},{1,17},{... | collective-permute-start | bytes 49160 | tf_op jit(solution)/shard_map/ppermute | solution.py:740
  65.7 1.3 %collective-permute-start.23 = (f32[32,128]{1,0:T(8,128)S(1)}, f32[32,128]{1,0:T(8,128)S(1)}, u32[]{:S(2)}, u32[]{:S(2)}) collective-permute-start(f32[32,128]{1,0:T(8,128)S(1)} %add_add_fusion.1), channel_id=1, source_target_pairs={{0,24},{4,28},{8,16},{12,20},{16,8},{20,12},{24,0},{28,4},{1,25},{... | collective-permute-start | bytes 49160 | tf_op jit(solution)/shard_map/ppermute | solution.py:740
  67.0 1.3 %collective-permute-start.22 = (f32[32,128]{1,0:T(8,128)S(1)}, f32[32,128]{1,0:T(8,128)S(1)}, u32[]{:S(2)}, u32[]{:S(2)}) collective-permute-start(f32[32,128]{1,0:T(8,128)S(1)} %add_add_fusion.1), channel_id=1, source_target_pairs={{0,8},{4,12},{8,0},{12,4},{16,24},{20,28},{24,16},{28,20},{1,9},{5... | collective-permute-start | bytes 49160 | tf_op jit(solution)/shard_map/ppermute | solution.py:740
  68.3 1.8 %collective-permute-done.24 = f32[32,128]{1,0:T(8,128)S(1)} collective-permute-done((f32[32,128]{1,0:T(8,128)S(1)}, f32[32,128]{1,0:T(8,128)S(1)}, u32[]{:S(2)}, u32[]{:S(2)}) %collective-permute-start.24) | collective-permute-done | bytes 16416 | tf_op jit(solution)/shard_map/ppermute | solution.py:740
  70.7 2.3 %collective-permute-start.27 = (f32[32,128]{1,0:T(8,128)S(1)}, f32[32,128]{1,0:T(8,128)S(1)}, u32[]{:S(2)}, u32[]{:S(2)}) collective-permute-start(f32[32,128]{1,0:T(8,128)S(1)} %add_add_fusion.refs_0_), channel_id=1, source_target_pairs={{0,64},{32,96},{64,0},{96,32},{1,65},{33,97},{65,1},{97,33},{2,66}... | collective-permute-start | bytes 49160 | tf_op jit(solution)/shard_map/ppermute | solution.py:740
  73.1 1.1 %collective-permute-start.26 = (f32[32,128]{1,0:T(8,128)S(1)}, f32[32,128]{1,0:T(8,128)S(1)}, u32[]{:S(2)}, u32[]{:S(2)}) collective-permute-start(f32[32,128]{1,0:T(8,128)S(1)} %add_add_fusion.refs_0_), channel_id=1, source_target_pairs={{0,96},{32,64},{64,32},{96,0},{1,97},{33,65},{65,33},{97,1},{2,98}... | collective-permute-start | bytes 49160 | tf_op jit(solution)/shard_map/ppermute | solution.py:740
  74.5 1.5 %collective-permute-done.27.refs_3_ = f32[32,128]{1,0:T(8,128)S(1)} collective-permute-done((f32[32,128]{1,0:T(8,128)S(1)}, f32[32,128]{1,0:T(8,128)S(1)}, u32[]{:S(2)}, u32[]{:S(2)}) %collective-permute-start.27) | collective-permute-done | bytes 16416 | tf_op jit(solution)/shard_map/ppermute | solution.py:740
  76.0 2.0 %collective-permute-done.26.refs_2_ = f32[32,128]{1,0:T(8,128)S(1)} collective-permute-done((f32[32,128]{1,0:T(8,128)S(1)}, f32[32,128]{1,0:T(8,128)S(1)}, u32[]{:S(2)}, u32[]{:S(2)}) %collective-permute-start.26) | collective-permute-done | bytes 16416 | tf_op jit(solution)/shard_map/ppermute | solution.py:740
  78.0 4.0 %solve_small.1.mix_ref = f32[64,128]{1,0:T(8,128)S(1)} custom-call(f32[32,128]{1,0:T(8,128)S(1)} %add_add_fusion.refs_0_, f32[32,128]{1,0:T(8,128)S(1)} %collective-permute-done.25.refs_1_, f32[32,128]{1,0:T(8,128)S(1)} %collective-permute-done.26.refs_2_, f32[32,128]{1,0:T(8,128)S(1)} %collective-permute-done.27.refs_3_), custom_call_target="tpu_custom_call" | custom-call | tf_op jit(solution)/shard_map/solve_small/pallas_call | solution.py:620
  82.0 5.2 %combine_fields.1 = (f32[32,16,16,128]{3,2,1,0:T(8,128)}, f32[32,16,16,128]{3,2,1,0:T(8,128)}) custom-call(f32[64,128]{1,0:T(8,128)S(1)} %solve_small.1.mix_ref, f32[16,16,32,128]{3,2,1,0:T(8,128)S(1)} %copy-done, f32[16,16,32,128]{3,2,1,0:T(8,128)S(1)} %get-tuple-element.61.refs_0_.refs_1_.one_ref, ...), custom_call_target="tpu_custom_call" | custom-call | tf_op jit(solution)/shard_map/combine_fields/pallas_call | solution.py:711
  (48 shorter events, 4.3 us)
Async XLA Ops:
  0.6 13.5 %copy-start.1 = (s32[32]{0:T(128)S(1)}, s32[32]{0:T(128)}, u32[]{:S(2)}) copy-start(s32[32]{0:T(128)} %param.6) | copy-start | bytes 388
  5.3 8.9 %collective-permute-start.1 = (f32[5,32,128]{2,1,0:T(8,128)S(1)}, f32[5,32,128]{2,1,0:T(8,128)S(1)}, u32[]{:S(2)}, u32[]{:S(2)}) collective-permute-start(f32[5,32,128]{2,1,0:T(8,128)S(1)} %get-tuple-element.48), channel_id=1, source_target_pairs={{1,0},{2,1},{3,2},{0,3},{5,4},{6,5},{7,6},{4,7},{9,8},{10,9},{11,1... | collective-permute-start | bytes 245768 | tf_op jit(solution)/shard_map/ppermute | solution.py:552
  9.5 5.7 %collective-permute-start = (f32[5,32,128]{2,1,0:T(8,128)S(1)}, f32[5,32,128]{2,1,0:T(8,128)S(1)}, u32[]{:S(2)}, u32[]{:S(2)}) collective-permute-start(f32[5,32,128]{2,1,0:T(8,128)S(1)} %get-tuple-element.48), channel_id=1, source_target_pairs={{0,1},{1,2},{2,3},{3,0},{4,5},{5,6},{6,7},{7,4},{8,9},{9,10},{10,1... | collective-permute-start | bytes 245768 | tf_op jit(solution)/shard_map/ppermute | solution.py:551
  9.5 15.7 %collective-permute-start.3 = (f32[17,32,128]{2,1,0:T(8,128)S(1)}, f32[17,32,128]{2,1,0:T(8,128)S(1)}, u32[]{:S(2)}, u32[]{:S(2)}) collective-permute-start(f32[17,32,128]{2,1,0:T(8,128)S(1)} %get-tuple-element.54.refs_1_), channel_id=1, source_target_pairs={{32,0},{64,32},{96,64},{0,96},{33,1},{65,33},{97,65},{1,97},{34,2}... | collective-permute-start | bytes 835592 | tf_op jit(solution)/shard_map/ppermute | solution.py:557
  12.3 13.0 %collective-permute-start.2 = (f32[17,32,128]{2,1,0:T(8,128)S(1)}, f32[17,32,128]{2,1,0:T(8,128)S(1)}, u32[]{:S(2)}, u32[]{:S(2)}) collective-permute-start(f32[17,32,128]{2,1,0:T(8,128)S(1)} %get-tuple-element.55.refs_2_), channel_id=1, source_target_pairs={{0,32},{32,64},{64,96},{96,0},{1,33},{33,65},{65,97},{97,1},{2,34}... | collective-permute-start | bytes 835592 | tf_op jit(solution)/shard_map/ppermute | solution.py:556
  12.3 13.0 %collective-permute-start.5 = (f32[17,32,128]{2,1,0:T(8,128)S(1)}, f32[17,32,128]{2,1,0:T(8,128)S(1)}, u32[]{:S(2)}, u32[]{:S(2)}) collective-permute-start(f32[17,32,128]{2,1,0:T(8,128)S(1)} %get-tuple-element.56.refs_3_), channel_id=1, source_target_pairs={{4,0},{8,4},{12,8},{16,12},{20,16},{24,20},{28,24},{0,28},{5,1},{9... | collective-permute-start | bytes 835592 | tf_op jit(solution)/shard_map/ppermute | solution.py:559
  15.1 10.1 %collective-permute-start.4 = (f32[17,32,128]{2,1,0:T(8,128)S(1)}, f32[17,32,128]{2,1,0:T(8,128)S(1)}, u32[]{:S(2)}, u32[]{:S(2)}) collective-permute-start(f32[17,32,128]{2,1,0:T(8,128)S(1)} %get-tuple-element.57.refs_4_), channel_id=1, source_target_pairs={{0,4},{4,8},{8,12},{12,16},{16,20},{20,24},{24,28},{28,0},{1,5},{5... | collective-permute-start | bytes 835592 | tf_op jit(solution)/shard_map/ppermute | solution.py:558
  25.7 7.4 %collective-permute-start.7 = (f32[4,32,128]{2,1,0:T(8,128)S(1)}, f32[4,32,128]{2,1,0:T(8,128)S(1)}, u32[]{:S(2)}, u32[]{:S(2)}) collective-permute-start(f32[4,32,128]{2,1,0:T(8,128)S(1)} %get-tuple-element.62), channel_id=1, source_target_pairs={{1,0},{2,1},{3,2},{0,3},{5,4},{6,5},{7,6},{4,7},{9,8},{10,9},{11,1... | collective-permute-start | bytes 196616 | tf_op jit(solution)/shard_map/ppermute | solution.py:552
  27.8 5.5 %collective-permute-start.6 = (f32[4,32,128]{2,1,0:T(8,128)S(1)}, f32[4,32,128]{2,1,0:T(8,128)S(1)}, u32[]{:S(2)}, u32[]{:S(2)}) collective-permute-start(f32[4,32,128]{2,1,0:T(8,128)S(1)} %get-tuple-element.62), channel_id=1, source_target_pairs={{0,1},{1,2},{2,3},{3,0},{4,5},{5,6},{6,7},{7,4},{8,9},{9,10},{10,1... | collective-permute-start | bytes 196616 | tf_op jit(solution)/shard_map/ppermute | solution.py:551
  27.8 12.3 %collective-permute-start.8 = (f32[16,32,128]{2,1,0:T(8,128)S(1)}, f32[16,32,128]{2,1,0:T(8,128)S(1)}, u32[]{:S(2)}, u32[]{:S(2)}) collective-permute-start(f32[16,32,128]{2,1,0:T(8,128)S(1)} %get-tuple-element.72), channel_id=1, source_target_pairs={{0,32},{32,64},{64,96},{96,0},{1,33},{33,65},{65,97},{97,1},{2,34}... | collective-permute-start | bytes 786440 | tf_op jit(solution)/shard_map/ppermute | solution.py:556
  29.3 10.8 %collective-permute-start.9 = (f32[16,32,128]{2,1,0:T(8,128)S(1)}, f32[16,32,128]{2,1,0:T(8,128)S(1)}, u32[]{:S(2)}, u32[]{:S(2)}) collective-permute-start(f32[16,32,128]{2,1,0:T(8,128)S(1)} %get-tuple-element.73), channel_id=1, source_target_pairs={{32,0},{64,32},{96,64},{0,96},{33,1},{65,33},{97,65},{1,97},{34,2}... | collective-permute-start | bytes 786440 | tf_op jit(solution)/shard_map/ppermute | solution.py:557
  31.0 9.1 %collective-permute-start.11 = (f32[16,32,128]{2,1,0:T(8,128)S(1)}, f32[16,32,128]{2,1,0:T(8,128)S(1)}, u32[]{:S(2)}, u32[]{:S(2)}) collective-permute-start(f32[16,32,128]{2,1,0:T(8,128)S(1)} %get-tuple-element.75), channel_id=1, source_target_pairs={{4,0},{8,4},{12,8},{16,12},{20,16},{24,20},{28,24},{0,28},{5,1},{9... | collective-permute-start | bytes 786440 | tf_op jit(solution)/shard_map/ppermute | solution.py:559
  33.3 7.0 %collective-permute-start.10 = (f32[16,32,128]{2,1,0:T(8,128)S(1)}, f32[16,32,128]{2,1,0:T(8,128)S(1)}, u32[]{:S(2)}, u32[]{:S(2)}) collective-permute-start(f32[16,32,128]{2,1,0:T(8,128)S(1)} %get-tuple-element.74), channel_id=1, source_target_pairs={{0,4},{4,8},{8,12},{12,16},{16,20},{20,24},{24,28},{28,0},{1,5},{5... | collective-permute-start | bytes 786440 | tf_op jit(solution)/shard_map/ppermute | solution.py:558
  41.0 8.1 %collective-permute-start.13 = (f32[4,32,128]{2,1,0:T(8,128)S(1)}, f32[4,32,128]{2,1,0:T(8,128)S(1)}, u32[]{:S(2)}, u32[]{:S(2)}) collective-permute-start(f32[4,32,128]{2,1,0:T(8,128)S(1)} %get-tuple-element.79), channel_id=1, source_target_pairs={{1,0},{2,1},{3,2},{0,3},{5,4},{6,5},{7,6},{4,7},{9,8},{10,9},{11,1... | collective-permute-start | bytes 196616 | tf_op jit(solution)/shard_map/ppermute | solution.py:552
  43.8 5.5 %collective-permute-start.12 = (f32[4,32,128]{2,1,0:T(8,128)S(1)}, f32[4,32,128]{2,1,0:T(8,128)S(1)}, u32[]{:S(2)}, u32[]{:S(2)}) collective-permute-start(f32[4,32,128]{2,1,0:T(8,128)S(1)} %get-tuple-element.79), channel_id=1, source_target_pairs={{0,1},{1,2},{2,3},{3,0},{4,5},{5,6},{6,7},{7,4},{8,9},{9,10},{10,1... | collective-permute-start | bytes 196616 | tf_op jit(solution)/shard_map/ppermute | solution.py:551
  43.8 11.3 %collective-permute-start.14 = (f32[16,32,128]{2,1,0:T(8,128)S(1)}, f32[16,32,128]{2,1,0:T(8,128)S(1)}, u32[]{:S(2)}, u32[]{:S(2)}) collective-permute-start(f32[16,32,128]{2,1,0:T(8,128)S(1)} %get-tuple-element.84), channel_id=1, source_target_pairs={{0,32},{32,64},{64,96},{96,0},{1,33},{33,65},{65,97},{97,1},{2,34}... | collective-permute-start | bytes 786440 | tf_op jit(solution)/shard_map/ppermute | solution.py:556
  44.0 11.2 %collective-permute-start.15 = (f32[16,32,128]{2,1,0:T(8,128)S(1)}, f32[16,32,128]{2,1,0:T(8,128)S(1)}, u32[]{:S(2)}, u32[]{:S(2)}) collective-permute-start(f32[16,32,128]{2,1,0:T(8,128)S(1)} %get-tuple-element.85), channel_id=1, source_target_pairs={{32,0},{64,32},{96,64},{0,96},{33,1},{65,33},{97,65},{1,97},{34,2}... | collective-permute-start | bytes 786440 | tf_op jit(solution)/shard_map/ppermute | solution.py:557
  47.1 8.1 %collective-permute-start.17 = (f32[16,32,128]{2,1,0:T(8,128)S(1)}, f32[16,32,128]{2,1,0:T(8,128)S(1)}, u32[]{:S(2)}, u32[]{:S(2)}) collective-permute-start(f32[16,32,128]{2,1,0:T(8,128)S(1)} %get-tuple-element.87), channel_id=1, source_target_pairs={{4,0},{8,4},{12,8},{16,12},{20,16},{24,20},{28,24},{0,28},{5,1},{9... | collective-permute-start | bytes 786440 | tf_op jit(solution)/shard_map/ppermute | solution.py:559
  49.3 7.0 %collective-permute-start.16 = (f32[16,32,128]{2,1,0:T(8,128)S(1)}, f32[16,32,128]{2,1,0:T(8,128)S(1)}, u32[]{:S(2)}, u32[]{:S(2)}) collective-permute-start(f32[16,32,128]{2,1,0:T(8,128)S(1)} %get-tuple-element.86), channel_id=1, source_target_pairs={{0,4},{4,8},{8,12},{12,16},{16,20},{20,24},{24,28},{28,0},{1,5},{5... | collective-permute-start | bytes 786440 | tf_op jit(solution)/shard_map/ppermute | solution.py:558
  56.3 25.7 %copy-start = (f32[16,16,32,128]{3,2,1,0:T(8,128)S(1)}, f32[16,16,32,128]{3,2,1,0:T(8,128)}, u32[]{:S(2)}) copy-start(f32[16,16,32,128]{3,2,1,0:T(8,128)} %get-tuple-element.47.away.guess_ref) | copy-start | bytes 12582916
  57.0 1.2 %collective-permute-start.18 = (f32[32,128]{1,0:T(8,128)S(1)}, f32[32,128]{1,0:T(8,128)S(1)}, u32[]{:S(2)}, u32[]{:S(2)}) collective-permute-start(f32[32,128]{1,0:T(8,128)S(1)} %get-tuple-element.90), channel_id=1, source_target_pairs={{0,4},{4,0},{8,12},{12,8},{16,20},{20,16},{24,28},{28,24},{1,5},{5... | collective-permute-start | bytes 49160 | tf_op jit(solution)/shard_map/ppermute | solution.py:735
  58.3 5.3 %collective-permute-start.21 = (f32[32,128]{1,0:T(8,128)S(1)}, f32[32,128]{1,0:T(8,128)S(1)}, u32[]{:S(2)}, u32[]{:S(2)}) collective-permute-start(f32[32,128]{1,0:T(8,128)S(1)} %add.42), channel_id=1, source_target_pairs={{0,2},{1,3},{2,0},{3,1},{4,6},{5,7},{6,4},{7,5},{8,10},{9,11},{10,... | collective-permute-start | bytes 49160 | tf_op jit(solution)/shard_map/ppermute | solution.py:740
  59.5 4.9 %collective-permute-start.20 = (f32[32,128]{1,0:T(8,128)S(1)}, f32[32,128]{1,0:T(8,128)S(1)}, u32[]{:S(2)}, u32[]{:S(2)}) collective-permute-start(f32[32,128]{1,0:T(8,128)S(1)} %add.42), channel_id=1, source_target_pairs={{0,3},{1,2},{2,1},{3,0},{4,7},{5,6},{6,5},{7,4},{8,11},{9,10},{10,... | collective-permute-start | bytes 49160 | tf_op jit(solution)/shard_map/ppermute | solution.py:740
  61.0 3.7 %collective-permute-start.19 = (f32[32,128]{1,0:T(8,128)S(1)}, f32[32,128]{1,0:T(8,128)S(1)}, u32[]{:S(2)}, u32[]{:S(2)}) collective-permute-start(f32[32,128]{1,0:T(8,128)S(1)} %add.42), channel_id=1, source_target_pairs={{0,1},{1,0},{2,3},{3,2},{4,5},{5,4},{6,7},{7,6},{8,9},{9,8},{10,11... | collective-permute-start | bytes 49160 | tf_op jit(solution)/shard_map/ppermute | solution.py:740
  64.8 5.2 %collective-permute-start.24 = (f32[32,128]{1,0:T(8,128)S(1)}, f32[32,128]{1,0:T(8,128)S(1)}, u32[]{:S(2)}, u32[]{:S(2)}) collective-permute-start(f32[32,128]{1,0:T(8,128)S(1)} %add_add_fusion.1), channel_id=1, source_target_pairs={{0,16},{4,20},{8,24},{12,28},{16,0},{20,4},{24,8},{28,12},{1,17},{... | collective-permute-start | bytes 49160 | tf_op jit(solution)/shard_map/ppermute | solution.py:740
  65.7 5.0 %collective-permute-start.23 = (f32[32,128]{1,0:T(8,128)S(1)}, f32[32,128]{1,0:T(8,128)S(1)}, u32[]{:S(2)}, u32[]{:S(2)}) collective-permute-start(f32[32,128]{1,0:T(8,128)S(1)} %add_add_fusion.1), channel_id=1, source_target_pairs={{0,24},{4,28},{8,16},{12,20},{16,8},{20,12},{24,0},{28,4},{1,25},{... | collective-permute-start | bytes 49160 | tf_op jit(solution)/shard_map/ppermute | solution.py:740
  67.0 3.7 %collective-permute-start.22 = (f32[32,128]{1,0:T(8,128)S(1)}, f32[32,128]{1,0:T(8,128)S(1)}, u32[]{:S(2)}, u32[]{:S(2)}) collective-permute-start(f32[32,128]{1,0:T(8,128)S(1)} %add_add_fusion.1), channel_id=1, source_target_pairs={{0,8},{4,12},{8,0},{12,4},{16,24},{20,28},{24,16},{28,20},{1,9},{5... | collective-permute-start | bytes 49160 | tf_op jit(solution)/shard_map/ppermute | solution.py:740
  70.7 5.3 %collective-permute-start.27 = (f32[32,128]{1,0:T(8,128)S(1)}, f32[32,128]{1,0:T(8,128)S(1)}, u32[]{:S(2)}, u32[]{:S(2)}) collective-permute-start(f32[32,128]{1,0:T(8,128)S(1)} %add_add_fusion.refs_0_), channel_id=1, source_target_pairs={{0,64},{32,96},{64,0},{96,32},{1,65},{33,97},{65,1},{97,33},{2,66}... | collective-permute-start | bytes 49160 | tf_op jit(solution)/shard_map/ppermute | solution.py:740
  73.1 4.9 %collective-permute-start.26 = (f32[32,128]{1,0:T(8,128)S(1)}, f32[32,128]{1,0:T(8,128)S(1)}, u32[]{:S(2)}, u32[]{:S(2)}) collective-permute-start(f32[32,128]{1,0:T(8,128)S(1)} %add_add_fusion.refs_0_), channel_id=1, source_target_pairs={{0,96},{32,64},{64,32},{96,0},{1,97},{33,65},{65,33},{97,1},{2,98}... | collective-permute-start | bytes 49160 | tf_op jit(solution)/shard_map/ppermute | solution.py:740
  74.1 3.9 %collective-permute-start.25 = (f32[32,128]{1,0:T(8,128)S(1)}, f32[32,128]{1,0:T(8,128)S(1)}, u32[]{:S(2)}, u32[]{:S(2)}) collective-permute-start(f32[32,128]{1,0:T(8,128)S(1)} %add_add_fusion.refs_0_), channel_id=1, source_target_pairs={{0,32},{32,0},{64,96},{96,64},{1,33},{33,1},{65,97},{97,65},{2,34}... | collective-permute-start | bytes 49160 | tf_op jit(solution)/shard_map/ppermute | solution.py:740
